TPU v7x, 32 devices: a whole 2x2x4 slice. The times are simulated.
32 devices in a mesh: gx: 4 (over x, core), gy: 4 (over z), gz: 2 (over y).
Axes of the slice: x: 2, y: 2, z: 4, core: 2. Of those that a mesh axis runs over, the one named last changes fastest.
Arguments:
- parts: float32 [52, 52, 14, 128], P('gx', 'gy', 'gz'), may hold values from -6 to 6
- cell_matrix: bfloat16 [343, 343], replicated, may hold values from -0.2 to 2
- cell_potential: float32 [343, 8, 8, 2], P(None, 'gx', 'gy', 'gz'), may hold values from 0 to 1
- projectors: bfloat16 [4, 4, 2, 343, 1536], P('gx', 'gy', 'gz'), may hold values from -0.15625 to 0.15625
- slot_atom: int32 [4, 4, 2, 32], P('gx', 'gy'), may hold values from -1 to 63, as said below
- slot_cells: int32 [4, 4, 2, 32, 4], P('gx', 'gy', 'gz'), may hold values from 0 to 3
- coupling: float32 [1024, 12, 12], P(('gx', 'gy')), may hold values from -1.75 to 1.75
Outputs:
- filtered: float32 [52, 52, 14, 128], P('gx', 'gy', 'gz')
Inputs may be any that keep to these rules, and one draw needn't show every extreme that they name: `slot_atom`: entry s of partition (i, j, k) is -1 (an empty slot) or the number, within the column (i, j), of an atom whose projectors reach into that partition. Slots c * 16 to c * 16 + 15 of every partition hold only atoms numbered c * 32 to c * 32 + 31, which are owned by partition c of the column along gz. An atom stands at most once in one partition's list.
All inputs are finite; a program needn't handle non-finite values.
Results may differ from a plain program's by a relative error of at most 0.0058.
Values may be sent and summed in bfloat16 or wider, within the bound.
No kernel may reach another device: no remote copies, remote signals or barrier semaphores. Data moves between devices by JAX's collectives and lax.ppermute only.
A program may use at most 64 MiB of HBM per device.

v0:
```python
import functools

import jax
import jax.numpy as jnp
import numpy as np
from jax import lax
from jax.experimental import pallas as pl
from jax.experimental.pallas import tpu as pltpu
from jax.sharding import PartitionSpec as P

ORDER = 6
STEPS = 3
PA = 12
POS = 32
BLK = 4

center_value = 2.0
half_width = 3.0

EDGE = ORDER + 1
PAD = 8
SLOTS = POS * PA
F32 = jnp.float32
BF16 = jnp.bfloat16
HALO = jnp.bfloat16


def up(value, multiple):
    return -(-value // multiple) * multiple


class Sizes:
    def __init__(self, nx, ny, nz, orbitals, links):
        assert nz == EDGE
        self.nx, self.ny, self.orb = nx, ny, orbitals
        self.cells = [(p, q) for p in range((nx - 1) // ORDER) for q in range((ny - 1) // ORDER)]
        self.rows = nx * ny * PAD
        self.line_x = ny * PAD
        self.xface = up(ny * PAD, 16)
        self.yface = up(nx * PAD, 16)
        self.face_b = up(ny, PAD)
        self.zface = up(nx * self.face_b, 16)
        self.cell_rows = EDGE * EDGE * PAD
        self.cell_pad = up(self.cell_rows, 16)
        self.all_pad = up(self.cell_pad * len(self.cells), 128)
        self.fcell = EDGE * PAD
        self.fall = up(self.fcell * len(self.cells), 256)
        self.links = links
        self.spill = 2 * PAD * PAD


VMEM = pl.BlockSpec(memory_space=pltpu.VMEM)
SMEM = pl.BlockSpec(memory_space=pltpu.SMEM)


def kernel_call(body, outs, scalars, arrays, scratch=(), flops=0, limit=24 << 20):
    nbytes = sum(int(np.prod(a.shape)) * a.dtype.itemsize for a in list(arrays) + list(outs))
    return pl.pallas_call(
        body,
        out_shape=outs,
        in_specs=[SMEM] * len(scalars) + [VMEM] * len(arrays),
        out_specs=[VMEM] * len(outs),
        scratch_shapes=list(scratch),
        compiler_params=pltpu.CompilerParams(vmem_limit_bytes=limit),
        cost_estimate=pl.CostEstimate(flops=flops, bytes_accessed=nbytes, transcendentals=0),
    )(*scalars, *arrays)


def shape(rows, cols, dtype):
    return jax.ShapeDtypeStruct((rows, cols), dtype)


def dot(a, b):
    return jnp.dot(a, b, preferred_element_type=F32)


def matrices_body(sz, proj, row_key, face_key, col_key, qt, *qt_faces):
    nodes = proj.shape[0]
    keys = jnp.concatenate([row_key[...]] + [f[...] for f in face_key], axis=0)
    expand = (keys == lax.broadcasted_iota(jnp.int32, (keys.shape[0], nodes), 1)).astype(BF16)
    spread = dot(expand, proj[...]).astype(BF16)
    cols = proj.shape[1]
    key = col_key[...]
    for g in range(len(sz.cells)):
        pick = (key == lax.broadcasted_iota(jnp.int32, (cols, SLOTS), 1) + g * SLOTS).astype(BF16)
        block = dot(spread, pick).astype(BF16)
        qt[g * sz.cell_pad : (g + 1) * sz.cell_pad, :] = block[: sz.cell_pad]
        for j, qf in enumerate(qt_faces):
            at = sz.cell_pad + j * PAD * PAD
            qf[g * PAD * PAD : (g + 1) * PAD * PAD, :] = block[at : at + PAD * PAD]
    rest = sz.all_pad - sz.cell_pad * len(sz.cells)
    if rest:
        qt[sz.cell_pad * len(sz.cells) :, :] = jnp.zeros((rest, SLOTS), BF16)


def make_matrices(sz, proj, row_key, face_keys, col_key):
    count = len(face_keys)

    def body(*refs):
        proj_r, row_r = refs[0], refs[1]
        faces = refs[2 : 2 + count]
        matrices_body(sz, proj_r, row_r, faces, refs[2 + count], *refs[3 + count :])

    outs = [shape(sz.all_pad, SLOTS, BF16)]
    outs += [shape(len(sz.cells) * PAD * PAD, SLOTS, BF16)] * count
    return kernel_call(
        body, outs, [], [proj, row_key, *face_keys, col_key], flops=3 * 10**9, limit=32 << 20
    )


def turn_body(sz, qt, kin, pot, row_key, lane_key, q, kout, vout):
    q[...] = qt[...].T
    nodes = kin.shape[0]
    expand = row_key[...] == lax.broadcasted_iota(jnp.int32, (sz.cell_pad, nodes), 1)
    gather = lane_key[...] == lax.broadcasted_iota(jnp.int32, (nodes, sz.cell_pad), 0)
    tall = dot(expand.astype(BF16), kin[...]).astype(BF16)
    kout[...] = dot(tall, gather.astype(BF16)).astype(BF16)
    values = jnp.dot(
        expand.astype(F32), pot[...], precision=lax.Precision.HIGHEST, preferred_element_type=F32
    )
    for g in range(len(sz.cells)):
        vout[g * sz.cell_pad : (g + 1) * sz.cell_pad, :] = jnp.broadcast_to(
            values[:, g : g + 1], (sz.cell_pad, sz.orb)
        )


def turn_matrices(sz, qt, kin, pot, row_key, lane_key):
    outs = [
        shape(SLOTS, sz.all_pad, BF16),
        shape(sz.cell_pad, sz.cell_pad, BF16),
        shape(len(sz.cells) * sz.cell_pad, sz.orb, F32),
    ]
    return kernel_call(
        functools.partial(turn_body, sz), outs, [], [qt, kin, pot, row_key, lane_key], flops=10**9
    )


def cell_block(sz, z, cell):
    p, q = cell
    layers = []
    for a in range(EDGE):
        start = (ORDER * p + a) * sz.line_x + ORDER * q * PAD
        layers.append(z[start : start + EDGE * PAD, :])
    layers.append(jnp.zeros((sz.cell_pad - sz.cell_rows, sz.orb), F32))
    return jnp.concatenate(layers, axis=0)


def write_faces(sz, r, sx_lo, sx_hi, sy_lo, sy_hi):
    pad_x = jnp.zeros((sz.xface - sz.line_x, sz.orb), F32)
    pad_y = jnp.zeros((sz.yface - sz.nx * PAD, sz.orb), F32)
    last = (sz.nx - 1) * sz.line_x
    sx_lo[...] = jnp.concatenate([r[0 : sz.line_x, :], pad_x], axis=0).astype(HALO)
    sx_hi[...] = jnp.concatenate([r[last : last + sz.line_x, :], pad_x], axis=0).astype(HALO)
    for out, b in ((sy_lo, 0), (sy_hi, sz.ny - 1)):
        rows = [r[a * sz.line_x + b * PAD : a * sz.line_x + (b + 1) * PAD, :] for a in range(sz.nx)]
        out[...] = jnp.concatenate(rows + [pad_y], axis=0)


def face_outs(sz):
    return [shape(sz.xface, sz.orb, HALO)] * 2 + [shape(sz.yface, sz.orb, F32)] * 2


def start_body(sz, parts, r4, sx_lo, sx_hi, sy_lo, sy_hi):
    nz = parts.shape[2]
    r4[...] = jnp.zeros(r4.shape, F32)
    r4[:, :, :nz, :] = parts[...]
    r = r4.reshape(sz.rows, sz.orb)
    write_faces(sz, r, sx_lo, sx_hi, sy_lo, sy_hi)


def start_faces(sz, parts):
    outs = [jax.ShapeDtypeStruct((sz.nx, sz.ny, PAD, sz.orb), F32)] + face_outs(sz)
    r4, *faces = kernel_call(functools.partial(start_body, sz), outs, [], [parts])
    return r4.reshape(sz.rows, sz.orb), faces


def cross_body(sz, xr_lo, xr_hi, ry_lo, ry_hi, sy_lo, sy_hi):
    last = (sz.nx - 1) * PAD
    lo, hi = xr_lo[...].astype(F32), xr_hi[...].astype(F32)
    for raw, out, b in ((ry_lo, sy_lo, 0), (ry_hi, sy_hi, sz.ny - 1)):
        value = raw[...]
        value = jnp.concatenate(
            [
                value[:PAD] + lo[b * PAD : (b + 1) * PAD],
                value[PAD:last],
                value[last : last + PAD] + hi[b * PAD : (b + 1) * PAD],
                value[last + PAD :],
            ],
            axis=0,
        )
        out[...] = value.astype(HALO)


def cross_faces(sz, xr_lo, xr_hi, ry_lo, ry_hi):
    outs = [shape(sz.yface, sz.orb, HALO)] * 2
    return kernel_call(functools.partial(cross_body, sz), outs, [], [xr_lo, xr_hi, ry_lo, ry_hi])


def add_xy(sz, ra, r, xr_lo, xr_hi, yr_lo, yr_hi):
    ra[0 : sz.rows, :] = r[...]
    last = (sz.nx - 1) * sz.line_x
    ra[0 : sz.line_x, :] += xr_lo[...].astype(F32)[: sz.line_x]
    ra[last : last + sz.line_x, :] += xr_hi[...].astype(F32)[: sz.line_x]
    for recv, b in ((yr_lo, 0), (yr_hi, sz.ny - 1)):
        value = recv[...].astype(F32)
        for a in range(sz.nx):
            at = a * sz.line_x + b * PAD
            ra[at : at + PAD, :] += value[a * PAD : (a + 1) * PAD]


def pack_z(sz, ra, c, valid):
    rows = []
    for a in range(sz.nx):
        for b in range(0, sz.face_b, PAD):
            rows.append(ra[pl.ds(a * sz.line_x + b * PAD + c, PAD, stride=PAD), :])
    rest = sz.zface - sz.nx * sz.face_b
    if rest:
        rows.append(jnp.zeros((rest, sz.orb), F32))
    return (jnp.concatenate(rows, axis=0) * valid).astype(HALO)


def add_z(sz, y, c, face):
    for a in range(sz.nx):
        for b in range(0, sz.ny, PAD):
            n = min(PAD, sz.ny - b)
            at = pl.ds(a * sz.line_x + b * PAD + c, n, stride=PAD)
            y[at, :] = y[at, :] + face[a * sz.face_b + b : a * sz.face_b + b + n]


def face_cells(sz, ra, c):
    rows = []
    for p, q in sz.cells:
        for a in range(EDGE):
            at = (ORDER * p + a) * sz.line_x + ORDER * q * PAD
            rows.append(ra[pl.ds(at + c, PAD, stride=PAD), :])
        rows.append(jnp.zeros((PAD, sz.orb), F32))
    return jnp.concatenate(rows, axis=0).astype(BF16)


def project_body(sz, shifts, has_local, refs):
    take = iter(refs)
    info = next(take)
    r = next(take)
    loc = next(take) if has_local else None
    halos = [next(take) for _ in range(4)]
    q = next(take)
    qfaces = [next(take) for _ in range(sz.links)]
    maps = next(take)
    y, own = next(take), next(take)
    messages = [next(take) for _ in range(shifts)]
    ra = next(take)
    ra[sz.rows :, :] = jnp.zeros((sz.spill, sz.orb), F32)
    add_xy(sz, ra, r, *halos)
    y[...] = ra[0 : sz.rows, :] + loc[...] if has_local else ra[0 : sz.rows, :]
    blocks = [cell_block(sz, y, cell).astype(BF16) for cell in sz.cells]
    rest = sz.all_pad - sz.cell_pad * len(sz.cells)
    if rest:
        blocks.append(jnp.zeros((rest, sz.orb), BF16))
    sums = [dot(q[...], jnp.concatenate(blocks, axis=0)).astype(BF16)]
    for j in range(sz.links):
        sums.append(dot(qfaces[j][...], face_cells(sz, ra, info[0, j])).astype(BF16))
    known = jnp.concatenate(sums, axis=0)
    mapped = dot(maps[...], known)
    own[...] = mapped[:SLOTS]
    link_of = link_shifts(sz, shifts)
    for s, message in enumerate(messages):
        message[0:SLOTS, :] = mapped[(s + 1) * SLOTS : (s + 2) * SLOTS].astype(HALO)
        for j, shift in enumerate(link_of):
            if shift == s + 1:
                face = pack_z(sz, ra, info[0, j], info[1, j].astype(F32))
                message[SLOTS : SLOTS + sz.zface, :] = face


def link_shifts(sz, shifts):
    return [1, shifts][: sz.links]


def project(sz, shifts, info, r, loc, halos, q, qfaces, maps):
    outs = [shape(sz.rows, sz.orb, F32), shape(SLOTS, sz.orb, F32)]
    for s in range(1, shifts + 1):
        rows = SLOTS + (sz.zface if s in link_shifts(sz, shifts) else 0)
        outs.append(shape(rows, sz.orb, HALO))
    arrays = [r] + ([loc] if loc is not None else []) + list(halos) + [q, *qfaces, maps]

    def body(*refs):
        project_body(sz, shifts, loc is not None, refs)

    limit = (32 << 20) if maps.size < 10**7 else (56 << 20)
    y, own, *messages = kernel_call(
        body,
        outs,
        [info],
        arrays,
        scratch=[pltpu.VMEM((sz.rows + sz.spill, sz.orb), F32)],
        flops=4 * 10**8,
        limit=limit,
    )
    return y, own, messages


def apply_body(sz, shifts, has_previous, scale, keep, refs):
    take = iter(refs)
    info = next(take)
    yin = next(take)
    previous = next(take) if has_previous else None
    own = next(take)
    messages = [next(take) for _ in range(shifts)]
    cblk, qt, kin, pot = next(take), next(take), next(take), next(take)
    r, loc, y = next(take), next(take), next(take)
    faces = [next(take) for _ in range(4)]
    totals = own[...]
    for message in messages:
        totals = totals + message[0:SLOTS, :].astype(F32)
    coef = dot(cblk[...], totals.astype(BF16)).astype(BF16)
    y[...] = yin[...]
    for j, shift in enumerate(link_shifts(sz, shifts)):
        add_z(sz, y, info[2, j], messages[shift - 1][SLOTS : SLOTS + sz.zface, :].astype(F32))
    blocks = [cell_block(sz, y, cell) for cell in sz.cells]
    stiff = dot(kin[...], jnp.concatenate([b.astype(BF16) for b in blocks], axis=1))
    r[...] = jnp.zeros(r.shape, F32)
    for g, (p, q) in enumerate(sz.cells):
        rows = slice(g * sz.cell_pad, (g + 1) * sz.cell_pad)
        value = stiff[:, g * sz.orb : (g + 1) * sz.orb] + pot[rows, :] * blocks[g]
        value = (value + dot(qt[rows, :], coef)) * scale
        for a in range(EDGE):
            start = (ORDER * p + a) * sz.line_x + ORDER * q * PAD
            r[start : start + EDGE * PAD, :] += value[a * EDGE * PAD : (a + 1) * EDGE * PAD]
    local = (-center_value * scale) * y[...]
    loc[...] = local - previous[...] if has_previous else local
    write_faces(sz, r, *faces)


def apply(sz, shifts, info, y, previous, own, messages, cblk, qt, kin, pot, scale):
    outs = [shape(sz.rows, sz.orb, F32)] * 3 + face_outs(sz)
    arrays = [y] + ([previous] if previous is not None else [])
    arrays += [own, *messages, cblk, qt, kin, pot]

    def body(*refs):
        apply_body(sz, shifts, previous is not None, scale, True, refs)

    r, loc, y, *faces = kernel_call(body, outs, [info], arrays, flops=6 * 10**8, limit=32 << 20)
    return r, loc, y, faces


def last_faces_body(sz, refs):
    take = iter(refs)
    info, r = next(take), next(take)
    halos = [next(take) for _ in range(4)]
    outs = [next(take) for _ in range(sz.links)]
    ra = next(take)
    ra[sz.rows :, :] = jnp.zeros((sz.spill, sz.orb), F32)
    add_xy(sz, ra, r, *halos)
    for j, out in enumerate(outs):
        out[...] = pack_z(sz, ra, info[0, j], info[1, j].astype(F32))


def last_faces(sz, info, r, halos):
    def body(*refs):
        last_faces_body(sz, refs)

    outs = [shape(sz.zface, sz.orb, HALO)] * sz.links
    scratch = [pltpu.VMEM((sz.rows + sz.spill, sz.orb), F32)]
    return kernel_call(body, outs, [info], [r, *halos], scratch=scratch)


def finish_body(sz, refs):
    take = iter(refs)
    info, r, loc = next(take), next(take), next(take)
    halos = [next(take) for _ in range(4)]
    zr = [next(take) for _ in range(sz.links)]
    out, ra = next(take), next(take)
    add_xy(sz, ra, r, *halos)
    for j, face in enumerate(zr):
        add_z(sz, ra, info[2, j], face[...].astype(F32))
    value = ra[0 : sz.rows, :] + loc[...]
    out[...] = value.reshape(sz.nx, sz.ny, PAD, sz.orb)[:, :, : out.shape[2], :]


def finish(sz, info, r, loc, halos, zr, nz):
    def body(*refs):
        finish_body(sz, refs)

    outs = [jax.ShapeDtypeStruct((sz.nx, sz.ny, nz, sz.orb), F32)]
    scratch = [pltpu.VMEM((sz.rows + sz.spill, sz.orb), F32)]
    return kernel_call(body, outs, [info], [r, loc, *halos, *zr], scratch=scratch)[0]


def swap_faces(axis, lo, hi):
    count = lax.axis_size(axis)
    forward = [(i, i + 1) for i in range(count - 1)]
    backward = [(target, source) for source, target in forward]
    return lax.ppermute(hi, axis, forward), lax.ppermute(lo, axis, backward)


def local(parts, cell_matrix, cell_potential, projectors, slot_atom, slot_cells, coupling):
    nx, ny, nz, orbitals = parts.shape
    nodes = cell_matrix.shape[0]
    devices = lax.axis_size("gz")
    shifts = devices - 1
    me = lax.axis_index("gz")
    links = min(2, shifts)
    sz = Sizes(nx, ny, nz, orbitals, links)
    cells = len(sz.cells)

    if devices == 2:
        layer = jnp.where(me == 0, ORDER, 0)
        info = jnp.stack([layer, jnp.ones_like(layer), layer])[:, None]
    else:
        send = jnp.array([ORDER, 0], jnp.int32)
        valid = jnp.stack([me < devices - 1, me > 0]).astype(jnp.int32)
        info = jnp.stack([send, valid, ORDER - send])
    info = info.astype(jnp.int32)
    ring = [[(i, (i + s) % devices) for i in range(devices)] for s in range(devices)]

    i = np.arange(sz.cell_pad)
    real = (i < sz.cell_rows) & (i % PAD < EDGE)
    node = np.where(real, i // PAD * EDGE + i % PAD, -1).astype(np.int32)
    row_key, lane_key = jnp.asarray(node[:, None]), jnp.asarray(node[None, :])
    i = np.arange(PAD * PAD)
    real = (i < sz.fcell) & (i % PAD < EDGE)
    base = np.where(real, (i // PAD * EDGE + i % PAD) * EDGE, -EDGE * PAD).astype(np.int32)
    face_keys = [jnp.asarray(base[:, None]) + info[2, j] for j in range(links)]
    i = np.arange(POS * BLK * PA)
    slot_row = (i // (BLK * PA) * PA + i % PA).astype(np.int32)
    cell_index = jnp.repeat(slot_cells.reshape(POS * BLK), PA)
    col_key = (cell_index * SLOTS + slot_row)[:, None]

    table = slot_atom.reshape(devices, POS)
    rotated = [table[(me + s) % devices] for s in range(devices)]

    def atom_keys(atoms, empty):
        offset = np.arange(PA, dtype=np.int32)
        keys = jnp.where(atoms[:, None] >= 0, atoms[:, None] * PA + offset, empty)
        return keys.reshape(SLOTS)

    known = [atom_keys(rotated[0], -2)]
    for j, shift in enumerate(link_shifts(sz, shifts)):
        known.append(jnp.where(info[1, j] > 0, atom_keys(rotated[shift], -2), -2))
    known = jnp.concatenate(known)
    wanted = jnp.concatenate([atom_keys(atoms, -1) for atoms in rotated])
    maps = (wanted[:, None] == known[None, :]).astype(BF16)
    picked = jnp.take(coupling, jnp.clip(rotated[0], 0, coupling.shape[0] - 1), axis=0)
    picked = jnp.where(rotated[0][:, None, None] >= 0, picked, 0.0).astype(BF16)
    eye = jnp.eye(POS, dtype=BF16)
    cblk = (picked[:, :, None, :] * eye[:, None, :, None]).reshape(SLOTS, SLOTS)

    r, (sx_lo, sx_hi, sy_lo, sy_hi) = start_faces(sz, parts)

    def exchange_xy(sx_lo, sx_hi, sy_lo, sy_hi):
        xr = swap_faces("gx", sx_lo, sx_hi)
        cross = cross_faces(sz, *xr, sy_lo, sy_hi)
        yr = swap_faces("gy", *cross)
        return (*xr, *yr)

    halos = exchange_xy(sx_lo, sx_hi, sy_lo, sy_hi)
    qt, *qt_faces = make_matrices(
        sz, projectors.reshape(nodes, POS * BLK * PA), row_key, face_keys, col_key
    )
    qfaces = []
    for j, shift in enumerate(link_shifts(sz, shifts)):
        back = [(target, source) for source, target in ring[shift]]
        qfaces.append(lax.ppermute(qt_faces[j], "gz", back).T)
    q, kin, pot = turn_matrices(
        sz, qt, cell_matrix, cell_potential.reshape(nodes, cells), row_key, lane_key
    )

    loc = previous = None
    scale = 1.0 / half_width
    for step in range(STEPS):
        y, own, messages = project(sz, shifts, info, r, loc, halos, q, qfaces, maps)
        received = [lax.ppermute(m, "gz", ring[s + 1]) for s, m in enumerate(messages)]
        r, loc, y, faces = apply(
            sz, shifts, info, y, previous, own, received, cblk, qt, kin, pot, scale
        )
        previous, scale = y, 2.0 / half_width
        halos = exchange_xy(*faces)
    sent = last_faces(sz, info, r, halos)
    zr = [lax.ppermute(f, "gz", ring[s]) for f, s in zip(sent, link_shifts(sz, shifts))]
    return finish(sz, info, r, loc, halos, zr, nz)


def solution(mesh):
    in_specs = (
        P("gx", "gy", "gz", None),
        P(),
        P(None, "gx", "gy", "gz"),
        P("gx", "gy", "gz", None, None),
        P("gx", "gy", None, None),
        P("gx", "gy", "gz", None, None),
        P(("gx", "gy"), None, None),
    )
    out_specs = P("gx", "gy", "gz", None)
    return jax.shard_map(local, mesh=mesh, in_specs=in_specs, out_specs=out_specs, check_vma=False)
```

profile of v0, /device:TPU:0, one launch (start us, length us, event | category | flops | bytes accessed | tf_op | source)
XLA Modules:
  0.0 133.0 jit_solution(5762751164159917054)
XLA Ops:
  0.0 0.7 broadcast_multiply_fusion.1
  0.9 0.9 broadcast_add_fusion
  2.1 0.8 broadcast_add_fusion.1.refs_2_
  2.8 1.2 copy-done.16
  4.1 0.9 copy-done.18
  5.0 3.9 %shard_map.147 = (bf16[1664,384]{1,0:T(8,128)(2,1)S(1)}, bf16[256,384]{1,0:T(8,128)(2,1)S(1)}) custom-call(bf16[343,1536]{1,0:T(8,128)(2,1)S(1)} %bitcast.30, s32[400,1]{1,0:T(8,128)S(1)} %copy-done.18, s32[64,1]{1,0:T(8,128)S(1)} %broadcast_add_fusion.1.refs_2_, s32[1536,1]{1,0:T(8,128)S(1)} %broadcast_in_dim.80.refs_3_), custom_call_target="tpu_custom_call" | custom-call | flops 3000000000 | bytes 2536256 | tf_op jit(solution)/shard_map/pallas_call | solution.py:58
  8.9 0.8 copy.45
  9.8 3.0 %collective-permute-start.4 = (bf16[256,384]{0,1:T(8,128)(2,1)}, bf16[256,384]{0,1:T(8,128)(2,1)S(1)}, u32[]{:S(2)}, u32[]{:S(2)}) collective-permute-start(bf16[256,384]{0,1:T(8,128)(2,1)} %copy.45), channel_id=1, source_target_pairs={{1,0},{0,1},{3,2},{2,3},{5,4},{4,5},{7,6},{6,7},{9,8},{8,9},{11,10... | collective-permute-start | bytes 589832 | tf_op jit(solution)/shard_map/ppermute | solution.py:462
  12.7 0.7 shard_map.145
  13.5 0.8 copy-done.10
  14.3 1.4 %collective-permute-start = (bf16[112,128]{1,0:T(8,128)(2,1)}, bf16[112,128]{1,0:T(8,128)(2,1)S(1)}, u32[]{:S(2)}, u32[]{:S(2)}) collective-permute-start(bf16[112,128]{1,0:T(8,128)(2,1)} %get-tuple-element.53), channel_id=1, source_target_pairs={{0,8},{8,16},{16,24},{1,9},{9,17},{17,25},{2,10},{10,18},{18,26},{... | collective-permute-start | bytes 86024 | tf_op jit(solution)/shard_map/ppermute | solution.py:392
  15.8 1.3 collective-permute-start.1
  18.8 0.8 select_convert_fusion
  19.9 0.8 copy.44.pot
  21.4 4.1 %collective-permute-start.2 = (bf16[112,128]{1,0:T(8,128)(2,1)}, bf16[112,128]{1,0:T(8,128)(2,1)}, u32[]{:S(2)}, u32[]{:S(2)}) collective-permute-start(bf16[112,128]{1,0:T(8,128)(2,1)} %get-tuple-element.57), channel_id=1, source_target_pairs={{0,2},{2,4},{4,6},{1,3},{3,5},{5,7},{8,10},{10,12},{12,14},{9,11},... | collective-permute-start | bytes 86024 | tf_op jit(solution)/shard_map/ppermute | solution.py:392
  25.5 1.3 collective-permute-start.3
  26.8 0.9 copy-done.15
  27.7 0.9 copy-done.17
  28.6 0.9 copy-done.19
  29.6 1.6 %shard_map.148 = (bf16[384,1664]{1,0:T(8,128)(2,1)S(1)}, bf16[400,400]{1,0:T(8,128)(2,1)S(1)}, f32[1600,128]{1,0:T(8,128)S(1)}) custom-call(bf16[1664,384]{1,0:T(8,128)(2,1)S(1)} %get-tuple-element.59.qt.refs_5_.refs_6_, bf16[343,343]{1,0:T(8,128)(2,1)S(1)} %copy-done.17, f32[343,4]{1,0:T(8,128)S(1)} %copy-done.15, s32[400,1]{1,0:T(8,128)S(1)} %copy-done.19, ...), custom_call_target="tpu_custom_call" | custom-call | flops 1000000000 | bytes 3939090 | tf_op jit(solution)/shard_map/pallas_call | solution.py:58
  31.2 1.0 copy-done
  32.2 0.8 copy-done.5
  33.1 1.3 copy-done.1
  34.4 1.1 copy-done.11
  35.5 2.9 %shard_map.149 = (f32[1352,128]{1,0:T(8,128)S(1)}, f32[384,128]{1,0:T(8,128)S(1)}, bf16[592,128]{1,0:T(8,128)(2,1)}) custom-call(s32[3,1]{1,0:T(4,128)S(1)} %copy.54.refs_0_, f32[1352,128]{1,0:T(8,128)S(1)} %bitcast.29, bf16[112,128]{1,0:T(8,128)(2,1)S(1)} %collective-permute-done.xr_lo.refs_2_, bf16[112,128]{1,0:T(8,128)(2,1)S(1)} %collective-permute-done.1.xr_hi.refs_3_, ...), custom_call_target="tpu_custom_call" | custom-call | flops 400000000 | bytes 4501504 | tf_op jit(solution)/shard_map/pallas_call | solution.py:58
  38.4 0.8 copy-done.8
  39.3 0.7 copy-done.13
  40.5 1.9 %broadcast_multiply_fusion = bf16[32,12,32,12]{3,2,1,0:T(8,128)(2,1)} fusion(bf16[32,32]{1,0:T(8,128)(2,1)S(1)} %fusion.4, bf16[32,12,12]{2,1,0:T(8,128)(2,1)S(1)} %copy-done.21), kind=kLoop, calls=%fused_computation.2 | loop fusion | flops 147456 | bytes 306176 | tf_op jit(solution)/shard_map/mul | solution.py:445
  42.4 7.0 %mul.65.refs_4_.refs_5_ = bf16[384,384]{1,0:T(8,128)(2,1)} reshape(bf16[32,12,32,12]{3,2,1,0:T(8,128)(2,1)} %broadcast_multiply_fusion) | data formatting | bytes 589824 | tf_op jit(solution)/shard_map/mul | solution.py:445
  49.4 1.1 copy-done.3
  50.4 1.0 copy-done.6
  51.4 1.1 copy-done.9
  52.5 0.9 copy-done.14
  53.5 1.9 %shard_map.150 = (f32[1352,128]{1,0:T(8,128)S(1)}, f32[1352,128]{1,0:T(8,128)S(1)}, f32[1352,128]{1,0:T(8,128)S(1)}, bf16[112,128]{1,0:T(8,128)(2,1)S(1)}, bf16[...) custom-call(s32[3,1]{1,0:T(4,128)S(1)} %copy.54.refs_0_, f32[1352,128]{1,0:T(8,128)S(1)} %copy-done.9, ...), custom_call_target="tpu_custom_call" | custom-call | flops 600000000 | bytes 6001152 | tf_op jit(solution)/shard_map/pallas_call | solution.py:58
  55.4 4.2 %collective-permute-start.6 = (bf16[112,128]{1,0:T(8,128)(2,1)S(1)}, bf16[112,128]{1,0:T(8,128)(2,1)S(1)}, u32[]{:S(2)}, u32[]{:S(2)}) collective-permute-start(bf16[112,128]{1,0:T(8,128)(2,1)S(1)} %get-tuple-element.69), channel_id=1, source_target_pairs={{0,8},{8,16},{16,24},{1,9},{9,17},{17,25},{2,10},{10,18},{18,26},{... | collective-permute-start | bytes 86024 | tf_op jit(solution)/shard_map/ppermute | solution.py:392
  59.6 1.3 collective-permute-start.7
  60.9 3.6 %collective-permute-done.7.xr_hi.refs_4_ = bf16[112,128]{1,0:T(8,128)(2,1)S(1)} collective-permute-done((bf16[112,128]{1,0:T(8,128)(2,1)S(1)}, bf16[112,128]{1,0:T(8,128)(2,1)S(1)}, u32[]{:S(2)}, u32[]{:S(2)}) %collective-permute-start.7) | collective-permute-done | bytes 28704 | tf_op jit(solution)/shard_map/ppermute | solution.py:392
  64.5 4.5 %collective-permute-start.8 = (bf16[112,128]{1,0:T(8,128)(2,1)S(1)}, bf16[112,128]{1,0:T(8,128)(2,1)S(1)}, u32[]{:S(2)}, u32[]{:S(2)}) collective-permute-start(bf16[112,128]{1,0:T(8,128)(2,1)S(1)} %get-tuple-element.73), channel_id=1, source_target_pairs={{0,2},{2,4},{4,6},{1,3},{3,5},{5,7},{8,10},{10,12},{12,14},{9,11},... | collective-permute-start | bytes 86024 | tf_op jit(solution)/shard_map/ppermute | solution.py:392
  69.1 1.5 %collective-permute-start.9 = (bf16[112,128]{1,0:T(8,128)(2,1)S(1)}, bf16[112,128]{1,0:T(8,128)(2,1)S(1)}, u32[]{:S(2)}, u32[]{:S(2)}) collective-permute-start(bf16[112,128]{1,0:T(8,128)(2,1)S(1)} %get-tuple-element.74), channel_id=1, source_target_pairs={{2,0},{4,2},{6,4},{3,1},{5,3},{7,5},{10,8},{12,10},{14,12},{11,9},... | collective-permute-start | bytes 86024 | tf_op jit(solution)/shard_map/ppermute | solution.py:392
  70.6 4.2 %collective-permute-done.9.refs_6_ = bf16[112,128]{1,0:T(8,128)(2,1)S(1)} collective-permute-done((bf16[112,128]{1,0:T(8,128)(2,1)S(1)}, bf16[112,128]{1,0:T(8,128)(2,1)S(1)}, u32[]{:S(2)}, u32[]{:S(2)}) %collective-permute-start.9) | collective-permute-done | bytes 28704 | tf_op jit(solution)/shard_map/ppermute | solution.py:392
  74.8 2.0 %shard_map.152 = (f32[1352,128]{1,0:T(8,128)S(1)}, f32[384,128]{1,0:T(8,128)S(1)}, bf16[592,128]{1,0:T(8,128)(2,1)S(1)}) custom-call(s32[3,1]{1,0:T(4,128)S(1)} %copy.54.refs_0_, f32[1352,128]{1,0:T(8,128)S(1)} %get-tuple-element.67.refs_1_, f32[1352,128]{1,0:T(8,128)S(1)} %get-tuple-element.68.refs_2_, ...), custom_call_target="tpu_custom_call" | custom-call | flops 400000000 | bytes 5193728 | tf_op jit(solution)/shard_map/pallas_call | solution.py:58
  76.9 1.6 %collective-permute-start.10 = (bf16[592,128]{1,0:T(8,128)(2,1)S(1)}, bf16[592,128]{1,0:T(8,128)(2,1)S(1)}, u32[]{:S(2)}, u32[]{:S(2)}) collective-permute-start(bf16[592,128]{1,0:T(8,128)(2,1)S(1)} %get-tuple-element.78), channel_id=1, source_target_pairs={{0,1},{1,0},{2,3},{3,2},{4,5},{5,4},{6,7},{7,6},{8,9},{9,8},{10,11... | collective-permute-start | bytes 454664 | tf_op jit(solution)/shard_map/ppermute | solution.py:471
  78.4 5.1 %collective-permute-done.10.refs_4_ = bf16[592,128]{1,0:T(8,128)(2,1)S(1)} collective-permute-done((bf16[592,128]{1,0:T(8,128)(2,1)S(1)}, bf16[592,128]{1,0:T(8,128)(2,1)S(1)}, u32[]{:S(2)}, u32[]{:S(2)}) %collective-permute-start.10) | collective-permute-done | bytes 151584 | tf_op jit(solution)/shard_map/ppermute | solution.py:471
  83.5 1.6 %shard_map.153 = (f32[1352,128]{1,0:T(8,128)S(1)}, f32[1352,128]{1,0:T(8,128)S(1)}, f32[1352,128]{1,0:T(8,128)S(1)}, bf16[112,128]{1,0:T(8,128)(2,1)S(1)}, bf16[...) custom-call(s32[3,1]{1,0:T(4,128)S(1)} %copy.54.refs_0_, ...), custom_call_target="tpu_custom_call" | custom-call | flops 600000000 | bytes 6693376 | tf_op jit(solution)/shard_map/pallas_call | solution.py:58
  85.2 2.0 %collective-permute-start.11 = (bf16[112,128]{1,0:T(8,128)(2,1)S(1)}, bf16[112,128]{1,0:T(8,128)(2,1)S(1)}, u32[]{:S(2)}, u32[]{:S(2)}) collective-permute-start(bf16[112,128]{1,0:T(8,128)(2,1)S(1)} %get-tuple-element.81), channel_id=1, source_target_pairs={{0,8},{8,16},{16,24},{1,9},{9,17},{17,25},{2,10},{10,18},{18,26},{... | collective-permute-start | bytes 86024 | tf_op jit(solution)/shard_map/ppermute | solution.py:392
  87.2 1.3 collective-permute-start.12
  88.5 2.3 %collective-permute-done.12.xr_hi.refs_4_ = bf16[112,128]{1,0:T(8,128)(2,1)S(1)} collective-permute-done((bf16[112,128]{1,0:T(8,128)(2,1)S(1)}, bf16[112,128]{1,0:T(8,128)(2,1)S(1)}, u32[]{:S(2)}, u32[]{:S(2)}) %collective-permute-start.12) | collective-permute-done | bytes 28704 | tf_op jit(solution)/shard_map/ppermute | solution.py:392
  90.9 3.1 %collective-permute-start.13 = (bf16[112,128]{1,0:T(8,128)(2,1)S(1)}, bf16[112,128]{1,0:T(8,128)(2,1)S(1)}, u32[]{:S(2)}, u32[]{:S(2)}) collective-permute-start(bf16[112,128]{1,0:T(8,128)(2,1)S(1)} %get-tuple-element.85), channel_id=1, source_target_pairs={{0,2},{2,4},{4,6},{1,3},{3,5},{5,7},{8,10},{10,12},{12,14},{9,11},... | collective-permute-start | bytes 86024 | tf_op jit(solution)/shard_map/ppermute | solution.py:392
  93.9 1.3 collective-permute-start.14
  95.5 4.2 %collective-permute-done.14.refs_6_ = bf16[112,128]{1,0:T(8,128)(2,1)S(1)} collective-permute-done((bf16[112,128]{1,0:T(8,128)(2,1)S(1)}, bf16[112,128]{1,0:T(8,128)(2,1)S(1)}, u32[]{:S(2)}, u32[]{:S(2)}) %collective-permute-start.14) | collective-permute-done | bytes 28704 | tf_op jit(solution)/shard_map/ppermute | solution.py:392
  99.7 2.1 %shard_map.155 = (f32[1352,128]{1,0:T(8,128)S(1)}, f32[384,128]{1,0:T(8,128)S(1)}, bf16[592,128]{1,0:T(8,128)(2,1)S(1)}) custom-call(s32[3,1]{1,0:T(4,128)S(1)} %copy.54.refs_0_, f32[1352,128]{1,0:T(8,128)S(1)} %get-tuple-element.79.refs_1_, f32[1352,128]{1,0:T(8,128)S(1)} %get-tuple-element.80.refs_2_, ...), custom_call_target="tpu_custom_call" | custom-call | flops 400000000 | bytes 5193728 | tf_op jit(solution)/shard_map/pallas_call | solution.py:58
  101.8 1.6 %collective-permute-start.15 = (bf16[592,128]{1,0:T(8,128)(2,1)S(1)}, bf16[592,128]{1,0:T(8,128)(2,1)S(1)}, u32[]{:S(2)}, u32[]{:S(2)}) collective-permute-start(bf16[592,128]{1,0:T(8,128)(2,1)S(1)} %get-tuple-element.90), channel_id=1, source_target_pairs={{0,1},{1,0},{2,3},{3,2},{4,5},{5,4},{6,7},{7,6},{8,9},{9,8},{10,11... | collective-permute-start | bytes 454664 | tf_op jit(solution)/shard_map/ppermute | solution.py:471
  103.4 4.9 %collective-permute-done.15.refs_4_ = bf16[592,128]{1,0:T(8,128)(2,1)S(1)} collective-permute-done((bf16[592,128]{1,0:T(8,128)(2,1)S(1)}, bf16[592,128]{1,0:T(8,128)(2,1)S(1)}, u32[]{:S(2)}, u32[]{:S(2)}) %collective-permute-start.15) | collective-permute-done | bytes 151584 | tf_op jit(solution)/shard_map/ppermute | solution.py:471
  108.2 2.4 %shard_map.156 = (f32[1352,128]{1,0:T(8,128)S(1)}, f32[1352,128]{1,0:T(8,128)S(1)}, f32[1352,128]{1,0:T(8,128)}, bf16[112,128]{1,0:T(8,128)(2,1)S(1)}, bf16[112,...) custom-call(s32[3,1]{1,0:T(4,128)S(1)} %copy.54.refs_0_, ...), custom_call_target="tpu_custom_call" | custom-call | flops 600000000 | bytes 6693376 | tf_op jit(solution)/shard_map/pallas_call | solution.py:58
  110.7 2.1 %collective-permute-start.16 = (bf16[112,128]{1,0:T(8,128)(2,1)S(1)}, bf16[112,128]{1,0:T(8,128)(2,1)S(1)}, u32[]{:S(2)}, u32[]{:S(2)}) collective-permute-start(bf16[112,128]{1,0:T(8,128)(2,1)S(1)} %get-tuple-element.93), channel_id=1, source_target_pairs={{0,8},{8,16},{16,24},{1,9},{9,17},{17,25},{2,10},{10,18},{18,26},{... | collective-permute-start | bytes 86024 | tf_op jit(solution)/shard_map/ppermute | solution.py:392
  112.8 1.3 collective-permute-start.17
  114.1 2.5 %collective-permute-done.17.xr_hi.refs_3_.refs_4_ = bf16[112,128]{1,0:T(8,128)(2,1)S(1)} collective-permute-done((bf16[112,128]{1,0:T(8,128)(2,1)S(1)}, bf16[112,128]{1,0:T(8,128)(2,1)S(1)}, u32[]{:S(2)}, u32[]{:S(2)}) %collective-permute-start.17) | collective-permute-done | bytes 28704 | tf_op jit(solution)/shard_map/ppermute | solution.py:392
  116.6 3.9 %collective-permute-start.18 = (bf16[112,128]{1,0:T(8,128)(2,1)S(1)}, bf16[112,128]{1,0:T(8,128)(2,1)S(1)}, u32[]{:S(2)}, u32[]{:S(2)}) collective-permute-start(bf16[112,128]{1,0:T(8,128)(2,1)S(1)} %get-tuple-element.97), channel_id=1, source_target_pairs={{0,2},{2,4},{4,6},{1,3},{3,5},{5,7},{8,10},{10,12},{12,14},{9,11},... | collective-permute-start | bytes 86024 | tf_op jit(solution)/shard_map/ppermute | solution.py:392
  120.5 1.3 collective-permute-start.19
  122.0 4.2 %collective-permute-done.19.refs_5_.refs_6_ = bf16[112,128]{1,0:T(8,128)(2,1)S(1)} collective-permute-done((bf16[112,128]{1,0:T(8,128)(2,1)S(1)}, bf16[112,128]{1,0:T(8,128)(2,1)S(1)}, u32[]{:S(2)}, u32[]{:S(2)}) %collective-permute-start.19) | collective-permute-done | bytes 28704 | tf_op jit(solution)/shard_map/ppermute | solution.py:392
  126.2 0.6 shard_map.158
  126.9 1.6 %collective-permute-start.20 = (bf16[208,128]{1,0:T(8,128)(2,1)S(1)}, bf16[208,128]{1,0:T(8,128)(2,1)S(1)}, u32[]{:S(2)}, u32[]{:S(2)}) collective-permute-start(bf16[208,128]{1,0:T(8,128)(2,1)S(1)} %shard_map.158), channel_id=1, source_target_pairs={{0,1},{1,0},{2,3},{3,2},{4,5},{5,4},{6,7},{7,6},{8,9},{9,8},{10,11... | collective-permute-start | bytes 159752 | tf_op jit(solution)/shard_map/ppermute | solution.py:478
  128.5 3.0 %collective-permute-done.20.refs_7_ = bf16[208,128]{1,0:T(8,128)(2,1)S(1)} collective-permute-done((bf16[208,128]{1,0:T(8,128)(2,1)S(1)}, bf16[208,128]{1,0:T(8,128)(2,1)S(1)}, u32[]{:S(2)}, u32[]{:S(2)}) %collective-permute-start.20) | collective-permute-done | bytes 53280 | tf_op jit(solution)/shard_map/ppermute | solution.py:478
  131.5 1.6 %shard_map.159 = f32[13,13,7,128]{3,2,1,0:T(8,128)} custom-call(s32[3,1]{1,0:T(4,128)S(1)} %copy.54.refs_0_, f32[1352,128]{1,0:T(8,128)S(1)} %get-tuple-element.91.refs_1_, f32[1352,128]{1,0:T(8,128)S(1)} %get-tuple-element.92.refs_2_, bf16[112,128]{1,0:T(8,128)(2,1)S(1)} %collective-permute-done.16.xr_lo.refs_2_.refs_3_, ...), custom_call_target="tpu_custom_call" | custom-call | bytes 2158080 | tf_op jit(solution)/shard_map/pallas_call | solution.py:58
  (76 shorter events, 4.3 us)
Async XLA Ops:
  2.8 1.2 copy-start.16
  4.1 0.9 copy-start.18
  5.0 7.7 %copy-start.12 = (f32[13,13,7,128]{3,2,1,0:T(8,128)S(1)}, f32[13,13,7,128]{3,2,1,0:T(8,128)}, u32[]{:S(2)}) copy-start(f32[13,13,7,128]{3,2,1,0:T(8,128)} %parts.1) | copy-start | bytes 1817092
  5.0 12.1 %copy-start.24 = (s32[1,1,2,32]{3,2,1,0:T(2,128)S(1)}, s32[1,1,2,32]{3,2,1,0:T(2,128)}, u32[]{:S(2)}) copy-start(s32[1,1,2,32]{3,2,1,0:T(2,128)} %param.19) | copy-start | bytes 772
  5.0 12.8 %copy-start.22 = (f32[64,12,12]{0,2,1:T(8,128)S(1)}, f32[64,12,12]{0,2,1:T(8,128)}, u32[]{:S(2)}) copy-start(f32[64,12,12]{0,2,1:T(8,128)} %param.21) | copy-start | bytes 110596
  8.9 11.0 %copy-start.23 = (f32[343,2,2,1]{0,3,2,1:T(1,128)S(1)}, f32[343,2,2,1]{0,3,2,1:T(1,128)}, u32[]{:S(2)}) copy-start(f32[343,2,2,1]{0,3,2,1:T(1,128)} %param.17) | copy-start | bytes 16468
  8.9 17.8 %copy-start.20 = (s32[1,400]{1,0:T(1,128)S(1)}, s32[1,400]{1,0:T(1,128)}, u32[]{:S(2)}) copy-start(s32[1,400]{1,0:T(1,128)} %constant.70.clone.lane_key) | copy-start | bytes 4804
  9.8 23.3 %collective-permute-start.4 = (bf16[256,384]{0,1:T(8,128)(2,1)}, bf16[256,384]{0,1:T(8,128)(2,1)S(1)}, u32[]{:S(2)}, u32[]{:S(2)}) collective-permute-start(bf16[256,384]{0,1:T(8,128)(2,1)} %copy.45), channel_id=1, source_target_pairs={{1,0},{0,1},{3,2},{2,3},{5,4},{4,5},{7,6},{6,7},{9,8},{8,9},{11,10... | collective-permute-start | bytes 589832 | tf_op jit(solution)/shard_map/ppermute | solution.py:462
  13.5 0.8 copy-start.10
  14.3 6.5 %collective-permute-start = (bf16[112,128]{1,0:T(8,128)(2,1)}, bf16[112,128]{1,0:T(8,128)(2,1)S(1)}, u32[]{:S(2)}, u32[]{:S(2)}) collective-permute-start(bf16[112,128]{1,0:T(8,128)(2,1)} %get-tuple-element.53), channel_id=1, source_target_pairs={{0,8},{8,16},{16,24},{1,9},{9,17},{17,25},{2,10},{10,18},{18,26},{... | collective-permute-start | bytes 86024 | tf_op jit(solution)/shard_map/ppermute | solution.py:392
  15.8 5.0 %collective-permute-start.1 = (bf16[112,128]{1,0:T(8,128)(2,1)}, bf16[112,128]{1,0:T(8,128)(2,1)S(1)}, u32[]{:S(2)}, u32[]{:S(2)}) collective-permute-start(bf16[112,128]{1,0:T(8,128)(2,1)} %get-tuple-element.54), channel_id=1, source_target_pairs={{8,0},{16,8},{24,16},{9,1},{17,9},{25,17},{10,2},{18,10},{26,18},{... | collective-permute-start | bytes 86024 | tf_op jit(solution)/shard_map/ppermute | solution.py:392
  21.4 11.7 %collective-permute-start.2 = (bf16[112,128]{1,0:T(8,128)(2,1)}, bf16[112,128]{1,0:T(8,128)(2,1)}, u32[]{:S(2)}, u32[]{:S(2)}) collective-permute-start(bf16[112,128]{1,0:T(8,128)(2,1)} %get-tuple-element.57), channel_id=1, source_target_pairs={{0,2},{2,4},{4,6},{1,3},{3,5},{5,7},{8,10},{10,12},{12,14},{9,11},... | collective-permute-start | bytes 86024 | tf_op jit(solution)/shard_map/ppermute | solution.py:392
  25.5 7.6 %collective-permute-start.3 = (bf16[112,128]{1,0:T(8,128)(2,1)}, bf16[112,128]{1,0:T(8,128)(2,1)}, u32[]{:S(2)}, u32[]{:S(2)}) collective-permute-start(bf16[112,128]{1,0:T(8,128)(2,1)} %get-tuple-element.58), channel_id=1, source_target_pairs={{2,0},{4,2},{6,4},{3,1},{5,3},{7,5},{10,8},{12,10},{14,12},{11,9},... | collective-permute-start | bytes 86024 | tf_op jit(solution)/shard_map/ppermute | solution.py:392
  26.8 0.9 copy-start.15
  27.7 1.0 copy-start.17
  28.6 0.9 copy-start.19
  31.1 1.0 copy-start
  32.2 0.8 copy-start.5
  33.1 1.3 copy-start.1
  34.4 1.1 copy-start.11
  35.5 5.0 %copy-start.21 = (bf16[32,12,12]{2,1,0:T(8,128)(2,1)S(1)}, bf16[32,12,12]{2,1,0:T(8,128)(2,1)}, u32[]{:S(2)}) copy-start(bf16[32,12,12]{2,1,0:T(8,128)(2,1)} %select_convert_fusion) | copy-start | bytes 27652
  38.4 0.8 copy-start.8
  39.3 0.7 copy-start.13
  40.0 9.4 %collective-permute-start.5 = (bf16[592,128]{1,0:T(8,128)(2,1)}, bf16[592,128]{1,0:T(8,128)(2,1)}, u32[]{:S(2)}, u32[]{:S(2)}) collective-permute-start(bf16[592,128]{1,0:T(8,128)(2,1)} %get-tuple-element.64), channel_id=1, source_target_pairs={{0,1},{1,0},{2,3},{3,2},{4,5},{5,4},{6,7},{7,6},{8,9},{9,8},{10,11... | collective-permute-start | bytes 454664 | tf_op jit(solution)/shard_map/ppermute | solution.py:471
  49.4 25.5 %copy-start.2 = (bf16[384,1664]{1,0:T(8,128)(2,1)S(1)}, bf16[384,1664]{1,0:T(8,128)(2,1)}, u32[]{:S(2)}) copy-start(bf16[384,1664]{1,0:T(8,128)(2,1)} %copy-done) | copy-start | bytes 3833860
  49.4 1.1 copy-start.3
  50.4 1.0 copy-start.6
  51.4 1.1 copy-start.9
  52.5 0.9 copy-start.14
  55.4 28.1 %copy-start.4 = (bf16[384,384]{1,0:T(8,128)(2,1)S(1)}, bf16[384,384]{1,0:T(8,128)(2,1)}, u32[]{:S(2)}) copy-start(bf16[384,384]{1,0:T(8,128)(2,1)} %mul.65.refs_4_.refs_5_) | copy-start | bytes 884740
  55.4 28.1 %copy-start.7 = (bf16[400,400]{1,0:T(8,128)(2,1)S(1)}, bf16[400,400]{1,0:T(8,128)(2,1)}, u32[]{:S(2)}) copy-start(bf16[400,400]{1,0:T(8,128)(2,1)} %copy-done.5) | copy-start | bytes 960004
  55.4 5.5 %collective-permute-start.6 = (bf16[112,128]{1,0:T(8,128)(2,1)S(1)}, bf16[112,128]{1,0:T(8,128)(2,1)S(1)}, u32[]{:S(2)}, u32[]{:S(2)}) collective-permute-start(bf16[112,128]{1,0:T(8,128)(2,1)S(1)} %get-tuple-element.69), channel_id=1, source_target_pairs={{0,8},{8,16},{16,24},{1,9},{9,17},{17,25},{2,10},{10,18},{18,26},{... | collective-permute-start | bytes 86024 | tf_op jit(solution)/shard_map/ppermute | solution.py:392
  59.6 4.9 %collective-permute-start.7 = (bf16[112,128]{1,0:T(8,128)(2,1)S(1)}, bf16[112,128]{1,0:T(8,128)(2,1)S(1)}, u32[]{:S(2)}, u32[]{:S(2)}) collective-permute-start(bf16[112,128]{1,0:T(8,128)(2,1)S(1)} %get-tuple-element.70), channel_id=1, source_target_pairs={{8,0},{16,8},{24,16},{9,1},{17,9},{25,17},{10,2},{18,10},{26,18},{... | collective-permute-start | bytes 86024 | tf_op jit(solution)/shard_map/ppermute | solution.py:392
  64.5 6.1 %collective-permute-start.8 = (bf16[112,128]{1,0:T(8,128)(2,1)S(1)}, bf16[112,128]{1,0:T(8,128)(2,1)S(1)}, u32[]{:S(2)}, u32[]{:S(2)}) collective-permute-start(bf16[112,128]{1,0:T(8,128)(2,1)S(1)} %get-tuple-element.73), channel_id=1, source_target_pairs={{0,2},{2,4},{4,6},{1,3},{3,5},{5,7},{8,10},{10,12},{12,14},{9,11},... | collective-permute-start | bytes 86024 | tf_op jit(solution)/shard_map/ppermute | solution.py:392
  69.1 5.8 %collective-permute-start.9 = (bf16[112,128]{1,0:T(8,128)(2,1)S(1)}, bf16[112,128]{1,0:T(8,128)(2,1)S(1)}, u32[]{:S(2)}, u32[]{:S(2)}) collective-permute-start(bf16[112,128]{1,0:T(8,128)(2,1)S(1)} %get-tuple-element.74), channel_id=1, source_target_pairs={{2,0},{4,2},{6,4},{3,1},{5,3},{7,5},{10,8},{12,10},{14,12},{11,9},... | collective-permute-start | bytes 86024 | tf_op jit(solution)/shard_map/ppermute | solution.py:392
  76.9 6.7 %collective-permute-start.10 = (bf16[592,128]{1,0:T(8,128)(2,1)S(1)}, bf16[592,128]{1,0:T(8,128)(2,1)S(1)}, u32[]{:S(2)}, u32[]{:S(2)}) collective-permute-start(bf16[592,128]{1,0:T(8,128)(2,1)S(1)} %get-tuple-element.78), channel_id=1, source_target_pairs={{0,1},{1,0},{2,3},{3,2},{4,5},{5,4},{6,7},{7,6},{8,9},{9,8},{10,11... | collective-permute-start | bytes 454664 | tf_op jit(solution)/shard_map/ppermute | solution.py:471
  85.2 3.3 %collective-permute-start.11 = (bf16[112,128]{1,0:T(8,128)(2,1)S(1)}, bf16[112,128]{1,0:T(8,128)(2,1)S(1)}, u32[]{:S(2)}, u32[]{:S(2)}) collective-permute-start(bf16[112,128]{1,0:T(8,128)(2,1)S(1)} %get-tuple-element.81), channel_id=1, source_target_pairs={{0,8},{8,16},{16,24},{1,9},{9,17},{17,25},{2,10},{10,18},{18,26},{... | collective-permute-start | bytes 86024 | tf_op jit(solution)/shard_map/ppermute | solution.py:392
  87.2 3.7 %collective-permute-start.12 = (bf16[112,128]{1,0:T(8,128)(2,1)S(1)}, bf16[112,128]{1,0:T(8,128)(2,1)S(1)}, u32[]{:S(2)}, u32[]{:S(2)}) collective-permute-start(bf16[112,128]{1,0:T(8,128)(2,1)S(1)} %get-tuple-element.82), channel_id=1, source_target_pairs={{8,0},{16,8},{24,16},{9,1},{17,9},{25,17},{10,2},{18,10},{26,18},{... | collective-permute-start | bytes 86024 | tf_op jit(solution)/shard_map/ppermute | solution.py:392
  90.9 4.6 %collective-permute-start.13 = (bf16[112,128]{1,0:T(8,128)(2,1)S(1)}, bf16[112,128]{1,0:T(8,128)(2,1)S(1)}, u32[]{:S(2)}, u32[]{:S(2)}) collective-permute-start(bf16[112,128]{1,0:T(8,128)(2,1)S(1)} %get-tuple-element.85), channel_id=1, source_target_pairs={{0,2},{2,4},{4,6},{1,3},{3,5},{5,7},{8,10},{10,12},{12,14},{9,11},... | collective-permute-start | bytes 86024 | tf_op jit(solution)/shard_map/ppermute | solution.py:392
  93.9 5.8 %collective-permute-start.14 = (bf16[112,128]{1,0:T(8,128)(2,1)S(1)}, bf16[112,128]{1,0:T(8,128)(2,1)S(1)}, u32[]{:S(2)}, u32[]{:S(2)}) collective-permute-start(bf16[112,128]{1,0:T(8,128)(2,1)S(1)} %get-tuple-element.86), channel_id=1, source_target_pairs={{2,0},{4,2},{6,4},{3,1},{5,3},{7,5},{10,8},{12,10},{14,12},{11,9},... | collective-permute-start | bytes 86024 | tf_op jit(solution)/shard_map/ppermute | solution.py:392
  101.8 6.5 %collective-permute-start.15 = (bf16[592,128]{1,0:T(8,128)(2,1)S(1)}, bf16[592,128]{1,0:T(8,128)(2,1)S(1)}, u32[]{:S(2)}, u32[]{:S(2)}) collective-permute-start(bf16[592,128]{1,0:T(8,128)(2,1)S(1)} %get-tuple-element.90), channel_id=1, source_target_pairs={{0,1},{1,0},{2,3},{3,2},{4,5},{5,4},{6,7},{7,6},{8,9},{9,8},{10,11... | collective-permute-start | bytes 454664 | tf_op jit(solution)/shard_map/ppermute | solution.py:471
  110.7 3.4 %collective-permute-start.16 = (bf16[112,128]{1,0:T(8,128)(2,1)S(1)}, bf16[112,128]{1,0:T(8,128)(2,1)S(1)}, u32[]{:S(2)}, u32[]{:S(2)}) collective-permute-start(bf16[112,128]{1,0:T(8,128)(2,1)S(1)} %get-tuple-element.93), channel_id=1, source_target_pairs={{0,8},{8,16},{16,24},{1,9},{9,17},{17,25},{2,10},{10,18},{18,26},{... | collective-permute-start | bytes 86024 | tf_op jit(solution)/shard_map/ppermute | solution.py:392
  112.8 3.8 %collective-permute-start.17 = (bf16[112,128]{1,0:T(8,128)(2,1)S(1)}, bf16[112,128]{1,0:T(8,128)(2,1)S(1)}, u32[]{:S(2)}, u32[]{:S(2)}) collective-permute-start(bf16[112,128]{1,0:T(8,128)(2,1)S(1)} %get-tuple-element.94), channel_id=1, source_target_pairs={{8,0},{16,8},{24,16},{9,1},{17,9},{25,17},{10,2},{18,10},{26,18},{... | collective-permute-start | bytes 86024 | tf_op jit(solution)/shard_map/ppermute | solution.py:392
  116.6 5.5 %collective-permute-start.18 = (bf16[112,128]{1,0:T(8,128)(2,1)S(1)}, bf16[112,128]{1,0:T(8,128)(2,1)S(1)}, u32[]{:S(2)}, u32[]{:S(2)}) collective-permute-start(bf16[112,128]{1,0:T(8,128)(2,1)S(1)} %get-tuple-element.97), channel_id=1, source_target_pairs={{0,2},{2,4},{4,6},{1,3},{3,5},{5,7},{8,10},{10,12},{12,14},{9,11},... | collective-permute-start | bytes 86024 | tf_op jit(solution)/shard_map/ppermute | solution.py:392
  120.5 5.8 %collective-permute-start.19 = (bf16[112,128]{1,0:T(8,128)(2,1)S(1)}, bf16[112,128]{1,0:T(8,128)(2,1)S(1)}, u32[]{:S(2)}, u32[]{:S(2)}) collective-permute-start(bf16[112,128]{1,0:T(8,128)(2,1)S(1)} %get-tuple-element.98), channel_id=1, source_target_pairs={{2,0},{4,2},{6,4},{3,1},{5,3},{7,5},{10,8},{12,10},{14,12},{11,9},... | collective-permute-start | bytes 86024 | tf_op jit(solution)/shard_map/ppermute | solution.py:392
  126.9 4.6 %collective-permute-start.20 = (bf16[208,128]{1,0:T(8,128)(2,1)S(1)}, bf16[208,128]{1,0:T(8,128)(2,1)S(1)}, u32[]{:S(2)}, u32[]{:S(2)}) collective-permute-start(bf16[208,128]{1,0:T(8,128)(2,1)S(1)} %shard_map.158), channel_id=1, source_target_pairs={{0,1},{1,0},{2,3},{3,2},{4,5},{5,4},{6,7},{7,6},{8,9},{9,8},{10,11... | collective-permute-start | bytes 159752 | tf_op jit(solution)/shard_map/ppermute | solution.py:478
where the time goes:
time: 134 us; the launch traced here: 133 us
  starting transfers between devices  44.1 us (33%)
  waiting for transfers between devices  34.6 us (26%)
  local copies, waits for them, and re-layouts  26.2 us (20%)
  Pallas kernels  22.1 us (16%)
  other arithmetic  5.66 us (4%)
    ppermute x16, starting transfers between devices, swap_faces(): return (lax.ppermute(hi, axis, forward), lax.ppermute(lo, axis, backward))  35.8 us
    pallas_call x15, Pallas kernels, kernel_call(): pl.pallas_call(body, out_shape=outs, in_specs=[SMEM] * len(scalars) + [VM...  22.1 us
    ppermute x16, waiting for transfers between devices, swap_faces(): return (lax.ppermute(hi, axis, forward), lax.ppermute(lo, axis, backward))  21.6 us
    unnamed x51, local copies, waits for them, and re-layouts  16 us
    ppermute x3, waiting for transfers between devices, local(): lax.ppermute(m, 'gz', ring[s + 1])  9.99 us
    mul x1, local copies, waits for them, and re-layouts, local(): cblk = (picked[:, :, None, :] * eye[:, None, :, None]).reshape(SLOTS, SLOTS)  6.97 us
    ppermute x3, starting transfers between devices, local(): lax.ppermute(m, 'gz', ring[s + 1])  3.68 us
    ppermute x1, waiting for transfers between devices, local(): lax.ppermute(f, 'gz', ring[s])  2.99 us
  transfers between devices with their start and end apart: 21, of which 12 were waited for; matrix products, arithmetic and copies ran while one was open for 9% of the time, Pallas kernels for 2%

commit v1 on v0

v1 whole, which is shorter than its diff:
```python
import functools

import jax
import jax.numpy as jnp
import numpy as np
from jax import lax
from jax.experimental import pallas as pl
from jax.experimental.pallas import tpu as pltpu
from jax.sharding import PartitionSpec as P

ORDER = 6
STEPS = 3
PA = 12
POS = 32
BLK = 4

center_value = 2.0
half_width = 3.0

EDGE = ORDER + 1
PAD = 8
SLOTS = POS * PA
F32 = jnp.float32
BF16 = jnp.bfloat16
HALO = jnp.bfloat16


def up(value, multiple):
    return -(-value // multiple) * multiple


class Sizes:
    def __init__(self, nx, ny, nz, orbitals, shifts):
        assert nz == EDGE
        self.nx, self.ny, self.orb = nx, ny, orbitals
        self.cells = [(p, q) for p in range((nx - 1) // ORDER) for q in range((ny - 1) // ORDER)]
        self.rows = nx * ny * PAD
        self.line_x = ny * PAD
        self.xface = up(ny * PAD, 16)
        self.yface = up(nx * PAD, 16)
        self.face_b = up(ny, PAD)
        self.zface = up(nx * self.face_b, 16)
        self.cell_rows = EDGE * EDGE * PAD
        self.cell_pad = up(self.cell_rows, 16)
        self.all_pad = up(self.cell_pad * len(self.cells), 128)
        self.fcell = EDGE * PAD
        self.fall = up(self.fcell * len(self.cells), 256)
        self.shifts, self.links = shifts, min(2, shifts)
        self.spill = 2 * PAD * PAD


VMEM = pl.BlockSpec(memory_space=pltpu.VMEM)


def kernel_call(body, outs, arrays, scratch=(), flops=0, limit=24 << 20):
    nbytes = sum(int(np.prod(a.shape)) * a.dtype.itemsize for a in list(arrays) + list(outs))
    return pl.pallas_call(
        body,
        out_shape=outs,
        in_specs=[VMEM] * len(arrays),
        out_specs=[VMEM] * len(outs),
        scratch_shapes=list(scratch),
        compiler_params=pltpu.CompilerParams(vmem_limit_bytes=limit),
        cost_estimate=pl.CostEstimate(flops=flops, bytes_accessed=nbytes, transcendentals=0),
    )(*arrays)


def shape(rows, cols, dtype):
    return jax.ShapeDtypeStruct((rows, cols), dtype)


def dot(a, b):
    return jnp.dot(a, b, preferred_element_type=F32)


def is_odd(axis):
    return lax.rem(lax.axis_index(axis), 2) == 1


def by_parity(axis, even, odd):
    return jnp.where(is_odd(axis), odd, even)


def link_shifts(sz):
    return [1, sz.shifts][: sz.links]


def layer_sent(sz, j):
    if sz.links == 1:
        return jnp.where(lax.axis_index("gz") == 0, ORDER, 0)
    return [ORDER, 0][j]


def layer_received(sz, j):
    return layer_sent(sz, 0) if sz.links == 1 else [0, ORDER][j]


def link_valid(sz, j):
    if sz.links == 1:
        return None
    me = lax.axis_index("gz")
    return jnp.where(me < sz.shifts, 1, 0) if j == 0 else jnp.where(me > 0, 1, 0)


def iota(rows, cols, dim):
    return lax.broadcasted_iota(jnp.int32, (rows, cols), dim)


def twelfth(value):
    return (value * (2**19 // PA + 1)) >> 19


def node_key(i):
    low = i & (PAD - 1)
    return jnp.where((low < EDGE) & (i < EDGE * EDGE * PAD), (i >> 3) * EDGE + low, -1)


def dot_last(a, b, precision=None):
    dims = (((1,), (1,)), ((), ()))
    return lax.dot_general(a, b, dims, precision=precision, preferred_element_type=F32)


def sum_body(sz, proj, cells, qt, *qt_faces):
    nodes, cols = proj.shape
    i = iota(cols, POS, 0)
    first = iota(cols, POS, 1) * (BLK * PA)
    in_slot = ((i >= first) & (i < first + BLK * PA)).astype(BF16)
    of_block = dot(in_slot, cells[...].astype(F32).astype(BF16))
    i = iota(cols, BLK, 0)
    block = twelfth(i)
    cell = jnp.sum(
        jnp.where((block & (BLK - 1)) == iota(cols, BLK, 1), of_block, 0.0), axis=1, keepdims=True
    )
    i, block = i[:, :1], block[:, :1]
    row = (block >> (BLK.bit_length() - 1)) * PA + (i - block * PA)
    key = cell.astype(jnp.int32) * SLOTS + row
    targets = len(sz.cells) * SLOTS
    pick = (key == iota(cols, targets, 1)).astype(BF16)
    summed = dot(proj[...], pick).astype(BF16)
    keys = [node_key(iota(sz.cell_pad, nodes, 0))]
    for j in range(sz.links):
        keys.append(
            jnp.where(
                iota(PAD * PAD, nodes, 0) < sz.fcell,
                node_key(iota(PAD * PAD, nodes, 0)) * EDGE + layer_received(sz, j),
                -1,
            )
        )
        low = iota(PAD * PAD, nodes, 0) & (PAD - 1)
        keys[-1] = jnp.where(low < EDGE, keys[-1], -1)
    expand = (jnp.concatenate(keys, axis=0) == iota(sz.cell_pad + sz.links * PAD * PAD, nodes, 1))
    full = dot(expand.astype(BF16), summed)
    for g in range(len(sz.cells)):
        value = full[:, g * SLOTS : (g + 1) * SLOTS]
        qt[g * sz.cell_pad : (g + 1) * sz.cell_pad, :] = value[: sz.cell_pad].astype(BF16)
    rest = sz.all_pad - sz.cell_pad * len(sz.cells)
    if rest:
        qt[sz.cell_pad * len(sz.cells) :, :] = jnp.zeros((rest, SLOTS), BF16)
    for j, qf in enumerate(qt_faces):
        at = sz.cell_pad + j * PAD * PAD
        rows = [full[at : at + PAD * PAD, g * SLOTS : (g + 1) * SLOTS] for g in range(len(sz.cells))]
        qf[...] = jnp.concatenate(rows, axis=0).T.astype(BF16)


def sum_matrices(sz, proj, cells):
    outs = [shape(sz.all_pad, SLOTS, BF16)]
    outs += [shape(SLOTS, len(sz.cells) * PAD * PAD, BF16)] * sz.links
    body = functools.partial(sum_body, sz)
    return kernel_call(body, outs, [proj, cells], flops=3 * 10**9, limit=32 << 20)


def slot_keys(sz, table, dim):
    exact = lax.Precision.HIGHEST
    shape2 = (SLOTS, POS) if dim == 0 else (POS, SLOTS)
    i, s = iota(*shape2, dim), iota(*shape2, 1 - dim)
    spread = ((i >= s * PA) & (i < s * PA + PA)).astype(F32)
    if dim == 0:
        atoms = dot_last(spread, table, exact)
    else:
        atoms = jnp.dot(table, spread, precision=exact, preferred_element_type=F32)
    devices = sz.shifts + 1
    at = iota(*atoms.shape, 1 - dim)
    me = lax.axis_index("gz")
    keys = []
    for shift in range(devices):
        chosen = jnp.where(at == lax.rem(me + shift, devices), atoms, 0.0)
        atom = jnp.sum(chosen, axis=1 - dim, keepdims=True).astype(jnp.int32)
        i = iota(*atom.shape, dim)
        keys.append((atom, jnp.where(atom >= 0, atom * PA + i - twelfth(i) * PA, -1)))
    return keys


def turn_body(sz, qt, kin, pot, atoms, coupling, *refs):
    q, kout, vout, maps = refs[:4]
    back = refs[4] if sz.links else None
    c_hi, c_lo, wide = refs[-3:]
    q[...] = qt[...].T
    nodes = kin.shape[0]
    expand = (node_key(iota(sz.cell_pad, nodes, 0)) == iota(sz.cell_pad, nodes, 1)).astype(BF16)
    gather = (node_key(iota(nodes, sz.cell_pad, 1)) == iota(nodes, sz.cell_pad, 0)).astype(BF16)
    tall = dot(expand, kin[...]).astype(BF16)
    kout[...] = dot(tall, gather).astype(BF16)
    value, values = pot[...], 0.0
    for _ in range(3):
        part = value.astype(BF16)
        values = values + dot_last(expand, part)
        value = value - part.astype(F32)
    for g in range(len(sz.cells)):
        vout[g * sz.cell_pad : (g + 1) * sz.cell_pad, :] = jnp.broadcast_to(
            values[:, g : g + 1], (sz.cell_pad, sz.orb)
        )
    table = atoms[...].astype(F32)
    rows, cols = slot_keys(sz, table, 0), slot_keys(sz, table, 1)
    known = [jnp.where(cols[0][1] >= 0, cols[0][1], -2)]
    for j, shift in enumerate(link_shifts(sz)):
        key = jnp.where(cols[shift][1] >= 0, cols[shift][1], -2)
        valid = link_valid(sz, j)
        known.append(key if valid is None else jnp.where(valid == 1, key, -2))
    for s in range(sz.shifts):
        for j, key in enumerate(known):
            maps[s * SLOTS : (s + 1) * SLOTS, j * SLOTS : (j + 1) * SLOTS] = (
                rows[s + 1][1] == key
            ).astype(BF16)
    for j, key in enumerate(known[1:]):
        back[:, j * SLOTS : (j + 1) * SLOTS] = (rows[0][1] == key).astype(BF16)
    pa, pb, atom_count = coupling.shape
    wide[...] = jnp.zeros(wide.shape, F32)
    wide[:, :pb, :] = coupling[...]
    table2 = wide[...].reshape(pa * 16, atom_count)
    hot = (rows[0][0] == iota(SLOTS, atom_count, 1)).astype(BF16)
    i, lane = iota(SLOTS, pa * 16, 0), iota(SLOTS, pa * 16, 1)
    own_row = (lane >> 4) == i - twelfth(i) * PA
    lane, j = iota(pa * 16, SLOTS, 0), iota(pa * 16, SLOTS, 1)
    fold = ((lane & 15) == j - twelfth(j) * PA).astype(BF16)
    same = twelfth(iota(SLOTS, SLOTS, 0)) == twelfth(iota(SLOTS, SLOTS, 1))
    for out in (c_hi, c_lo):
        part = table2.astype(BF16)
        table2 = table2 - part.astype(F32)
        picked = jnp.where(own_row, dot_last(hot, part), 0.0).astype(BF16)
        out[...] = jnp.where(same, dot(picked, fold), 0.0).astype(BF16)


def turn_matrices(sz, qt, kin, pot, atoms, coupling):
    known = (1 + sz.links) * SLOTS
    outs = [
        shape(SLOTS, sz.all_pad, BF16),
        shape(sz.cell_pad, sz.cell_pad, BF16),
        shape(len(sz.cells) * sz.cell_pad, sz.orb, F32),
        shape(sz.shifts * SLOTS, known, BF16),
        shape(SLOTS, sz.links * SLOTS, BF16),
        shape(SLOTS, SLOTS, BF16),
        shape(SLOTS, SLOTS, BF16),
    ]
    limit = (32 << 20) if sz.shifts < 8 else (56 << 20)
    return kernel_call(
        functools.partial(turn_body, sz),
        outs,
        [qt, kin, pot, atoms, coupling],
        scratch=[pltpu.VMEM((coupling.shape[0], 16, coupling.shape[2]), F32)],
        flops=10**9,
        limit=limit,
    )


def cell_block(sz, z, cell):
    p, q = cell
    layers = []
    for a in range(EDGE):
        start = (ORDER * p + a) * sz.line_x + ORDER * q * PAD
        layers.append(z[start : start + EDGE * PAD, :])
    layers.append(jnp.zeros((sz.cell_pad - sz.cell_rows, sz.orb), F32))
    return jnp.concatenate(layers, axis=0)


def write_pair(axis, low, high, first, second):
    first[...] = by_parity(axis, low, high).astype(first.dtype)
    second[...] = by_parity(axis, high, low).astype(second.dtype)


def read_pair(axis, first, second):
    one, two = first[...].astype(F32), second[...].astype(F32)
    return by_parity(axis, one, two), by_parity(axis, two, one)


def write_faces(sz, r, sx_one, sx_two, sy_lo, sy_hi):
    pad_x = jnp.zeros((sz.xface - sz.line_x, sz.orb), F32)
    pad_y = jnp.zeros((sz.yface - sz.nx * PAD, sz.orb), F32)
    last = (sz.nx - 1) * sz.line_x
    low = jnp.concatenate([r[0 : sz.line_x, :], pad_x], axis=0)
    high = jnp.concatenate([r[last : last + sz.line_x, :], pad_x], axis=0)
    write_pair("gx", low, high, sx_one, sx_two)
    for out, b in ((sy_lo, 0), (sy_hi, sz.ny - 1)):
        rows = [r[a * sz.line_x + b * PAD : a * sz.line_x + (b + 1) * PAD, :] for a in range(sz.nx)]
        out[...] = jnp.concatenate(rows + [pad_y], axis=0)


def face_outs(sz):
    return [shape(sz.xface, sz.orb, HALO)] * 2 + [shape(sz.yface, sz.orb, F32)] * 2


def start_body(sz, parts, r4, *faces):
    nz = parts.shape[2]
    r4[...] = jnp.zeros(r4.shape, F32)
    r4[:, :, :nz, :] = parts[...]
    write_faces(sz, r4.reshape(sz.rows, sz.orb), *faces)


def start_faces(sz, parts):
    outs = [jax.ShapeDtypeStruct((sz.nx, sz.ny, PAD, sz.orb), F32)] + face_outs(sz)
    r4, *faces = kernel_call(functools.partial(start_body, sz), outs, [parts])
    return r4.reshape(sz.rows, sz.orb), faces


def cross_body(sz, xr_one, xr_two, ry_lo, ry_hi, sy_one, sy_two):
    last = (sz.nx - 1) * PAD
    lo, hi = read_pair("gx", xr_one, xr_two)
    faces = []
    for raw, b in ((ry_lo, 0), (ry_hi, sz.ny - 1)):
        value = raw[...]
        parts = [
            value[:PAD] + lo[b * PAD : (b + 1) * PAD],
            value[PAD:last],
            value[last : last + PAD] + hi[b * PAD : (b + 1) * PAD],
            value[last + PAD :],
        ]
        faces.append(jnp.concatenate(parts, axis=0))
    write_pair("gy", *faces, sy_one, sy_two)


def cross_faces(sz, *faces):
    outs = [shape(sz.yface, sz.orb, HALO)] * 2
    return kernel_call(functools.partial(cross_body, sz), outs, list(faces))


def add_xy(sz, ra, r, xr_one, xr_two, yr_one, yr_two):
    ra[0 : sz.rows, :] = r[...]
    last = (sz.nx - 1) * sz.line_x
    low, high = read_pair("gx", xr_one, xr_two)
    ra[0 : sz.line_x, :] += low[: sz.line_x]
    ra[last : last + sz.line_x, :] += high[: sz.line_x]
    for value, b in zip(read_pair("gy", yr_one, yr_two), (0, sz.ny - 1)):
        for a in range(sz.nx):
            at = a * sz.line_x + b * PAD
            ra[at : at + PAD, :] += value[a * PAD : (a + 1) * PAD]


def pack_z(sz, ra, j):
    rows, c = [], layer_sent(sz, j)
    for a in range(sz.nx):
        for b in range(0, sz.face_b, PAD):
            rows.append(ra[pl.ds(a * sz.line_x + b * PAD + c, PAD, stride=PAD), :])
    rest = sz.zface - sz.nx * sz.face_b
    if rest:
        rows.append(jnp.zeros((rest, sz.orb), F32))
    value, valid = jnp.concatenate(rows, axis=0), link_valid(sz, j)
    return (value if valid is None else value * valid.astype(F32)).astype(HALO)


def add_z(sz, y, j, face):
    c = layer_received(sz, j)
    for a in range(sz.nx):
        for b in range(0, sz.ny, PAD):
            n = min(PAD, sz.ny - b)
            at = pl.ds(a * sz.line_x + b * PAD + c, n, stride=PAD)
            y[at, :] = y[at, :] + face[a * sz.face_b + b : a * sz.face_b + b + n]


def face_cells(sz, ra, j):
    rows, c = [], layer_sent(sz, j)
    for p, q in sz.cells:
        for a in range(EDGE):
            at = (ORDER * p + a) * sz.line_x + ORDER * q * PAD
            rows.append(ra[pl.ds(at + c, PAD, stride=PAD), :])
        rows.append(jnp.zeros((PAD, sz.orb), F32))
    return jnp.concatenate(rows, axis=0).astype(BF16)


def project_body(sz, has_local, refs):
    take = iter(refs)
    r = next(take)
    loc = next(take) if has_local else None
    halos = [next(take) for _ in range(4)]
    q = next(take)
    qfaces = [next(take) for _ in range(sz.links)]
    maps, back = next(take), next(take)
    y, own = next(take), next(take)
    messages = [next(take) for _ in range(sz.shifts)]
    ra = next(take)
    ra[sz.rows :, :] = jnp.zeros((sz.spill, sz.orb), F32)
    add_xy(sz, ra, r, *halos)
    y[...] = ra[0 : sz.rows, :] + loc[...] if has_local else ra[0 : sz.rows, :]
    blocks = [cell_block(sz, y, cell).astype(BF16) for cell in sz.cells]
    rest = sz.all_pad - sz.cell_pad * len(sz.cells)
    if rest:
        blocks.append(jnp.zeros((rest, sz.orb), BF16))
    beside = [dot(f[...], face_cells(sz, ra, j)).astype(BF16) for j, f in enumerate(qfaces)]
    sums = dot(q[...], jnp.concatenate(blocks, axis=0))
    mapped = dot(maps[...], jnp.concatenate([sums.astype(BF16)] + beside, axis=0))
    for s, message in enumerate(messages):
        message[0:SLOTS, :] = mapped[s * SLOTS : (s + 1) * SLOTS].astype(HALO)
        for j, shift in enumerate(link_shifts(sz)):
            if shift == s + 1:
                message[SLOTS : SLOTS + sz.zface, :] = pack_z(sz, ra, j)
    own[...] = sums + dot(back[...], jnp.concatenate(beside, axis=0))


def project(sz, r, loc, halos, q, qfaces, maps, back):
    outs = [shape(sz.rows, sz.orb, F32), shape(SLOTS, sz.orb, F32)]
    for s in range(1, sz.shifts + 1):
        outs.append(shape(SLOTS + (sz.zface if s in link_shifts(sz) else 0), sz.orb, HALO))
    arrays = [r] + ([loc] if loc is not None else []) + list(halos) + [q, *qfaces, maps, back]

    def body(*refs):
        project_body(sz, loc is not None, refs)

    y, own, *messages = kernel_call(
        body,
        outs,
        arrays,
        scratch=[pltpu.VMEM((sz.rows + sz.spill, sz.orb), F32)],
        flops=4 * 10**8,
        limit=(32 << 20) if sz.shifts < 8 else (56 << 20),
    )
    return y, own, messages


def apply_body(sz, has_previous, scale, refs):
    take = iter(refs)
    yin = next(take)
    previous = next(take) if has_previous else None
    own = next(take)
    messages = [next(take) for _ in range(sz.shifts)]
    c_hi, c_lo, qt, kin, pot = [next(take) for _ in range(5)]
    r, loc, y = next(take), next(take), next(take)
    faces = [next(take) for _ in range(4)]
    totals = own[...]
    for message in messages:
        totals = totals + message[0:SLOTS, :].astype(F32)
    high = totals.astype(BF16)
    low = (totals - high.astype(F32)).astype(BF16)
    coef = (dot(c_hi[...], high) + (dot(c_hi[...], low) + dot(c_lo[...], high))).astype(BF16)
    y[...] = yin[...]
    for j, shift in enumerate(link_shifts(sz)):
        add_z(sz, y, j, messages[shift - 1][SLOTS : SLOTS + sz.zface, :].astype(F32))
    blocks = [cell_block(sz, y, cell) for cell in sz.cells]
    stiff = dot(kin[...], jnp.concatenate([b.astype(BF16) for b in blocks], axis=1))
    r[...] = jnp.zeros(r.shape, F32)
    for g, (p, q) in enumerate(sz.cells):
        rows = slice(g * sz.cell_pad, (g + 1) * sz.cell_pad)
        value = stiff[:, g * sz.orb : (g + 1) * sz.orb] + pot[rows, :] * blocks[g]
        value = (value + dot(qt[rows, :], coef)) * scale
        for a in range(EDGE):
            start = (ORDER * p + a) * sz.line_x + ORDER * q * PAD
            r[start : start + EDGE * PAD, :] += value[a * EDGE * PAD : (a + 1) * EDGE * PAD]
    local = (-center_value * scale) * y[...]
    loc[...] = local - previous[...] if has_previous else local
    write_faces(sz, r, *faces)


def apply(sz, y, previous, own, messages, c_hi, c_lo, qt, kin, pot, scale):
    outs = [shape(sz.rows, sz.orb, F32)] * 3 + face_outs(sz)
    arrays = [y] + ([previous] if previous is not None else [])
    arrays += [own, *messages, c_hi, c_lo, qt, kin, pot]

    def body(*refs):
        apply_body(sz, previous is not None, scale, refs)

    r, loc, y, *faces = kernel_call(body, outs, arrays, flops=6 * 10**8, limit=32 << 20)
    return r, loc, y, faces


def last_faces_body(sz, refs):
    take = iter(refs)
    r = next(take)
    halos = [next(take) for _ in range(4)]
    outs = [next(take) for _ in range(sz.links)]
    ra = next(take)
    ra[sz.rows :, :] = jnp.zeros((sz.spill, sz.orb), F32)
    add_xy(sz, ra, r, *halos)
    for j, out in enumerate(outs):
        out[...] = pack_z(sz, ra, j)


def last_faces(sz, r, halos):
    def body(*refs):
        last_faces_body(sz, refs)

    outs = [shape(sz.zface, sz.orb, HALO)] * sz.links
    scratch = [pltpu.VMEM((sz.rows + sz.spill, sz.orb), F32)]
    return kernel_call(body, outs, [r, *halos], scratch=scratch)


def finish_body(sz, refs):
    take = iter(refs)
    r, loc = next(take), next(take)
    halos = [next(take) for _ in range(4)]
    zr = [next(take) for _ in range(sz.links)]
    out, ra = next(take), next(take)
    add_xy(sz, ra, r, *halos)
    for j, face in enumerate(zr):
        add_z(sz, ra, j, face[...].astype(F32))
    value = ra[0 : sz.rows, :] + loc[...]
    out[...] = value.reshape(sz.nx, sz.ny, PAD, sz.orb)[:, :, : out.shape[2], :]


def finish(sz, r, loc, halos, zr, nz):
    def body(*refs):
        finish_body(sz, refs)

    outs = [jax.ShapeDtypeStruct((sz.nx, sz.ny, nz, sz.orb), F32)]
    scratch = [pltpu.VMEM((sz.rows + sz.spill, sz.orb), F32)]
    return kernel_call(body, outs, [r, loc, *halos, *zr], scratch=scratch)[0]


def swap_faces(axis, one, two):
    count = lax.axis_size(axis)
    pairs = []
    for low in (1, 0):
        lows = range(low, count - 1, 2)
        pairs.append([(i, i + 1) for i in lows] + [(i + 1, i) for i in lows])
    return lax.ppermute(one, axis, pairs[0]), lax.ppermute(two, axis, pairs[1])


def local(parts, cell_matrix, cell_potential, projectors, slot_atom, slot_cells, coupling):
    nx, ny, nz, orbitals = parts.shape
    nodes = cell_matrix.shape[0]
    devices = lax.axis_size("gz")
    sz = Sizes(nx, ny, nz, orbitals, devices - 1)
    ring = [[(i, (i + s) % devices) for i in range(devices)] for s in range(devices)]

    r, faces = start_faces(sz, parts)

    def exchange_xy(sx_one, sx_two, sy_lo, sy_hi):
        xr = swap_faces("gx", sx_one, sx_two)
        cross = cross_faces(sz, *xr, sy_lo, sy_hi)
        yr = swap_faces("gy", *cross)
        return (*xr, *yr)

    halos = exchange_xy(*faces)
    proj = projectors.reshape(nodes, POS * BLK * PA)
    qt, *face_rows = sum_matrices(sz, proj, slot_cells.reshape(POS, BLK))
    qfaces = []
    for j, shift in enumerate(link_shifts(sz)):
        back = [(target, source) for source, target in ring[shift]]
        qfaces.append(lax.ppermute(face_rows[j], "gz", back))
    pot = jnp.transpose(cell_potential, (1, 2, 3, 0)).reshape(len(sz.cells), nodes)
    q, kin, pot, maps, back, c_hi, c_lo = turn_matrices(
        sz,
        qt,
        cell_matrix,
        pot,
        slot_atom.reshape(devices, POS),
        jnp.transpose(coupling, (1, 2, 0)),
    )

    loc = previous = None
    scale = 1.0 / half_width
    for step in range(STEPS):
        y, own, messages = project(sz, r, loc, halos, q, qfaces, maps, back)
        received = [lax.ppermute(m, "gz", ring[s + 1]) for s, m in enumerate(messages)]
        r, loc, y, faces = apply(sz, y, previous, own, received, c_hi, c_lo, qt, kin, pot, scale)
        previous, scale = y, 2.0 / half_width
        halos = exchange_xy(*faces)
    sent = last_faces(sz, r, halos)
    zr = [lax.ppermute(f, "gz", ring[s]) for f, s in zip(sent, link_shifts(sz))]
    return finish(sz, r, loc, halos, zr, nz)


def solution(mesh):
    in_specs = (
        P("gx", "gy", "gz", None),
        P(),
        P(None, "gx", "gy", "gz"),
        P("gx", "gy", "gz", None, None),
        P("gx", "gy", None, None),
        P("gx", "gy", "gz", None, None),
        P(("gx", "gy"), None, None),
    )
    out_specs = P("gx", "gy", "gz", None)
    return jax.shard_map(local, mesh=mesh, in_specs=in_specs, out_specs=out_specs, check_vma=False)
```

time: 134 us -> 82.7 us (0.62)
  local copies, waits for them, and re-layouts: 26.2 us -> 3.17 us
  waiting for transfers between devices: 34.6 us -> 24.6 us
  Pallas kernels: 22.1 us -> 14 us
  other arithmetic: 5.66 us -> 0 us
  starting transfers between devices: 44.1 us -> 40.3 us
    unnamed x51 -> x12, local copies, waits for them, and re-layouts: 16 us -> 2.36 us
    ppermute x18, waiting for transfers between devices: 24.6 us -> 11 us  [the longest x8 8.1 us: swap_faces(): lax.ppermute(two, axis, pairs[1])]
    pallas_call x15, Pallas kernels: 22.1 us -> 14 us  [kernel_call(): pl.pallas_call(body, out_shape=outs, in_specs=[VMEM] * len(arrays), out_s...]
    mul x3 -> x0, local copies, waits for them, and re-layouts: 7.17 us -> none  [the longest x1 6.97 us: local(): cblk = (picked[:, :, None, :] * eye[:, None, :, None]).reshape(SLOTS, SLOTS)]
    ppermute x3, waiting for transfers between devices: 9.99 us -> 13.6 us  [local(): lax.ppermute(m, 'gz', ring[s + 1])]
    mul x4 -> x0, other arithmetic: 2.6 us -> none  [the longest x1 1.91 us: local(): cblk = (picked[:, :, None, :] * eye[:, None, :, None]).reshape(SLOTS, SLOTS)]
    ppermute x18, starting transfers between devices: 40.4 us -> 37.9 us  [the longest x8 29.7 us: swap_faces(): lax.ppermute(two, axis, pairs[1])]
    add x2 -> x0, other arithmetic: 1.69 us -> none  [the longest x1 0.92 us: local(): col_key = (cell_index * SLOTS + slot_row)[:, None]]
  transfers between devices with their start and end apart: 21 -> 21, of which waited for: 12 -> 10; matrix products, arithmetic and copies ran while one was open for 9% -> 1% of each run, Pallas kernels for 2% -> 6%
where the time goes in v1:
time: 82.7 us; the launch traced here: 82.3 us
  starting transfers between devices  40.3 us (49%)
  waiting for transfers between devices  24.6 us (30%)
  Pallas kernels  14 us (17%)
  local copies, waits for them, and re-layouts  3.17 us (4%)
    ppermute x8, starting transfers between devices, swap_faces(): lax.ppermute(two, axis, pairs[1])  29.7 us
    pallas_call x15, Pallas kernels, kernel_call(): pl.pallas_call(body, out_shape=outs, in_specs=[VMEM] * len(arrays), out_s...  14 us
    ppermute x3, waiting for transfers between devices, local(): lax.ppermute(m, 'gz', ring[s + 1])  13.6 us
    ppermute x8, waiting for transfers between devices, swap_faces(): lax.ppermute(two, axis, pairs[1])  8.1 us
    ppermute x8, starting transfers between devices, swap_faces(): lax.ppermute(one, axis, pairs[0])  5.29 us
    ppermute x1, waiting for transfers between devices, local(): zr = [lax.ppermute(f, 'gz', ring[s]) for f, s in zip(sent, link_shifts(sz))]  2.87 us
    ppermute x3, starting transfers between devices, local(): lax.ppermute(m, 'gz', ring[s + 1])  2.45 us
    unnamed x12, local copies, waits for them, and re-layouts  2.36 us
  transfers between devices with their start and end apart: 21, of which 10 were waited for; matrix products, arithmetic and copies ran while one was open for 1% of the time, Pallas kernels for 6%

profile of v1, /device:TPU:0, one launch (start us, length us, event | category | flops | bytes accessed | tf_op | source)
XLA Modules:
  0.0 82.3 jit_solution(3815291087191689822)
XLA Ops:
  0.0 0.0 copy-start
  0.0 0.0 copy-start.1
  0.0 1.1 %copy-done.1 = f32[13,13,7,128]{3,2,1,0:T(8,128)S(1)} copy-done((f32[13,13,7,128]{3,2,1,0:T(8,128)S(1)}, f32[13,13,7,128]{3,2,1,0:T(8,128)}, u32[]{:S(2)}) %copy-start.1) | copy-done | bytes 605720
  1.1 0.1 shard_map.73
  1.2 0.7 collective-permute-start
  1.9 4.4 %collective-permute-start.1 = (bf16[112,128]{1,0:T(8,128)(2,1)S(1)}, bf16[112,128]{1,0:T(8,128)(2,1)S(1)}, u32[]{:S(2)}, u32[]{:S(2)}) collective-permute-start(bf16[112,128]{1,0:T(8,128)(2,1)S(1)} %get-tuple-element.58), channel_id=1, source_target_pairs={{0,8},{16,24},{8,0},{24,16},{1,9},{17,25},{9,1},{25,17},{2,10},{18... | collective-permute-start | bytes 86024 | tf_op jit(solution)/shard_map/ppermute | solution.py:521
  6.3 0.8 copy.8.cells
  7.0 0.0 copy-start.2
  7.0 1.2 %copy-done.2 = bf16[1,1,1,343,1536]{4,3,2,1,0:T(8,128)(2,1)S(1)} copy-done((bf16[1,1,1,343,1536]{4,3,2,1,0:T(8,128)(2,1)S(1)}, bf16[1,1,1,343,1536]{4,3,2,1,0:T(8,128)(2,1)}, u32[]{:S(2)}) %copy-start.2) | copy-done | bytes 1053720
  8.3 0.0 copy-start.3
  8.3 3.1 %shard_map.75 = (bf16[1664,384]{1,0:T(8,128)(2,1)S(1)}, bf16[384,256]{1,0:T(8,128)(2,1)S(1)}) custom-call(bf16[343,1536]{1,0:T(8,128)(2,1)S(1)} %bitcast.8, s32[32,4]{1,0:T(8,128)S(1)} %copy.8.cells), custom_call_target="tpu_custom_call" | custom-call | flops 3000000000 | bytes 2528768 | tf_op jit(solution)/shard_map/pallas_call | solution.py:57
  11.4 1.6 %collective-permute-start.4 = (bf16[384,256]{1,0:T(8,128)(2,1)S(1)}, bf16[384,256]{1,0:T(8,128)(2,1)S(1)}, u32[]{:S(2)}, u32[]{:S(2)}) collective-permute-start(bf16[384,256]{1,0:T(8,128)(2,1)S(1)} %get-tuple-element.65), channel_id=1, source_target_pairs={{1,0},{0,1},{3,2},{2,3},{5,4},{4,5},{7,6},{6,7},{9,8},{8,9},{11,10... | collective-permute-start | bytes 589832 | tf_op jit(solution)/shard_map/ppermute | solution.py:545
  13.0 0.0 copy-done
  13.0 0.0 collective-permute-done.xr_one.refs_1_
  13.0 0.0 collective-permute-done.1.xr_two.refs_2_
  13.1 0.7 collective-permute-start.2
  13.7 4.5 %collective-permute-start.3 = (bf16[112,128]{1,0:T(8,128)(2,1)S(1)}, bf16[112,128]{1,0:T(8,128)(2,1)S(1)}, u32[]{:S(2)}, u32[]{:S(2)}) collective-permute-start(bf16[112,128]{1,0:T(8,128)(2,1)S(1)} %get-tuple-element.62), channel_id=1, source_target_pairs={{0,2},{4,6},{2,0},{6,4},{1,3},{5,7},{3,1},{7,5},{8,10},{12,14},{10... | collective-permute-start | bytes 86024 | tf_op jit(solution)/shard_map/ppermute | solution.py:521
  18.2 0.0 copy-done.3
  18.2 0.0 copy-done.4
  18.2 0.0 copy-done.5
  18.2 1.8 %shard_map.76 = (bf16[384,1664]{1,0:T(8,128)(2,1)S(1)}, bf16[400,400]{1,0:T(8,128)(2,1)S(1)}, f32[1600,128]{1,0:T(8,128)S(1)}, bf16[384,768]{1,0:T(8,128)(2,1)S(...) custom-call(bf16[1664,384]{1,0:T(8,128)(2,1)S(1)} %get-tuple-element.63.qt.refs_5_.refs, ...), custom_call_target="tpu_custom_call" | custom-call | flops 1000000000 | bytes 5447570 | tf_op jit(solution)/shard_map/pallas_call | solution.py:57
  20.1 0.0 collective-permute-done.2.refs_3_
  20.1 0.0 collective-permute-done.3.refs_4_
  20.1 0.0 collective-permute-done.4.refs_6_.refs_7_
  20.1 1.4 %shard_map.77 = (f32[1352,128]{1,0:T(8,128)S(1)}, f32[384,128]{1,0:T(8,128)S(1)}, bf16[592,128]{1,0:T(8,128)(2,1)S(1)}) custom-call(f32[1352,128]{1,0:T(8,128)S(1)} %bitcast.7, bf16[112,128]{1,0:T(8,128)(2,1)S(1)} %collective-permute-done.xr_one.refs_1_, bf16[112,128]{1,0:T(8,128)(2,1)S(1)} %collective-permute-done.1.xr_two.refs_2_, ...), custom_call_target="tpu_custom_call" | custom-call | flops 400000000 | bytes 4206592 | tf_op jit(solution)/shard_map/pallas_call | solution.py:57
  21.5 0.6 collective-permute-start.5
  22.0 4.7 %collective-permute-done.5.refs_2_ = bf16[592,128]{1,0:T(8,128)(2,1)S(1)} collective-permute-done((bf16[592,128]{1,0:T(8,128)(2,1)S(1)}, bf16[592,128]{1,0:T(8,128)(2,1)S(1)}, u32[]{:S(2)}, u32[]{:S(2)}) %collective-permute-start.5) | collective-permute-done | bytes 151584 | tf_op jit(solution)/shard_map/ppermute | solution.py:560
  26.7 1.2 %shard_map.78 = (f32[1352,128]{1,0:T(8,128)S(1)}, f32[1352,128]{1,0:T(8,128)S(1)}, f32[1352,128]{1,0:T(8,128)S(1)}, bf16[112,128]{1,0:T(8,128)(2,1)S(1)}, bf16[1...) custom-call(f32[1352,128]{1,0:T(8,128)S(1)} %get-tuple-element.68.refs_0_, ...), custom_call_target="tpu_custom_call" | custom-call | flops 600000000 | bytes 6296064 | tf_op jit(solution)/shard_map/pallas_call | solution.py:57
  27.9 0.7 collective-permute-start.6
  28.6 1.6 %collective-permute-start.7 = (bf16[112,128]{1,0:T(8,128)(2,1)S(1)}, bf16[112,128]{1,0:T(8,128)(2,1)S(1)}, u32[]{:S(2)}, u32[]{:S(2)}) collective-permute-start(bf16[112,128]{1,0:T(8,128)(2,1)S(1)} %get-tuple-element.78), channel_id=1, source_target_pairs={{0,8},{16,24},{8,0},{24,16},{1,9},{17,25},{9,1},{25,17},{2,10},{18... | collective-permute-start | bytes 86024 | tf_op jit(solution)/shard_map/ppermute | solution.py:521
  30.2 0.0 collective-permute-done.6.xr_one.refs_2_
  30.2 0.9 %collective-permute-done.7.xr_two.refs_3_ = bf16[112,128]{1,0:T(8,128)(2,1)S(1)} collective-permute-done((bf16[112,128]{1,0:T(8,128)(2,1)S(1)}, bf16[112,128]{1,0:T(8,128)(2,1)S(1)}, u32[]{:S(2)}, u32[]{:S(2)}) %collective-permute-start.7) | collective-permute-done | bytes 28704 | tf_op jit(solution)/shard_map/ppermute | solution.py:521
  31.1 0.7 collective-permute-start.8
  31.8 3.5 %collective-permute-start.9 = (bf16[112,128]{1,0:T(8,128)(2,1)S(1)}, bf16[112,128]{1,0:T(8,128)(2,1)S(1)}, u32[]{:S(2)}, u32[]{:S(2)}) collective-permute-start(bf16[112,128]{1,0:T(8,128)(2,1)S(1)} %get-tuple-element.82), channel_id=1, source_target_pairs={{0,2},{4,6},{2,0},{6,4},{1,3},{5,7},{3,1},{7,5},{8,10},{12,14},{10... | collective-permute-start | bytes 86024 | tf_op jit(solution)/shard_map/ppermute | solution.py:521
  35.2 0.0 collective-permute-done.8.refs_4_
  35.2 1.8 %collective-permute-done.9.refs_5_ = bf16[112,128]{1,0:T(8,128)(2,1)S(1)} collective-permute-done((bf16[112,128]{1,0:T(8,128)(2,1)S(1)}, bf16[112,128]{1,0:T(8,128)(2,1)S(1)}, u32[]{:S(2)}, u32[]{:S(2)}) %collective-permute-start.9) | collective-permute-done | bytes 28704 | tf_op jit(solution)/shard_map/ppermute | solution.py:521
  37.1 1.4 %shard_map.80 = (f32[1352,128]{1,0:T(8,128)S(1)}, f32[384,128]{1,0:T(8,128)S(1)}, bf16[592,128]{1,0:T(8,128)(2,1)S(1)}) custom-call(f32[1352,128]{1,0:T(8,128)S(1)} %get-tuple-element.75.refs_0_, f32[1352,128]{1,0:T(8,128)S(1)} %get-tuple-element.76.refs_1_, bf16[112,128]{1,0:T(8,128)(2,1)S(1)} %collective-permute-done.6.xr_one.refs_2_, ...), custom_call_target="tpu_custom_call" | custom-call | flops 400000000 | bytes 4898816 | tf_op jit(solution)/shard_map/pallas_call | solution.py:57
  38.5 1.3 %collective-permute-start.10 = (bf16[592,128]{1,0:T(8,128)(2,1)S(1)}, bf16[592,128]{1,0:T(8,128)(2,1)S(1)}, u32[]{:S(2)}, u32[]{:S(2)}) collective-permute-start(bf16[592,128]{1,0:T(8,128)(2,1)S(1)} %get-tuple-element.86), channel_id=1, source_target_pairs={{0,1},{1,0},{2,3},{3,2},{4,5},{5,4},{6,7},{7,6},{8,9},{9,8},{10,11... | collective-permute-start | bytes 454664 | tf_op jit(solution)/shard_map/ppermute | solution.py:560
  39.8 4.1 %collective-permute-done.10.refs_3_ = bf16[592,128]{1,0:T(8,128)(2,1)S(1)} collective-permute-done((bf16[592,128]{1,0:T(8,128)(2,1)S(1)}, bf16[592,128]{1,0:T(8,128)(2,1)S(1)}, u32[]{:S(2)}, u32[]{:S(2)}) %collective-permute-start.10) | collective-permute-done | bytes 151584 | tf_op jit(solution)/shard_map/ppermute | solution.py:560
  43.9 1.2 %shard_map.81 = (f32[1352,128]{1,0:T(8,128)S(1)}, f32[1352,128]{1,0:T(8,128)S(1)}, f32[1352,128]{1,0:T(8,128)S(1)}, bf16[112,128]{1,0:T(8,128)(2,1)S(1)}, bf16[1...) custom-call(f32[1352,128]{1,0:T(8,128)S(1)} %get-tuple-element.83.refs_0_, ...), custom_call_target="tpu_custom_call" | custom-call | flops 600000000 | bytes 6988288 | tf_op jit(solution)/shard_map/pallas_call | solution.py:57
  45.0 0.7 collective-permute-start.11
  45.7 3.5 %collective-permute-start.12 = (bf16[112,128]{1,0:T(8,128)(2,1)S(1)}, bf16[112,128]{1,0:T(8,128)(2,1)S(1)}, u32[]{:S(2)}, u32[]{:S(2)}) collective-permute-start(bf16[112,128]{1,0:T(8,128)(2,1)S(1)} %get-tuple-element.90), channel_id=1, source_target_pairs={{0,8},{16,24},{8,0},{24,16},{1,9},{17,25},{9,1},{25,17},{2,10},{18... | collective-permute-start | bytes 86024 | tf_op jit(solution)/shard_map/ppermute | solution.py:521
  49.2 0.0 collective-permute-done.11.xr_one.refs_2_
  49.2 0.9 %collective-permute-done.12.xr_two.refs_3_ = bf16[112,128]{1,0:T(8,128)(2,1)S(1)} collective-permute-done((bf16[112,128]{1,0:T(8,128)(2,1)S(1)}, bf16[112,128]{1,0:T(8,128)(2,1)S(1)}, u32[]{:S(2)}, u32[]{:S(2)}) %collective-permute-start.12) | collective-permute-done | bytes 28704 | tf_op jit(solution)/shard_map/ppermute | solution.py:521
  50.1 0.7 collective-permute-start.13
  50.8 4.9 %collective-permute-start.14 = (bf16[112,128]{1,0:T(8,128)(2,1)S(1)}, bf16[112,128]{1,0:T(8,128)(2,1)S(1)}, u32[]{:S(2)}, u32[]{:S(2)}) collective-permute-start(bf16[112,128]{1,0:T(8,128)(2,1)S(1)} %get-tuple-element.94), channel_id=1, source_target_pairs={{0,2},{4,6},{2,0},{6,4},{1,3},{5,7},{3,1},{7,5},{8,10},{12,14},{10... | collective-permute-start | bytes 86024 | tf_op jit(solution)/shard_map/ppermute | solution.py:521
  55.7 0.0 collective-permute-done.13.refs_4_
  55.7 1.8 %collective-permute-done.14.refs_5_ = bf16[112,128]{1,0:T(8,128)(2,1)S(1)} collective-permute-done((bf16[112,128]{1,0:T(8,128)(2,1)S(1)}, bf16[112,128]{1,0:T(8,128)(2,1)S(1)}, u32[]{:S(2)}, u32[]{:S(2)}) %collective-permute-start.14) | collective-permute-done | bytes 28704 | tf_op jit(solution)/shard_map/ppermute | solution.py:521
  57.5 1.4 %shard_map.83 = (f32[1352,128]{1,0:T(8,128)S(1)}, f32[384,128]{1,0:T(8,128)S(1)}, bf16[592,128]{1,0:T(8,128)(2,1)S(1)}) custom-call(f32[1352,128]{1,0:T(8,128)S(1)} %get-tuple-element.87.refs_0_, f32[1352,128]{1,0:T(8,128)S(1)} %get-tuple-element.88.refs_1_, bf16[112,128]{1,0:T(8,128)(2,1)S(1)} %collective-permute-done.11.xr_one.refs_2_, ...), custom_call_target="tpu_custom_call" | custom-call | flops 400000000 | bytes 4898816 | tf_op jit(solution)/shard_map/pallas_call | solution.py:57
  58.9 0.6 collective-permute-start.15
  59.5 4.8 %collective-permute-done.15.refs_3_ = bf16[592,128]{1,0:T(8,128)(2,1)S(1)} collective-permute-done((bf16[592,128]{1,0:T(8,128)(2,1)S(1)}, bf16[592,128]{1,0:T(8,128)(2,1)S(1)}, u32[]{:S(2)}, u32[]{:S(2)}) %collective-permute-start.15) | collective-permute-done | bytes 151584 | tf_op jit(solution)/shard_map/ppermute | solution.py:560
  64.3 1.3 %shard_map.84 = (f32[1352,128]{1,0:T(8,128)S(1)}, f32[1352,128]{1,0:T(8,128)S(1)}, f32[1352,128]{1,0:T(8,128)}, bf16[112,128]{1,0:T(8,128)(2,1)S(1)}, bf16[112,1...) custom-call(f32[1352,128]{1,0:T(8,128)S(1)} %get-tuple-element.95.refs_0_, ...), custom_call_target="tpu_custom_call" | custom-call | flops 600000000 | bytes 6988288 | tf_op jit(solution)/shard_map/pallas_call | solution.py:57
  65.6 0.7 collective-permute-start.16
  66.3 3.5 %collective-permute-start.17 = (bf16[112,128]{1,0:T(8,128)(2,1)S(1)}, bf16[112,128]{1,0:T(8,128)(2,1)S(1)}, u32[]{:S(2)}, u32[]{:S(2)}) collective-permute-start(bf16[112,128]{1,0:T(8,128)(2,1)S(1)} %get-tuple-element.102), channel_id=1, source_target_pairs={{0,8},{16,24},{8,0},{24,16},{1,9},{17,25},{9,1},{25,17},{2,10},{18... | collective-permute-start | bytes 86024 | tf_op jit(solution)/shard_map/ppermute | solution.py:521
  69.8 0.0 collective-permute-done.16.xr_one.refs_1_.refs_2_
  69.8 0.9 %collective-permute-done.17.xr_two.refs_2_.refs_3_ = bf16[112,128]{1,0:T(8,128)(2,1)S(1)} collective-permute-done((bf16[112,128]{1,0:T(8,128)(2,1)S(1)}, bf16[112,128]{1,0:T(8,128)(2,1)S(1)}, u32[]{:S(2)}, u32[]{:S(2)}) %collective-permute-start.17) | collective-permute-done | bytes 28704 | tf_op jit(solution)/shard_map/ppermute | solution.py:521
  70.7 0.7 collective-permute-start.18
  71.4 3.8 %collective-permute-start.19 = (bf16[112,128]{1,0:T(8,128)(2,1)S(1)}, bf16[112,128]{1,0:T(8,128)(2,1)S(1)}, u32[]{:S(2)}, u32[]{:S(2)}) collective-permute-start(bf16[112,128]{1,0:T(8,128)(2,1)S(1)} %get-tuple-element.106), channel_id=1, source_target_pairs={{0,2},{4,6},{2,0},{6,4},{1,3},{5,7},{3,1},{7,5},{8,10},{12,14},{10... | collective-permute-start | bytes 86024 | tf_op jit(solution)/shard_map/ppermute | solution.py:521
  75.1 0.0 collective-permute-done.18.refs_3_.refs_4_
  75.1 1.8 %collective-permute-done.19.refs_4_.refs_5_ = bf16[112,128]{1,0:T(8,128)(2,1)S(1)} collective-permute-done((bf16[112,128]{1,0:T(8,128)(2,1)S(1)}, bf16[112,128]{1,0:T(8,128)(2,1)S(1)}, u32[]{:S(2)}, u32[]{:S(2)}) %collective-permute-start.19) | collective-permute-done | bytes 28704 | tf_op jit(solution)/shard_map/ppermute | solution.py:521
  77.0 0.1 shard_map.86
  77.1 1.3 %collective-permute-start.20 = (bf16[208,128]{1,0:T(8,128)(2,1)S(1)}, bf16[208,128]{1,0:T(8,128)(2,1)S(1)}, u32[]{:S(2)}, u32[]{:S(2)}) collective-permute-start(bf16[208,128]{1,0:T(8,128)(2,1)S(1)} %shard_map.86), channel_id=1, source_target_pairs={{0,1},{1,0},{2,3},{3,2},{4,5},{5,4},{6,7},{7,6},{8,9},{9,8},{10,11... | collective-permute-start | bytes 159752 | tf_op jit(solution)/shard_map/ppermute | solution.py:565
  78.4 2.9 %collective-permute-done.20.refs_6_ = bf16[208,128]{1,0:T(8,128)(2,1)S(1)} collective-permute-done((bf16[208,128]{1,0:T(8,128)(2,1)S(1)}, bf16[208,128]{1,0:T(8,128)(2,1)S(1)}, u32[]{:S(2)}, u32[]{:S(2)}) %collective-permute-start.20) | collective-permute-done | bytes 53280 | tf_op jit(solution)/shard_map/ppermute | solution.py:565
  81.3 1.0 %shard_map.87 = f32[13,13,7,128]{3,2,1,0:T(8,128)} custom-call(f32[1352,128]{1,0:T(8,128)S(1)} %get-tuple-element.99.refs_0_, f32[1352,128]{1,0:T(8,128)S(1)} %get-tuple-element.100.refs_1_, bf16[112,128]{1,0:T(8,128)(2,1)S(1)} %collective-permute-done.16.xr_one.refs_1_.refs_2_, bf16[112,128]{1,0:T(8,128)(2,1)S(1)} %collective-permute-done.17.xr_two.refs_2_.refs_3_, ...), custom_call_target="tpu_custom_call" | custom-call | bytes 2158080 | tf_op jit(solution)/shard_map/pallas_call | solution.py:57
  (8 shorter events, 0.1 us)
Async XLA Ops:
  0.0 13.0 %copy-start = (f32[343,2,2,1]{0,3,2,1:T(1,128)S(1)}, f32[343,2,2,1]{0,3,2,1:T(1,128)}, u32[]{:S(2)}) copy-start(f32[343,2,2,1]{0,3,2,1:T(1,128)} %param.9) | copy-start | bytes 16468
  0.0 1.1 %copy-start.1 = (f32[13,13,7,128]{3,2,1,0:T(8,128)S(1)}, f32[13,13,7,128]{3,2,1,0:T(8,128)}, u32[]{:S(2)}) copy-start(f32[13,13,7,128]{3,2,1,0:T(8,128)} %parts.1) | copy-start | bytes 1817092
  1.2 11.8 %collective-permute-start = (bf16[112,128]{1,0:T(8,128)(2,1)S(1)}, bf16[112,128]{1,0:T(8,128)(2,1)S(1)}, u32[]{:S(2)}, u32[]{:S(2)}) collective-permute-start(bf16[112,128]{1,0:T(8,128)(2,1)S(1)} %get-tuple-element.57), channel_id=1, source_target_pairs={{8,16},{16,8},{9,17},{17,9},{10,18},{18,10},{11,19},{19,11},{12,20... | collective-permute-start | bytes 86024 | tf_op jit(solution)/shard_map/ppermute | solution.py:521
  1.9 11.1 %collective-permute-start.1 = (bf16[112,128]{1,0:T(8,128)(2,1)S(1)}, bf16[112,128]{1,0:T(8,128)(2,1)S(1)}, u32[]{:S(2)}, u32[]{:S(2)}) collective-permute-start(bf16[112,128]{1,0:T(8,128)(2,1)S(1)} %get-tuple-element.58), channel_id=1, source_target_pairs={{0,8},{16,24},{8,0},{24,16},{1,9},{17,25},{9,1},{25,17},{2,10},{18... | collective-permute-start | bytes 86024 | tf_op jit(solution)/shard_map/ppermute | solution.py:521
  7.0 1.2 %copy-start.2 = (bf16[1,1,1,343,1536]{4,3,2,1,0:T(8,128)(2,1)S(1)}, bf16[1,1,1,343,1536]{4,3,2,1,0:T(8,128)(2,1)}, u32[]{:S(2)}) copy-start(bf16[1,1,1,343,1536]{4,3,2,1,0:T(8,128)(2,1)} %param.10) | copy-start | bytes 3161092
  8.3 10.0 %copy-start.3 = (bf16[343,343]{1,0:T(8,128)(2,1)S(1)}, bf16[343,343]{1,0:T(8,128)(2,1)}, u32[]{:S(2)}) copy-start(bf16[343,343]{1,0:T(8,128)(2,1)} %kin.1) | copy-start | bytes 705898
  8.3 10.0 %copy-start.4 = (f32[64,12,12]{0,2,1:T(8,128)S(1)}, f32[64,12,12]{0,2,1:T(8,128)}, u32[]{:S(2)}) copy-start(f32[64,12,12]{0,2,1:T(8,128)} %param.13) | copy-start | bytes 110596
  8.3 10.0 %copy-start.5 = (s32[1,1,2,32]{3,2,1,0:T(2,128)S(1)}, s32[1,1,2,32]{3,2,1,0:T(2,128)}, u32[]{:S(2)}) copy-start(s32[1,1,2,32]{3,2,1,0:T(2,128)} %param.11) | copy-start | bytes 772
  11.4 8.7 %collective-permute-start.4 = (bf16[384,256]{1,0:T(8,128)(2,1)S(1)}, bf16[384,256]{1,0:T(8,128)(2,1)S(1)}, u32[]{:S(2)}, u32[]{:S(2)}) collective-permute-start(bf16[384,256]{1,0:T(8,128)(2,1)S(1)} %get-tuple-element.65), channel_id=1, source_target_pairs={{1,0},{0,1},{3,2},{2,3},{5,4},{4,5},{7,6},{6,7},{9,8},{8,9},{11,10... | collective-permute-start | bytes 589832 | tf_op jit(solution)/shard_map/ppermute | solution.py:545
  13.1 7.0 %collective-permute-start.2 = (bf16[112,128]{1,0:T(8,128)(2,1)S(1)}, bf16[112,128]{1,0:T(8,128)(2,1)S(1)}, u32[]{:S(2)}, u32[]{:S(2)}) collective-permute-start(bf16[112,128]{1,0:T(8,128)(2,1)S(1)} %get-tuple-element.61), channel_id=1, source_target_pairs={{2,4},{4,2},{3,5},{5,3},{10,12},{12,10},{11,13},{13,11},{18,20},{2... | collective-permute-start | bytes 86024 | tf_op jit(solution)/shard_map/ppermute | solution.py:521
  13.7 6.3 %collective-permute-start.3 = (bf16[112,128]{1,0:T(8,128)(2,1)S(1)}, bf16[112,128]{1,0:T(8,128)(2,1)S(1)}, u32[]{:S(2)}, u32[]{:S(2)}) collective-permute-start(bf16[112,128]{1,0:T(8,128)(2,1)S(1)} %get-tuple-element.62), channel_id=1, source_target_pairs={{0,2},{4,6},{2,0},{6,4},{1,3},{5,7},{3,1},{7,5},{8,10},{12,14},{10... | collective-permute-start | bytes 86024 | tf_op jit(solution)/shard_map/ppermute | solution.py:521
  21.5 5.3 %collective-permute-start.5 = (bf16[592,128]{1,0:T(8,128)(2,1)S(1)}, bf16[592,128]{1,0:T(8,128)(2,1)S(1)}, u32[]{:S(2)}, u32[]{:S(2)}) collective-permute-start(bf16[592,128]{1,0:T(8,128)(2,1)S(1)} %get-tuple-element.70), channel_id=1, source_target_pairs={{0,1},{1,0},{2,3},{3,2},{4,5},{5,4},{6,7},{7,6},{8,9},{9,8},{10,11... | collective-permute-start | bytes 454664 | tf_op jit(solution)/shard_map/ppermute | solution.py:560
  27.9 2.3 %collective-permute-start.6 = (bf16[112,128]{1,0:T(8,128)(2,1)S(1)}, bf16[112,128]{1,0:T(8,128)(2,1)S(1)}, u32[]{:S(2)}, u32[]{:S(2)}) collective-permute-start(bf16[112,128]{1,0:T(8,128)(2,1)S(1)} %get-tuple-element.77), channel_id=1, source_target_pairs={{8,16},{16,8},{9,17},{17,9},{10,18},{18,10},{11,19},{19,11},{12,20... | collective-permute-start | bytes 86024 | tf_op jit(solution)/shard_map/ppermute | solution.py:521
  28.6 2.5 %collective-permute-start.7 = (bf16[112,128]{1,0:T(8,128)(2,1)S(1)}, bf16[112,128]{1,0:T(8,128)(2,1)S(1)}, u32[]{:S(2)}, u32[]{:S(2)}) collective-permute-start(bf16[112,128]{1,0:T(8,128)(2,1)S(1)} %get-tuple-element.78), channel_id=1, source_target_pairs={{0,8},{16,24},{8,0},{24,16},{1,9},{17,25},{9,1},{25,17},{2,10},{18... | collective-permute-start | bytes 86024 | tf_op jit(solution)/shard_map/ppermute | solution.py:521
  31.1 4.1 %collective-permute-start.8 = (bf16[112,128]{1,0:T(8,128)(2,1)S(1)}, bf16[112,128]{1,0:T(8,128)(2,1)S(1)}, u32[]{:S(2)}, u32[]{:S(2)}) collective-permute-start(bf16[112,128]{1,0:T(8,128)(2,1)S(1)} %get-tuple-element.81), channel_id=1, source_target_pairs={{2,4},{4,2},{3,5},{5,3},{10,12},{12,10},{11,13},{13,11},{18,20},{2... | collective-permute-start | bytes 86024 | tf_op jit(solution)/shard_map/ppermute | solution.py:521
  31.8 5.3 %collective-permute-start.9 = (bf16[112,128]{1,0:T(8,128)(2,1)S(1)}, bf16[112,128]{1,0:T(8,128)(2,1)S(1)}, u32[]{:S(2)}, u32[]{:S(2)}) collective-permute-start(bf16[112,128]{1,0:T(8,128)(2,1)S(1)} %get-tuple-element.82), channel_id=1, source_target_pairs={{0,2},{4,6},{2,0},{6,4},{1,3},{5,7},{3,1},{7,5},{8,10},{12,14},{10... | collective-permute-start | bytes 86024 | tf_op jit(solution)/shard_map/ppermute | solution.py:521
  38.5 5.4 %collective-permute-start.10 = (bf16[592,128]{1,0:T(8,128)(2,1)S(1)}, bf16[592,128]{1,0:T(8,128)(2,1)S(1)}, u32[]{:S(2)}, u32[]{:S(2)}) collective-permute-start(bf16[592,128]{1,0:T(8,128)(2,1)S(1)} %get-tuple-element.86), channel_id=1, source_target_pairs={{0,1},{1,0},{2,3},{3,2},{4,5},{5,4},{6,7},{7,6},{8,9},{9,8},{10,11... | collective-permute-start | bytes 454664 | tf_op jit(solution)/shard_map/ppermute | solution.py:560
  45.0 4.2 %collective-permute-start.11 = (bf16[112,128]{1,0:T(8,128)(2,1)S(1)}, bf16[112,128]{1,0:T(8,128)(2,1)S(1)}, u32[]{:S(2)}, u32[]{:S(2)}) collective-permute-start(bf16[112,128]{1,0:T(8,128)(2,1)S(1)} %get-tuple-element.89), channel_id=1, source_target_pairs={{8,16},{16,8},{9,17},{17,9},{10,18},{18,10},{11,19},{19,11},{12,20... | collective-permute-start | bytes 86024 | tf_op jit(solution)/shard_map/ppermute | solution.py:521
  45.7 4.4 %collective-permute-start.12 = (bf16[112,128]{1,0:T(8,128)(2,1)S(1)}, bf16[112,128]{1,0:T(8,128)(2,1)S(1)}, u32[]{:S(2)}, u32[]{:S(2)}) collective-permute-start(bf16[112,128]{1,0:T(8,128)(2,1)S(1)} %get-tuple-element.90), channel_id=1, source_target_pairs={{0,8},{16,24},{8,0},{24,16},{1,9},{17,25},{9,1},{25,17},{2,10},{18... | collective-permute-start | bytes 86024 | tf_op jit(solution)/shard_map/ppermute | solution.py:521
  50.1 5.6 %collective-permute-start.13 = (bf16[112,128]{1,0:T(8,128)(2,1)S(1)}, bf16[112,128]{1,0:T(8,128)(2,1)S(1)}, u32[]{:S(2)}, u32[]{:S(2)}) collective-permute-start(bf16[112,128]{1,0:T(8,128)(2,1)S(1)} %get-tuple-element.93), channel_id=1, source_target_pairs={{2,4},{4,2},{3,5},{5,3},{10,12},{12,10},{11,13},{13,11},{18,20},{2... | collective-permute-start | bytes 86024 | tf_op jit(solution)/shard_map/ppermute | solution.py:521
  50.8 6.8 %collective-permute-start.14 = (bf16[112,128]{1,0:T(8,128)(2,1)S(1)}, bf16[112,128]{1,0:T(8,128)(2,1)S(1)}, u32[]{:S(2)}, u32[]{:S(2)}) collective-permute-start(bf16[112,128]{1,0:T(8,128)(2,1)S(1)} %get-tuple-element.94), channel_id=1, source_target_pairs={{0,2},{4,6},{2,0},{6,4},{1,3},{5,7},{3,1},{7,5},{8,10},{12,14},{10... | collective-permute-start | bytes 86024 | tf_op jit(solution)/shard_map/ppermute | solution.py:521
  58.9 5.4 %collective-permute-start.15 = (bf16[592,128]{1,0:T(8,128)(2,1)S(1)}, bf16[592,128]{1,0:T(8,128)(2,1)S(1)}, u32[]{:S(2)}, u32[]{:S(2)}) collective-permute-start(bf16[592,128]{1,0:T(8,128)(2,1)S(1)} %get-tuple-element.98), channel_id=1, source_target_pairs={{0,1},{1,0},{2,3},{3,2},{4,5},{5,4},{6,7},{7,6},{8,9},{9,8},{10,11... | collective-permute-start | bytes 454664 | tf_op jit(solution)/shard_map/ppermute | solution.py:560
  65.6 4.2 %collective-permute-start.16 = (bf16[112,128]{1,0:T(8,128)(2,1)S(1)}, bf16[112,128]{1,0:T(8,128)(2,1)S(1)}, u32[]{:S(2)}, u32[]{:S(2)}) collective-permute-start(bf16[112,128]{1,0:T(8,128)(2,1)S(1)} %get-tuple-element.101), channel_id=1, source_target_pairs={{8,16},{16,8},{9,17},{17,9},{10,18},{18,10},{11,19},{19,11},{12,20... | collective-permute-start | bytes 86024 | tf_op jit(solution)/shard_map/ppermute | solution.py:521
  66.3 4.4 %collective-permute-start.17 = (bf16[112,128]{1,0:T(8,128)(2,1)S(1)}, bf16[112,128]{1,0:T(8,128)(2,1)S(1)}, u32[]{:S(2)}, u32[]{:S(2)}) collective-permute-start(bf16[112,128]{1,0:T(8,128)(2,1)S(1)} %get-tuple-element.102), channel_id=1, source_target_pairs={{0,8},{16,24},{8,0},{24,16},{1,9},{17,25},{9,1},{25,17},{2,10},{18... | collective-permute-start | bytes 86024 | tf_op jit(solution)/shard_map/ppermute | solution.py:521
  70.7 4.5 %collective-permute-start.18 = (bf16[112,128]{1,0:T(8,128)(2,1)S(1)}, bf16[112,128]{1,0:T(8,128)(2,1)S(1)}, u32[]{:S(2)}, u32[]{:S(2)}) collective-permute-start(bf16[112,128]{1,0:T(8,128)(2,1)S(1)} %get-tuple-element.105), channel_id=1, source_target_pairs={{2,4},{4,2},{3,5},{5,3},{10,12},{12,10},{11,13},{13,11},{18,20},{2... | collective-permute-start | bytes 86024 | tf_op jit(solution)/shard_map/ppermute | solution.py:521
  71.4 5.6 %collective-permute-start.19 = (bf16[112,128]{1,0:T(8,128)(2,1)S(1)}, bf16[112,128]{1,0:T(8,128)(2,1)S(1)}, u32[]{:S(2)}, u32[]{:S(2)}) collective-permute-start(bf16[112,128]{1,0:T(8,128)(2,1)S(1)} %get-tuple-element.106), channel_id=1, source_target_pairs={{0,2},{4,6},{2,0},{6,4},{1,3},{5,7},{3,1},{7,5},{8,10},{12,14},{10... | collective-permute-start | bytes 86024 | tf_op jit(solution)/shard_map/ppermute | solution.py:521
  77.1 4.2 %collective-permute-start.20 = (bf16[208,128]{1,0:T(8,128)(2,1)S(1)}, bf16[208,128]{1,0:T(8,128)(2,1)S(1)}, u32[]{:S(2)}, u32[]{:S(2)}) collective-permute-start(bf16[208,128]{1,0:T(8,128)(2,1)S(1)} %shard_map.86), channel_id=1, source_target_pairs={{0,1},{1,0},{2,3},{3,2},{4,5},{5,4},{6,7},{7,6},{8,9},{9,8},{10,11... | collective-permute-start | bytes 159752 | tf_op jit(solution)/shard_map/ppermute | solution.py:565

commit v2 on v1

--- a/solution.py
+++ b/solution.py
@@ -125,7 +125,7 @@
     i = iota(cols, POS, 0)
     first = iota(cols, POS, 1) * (BLK * PA)
     in_slot = ((i >= first) & (i < first + BLK * PA)).astype(BF16)
-    of_block = dot(in_slot, cells[...].astype(F32).astype(BF16))
+    of_block = dot_last(in_slot, cells[...].astype(F32).astype(BF16))
     i = iota(cols, BLK, 0)
     block = twelfth(i)
     cell = jnp.sum(
@@ -136,7 +136,6 @@
     key = cell.astype(jnp.int32) * SLOTS + row
     targets = len(sz.cells) * SLOTS
     pick = (key == iota(cols, targets, 1)).astype(BF16)
-    summed = dot(proj[...], pick).astype(BF16)
     keys = [node_key(iota(sz.cell_pad, nodes, 0))]
     for j in range(sz.links):
         keys.append(
@@ -149,6 +148,7 @@
         low = iota(PAD * PAD, nodes, 0) & (PAD - 1)
         keys[-1] = jnp.where(low < EDGE, keys[-1], -1)
     expand = (jnp.concatenate(keys, axis=0) == iota(sz.cell_pad + sz.links * PAD * PAD, nodes, 1))
+    summed = dot(proj[...], pick).astype(BF16)
     full = dot(expand.astype(BF16), summed)
     for g in range(len(sz.cells)):
         value = full[:, g * SLOTS : (g + 1) * SLOTS]
@@ -279,7 +279,9 @@
 
 def read_pair(axis, first, second):
     one, two = first[...].astype(F32), second[...].astype(F32)
-    return by_parity(axis, one, two), by_parity(axis, two, one)
+    low, high = by_parity(axis, one, two), by_parity(axis, two, one)
+    at, last = lax.axis_index(axis), lax.axis_size(axis) - 1
+    return jnp.where(at > 0, low, 0.0), jnp.where(at < last, high, 0.0)
 
 
 def write_faces(sz, r, sx_one, sx_two, sy_lo, sy_hi):
@@ -517,7 +519,9 @@
     pairs = []
     for low in (1, 0):
         lows = range(low, count - 1, 2)
-        pairs.append([(i, i + 1) for i in lows] + [(i + 1, i) for i in lows])
+        pair = [(i, i + 1) for i in lows] + [(i + 1, i) for i in lows]
+        alone = set(range(count)) - {source for source, _ in pair}
+        pairs.append(pair + [(i, i) for i in sorted(alone)])
     return lax.ppermute(one, axis, pairs[0]), lax.ppermute(two, axis, pairs[1])
 
 
@@ -528,6 +532,8 @@
     sz = Sizes(nx, ny, nz, orbitals, devices - 1)
     ring = [[(i, (i + s) % devices) for i in range(devices)] for s in range(devices)]
 
+    proj = projectors.reshape(nodes, POS * BLK * PA)
+    cells = jnp.transpose(slot_cells.reshape(POS, BLK))
     r, faces = start_faces(sz, parts)
 
     def exchange_xy(sx_one, sx_two, sy_lo, sy_hi):
@@ -537,8 +543,7 @@
         return (*xr, *yr)
 
     halos = exchange_xy(*faces)
-    proj = projectors.reshape(nodes, POS * BLK * PA)
-    qt, *face_rows = sum_matrices(sz, proj, slot_cells.reshape(POS, BLK))
+    qt, *face_rows = sum_matrices(sz, proj, cells)
     qfaces = []
     for j, shift in enumerate(link_shifts(sz)):
         back = [(target, source) for source, target in ring[shift]]

time: 82.7 us -> 82.6 us (level)
    unnamed x12 -> x14, local copies, waits for them, and re-layouts: 2.36 us -> 3.04 us
  transfers between devices with their start and end apart: 21 -> 21, of which waited for: 10 -> 10; matrix products, arithmetic and copies ran while one was open for 1% -> 0% of each run, Pallas kernels for 6% -> 6%
where the time goes in v2:
time: 82.6 us; the launch traced here: 82.2 us
  starting transfers between devices  40.4 us (49%)
  waiting for transfers between devices  24.5 us (30%)
  Pallas kernels  14 us (17%)
  local copies, waits for them, and re-layouts  3.08 us (4%)
    ppermute x8, starting transfers between devices, swap_faces(): lax.ppermute(two, axis, pairs[1])  29.7 us
    pallas_call x15, Pallas kernels, kernel_call(): pl.pallas_call(body, out_shape=outs, in_specs=[VMEM] * len(arrays), out_s...  14 us
    ppermute x3, waiting for transfers between devices, local(): lax.ppermute(m, 'gz', ring[s + 1])  13.5 us
    ppermute x8, waiting for transfers between devices, swap_faces(): lax.ppermute(two, axis, pairs[1])  8.1 us
    ppermute x8, starting transfers between devices, swap_faces(): lax.ppermute(one, axis, pairs[0])  5.29 us
    unnamed x14, local copies, waits for them, and re-layouts  3.04 us
    ppermute x1, waiting for transfers between devices, local(): zr = [lax.ppermute(f, 'gz', ring[s]) for f, s in zip(sent, link_shifts(sz))]  2.86 us
    ppermute x3, starting transfers between devices, local(): lax.ppermute(m, 'gz', ring[s + 1])  2.49 us
  transfers between devices with their start and end apart: 21, of which 10 were waited for; matrix products, arithmetic and copies ran while one was open for 0% of the time, Pallas kernels for 6%

profile of v2, /device:TPU:0, one launch (start us, length us, event | category | flops | bytes accessed | tf_op | source)
XLA Modules:
  0.0 82.2 jit_solution(16607407262194638116)
XLA Ops:
  0.0 0.0 copy-start
  0.0 0.0 copy-start.1
  0.0 1.1 %copy-done.1 = f32[13,13,7,128]{3,2,1,0:T(8,128)S(1)} copy-done((f32[13,13,7,128]{3,2,1,0:T(8,128)S(1)}, f32[13,13,7,128]{3,2,1,0:T(8,128)}, u32[]{:S(2)}) %copy-start.1) | copy-done | bytes 605720
  1.1 0.1 shard_map.73
  1.2 0.7 collective-permute-start
  1.9 4.4 %collective-permute-start.1 = (bf16[112,128]{1,0:T(8,128)(2,1)S(1)}, bf16[112,128]{1,0:T(8,128)(2,1)S(1)}, u32[]{:S(2)}, u32[]{:S(2)}) collective-permute-start(bf16[112,128]{1,0:T(8,128)(2,1)S(1)} %get-tuple-element.58), channel_id=1, source_target_pairs={{0,8},{16,24},{8,0},{24,16},{1,9},{17,25},{9,1},{25,17},{2,10},{18... | collective-permute-start | bytes 86024 | tf_op jit(solution)/shard_map/ppermute | solution.py:525
  6.3 0.0 copy-start.2
  6.3 1.2 %copy-done.2 = bf16[1,1,1,343,1536]{4,3,2,1,0:T(8,128)(2,1)S(1)} copy-done((bf16[1,1,1,343,1536]{4,3,2,1,0:T(8,128)(2,1)S(1)}, bf16[1,1,1,343,1536]{4,3,2,1,0:T(8,128)(2,1)}, u32[]{:S(2)}) %copy-start.2) | copy-done | bytes 1053720
  7.5 0.0 copy-start.5
  7.5 0.7 copy-done.5
  8.2 3.1 %shard_map.75 = (bf16[1664,384]{1,0:T(8,128)(2,1)S(1)}, bf16[384,256]{1,0:T(8,128)(2,1)S(1)}) custom-call(bf16[343,1536]{1,0:T(8,128)(2,1)S(1)} %bitcast.10, s32[4,32]{1,0:T(4,128)S(1)} %bitcast.12), custom_call_target="tpu_custom_call" | custom-call | flops 3000000000 | bytes 2528768 | tf_op jit(solution)/shard_map/pallas_call | solution.py:57
  11.3 1.6 %collective-permute-start.4 = (bf16[384,256]{1,0:T(8,128)(2,1)S(1)}, bf16[384,256]{1,0:T(8,128)(2,1)S(1)}, u32[]{:S(2)}, u32[]{:S(2)}) collective-permute-start(bf16[384,256]{1,0:T(8,128)(2,1)S(1)} %get-tuple-element.65), channel_id=1, source_target_pairs={{1,0},{0,1},{3,2},{2,3},{5,4},{4,5},{7,6},{6,7},{9,8},{8,9},{11,10... | collective-permute-start | bytes 589832 | tf_op jit(solution)/shard_map/ppermute | solution.py:550
  12.9 0.0 copy-done
  12.9 0.0 collective-permute-done.xr_one.refs_1_
  12.9 0.0 collective-permute-done.1.xr_two.refs_2_
  13.0 0.7 collective-permute-start.2
  13.7 4.5 %collective-permute-start.3 = (bf16[112,128]{1,0:T(8,128)(2,1)S(1)}, bf16[112,128]{1,0:T(8,128)(2,1)S(1)}, u32[]{:S(2)}, u32[]{:S(2)}) collective-permute-start(bf16[112,128]{1,0:T(8,128)(2,1)S(1)} %get-tuple-element.62), channel_id=1, source_target_pairs={{0,2},{4,6},{2,0},{6,4},{1,3},{5,7},{3,1},{7,5},{8,10},{12,14},{10... | collective-permute-start | bytes 86024 | tf_op jit(solution)/shard_map/ppermute | solution.py:525
  18.1 0.0 copy-done.3
  18.1 0.0 copy-done.4
  18.1 0.0 copy-done.6
  18.1 1.8 %shard_map.76 = (bf16[384,1664]{1,0:T(8,128)(2,1)S(1)}, bf16[400,400]{1,0:T(8,128)(2,1)S(1)}, f32[1600,128]{1,0:T(8,128)S(1)}, bf16[384,768]{1,0:T(8,128)(2,1)S(...) custom-call(bf16[1664,384]{1,0:T(8,128)(2,1)S(1)} %get-tuple-element.63.qt.refs_5_.refs, ...), custom_call_target="tpu_custom_call" | custom-call | flops 1000000000 | bytes 5447570 | tf_op jit(solution)/shard_map/pallas_call | solution.py:57
  20.0 0.0 collective-permute-done.2.refs_3_
  20.0 0.0 collective-permute-done.3.refs_4_
  20.0 0.0 collective-permute-done.4.refs_6_.refs_7_
  20.0 1.4 %shard_map.77 = (f32[1352,128]{1,0:T(8,128)S(1)}, f32[384,128]{1,0:T(8,128)S(1)}, bf16[592,128]{1,0:T(8,128)(2,1)S(1)}) custom-call(f32[1352,128]{1,0:T(8,128)S(1)} %bitcast.9, bf16[112,128]{1,0:T(8,128)(2,1)S(1)} %collective-permute-done.xr_one.refs_1_, bf16[112,128]{1,0:T(8,128)(2,1)S(1)} %collective-permute-done.1.xr_two.refs_2_, ...), custom_call_target="tpu_custom_call" | custom-call | flops 400000000 | bytes 4206592 | tf_op jit(solution)/shard_map/pallas_call | solution.py:57
  21.4 0.6 collective-permute-start.5
  22.0 4.7 %collective-permute-done.5.refs_2_ = bf16[592,128]{1,0:T(8,128)(2,1)S(1)} collective-permute-done((bf16[592,128]{1,0:T(8,128)(2,1)S(1)}, bf16[592,128]{1,0:T(8,128)(2,1)S(1)}, u32[]{:S(2)}, u32[]{:S(2)}) %collective-permute-start.5) | collective-permute-done | bytes 151584 | tf_op jit(solution)/shard_map/ppermute | solution.py:565
  26.6 1.2 %shard_map.78 = (f32[1352,128]{1,0:T(8,128)S(1)}, f32[1352,128]{1,0:T(8,128)S(1)}, f32[1352,128]{1,0:T(8,128)S(1)}, bf16[112,128]{1,0:T(8,128)(2,1)S(1)}, bf16[1...) custom-call(f32[1352,128]{1,0:T(8,128)S(1)} %get-tuple-element.68.refs_0_, ...), custom_call_target="tpu_custom_call" | custom-call | flops 600000000 | bytes 6296064 | tf_op jit(solution)/shard_map/pallas_call | solution.py:57
  27.8 0.7 collective-permute-start.6
  28.5 1.7 %collective-permute-start.7 = (bf16[112,128]{1,0:T(8,128)(2,1)S(1)}, bf16[112,128]{1,0:T(8,128)(2,1)S(1)}, u32[]{:S(2)}, u32[]{:S(2)}) collective-permute-start(bf16[112,128]{1,0:T(8,128)(2,1)S(1)} %get-tuple-element.78), channel_id=1, source_target_pairs={{0,8},{16,24},{8,0},{24,16},{1,9},{17,25},{9,1},{25,17},{2,10},{18... | collective-permute-start | bytes 86024 | tf_op jit(solution)/shard_map/ppermute | solution.py:525
  30.1 0.0 collective-permute-done.6.xr_one.refs_2_
  30.1 0.9 %collective-permute-done.7.xr_two.refs_3_ = bf16[112,128]{1,0:T(8,128)(2,1)S(1)} collective-permute-done((bf16[112,128]{1,0:T(8,128)(2,1)S(1)}, bf16[112,128]{1,0:T(8,128)(2,1)S(1)}, u32[]{:S(2)}, u32[]{:S(2)}) %collective-permute-start.7) | collective-permute-done | bytes 28704 | tf_op jit(solution)/shard_map/ppermute | solution.py:525
  31.0 0.7 collective-permute-start.8
  31.7 3.4 %collective-permute-start.9 = (bf16[112,128]{1,0:T(8,128)(2,1)S(1)}, bf16[112,128]{1,0:T(8,128)(2,1)S(1)}, u32[]{:S(2)}, u32[]{:S(2)}) collective-permute-start(bf16[112,128]{1,0:T(8,128)(2,1)S(1)} %get-tuple-element.82), channel_id=1, source_target_pairs={{0,2},{4,6},{2,0},{6,4},{1,3},{5,7},{3,1},{7,5},{8,10},{12,14},{10... | collective-permute-start | bytes 86024 | tf_op jit(solution)/shard_map/ppermute | solution.py:525
  35.1 0.0 collective-permute-done.8.refs_4_
  35.1 1.8 %collective-permute-done.9.refs_5_ = bf16[112,128]{1,0:T(8,128)(2,1)S(1)} collective-permute-done((bf16[112,128]{1,0:T(8,128)(2,1)S(1)}, bf16[112,128]{1,0:T(8,128)(2,1)S(1)}, u32[]{:S(2)}, u32[]{:S(2)}) %collective-permute-start.9) | collective-permute-done | bytes 28704 | tf_op jit(solution)/shard_map/ppermute | solution.py:525
  37.0 1.4 %shard_map.80 = (f32[1352,128]{1,0:T(8,128)S(1)}, f32[384,128]{1,0:T(8,128)S(1)}, bf16[592,128]{1,0:T(8,128)(2,1)S(1)}) custom-call(f32[1352,128]{1,0:T(8,128)S(1)} %get-tuple-element.75.refs_0_, f32[1352,128]{1,0:T(8,128)S(1)} %get-tuple-element.76.refs_1_, bf16[112,128]{1,0:T(8,128)(2,1)S(1)} %collective-permute-done.6.xr_one.refs_2_, ...), custom_call_target="tpu_custom_call" | custom-call | flops 400000000 | bytes 4898816 | tf_op jit(solution)/shard_map/pallas_call | solution.py:57
  38.4 1.3 %collective-permute-start.10 = (bf16[592,128]{1,0:T(8,128)(2,1)S(1)}, bf16[592,128]{1,0:T(8,128)(2,1)S(1)}, u32[]{:S(2)}, u32[]{:S(2)}) collective-permute-start(bf16[592,128]{1,0:T(8,128)(2,1)S(1)} %get-tuple-element.86), channel_id=1, source_target_pairs={{0,1},{1,0},{2,3},{3,2},{4,5},{5,4},{6,7},{7,6},{8,9},{9,8},{10,11... | collective-permute-start | bytes 454664 | tf_op jit(solution)/shard_map/ppermute | solution.py:565
  39.7 4.0 %collective-permute-done.10.refs_3_ = bf16[592,128]{1,0:T(8,128)(2,1)S(1)} collective-permute-done((bf16[592,128]{1,0:T(8,128)(2,1)S(1)}, bf16[592,128]{1,0:T(8,128)(2,1)S(1)}, u32[]{:S(2)}, u32[]{:S(2)}) %collective-permute-start.10) | collective-permute-done | bytes 151584 | tf_op jit(solution)/shard_map/ppermute | solution.py:565
  43.8 1.2 %shard_map.81 = (f32[1352,128]{1,0:T(8,128)S(1)}, f32[1352,128]{1,0:T(8,128)S(1)}, f32[1352,128]{1,0:T(8,128)S(1)}, bf16[112,128]{1,0:T(8,128)(2,1)S(1)}, bf16[1...) custom-call(f32[1352,128]{1,0:T(8,128)S(1)} %get-tuple-element.83.refs_0_, ...), custom_call_target="tpu_custom_call" | custom-call | flops 600000000 | bytes 6988288 | tf_op jit(solution)/shard_map/pallas_call | solution.py:57
  44.9 0.7 collective-permute-start.11
  45.6 3.5 %collective-permute-start.12 = (bf16[112,128]{1,0:T(8,128)(2,1)S(1)}, bf16[112,128]{1,0:T(8,128)(2,1)S(1)}, u32[]{:S(2)}, u32[]{:S(2)}) collective-permute-start(bf16[112,128]{1,0:T(8,128)(2,1)S(1)} %get-tuple-element.90), channel_id=1, source_target_pairs={{0,8},{16,24},{8,0},{24,16},{1,9},{17,25},{9,1},{25,17},{2,10},{18... | collective-permute-start | bytes 86024 | tf_op jit(solution)/shard_map/ppermute | solution.py:525
  49.1 0.0 collective-permute-done.11.xr_one.refs_2_
  49.1 0.9 %collective-permute-done.12.xr_two.refs_3_ = bf16[112,128]{1,0:T(8,128)(2,1)S(1)} collective-permute-done((bf16[112,128]{1,0:T(8,128)(2,1)S(1)}, bf16[112,128]{1,0:T(8,128)(2,1)S(1)}, u32[]{:S(2)}, u32[]{:S(2)}) %collective-permute-start.12) | collective-permute-done | bytes 28704 | tf_op jit(solution)/shard_map/ppermute | solution.py:525
  50.0 0.7 collective-permute-start.13
  50.7 4.9 %collective-permute-start.14 = (bf16[112,128]{1,0:T(8,128)(2,1)S(1)}, bf16[112,128]{1,0:T(8,128)(2,1)S(1)}, u32[]{:S(2)}, u32[]{:S(2)}) collective-permute-start(bf16[112,128]{1,0:T(8,128)(2,1)S(1)} %get-tuple-element.94), channel_id=1, source_target_pairs={{0,2},{4,6},{2,0},{6,4},{1,3},{5,7},{3,1},{7,5},{8,10},{12,14},{10... | collective-permute-start | bytes 86024 | tf_op jit(solution)/shard_map/ppermute | solution.py:525
  55.6 0.0 collective-permute-done.13.refs_4_
  55.6 1.8 %collective-permute-done.14.refs_5_ = bf16[112,128]{1,0:T(8,128)(2,1)S(1)} collective-permute-done((bf16[112,128]{1,0:T(8,128)(2,1)S(1)}, bf16[112,128]{1,0:T(8,128)(2,1)S(1)}, u32[]{:S(2)}, u32[]{:S(2)}) %collective-permute-start.14) | collective-permute-done | bytes 28704 | tf_op jit(solution)/shard_map/ppermute | solution.py:525
  57.5 1.4 %shard_map.83 = (f32[1352,128]{1,0:T(8,128)S(1)}, f32[384,128]{1,0:T(8,128)S(1)}, bf16[592,128]{1,0:T(8,128)(2,1)S(1)}) custom-call(f32[1352,128]{1,0:T(8,128)S(1)} %get-tuple-element.87.refs_0_, f32[1352,128]{1,0:T(8,128)S(1)} %get-tuple-element.88.refs_1_, bf16[112,128]{1,0:T(8,128)(2,1)S(1)} %collective-permute-done.11.xr_one.refs_2_, ...), custom_call_target="tpu_custom_call" | custom-call | flops 400000000 | bytes 4898816 | tf_op jit(solution)/shard_map/pallas_call | solution.py:57
  58.9 0.6 collective-permute-start.15
  59.4 4.8 %collective-permute-done.15.refs_3_ = bf16[592,128]{1,0:T(8,128)(2,1)S(1)} collective-permute-done((bf16[592,128]{1,0:T(8,128)(2,1)S(1)}, bf16[592,128]{1,0:T(8,128)(2,1)S(1)}, u32[]{:S(2)}, u32[]{:S(2)}) %collective-permute-start.15) | collective-permute-done | bytes 151584 | tf_op jit(solution)/shard_map/ppermute | solution.py:565
  64.2 1.3 %shard_map.84 = (f32[1352,128]{1,0:T(8,128)S(1)}, f32[1352,128]{1,0:T(8,128)S(1)}, f32[1352,128]{1,0:T(8,128)}, bf16[112,128]{1,0:T(8,128)(2,1)S(1)}, bf16[112,1...) custom-call(f32[1352,128]{1,0:T(8,128)S(1)} %get-tuple-element.95.refs_0_, ...), custom_call_target="tpu_custom_call" | custom-call | flops 600000000 | bytes 6988288 | tf_op jit(solution)/shard_map/pallas_call | solution.py:57
  65.5 0.7 collective-permute-start.16
  66.2 3.5 %collective-permute-start.17 = (bf16[112,128]{1,0:T(8,128)(2,1)S(1)}, bf16[112,128]{1,0:T(8,128)(2,1)S(1)}, u32[]{:S(2)}, u32[]{:S(2)}) collective-permute-start(bf16[112,128]{1,0:T(8,128)(2,1)S(1)} %get-tuple-element.102), channel_id=1, source_target_pairs={{0,8},{16,24},{8,0},{24,16},{1,9},{17,25},{9,1},{25,17},{2,10},{18... | collective-permute-start | bytes 86024 | tf_op jit(solution)/shard_map/ppermute | solution.py:525
  69.7 0.0 collective-permute-done.16.xr_one.refs_1_.refs_2_
  69.7 0.9 %collective-permute-done.17.xr_two.refs_2_.refs_3_ = bf16[112,128]{1,0:T(8,128)(2,1)S(1)} collective-permute-done((bf16[112,128]{1,0:T(8,128)(2,1)S(1)}, bf16[112,128]{1,0:T(8,128)(2,1)S(1)}, u32[]{:S(2)}, u32[]{:S(2)}) %collective-permute-start.17) | collective-permute-done | bytes 28704 | tf_op jit(solution)/shard_map/ppermute | solution.py:525
  70.6 0.7 collective-permute-start.18
  71.3 3.8 %collective-permute-start.19 = (bf16[112,128]{1,0:T(8,128)(2,1)S(1)}, bf16[112,128]{1,0:T(8,128)(2,1)S(1)}, u32[]{:S(2)}, u32[]{:S(2)}) collective-permute-start(bf16[112,128]{1,0:T(8,128)(2,1)S(1)} %get-tuple-element.106), channel_id=1, source_target_pairs={{0,2},{4,6},{2,0},{6,4},{1,3},{5,7},{3,1},{7,5},{8,10},{12,14},{10... | collective-permute-start | bytes 86024 | tf_op jit(solution)/shard_map/ppermute | solution.py:525
  75.0 0.0 collective-permute-done.18.refs_3_.refs_4_
  75.0 1.8 %collective-permute-done.19.refs_4_.refs_5_ = bf16[112,128]{1,0:T(8,128)(2,1)S(1)} collective-permute-done((bf16[112,128]{1,0:T(8,128)(2,1)S(1)}, bf16[112,128]{1,0:T(8,128)(2,1)S(1)}, u32[]{:S(2)}, u32[]{:S(2)}) %collective-permute-start.19) | collective-permute-done | bytes 28704 | tf_op jit(solution)/shard_map/ppermute | solution.py:525
  76.9 0.1 shard_map.86
  77.0 1.3 %collective-permute-start.20 = (bf16[208,128]{1,0:T(8,128)(2,1)S(1)}, bf16[208,128]{1,0:T(8,128)(2,1)S(1)}, u32[]{:S(2)}, u32[]{:S(2)}) collective-permute-start(bf16[208,128]{1,0:T(8,128)(2,1)S(1)} %shard_map.86), channel_id=1, source_target_pairs={{0,1},{1,0},{2,3},{3,2},{4,5},{5,4},{6,7},{7,6},{8,9},{9,8},{10,11... | collective-permute-start | bytes 159752 | tf_op jit(solution)/shard_map/ppermute | solution.py:570
  78.3 2.9 %collective-permute-done.20.refs_6_ = bf16[208,128]{1,0:T(8,128)(2,1)S(1)} collective-permute-done((bf16[208,128]{1,0:T(8,128)(2,1)S(1)}, bf16[208,128]{1,0:T(8,128)(2,1)S(1)}, u32[]{:S(2)}, u32[]{:S(2)}) %collective-permute-start.20) | collective-permute-done | bytes 53280 | tf_op jit(solution)/shard_map/ppermute | solution.py:570
  81.2 1.0 %shard_map.87 = f32[13,13,7,128]{3,2,1,0:T(8,128)} custom-call(f32[1352,128]{1,0:T(8,128)S(1)} %get-tuple-element.99.refs_0_, f32[1352,128]{1,0:T(8,128)S(1)} %get-tuple-element.100.refs_1_, bf16[112,128]{1,0:T(8,128)(2,1)S(1)} %collective-permute-done.16.xr_one.refs_1_.refs_2_, bf16[112,128]{1,0:T(8,128)(2,1)S(1)} %collective-permute-done.17.xr_two.refs_2_.refs_3_, ...), custom_call_target="tpu_custom_call" | custom-call | bytes 2158080 | tf_op jit(solution)/shard_map/pallas_call | solution.py:57
  (9 shorter events, 0.1 us)
Async XLA Ops:
  0.0 12.9 %copy-start = (f32[343,2,2,1]{0,3,2,1:T(1,128)S(1)}, f32[343,2,2,1]{0,3,2,1:T(1,128)}, u32[]{:S(2)}) copy-start(f32[343,2,2,1]{0,3,2,1:T(1,128)} %param.9) | copy-start | bytes 16468
  0.0 1.1 %copy-start.1 = (f32[13,13,7,128]{3,2,1,0:T(8,128)S(1)}, f32[13,13,7,128]{3,2,1,0:T(8,128)}, u32[]{:S(2)}) copy-start(f32[13,13,7,128]{3,2,1,0:T(8,128)} %parts.1) | copy-start | bytes 1817092
  1.2 11.7 %collective-permute-start = (bf16[112,128]{1,0:T(8,128)(2,1)S(1)}, bf16[112,128]{1,0:T(8,128)(2,1)S(1)}, u32[]{:S(2)}, u32[]{:S(2)}) collective-permute-start(bf16[112,128]{1,0:T(8,128)(2,1)S(1)} %get-tuple-element.57), channel_id=1, source_target_pairs={{8,16},{16,8},{0,0},{24,24},{9,17},{17,9},{1,1},{25,25},{10,18},{1... | collective-permute-start | bytes 86024 | tf_op jit(solution)/shard_map/ppermute | solution.py:525
  1.9 11.0 %collective-permute-start.1 = (bf16[112,128]{1,0:T(8,128)(2,1)S(1)}, bf16[112,128]{1,0:T(8,128)(2,1)S(1)}, u32[]{:S(2)}, u32[]{:S(2)}) collective-permute-start(bf16[112,128]{1,0:T(8,128)(2,1)S(1)} %get-tuple-element.58), channel_id=1, source_target_pairs={{0,8},{16,24},{8,0},{24,16},{1,9},{17,25},{9,1},{25,17},{2,10},{18... | collective-permute-start | bytes 86024 | tf_op jit(solution)/shard_map/ppermute | solution.py:525
  6.3 1.2 %copy-start.2 = (bf16[1,1,1,343,1536]{4,3,2,1,0:T(8,128)(2,1)S(1)}, bf16[1,1,1,343,1536]{4,3,2,1,0:T(8,128)(2,1)}, u32[]{:S(2)}) copy-start(bf16[1,1,1,343,1536]{4,3,2,1,0:T(8,128)(2,1)} %param.10) | copy-start | bytes 3161092
  7.5 0.7 copy-start.5
  8.2 9.9 %copy-start.3 = (bf16[343,343]{1,0:T(8,128)(2,1)S(1)}, bf16[343,343]{1,0:T(8,128)(2,1)}, u32[]{:S(2)}) copy-start(bf16[343,343]{1,0:T(8,128)(2,1)} %kin.1) | copy-start | bytes 705898
  8.2 9.9 %copy-start.4 = (f32[64,12,12]{0,2,1:T(8,128)S(1)}, f32[64,12,12]{0,2,1:T(8,128)}, u32[]{:S(2)}) copy-start(f32[64,12,12]{0,2,1:T(8,128)} %param.13) | copy-start | bytes 110596
  8.2 9.9 %copy-start.6 = (s32[1,1,2,32]{3,2,1,0:T(2,128)S(1)}, s32[1,1,2,32]{3,2,1,0:T(2,128)}, u32[]{:S(2)}) copy-start(s32[1,1,2,32]{3,2,1,0:T(2,128)} %param.11) | copy-start | bytes 772
  11.3 8.7 %collective-permute-start.4 = (bf16[384,256]{1,0:T(8,128)(2,1)S(1)}, bf16[384,256]{1,0:T(8,128)(2,1)S(1)}, u32[]{:S(2)}, u32[]{:S(2)}) collective-permute-start(bf16[384,256]{1,0:T(8,128)(2,1)S(1)} %get-tuple-element.65), channel_id=1, source_target_pairs={{1,0},{0,1},{3,2},{2,3},{5,4},{4,5},{7,6},{6,7},{9,8},{8,9},{11,10... | collective-permute-start | bytes 589832 | tf_op jit(solution)/shard_map/ppermute | solution.py:550
  13.0 7.0 %collective-permute-start.2 = (bf16[112,128]{1,0:T(8,128)(2,1)S(1)}, bf16[112,128]{1,0:T(8,128)(2,1)S(1)}, u32[]{:S(2)}, u32[]{:S(2)}) collective-permute-start(bf16[112,128]{1,0:T(8,128)(2,1)S(1)} %get-tuple-element.61), channel_id=1, source_target_pairs={{2,4},{4,2},{0,0},{6,6},{3,5},{5,3},{1,1},{7,7},{10,12},{12,10},{8... | collective-permute-start | bytes 86024 | tf_op jit(solution)/shard_map/ppermute | solution.py:525
  13.7 6.3 %collective-permute-start.3 = (bf16[112,128]{1,0:T(8,128)(2,1)S(1)}, bf16[112,128]{1,0:T(8,128)(2,1)S(1)}, u32[]{:S(2)}, u32[]{:S(2)}) collective-permute-start(bf16[112,128]{1,0:T(8,128)(2,1)S(1)} %get-tuple-element.62), channel_id=1, source_target_pairs={{0,2},{4,6},{2,0},{6,4},{1,3},{5,7},{3,1},{7,5},{8,10},{12,14},{10... | collective-permute-start | bytes 86024 | tf_op jit(solution)/shard_map/ppermute | solution.py:525
  21.4 5.3 %collective-permute-start.5 = (bf16[592,128]{1,0:T(8,128)(2,1)S(1)}, bf16[592,128]{1,0:T(8,128)(2,1)S(1)}, u32[]{:S(2)}, u32[]{:S(2)}) collective-permute-start(bf16[592,128]{1,0:T(8,128)(2,1)S(1)} %get-tuple-element.70), channel_id=1, source_target_pairs={{0,1},{1,0},{2,3},{3,2},{4,5},{5,4},{6,7},{7,6},{8,9},{9,8},{10,11... | collective-permute-start | bytes 454664 | tf_op jit(solution)/shard_map/ppermute | solution.py:565
  27.8 2.3 %collective-permute-start.6 = (bf16[112,128]{1,0:T(8,128)(2,1)S(1)}, bf16[112,128]{1,0:T(8,128)(2,1)S(1)}, u32[]{:S(2)}, u32[]{:S(2)}) collective-permute-start(bf16[112,128]{1,0:T(8,128)(2,1)S(1)} %get-tuple-element.77), channel_id=1, source_target_pairs={{8,16},{16,8},{0,0},{24,24},{9,17},{17,9},{1,1},{25,25},{10,18},{1... | collective-permute-start | bytes 86024 | tf_op jit(solution)/shard_map/ppermute | solution.py:525
  28.5 2.5 %collective-permute-start.7 = (bf16[112,128]{1,0:T(8,128)(2,1)S(1)}, bf16[112,128]{1,0:T(8,128)(2,1)S(1)}, u32[]{:S(2)}, u32[]{:S(2)}) collective-permute-start(bf16[112,128]{1,0:T(8,128)(2,1)S(1)} %get-tuple-element.78), channel_id=1, source_target_pairs={{0,8},{16,24},{8,0},{24,16},{1,9},{17,25},{9,1},{25,17},{2,10},{18... | collective-permute-start | bytes 86024 | tf_op jit(solution)/shard_map/ppermute | solution.py:525
  31.0 4.1 %collective-permute-start.8 = (bf16[112,128]{1,0:T(8,128)(2,1)S(1)}, bf16[112,128]{1,0:T(8,128)(2,1)S(1)}, u32[]{:S(2)}, u32[]{:S(2)}) collective-permute-start(bf16[112,128]{1,0:T(8,128)(2,1)S(1)} %get-tuple-element.81), channel_id=1, source_target_pairs={{2,4},{4,2},{0,0},{6,6},{3,5},{5,3},{1,1},{7,7},{10,12},{12,10},{8... | collective-permute-start | bytes 86024 | tf_op jit(solution)/shard_map/ppermute | solution.py:525
  31.7 5.3 %collective-permute-start.9 = (bf16[112,128]{1,0:T(8,128)(2,1)S(1)}, bf16[112,128]{1,0:T(8,128)(2,1)S(1)}, u32[]{:S(2)}, u32[]{:S(2)}) collective-permute-start(bf16[112,128]{1,0:T(8,128)(2,1)S(1)} %get-tuple-element.82), channel_id=1, source_target_pairs={{0,2},{4,6},{2,0},{6,4},{1,3},{5,7},{3,1},{7,5},{8,10},{12,14},{10... | collective-permute-start | bytes 86024 | tf_op jit(solution)/shard_map/ppermute | solution.py:525
  38.4 5.4 %collective-permute-start.10 = (bf16[592,128]{1,0:T(8,128)(2,1)S(1)}, bf16[592,128]{1,0:T(8,128)(2,1)S(1)}, u32[]{:S(2)}, u32[]{:S(2)}) collective-permute-start(bf16[592,128]{1,0:T(8,128)(2,1)S(1)} %get-tuple-element.86), channel_id=1, source_target_pairs={{0,1},{1,0},{2,3},{3,2},{4,5},{5,4},{6,7},{7,6},{8,9},{9,8},{10,11... | collective-permute-start | bytes 454664 | tf_op jit(solution)/shard_map/ppermute | solution.py:565
  44.9 4.2 %collective-permute-start.11 = (bf16[112,128]{1,0:T(8,128)(2,1)S(1)}, bf16[112,128]{1,0:T(8,128)(2,1)S(1)}, u32[]{:S(2)}, u32[]{:S(2)}) collective-permute-start(bf16[112,128]{1,0:T(8,128)(2,1)S(1)} %get-tuple-element.89), channel_id=1, source_target_pairs={{8,16},{16,8},{0,0},{24,24},{9,17},{17,9},{1,1},{25,25},{10,18},{1... | collective-permute-start | bytes 86024 | tf_op jit(solution)/shard_map/ppermute | solution.py:525
  45.6 4.4 %collective-permute-start.12 = (bf16[112,128]{1,0:T(8,128)(2,1)S(1)}, bf16[112,128]{1,0:T(8,128)(2,1)S(1)}, u32[]{:S(2)}, u32[]{:S(2)}) collective-permute-start(bf16[112,128]{1,0:T(8,128)(2,1)S(1)} %get-tuple-element.90), channel_id=1, source_target_pairs={{0,8},{16,24},{8,0},{24,16},{1,9},{17,25},{9,1},{25,17},{2,10},{18... | collective-permute-start | bytes 86024 | tf_op jit(solution)/shard_map/ppermute | solution.py:525
  50.0 5.6 %collective-permute-start.13 = (bf16[112,128]{1,0:T(8,128)(2,1)S(1)}, bf16[112,128]{1,0:T(8,128)(2,1)S(1)}, u32[]{:S(2)}, u32[]{:S(2)}) collective-permute-start(bf16[112,128]{1,0:T(8,128)(2,1)S(1)} %get-tuple-element.93), channel_id=1, source_target_pairs={{2,4},{4,2},{0,0},{6,6},{3,5},{5,3},{1,1},{7,7},{10,12},{12,10},{8... | collective-permute-start | bytes 86024 | tf_op jit(solution)/shard_map/ppermute | solution.py:525
  50.7 6.8 %collective-permute-start.14 = (bf16[112,128]{1,0:T(8,128)(2,1)S(1)}, bf16[112,128]{1,0:T(8,128)(2,1)S(1)}, u32[]{:S(2)}, u32[]{:S(2)}) collective-permute-start(bf16[112,128]{1,0:T(8,128)(2,1)S(1)} %get-tuple-element.94), channel_id=1, source_target_pairs={{0,2},{4,6},{2,0},{6,4},{1,3},{5,7},{3,1},{7,5},{8,10},{12,14},{10... | collective-permute-start | bytes 86024 | tf_op jit(solution)/shard_map/ppermute | solution.py:525
  58.9 5.4 %collective-permute-start.15 = (bf16[592,128]{1,0:T(8,128)(2,1)S(1)}, bf16[592,128]{1,0:T(8,128)(2,1)S(1)}, u32[]{:S(2)}, u32[]{:S(2)}) collective-permute-start(bf16[592,128]{1,0:T(8,128)(2,1)S(1)} %get-tuple-element.98), channel_id=1, source_target_pairs={{0,1},{1,0},{2,3},{3,2},{4,5},{5,4},{6,7},{7,6},{8,9},{9,8},{10,11... | collective-permute-start | bytes 454664 | tf_op jit(solution)/shard_map/ppermute | solution.py:565
  65.5 4.2 %collective-permute-start.16 = (bf16[112,128]{1,0:T(8,128)(2,1)S(1)}, bf16[112,128]{1,0:T(8,128)(2,1)S(1)}, u32[]{:S(2)}, u32[]{:S(2)}) collective-permute-start(bf16[112,128]{1,0:T(8,128)(2,1)S(1)} %get-tuple-element.101), channel_id=1, source_target_pairs={{8,16},{16,8},{0,0},{24,24},{9,17},{17,9},{1,1},{25,25},{10,18},{1... | collective-permute-start | bytes 86024 | tf_op jit(solution)/shard_map/ppermute | solution.py:525
  66.2 4.4 %collective-permute-start.17 = (bf16[112,128]{1,0:T(8,128)(2,1)S(1)}, bf16[112,128]{1,0:T(8,128)(2,1)S(1)}, u32[]{:S(2)}, u32[]{:S(2)}) collective-permute-start(bf16[112,128]{1,0:T(8,128)(2,1)S(1)} %get-tuple-element.102), channel_id=1, source_target_pairs={{0,8},{16,24},{8,0},{24,16},{1,9},{17,25},{9,1},{25,17},{2,10},{18... | collective-permute-start | bytes 86024 | tf_op jit(solution)/shard_map/ppermute | solution.py:525
  70.6 4.4 %collective-permute-start.18 = (bf16[112,128]{1,0:T(8,128)(2,1)S(1)}, bf16[112,128]{1,0:T(8,128)(2,1)S(1)}, u32[]{:S(2)}, u32[]{:S(2)}) collective-permute-start(bf16[112,128]{1,0:T(8,128)(2,1)S(1)} %get-tuple-element.105), channel_id=1, source_target_pairs={{2,4},{4,2},{0,0},{6,6},{3,5},{5,3},{1,1},{7,7},{10,12},{12,10},{8... | collective-permute-start | bytes 86024 | tf_op jit(solution)/shard_map/ppermute | solution.py:525
  71.3 5.6 %collective-permute-start.19 = (bf16[112,128]{1,0:T(8,128)(2,1)S(1)}, bf16[112,128]{1,0:T(8,128)(2,1)S(1)}, u32[]{:S(2)}, u32[]{:S(2)}) collective-permute-start(bf16[112,128]{1,0:T(8,128)(2,1)S(1)} %get-tuple-element.106), channel_id=1, source_target_pairs={{0,2},{4,6},{2,0},{6,4},{1,3},{5,7},{3,1},{7,5},{8,10},{12,14},{10... | collective-permute-start | bytes 86024 | tf_op jit(solution)/shard_map/ppermute | solution.py:525
  77.0 4.2 %collective-permute-start.20 = (bf16[208,128]{1,0:T(8,128)(2,1)S(1)}, bf16[208,128]{1,0:T(8,128)(2,1)S(1)}, u32[]{:S(2)}, u32[]{:S(2)}) collective-permute-start(bf16[208,128]{1,0:T(8,128)(2,1)S(1)} %shard_map.86), channel_id=1, source_target_pairs={{0,1},{1,0},{2,3},{3,2},{4,5},{5,4},{6,7},{7,6},{8,9},{9,8},{10,11... | collective-permute-start | bytes 159752 | tf_op jit(solution)/shard_map/ppermute | solution.py:570

commit v3 on v2

--- a/solution.py
+++ b/solution.py
@@ -520,8 +520,8 @@
     for low in (1, 0):
         lows = range(low, count - 1, 2)
         pair = [(i, i + 1) for i in lows] + [(i + 1, i) for i in lows]
-        alone = set(range(count)) - {source for source, _ in pair}
-        pairs.append(pair + [(i, i) for i in sorted(alone)])
+        alone = sorted(set(range(count)) - {source for source, _ in pair})
+        pairs.append(pair + list(zip(alone, alone[::-1])))
     return lax.ppermute(one, axis, pairs[0]), lax.ppermute(two, axis, pairs[1])
 
 

time: 82.6 us -> 75.9 us (0.919)
  starting transfers between devices: 40.4 us -> 19.4 us
  waiting for transfers between devices: 24.5 us -> 39.1 us
    ppermute x8, starting transfers between devices: 29.7 us -> 3.22 us  [swap_faces(): lax.ppermute(two, axis, pairs[1])]
    ppermute x8, waiting for transfers between devices: 0.02 us -> 19.2 us  [swap_faces(): lax.ppermute(one, axis, pairs[0])]
    ppermute x8, starting transfers between devices: 5.29 us -> 11.8 us  [swap_faces(): lax.ppermute(one, axis, pairs[0])]
    ppermute x8, waiting for transfers between devices: 8.1 us -> 2.65 us  [swap_faces(): lax.ppermute(two, axis, pairs[1])]
  transfers between devices with their start and end apart: 21 -> 21, of which waited for: 10 -> 15; matrix products, arithmetic and copies ran while one was open for 0% -> 0% of each run, Pallas kernels for 6% -> 7%
where the time goes in v3:
time: 75.9 us; the launch traced here: 75.7 us
  waiting for transfers between devices  39.1 us (52%)
  starting transfers between devices  19.4 us (26%)
  Pallas kernels  14.1 us (19%)
  local copies, waits for them, and re-layouts  3.08 us (4%)
    ppermute x8, waiting for transfers between devices, swap_faces(): lax.ppermute(one, axis, pairs[0])  19.2 us
    pallas_call x15, Pallas kernels, kernel_call(): pl.pallas_call(body, out_shape=outs, in_specs=[VMEM] * len(arrays), out_s...  14.1 us
    ppermute x3, waiting for transfers between devices, local(): lax.ppermute(m, 'gz', ring[s + 1])  13.7 us
    ppermute x8, starting transfers between devices, swap_faces(): lax.ppermute(one, axis, pairs[0])  11.8 us
    ppermute x1, waiting for transfers between devices, local(): zr = [lax.ppermute(f, 'gz', ring[s]) for f, s in zip(sent, link_shifts(sz))]  3.48 us
    ppermute x8, starting transfers between devices, swap_faces(): lax.ppermute(two, axis, pairs[1])  3.22 us
    unnamed x14, local copies, waits for them, and re-layouts  3.04 us
    ppermute x8, waiting for transfers between devices, swap_faces(): lax.ppermute(two, axis, pairs[1])  2.65 us
  transfers between devices with their start and end apart: 21, of which 15 were waited for; matrix products, arithmetic and copies ran while one was open for 0% of the time, Pallas kernels for 7%

profile of v3, /device:TPU:0, one launch (start us, length us, event | category | flops | bytes accessed | tf_op | source)
XLA Modules:
  0.0 75.7 jit_solution(14583640638941047578)
XLA Ops:
  0.0 0.0 copy-start
  0.0 0.0 copy-start.1
  0.0 1.1 %copy-done.1 = f32[13,13,7,128]{3,2,1,0:T(8,128)S(1)} copy-done((f32[13,13,7,128]{3,2,1,0:T(8,128)S(1)}, f32[13,13,7,128]{3,2,1,0:T(8,128)}, u32[]{:S(2)}) %copy-start.1) | copy-done | bytes 605720
  1.1 0.1 shard_map.73
  1.2 2.4 %collective-permute-start = (bf16[112,128]{1,0:T(8,128)(2,1)S(1)}, bf16[112,128]{1,0:T(8,128)(2,1)S(1)}, u32[]{:S(2)}, u32[]{:S(2)}) collective-permute-start(bf16[112,128]{1,0:T(8,128)(2,1)S(1)} %get-tuple-element.57), channel_id=1, source_target_pairs={{8,16},{16,8},{0,24},{24,0},{9,17},{17,9},{1,25},{25,1},{10,18},{1... | collective-permute-start | bytes 86024 | tf_op jit(solution)/shard_map/ppermute | solution.py:525
  3.7 0.7 collective-permute-start.1
  4.4 0.0 copy-start.2
  4.4 1.2 %copy-done.2 = bf16[1,1,1,343,1536]{4,3,2,1,0:T(8,128)(2,1)S(1)} copy-done((bf16[1,1,1,343,1536]{4,3,2,1,0:T(8,128)(2,1)S(1)}, bf16[1,1,1,343,1536]{4,3,2,1,0:T(8,128)(2,1)}, u32[]{:S(2)}) %copy-start.2) | copy-done | bytes 1053720
  5.6 0.0 copy-start.5
  5.6 0.7 copy-done.5
  6.3 3.1 %shard_map.75 = (bf16[1664,384]{1,0:T(8,128)(2,1)S(1)}, bf16[384,256]{1,0:T(8,128)(2,1)S(1)}) custom-call(bf16[343,1536]{1,0:T(8,128)(2,1)S(1)} %bitcast.10, s32[4,32]{1,0:T(4,128)S(1)} %bitcast.12), custom_call_target="tpu_custom_call" | custom-call | flops 3000000000 | bytes 2528768 | tf_op jit(solution)/shard_map/pallas_call | solution.py:57
  9.4 1.6 %collective-permute-start.4 = (bf16[384,256]{1,0:T(8,128)(2,1)S(1)}, bf16[384,256]{1,0:T(8,128)(2,1)S(1)}, u32[]{:S(2)}, u32[]{:S(2)}) collective-permute-start(bf16[384,256]{1,0:T(8,128)(2,1)S(1)} %get-tuple-element.65), channel_id=1, source_target_pairs={{1,0},{0,1},{3,2},{2,3},{5,4},{4,5},{7,6},{6,7},{9,8},{8,9},{11,10... | collective-permute-start | bytes 589832 | tf_op jit(solution)/shard_map/ppermute | solution.py:550
  11.0 0.0 copy-done
  11.0 0.0 collective-permute-done.xr_one.refs_1_
  11.0 0.0 collective-permute-done.1.xr_two.refs_2_
  11.1 3.7 %collective-permute-start.2 = (bf16[112,128]{1,0:T(8,128)(2,1)S(1)}, bf16[112,128]{1,0:T(8,128)(2,1)S(1)}, u32[]{:S(2)}, u32[]{:S(2)}) collective-permute-start(bf16[112,128]{1,0:T(8,128)(2,1)S(1)} %get-tuple-element.61), channel_id=1, source_target_pairs={{2,4},{4,2},{0,6},{6,0},{3,5},{5,3},{1,7},{7,1},{10,12},{12,10},{8... | collective-permute-start | bytes 86024 | tf_op jit(solution)/shard_map/ppermute | solution.py:525
  14.7 0.0 collective-permute-start.3
  14.7 0.0 copy-done.3
  14.7 0.0 copy-done.4
  14.7 0.0 copy-done.6
  14.8 1.8 %shard_map.76 = (bf16[384,1664]{1,0:T(8,128)(2,1)S(1)}, bf16[400,400]{1,0:T(8,128)(2,1)S(1)}, f32[1600,128]{1,0:T(8,128)S(1)}, bf16[384,768]{1,0:T(8,128)(2,1)S(...) custom-call(bf16[1664,384]{1,0:T(8,128)(2,1)S(1)} %get-tuple-element.63.qt.refs_5_.refs, ...), custom_call_target="tpu_custom_call" | custom-call | flops 1000000000 | bytes 5447570 | tf_op jit(solution)/shard_map/pallas_call | solution.py:57
  16.6 0.2 collective-permute-done.2.refs_3_
  16.8 1.8 %collective-permute-done.3.refs_4_ = bf16[112,128]{1,0:T(8,128)(2,1)S(1)} collective-permute-done((bf16[112,128]{1,0:T(8,128)(2,1)S(1)}, bf16[112,128]{1,0:T(8,128)(2,1)S(1)}, u32[]{:S(2)}, u32[]{:S(2)}) %collective-permute-start.3) | collective-permute-done | bytes 28704 | tf_op jit(solution)/shard_map/ppermute | solution.py:525
  18.6 0.0 collective-permute-done.4.refs_6_.refs_7_
  18.6 1.4 %shard_map.77 = (f32[1352,128]{1,0:T(8,128)S(1)}, f32[384,128]{1,0:T(8,128)S(1)}, bf16[592,128]{1,0:T(8,128)(2,1)S(1)}) custom-call(f32[1352,128]{1,0:T(8,128)S(1)} %bitcast.9, bf16[112,128]{1,0:T(8,128)(2,1)S(1)} %collective-permute-done.xr_one.refs_1_, bf16[112,128]{1,0:T(8,128)(2,1)S(1)} %collective-permute-done.1.xr_two.refs_2_, ...), custom_call_target="tpu_custom_call" | custom-call | flops 400000000 | bytes 4206592 | tf_op jit(solution)/shard_map/pallas_call | solution.py:57
  20.0 0.6 collective-permute-start.5
  20.6 4.7 %collective-permute-done.5.refs_2_ = bf16[592,128]{1,0:T(8,128)(2,1)S(1)} collective-permute-done((bf16[592,128]{1,0:T(8,128)(2,1)S(1)}, bf16[592,128]{1,0:T(8,128)(2,1)S(1)}, u32[]{:S(2)}, u32[]{:S(2)}) %collective-permute-start.5) | collective-permute-done | bytes 151584 | tf_op jit(solution)/shard_map/ppermute | solution.py:565
  25.3 1.2 %shard_map.78 = (f32[1352,128]{1,0:T(8,128)S(1)}, f32[1352,128]{1,0:T(8,128)S(1)}, f32[1352,128]{1,0:T(8,128)S(1)}, bf16[112,128]{1,0:T(8,128)(2,1)S(1)}, bf16[1...) custom-call(f32[1352,128]{1,0:T(8,128)S(1)} %get-tuple-element.68.refs_0_, ...), custom_call_target="tpu_custom_call" | custom-call | flops 600000000 | bytes 6296064 | tf_op jit(solution)/shard_map/pallas_call | solution.py:57
  26.4 0.1 collective-permute-start.6
  26.5 0.6 collective-permute-start.7
  27.1 2.6 %collective-permute-done.6.xr_one.refs_2_ = bf16[112,128]{1,0:T(8,128)(2,1)S(1)} collective-permute-done((bf16[112,128]{1,0:T(8,128)(2,1)S(1)}, bf16[112,128]{1,0:T(8,128)(2,1)S(1)}, u32[]{:S(2)}, u32[]{:S(2)}) %collective-permute-start.6) | collective-permute-done | bytes 28704 | tf_op jit(solution)/shard_map/ppermute | solution.py:525
  29.8 0.0 collective-permute-done.7.xr_two.refs_3_
  29.8 1.9 %collective-permute-start.8 = (bf16[112,128]{1,0:T(8,128)(2,1)S(1)}, bf16[112,128]{1,0:T(8,128)(2,1)S(1)}, u32[]{:S(2)}, u32[]{:S(2)}) collective-permute-start(bf16[112,128]{1,0:T(8,128)(2,1)S(1)} %get-tuple-element.81), channel_id=1, source_target_pairs={{2,4},{4,2},{0,6},{6,0},{3,5},{5,3},{1,7},{7,1},{10,12},{12,10},{8... | collective-permute-start | bytes 86024 | tf_op jit(solution)/shard_map/ppermute | solution.py:525
  31.7 0.0 collective-permute-start.9
  31.7 3.9 %collective-permute-done.8.refs_4_ = bf16[112,128]{1,0:T(8,128)(2,1)S(1)} collective-permute-done((bf16[112,128]{1,0:T(8,128)(2,1)S(1)}, bf16[112,128]{1,0:T(8,128)(2,1)S(1)}, u32[]{:S(2)}, u32[]{:S(2)}) %collective-permute-start.8) | collective-permute-done | bytes 28704 | tf_op jit(solution)/shard_map/ppermute | solution.py:525
  35.6 0.3 collective-permute-done.9.refs_5_
  35.9 1.4 %shard_map.80 = (f32[1352,128]{1,0:T(8,128)S(1)}, f32[384,128]{1,0:T(8,128)S(1)}, bf16[592,128]{1,0:T(8,128)(2,1)S(1)}) custom-call(f32[1352,128]{1,0:T(8,128)S(1)} %get-tuple-element.75.refs_0_, f32[1352,128]{1,0:T(8,128)S(1)} %get-tuple-element.76.refs_1_, bf16[112,128]{1,0:T(8,128)(2,1)S(1)} %collective-permute-done.6.xr_one.refs_2_, ...), custom_call_target="tpu_custom_call" | custom-call | flops 400000000 | bytes 4898816 | tf_op jit(solution)/shard_map/pallas_call | solution.py:57
  37.3 0.7 collective-permute-start.10
  38.0 4.5 %collective-permute-done.10.refs_3_ = bf16[592,128]{1,0:T(8,128)(2,1)S(1)} collective-permute-done((bf16[592,128]{1,0:T(8,128)(2,1)S(1)}, bf16[592,128]{1,0:T(8,128)(2,1)S(1)}, u32[]{:S(2)}, u32[]{:S(2)}) %collective-permute-start.10) | collective-permute-done | bytes 151584 | tf_op jit(solution)/shard_map/ppermute | solution.py:565
  42.5 1.2 %shard_map.81 = (f32[1352,128]{1,0:T(8,128)S(1)}, f32[1352,128]{1,0:T(8,128)S(1)}, f32[1352,128]{1,0:T(8,128)S(1)}, bf16[112,128]{1,0:T(8,128)(2,1)S(1)}, bf16[1...) custom-call(f32[1352,128]{1,0:T(8,128)S(1)} %get-tuple-element.83.refs_0_, ...), custom_call_target="tpu_custom_call" | custom-call | flops 600000000 | bytes 6988288 | tf_op jit(solution)/shard_map/pallas_call | solution.py:57
  43.7 0.1 collective-permute-start.11
  43.8 0.9 %collective-permute-start.12 = (bf16[112,128]{1,0:T(8,128)(2,1)S(1)}, bf16[112,128]{1,0:T(8,128)(2,1)S(1)}, u32[]{:S(2)}, u32[]{:S(2)}) collective-permute-start(bf16[112,128]{1,0:T(8,128)(2,1)S(1)} %get-tuple-element.90), channel_id=1, source_target_pairs={{0,8},{16,24},{8,0},{24,16},{1,9},{17,25},{9,1},{25,17},{2,10},{18... | collective-permute-start | bytes 86024 | tf_op jit(solution)/shard_map/ppermute | solution.py:525
  44.7 2.4 %collective-permute-done.11.xr_one.refs_2_ = bf16[112,128]{1,0:T(8,128)(2,1)S(1)} collective-permute-done((bf16[112,128]{1,0:T(8,128)(2,1)S(1)}, bf16[112,128]{1,0:T(8,128)(2,1)S(1)}, u32[]{:S(2)}, u32[]{:S(2)}) %collective-permute-start.11) | collective-permute-done | bytes 28704 | tf_op jit(solution)/shard_map/ppermute | solution.py:525
  47.0 0.0 collective-permute-done.12.xr_two.refs_3_
  47.1 1.9 %collective-permute-start.13 = (bf16[112,128]{1,0:T(8,128)(2,1)S(1)}, bf16[112,128]{1,0:T(8,128)(2,1)S(1)}, u32[]{:S(2)}, u32[]{:S(2)}) collective-permute-start(bf16[112,128]{1,0:T(8,128)(2,1)S(1)} %get-tuple-element.93), channel_id=1, source_target_pairs={{2,4},{4,2},{0,6},{6,0},{3,5},{5,3},{1,7},{7,1},{10,12},{12,10},{8... | collective-permute-start | bytes 86024 | tf_op jit(solution)/shard_map/ppermute | solution.py:525
  48.9 0.0 collective-permute-start.14
  48.9 3.9 %collective-permute-done.13.refs_4_ = bf16[112,128]{1,0:T(8,128)(2,1)S(1)} collective-permute-done((bf16[112,128]{1,0:T(8,128)(2,1)S(1)}, bf16[112,128]{1,0:T(8,128)(2,1)S(1)}, u32[]{:S(2)}, u32[]{:S(2)}) %collective-permute-start.13) | collective-permute-done | bytes 28704 | tf_op jit(solution)/shard_map/ppermute | solution.py:525
  52.8 0.3 collective-permute-done.14.refs_5_
  53.1 1.4 %shard_map.83 = (f32[1352,128]{1,0:T(8,128)S(1)}, f32[384,128]{1,0:T(8,128)S(1)}, bf16[592,128]{1,0:T(8,128)(2,1)S(1)}) custom-call(f32[1352,128]{1,0:T(8,128)S(1)} %get-tuple-element.87.refs_0_, f32[1352,128]{1,0:T(8,128)S(1)} %get-tuple-element.88.refs_1_, bf16[112,128]{1,0:T(8,128)(2,1)S(1)} %collective-permute-done.11.xr_one.refs_2_, ...), custom_call_target="tpu_custom_call" | custom-call | flops 400000000 | bytes 4898816 | tf_op jit(solution)/shard_map/pallas_call | solution.py:57
  54.5 0.7 collective-permute-start.15
  55.2 4.5 %collective-permute-done.15.refs_3_ = bf16[592,128]{1,0:T(8,128)(2,1)S(1)} collective-permute-done((bf16[592,128]{1,0:T(8,128)(2,1)S(1)}, bf16[592,128]{1,0:T(8,128)(2,1)S(1)}, u32[]{:S(2)}, u32[]{:S(2)}) %collective-permute-start.15) | collective-permute-done | bytes 151584 | tf_op jit(solution)/shard_map/ppermute | solution.py:565
  59.8 1.3 %shard_map.84 = (f32[1352,128]{1,0:T(8,128)S(1)}, f32[1352,128]{1,0:T(8,128)S(1)}, f32[1352,128]{1,0:T(8,128)}, bf16[112,128]{1,0:T(8,128)(2,1)S(1)}, bf16[112,1...) custom-call(f32[1352,128]{1,0:T(8,128)S(1)} %get-tuple-element.95.refs_0_, ...), custom_call_target="tpu_custom_call" | custom-call | flops 600000000 | bytes 6988288 | tf_op jit(solution)/shard_map/pallas_call | solution.py:57
  61.1 0.0 collective-permute-start.16
  61.1 1.0 %collective-permute-start.17 = (bf16[112,128]{1,0:T(8,128)(2,1)S(1)}, bf16[112,128]{1,0:T(8,128)(2,1)S(1)}, u32[]{:S(2)}, u32[]{:S(2)}) collective-permute-start(bf16[112,128]{1,0:T(8,128)(2,1)S(1)} %get-tuple-element.102), channel_id=1, source_target_pairs={{0,8},{16,24},{8,0},{24,16},{1,9},{17,25},{9,1},{25,17},{2,10},{18... | collective-permute-start | bytes 86024 | tf_op jit(solution)/shard_map/ppermute | solution.py:525
  62.1 2.3 %collective-permute-done.16.xr_one.refs_1_.refs_2_ = bf16[112,128]{1,0:T(8,128)(2,1)S(1)} collective-permute-done((bf16[112,128]{1,0:T(8,128)(2,1)S(1)}, bf16[112,128]{1,0:T(8,128)(2,1)S(1)}, u32[]{:S(2)}, u32[]{:S(2)}) %collective-permute-start.16) | collective-permute-done | bytes 28704 | tf_op jit(solution)/shard_map/ppermute | solution.py:525
  64.4 0.0 collective-permute-done.17.xr_two.refs_2_.refs_3_
  64.4 1.9 %collective-permute-start.18 = (bf16[112,128]{1,0:T(8,128)(2,1)S(1)}, bf16[112,128]{1,0:T(8,128)(2,1)S(1)}, u32[]{:S(2)}, u32[]{:S(2)}) collective-permute-start(bf16[112,128]{1,0:T(8,128)(2,1)S(1)} %get-tuple-element.105), channel_id=1, source_target_pairs={{2,4},{4,2},{0,6},{6,0},{3,5},{5,3},{1,7},{7,1},{10,12},{12,10},{8... | collective-permute-start | bytes 86024 | tf_op jit(solution)/shard_map/ppermute | solution.py:525
  66.3 0.0 collective-permute-start.19
  66.3 3.9 %collective-permute-done.18.refs_3_.refs_4_ = bf16[112,128]{1,0:T(8,128)(2,1)S(1)} collective-permute-done((bf16[112,128]{1,0:T(8,128)(2,1)S(1)}, bf16[112,128]{1,0:T(8,128)(2,1)S(1)}, u32[]{:S(2)}, u32[]{:S(2)}) %collective-permute-start.18) | collective-permute-done | bytes 28704 | tf_op jit(solution)/shard_map/ppermute | solution.py:525
  70.2 0.3 collective-permute-done.19.refs_4_.refs_5_
  70.4 0.1 shard_map.86
  70.5 0.7 collective-permute-start.20
  71.2 3.5 %collective-permute-done.20.refs_6_ = bf16[208,128]{1,0:T(8,128)(2,1)S(1)} collective-permute-done((bf16[208,128]{1,0:T(8,128)(2,1)S(1)}, bf16[208,128]{1,0:T(8,128)(2,1)S(1)}, u32[]{:S(2)}, u32[]{:S(2)}) %collective-permute-start.20) | collective-permute-done | bytes 53280 | tf_op jit(solution)/shard_map/ppermute | solution.py:570
  74.7 1.0 %shard_map.87 = f32[13,13,7,128]{3,2,1,0:T(8,128)} custom-call(f32[1352,128]{1,0:T(8,128)S(1)} %get-tuple-element.99.refs_0_, f32[1352,128]{1,0:T(8,128)S(1)} %get-tuple-element.100.refs_1_, bf16[112,128]{1,0:T(8,128)(2,1)S(1)} %collective-permute-done.16.xr_one.refs_1_.refs_2_, bf16[112,128]{1,0:T(8,128)(2,1)S(1)} %collective-permute-done.17.xr_two.refs_2_.refs_3_, ...), custom_call_target="tpu_custom_call" | custom-call | bytes 2158080 | tf_op jit(solution)/shard_map/pallas_call | solution.py:57
  (9 shorter events, 0.2 us)
Async XLA Ops:
  0.0 11.0 %copy-start = (f32[343,2,2,1]{0,3,2,1:T(1,128)S(1)}, f32[343,2,2,1]{0,3,2,1:T(1,128)}, u32[]{:S(2)}) copy-start(f32[343,2,2,1]{0,3,2,1:T(1,128)} %param.9) | copy-start | bytes 16468
  0.0 1.1 %copy-start.1 = (f32[13,13,7,128]{3,2,1,0:T(8,128)S(1)}, f32[13,13,7,128]{3,2,1,0:T(8,128)}, u32[]{:S(2)}) copy-start(f32[13,13,7,128]{3,2,1,0:T(8,128)} %parts.1) | copy-start | bytes 1817092
  1.2 9.8 %collective-permute-start = (bf16[112,128]{1,0:T(8,128)(2,1)S(1)}, bf16[112,128]{1,0:T(8,128)(2,1)S(1)}, u32[]{:S(2)}, u32[]{:S(2)}) collective-permute-start(bf16[112,128]{1,0:T(8,128)(2,1)S(1)} %get-tuple-element.57), channel_id=1, source_target_pairs={{8,16},{16,8},{0,24},{24,0},{9,17},{17,9},{1,25},{25,1},{10,18},{1... | collective-permute-start | bytes 86024 | tf_op jit(solution)/shard_map/ppermute | solution.py:525
  3.7 7.4 %collective-permute-start.1 = (bf16[112,128]{1,0:T(8,128)(2,1)S(1)}, bf16[112,128]{1,0:T(8,128)(2,1)S(1)}, u32[]{:S(2)}, u32[]{:S(2)}) collective-permute-start(bf16[112,128]{1,0:T(8,128)(2,1)S(1)} %get-tuple-element.58), channel_id=1, source_target_pairs={{0,8},{16,24},{8,0},{24,16},{1,9},{17,25},{9,1},{25,17},{2,10},{18... | collective-permute-start | bytes 86024 | tf_op jit(solution)/shard_map/ppermute | solution.py:525
  4.4 1.2 %copy-start.2 = (bf16[1,1,1,343,1536]{4,3,2,1,0:T(8,128)(2,1)S(1)}, bf16[1,1,1,343,1536]{4,3,2,1,0:T(8,128)(2,1)}, u32[]{:S(2)}) copy-start(bf16[1,1,1,343,1536]{4,3,2,1,0:T(8,128)(2,1)} %param.10) | copy-start | bytes 3161092
  5.6 0.7 copy-start.5
  6.3 8.5 %copy-start.3 = (bf16[343,343]{1,0:T(8,128)(2,1)S(1)}, bf16[343,343]{1,0:T(8,128)(2,1)}, u32[]{:S(2)}) copy-start(bf16[343,343]{1,0:T(8,128)(2,1)} %kin.1) | copy-start | bytes 705898
  6.3 8.5 %copy-start.4 = (f32[64,12,12]{0,2,1:T(8,128)S(1)}, f32[64,12,12]{0,2,1:T(8,128)}, u32[]{:S(2)}) copy-start(f32[64,12,12]{0,2,1:T(8,128)} %param.13) | copy-start | bytes 110596
  6.3 8.5 %copy-start.6 = (s32[1,1,2,32]{3,2,1,0:T(2,128)S(1)}, s32[1,1,2,32]{3,2,1,0:T(2,128)}, u32[]{:S(2)}) copy-start(s32[1,1,2,32]{3,2,1,0:T(2,128)} %param.11) | copy-start | bytes 772
  9.4 9.2 %collective-permute-start.4 = (bf16[384,256]{1,0:T(8,128)(2,1)S(1)}, bf16[384,256]{1,0:T(8,128)(2,1)S(1)}, u32[]{:S(2)}, u32[]{:S(2)}) collective-permute-start(bf16[384,256]{1,0:T(8,128)(2,1)S(1)} %get-tuple-element.65), channel_id=1, source_target_pairs={{1,0},{0,1},{3,2},{2,3},{5,4},{4,5},{7,6},{6,7},{9,8},{8,9},{11,10... | collective-permute-start | bytes 589832 | tf_op jit(solution)/shard_map/ppermute | solution.py:550
  11.1 5.7 %collective-permute-start.2 = (bf16[112,128]{1,0:T(8,128)(2,1)S(1)}, bf16[112,128]{1,0:T(8,128)(2,1)S(1)}, u32[]{:S(2)}, u32[]{:S(2)}) collective-permute-start(bf16[112,128]{1,0:T(8,128)(2,1)S(1)} %get-tuple-element.61), channel_id=1, source_target_pairs={{2,4},{4,2},{0,6},{6,0},{3,5},{5,3},{1,7},{7,1},{10,12},{12,10},{8... | collective-permute-start | bytes 86024 | tf_op jit(solution)/shard_map/ppermute | solution.py:525
  14.7 3.9 %collective-permute-start.3 = (bf16[112,128]{1,0:T(8,128)(2,1)S(1)}, bf16[112,128]{1,0:T(8,128)(2,1)S(1)}, u32[]{:S(2)}, u32[]{:S(2)}) collective-permute-start(bf16[112,128]{1,0:T(8,128)(2,1)S(1)} %get-tuple-element.62), channel_id=1, source_target_pairs={{0,2},{4,6},{2,0},{6,4},{1,3},{5,7},{3,1},{7,5},{8,10},{12,14},{10... | collective-permute-start | bytes 86024 | tf_op jit(solution)/shard_map/ppermute | solution.py:525
  20.0 5.3 %collective-permute-start.5 = (bf16[592,128]{1,0:T(8,128)(2,1)S(1)}, bf16[592,128]{1,0:T(8,128)(2,1)S(1)}, u32[]{:S(2)}, u32[]{:S(2)}) collective-permute-start(bf16[592,128]{1,0:T(8,128)(2,1)S(1)} %get-tuple-element.70), channel_id=1, source_target_pairs={{0,1},{1,0},{2,3},{3,2},{4,5},{5,4},{6,7},{7,6},{8,9},{9,8},{10,11... | collective-permute-start | bytes 454664 | tf_op jit(solution)/shard_map/ppermute | solution.py:565
  26.4 3.4 %collective-permute-start.6 = (bf16[112,128]{1,0:T(8,128)(2,1)S(1)}, bf16[112,128]{1,0:T(8,128)(2,1)S(1)}, u32[]{:S(2)}, u32[]{:S(2)}) collective-permute-start(bf16[112,128]{1,0:T(8,128)(2,1)S(1)} %get-tuple-element.77), channel_id=1, source_target_pairs={{8,16},{16,8},{0,24},{24,0},{9,17},{17,9},{1,25},{25,1},{10,18},{1... | collective-permute-start | bytes 86024 | tf_op jit(solution)/shard_map/ppermute | solution.py:525
  26.5 3.3 %collective-permute-start.7 = (bf16[112,128]{1,0:T(8,128)(2,1)S(1)}, bf16[112,128]{1,0:T(8,128)(2,1)S(1)}, u32[]{:S(2)}, u32[]{:S(2)}) collective-permute-start(bf16[112,128]{1,0:T(8,128)(2,1)S(1)} %get-tuple-element.78), channel_id=1, source_target_pairs={{0,8},{16,24},{8,0},{24,16},{1,9},{17,25},{9,1},{25,17},{2,10},{18... | collective-permute-start | bytes 86024 | tf_op jit(solution)/shard_map/ppermute | solution.py:525
  29.8 5.8 %collective-permute-start.8 = (bf16[112,128]{1,0:T(8,128)(2,1)S(1)}, bf16[112,128]{1,0:T(8,128)(2,1)S(1)}, u32[]{:S(2)}, u32[]{:S(2)}) collective-permute-start(bf16[112,128]{1,0:T(8,128)(2,1)S(1)} %get-tuple-element.81), channel_id=1, source_target_pairs={{2,4},{4,2},{0,6},{6,0},{3,5},{5,3},{1,7},{7,1},{10,12},{12,10},{8... | collective-permute-start | bytes 86024 | tf_op jit(solution)/shard_map/ppermute | solution.py:525
  31.7 4.2 %collective-permute-start.9 = (bf16[112,128]{1,0:T(8,128)(2,1)S(1)}, bf16[112,128]{1,0:T(8,128)(2,1)S(1)}, u32[]{:S(2)}, u32[]{:S(2)}) collective-permute-start(bf16[112,128]{1,0:T(8,128)(2,1)S(1)} %get-tuple-element.82), channel_id=1, source_target_pairs={{0,2},{4,6},{2,0},{6,4},{1,3},{5,7},{3,1},{7,5},{8,10},{12,14},{10... | collective-permute-start | bytes 86024 | tf_op jit(solution)/shard_map/ppermute | solution.py:525
  37.3 5.3 %collective-permute-start.10 = (bf16[592,128]{1,0:T(8,128)(2,1)S(1)}, bf16[592,128]{1,0:T(8,128)(2,1)S(1)}, u32[]{:S(2)}, u32[]{:S(2)}) collective-permute-start(bf16[592,128]{1,0:T(8,128)(2,1)S(1)} %get-tuple-element.86), channel_id=1, source_target_pairs={{0,1},{1,0},{2,3},{3,2},{4,5},{5,4},{6,7},{7,6},{8,9},{9,8},{10,11... | collective-permute-start | bytes 454664 | tf_op jit(solution)/shard_map/ppermute | solution.py:565
  43.7 3.4 %collective-permute-start.11 = (bf16[112,128]{1,0:T(8,128)(2,1)S(1)}, bf16[112,128]{1,0:T(8,128)(2,1)S(1)}, u32[]{:S(2)}, u32[]{:S(2)}) collective-permute-start(bf16[112,128]{1,0:T(8,128)(2,1)S(1)} %get-tuple-element.89), channel_id=1, source_target_pairs={{8,16},{16,8},{0,24},{24,0},{9,17},{17,9},{1,25},{25,1},{10,18},{1... | collective-permute-start | bytes 86024 | tf_op jit(solution)/shard_map/ppermute | solution.py:525
  43.8 3.3 %collective-permute-start.12 = (bf16[112,128]{1,0:T(8,128)(2,1)S(1)}, bf16[112,128]{1,0:T(8,128)(2,1)S(1)}, u32[]{:S(2)}, u32[]{:S(2)}) collective-permute-start(bf16[112,128]{1,0:T(8,128)(2,1)S(1)} %get-tuple-element.90), channel_id=1, source_target_pairs={{0,8},{16,24},{8,0},{24,16},{1,9},{17,25},{9,1},{25,17},{2,10},{18... | collective-permute-start | bytes 86024 | tf_op jit(solution)/shard_map/ppermute | solution.py:525
  47.1 5.8 %collective-permute-start.13 = (bf16[112,128]{1,0:T(8,128)(2,1)S(1)}, bf16[112,128]{1,0:T(8,128)(2,1)S(1)}, u32[]{:S(2)}, u32[]{:S(2)}) collective-permute-start(bf16[112,128]{1,0:T(8,128)(2,1)S(1)} %get-tuple-element.93), channel_id=1, source_target_pairs={{2,4},{4,2},{0,6},{6,0},{3,5},{5,3},{1,7},{7,1},{10,12},{12,10},{8... | collective-permute-start | bytes 86024 | tf_op jit(solution)/shard_map/ppermute | solution.py:525
  48.9 4.2 %collective-permute-start.14 = (bf16[112,128]{1,0:T(8,128)(2,1)S(1)}, bf16[112,128]{1,0:T(8,128)(2,1)S(1)}, u32[]{:S(2)}, u32[]{:S(2)}) collective-permute-start(bf16[112,128]{1,0:T(8,128)(2,1)S(1)} %get-tuple-element.94), channel_id=1, source_target_pairs={{0,2},{4,6},{2,0},{6,4},{1,3},{5,7},{3,1},{7,5},{8,10},{12,14},{10... | collective-permute-start | bytes 86024 | tf_op jit(solution)/shard_map/ppermute | solution.py:525
  54.5 5.3 %collective-permute-start.15 = (bf16[592,128]{1,0:T(8,128)(2,1)S(1)}, bf16[592,128]{1,0:T(8,128)(2,1)S(1)}, u32[]{:S(2)}, u32[]{:S(2)}) collective-permute-start(bf16[592,128]{1,0:T(8,128)(2,1)S(1)} %get-tuple-element.98), channel_id=1, source_target_pairs={{0,1},{1,0},{2,3},{3,2},{4,5},{5,4},{6,7},{7,6},{8,9},{9,8},{10,11... | collective-permute-start | bytes 454664 | tf_op jit(solution)/shard_map/ppermute | solution.py:565
  61.1 3.3 %collective-permute-start.16 = (bf16[112,128]{1,0:T(8,128)(2,1)S(1)}, bf16[112,128]{1,0:T(8,128)(2,1)S(1)}, u32[]{:S(2)}, u32[]{:S(2)}) collective-permute-start(bf16[112,128]{1,0:T(8,128)(2,1)S(1)} %get-tuple-element.101), channel_id=1, source_target_pairs={{8,16},{16,8},{0,24},{24,0},{9,17},{17,9},{1,25},{25,1},{10,18},{1... | collective-permute-start | bytes 86024 | tf_op jit(solution)/shard_map/ppermute | solution.py:525
  61.1 3.3 %collective-permute-start.17 = (bf16[112,128]{1,0:T(8,128)(2,1)S(1)}, bf16[112,128]{1,0:T(8,128)(2,1)S(1)}, u32[]{:S(2)}, u32[]{:S(2)}) collective-permute-start(bf16[112,128]{1,0:T(8,128)(2,1)S(1)} %get-tuple-element.102), channel_id=1, source_target_pairs={{0,8},{16,24},{8,0},{24,16},{1,9},{17,25},{9,1},{25,17},{2,10},{18... | collective-permute-start | bytes 86024 | tf_op jit(solution)/shard_map/ppermute | solution.py:525
  64.4 5.8 %collective-permute-start.18 = (bf16[112,128]{1,0:T(8,128)(2,1)S(1)}, bf16[112,128]{1,0:T(8,128)(2,1)S(1)}, u32[]{:S(2)}, u32[]{:S(2)}) collective-permute-start(bf16[112,128]{1,0:T(8,128)(2,1)S(1)} %get-tuple-element.105), channel_id=1, source_target_pairs={{2,4},{4,2},{0,6},{6,0},{3,5},{5,3},{1,7},{7,1},{10,12},{12,10},{8... | collective-permute-start | bytes 86024 | tf_op jit(solution)/shard_map/ppermute | solution.py:525
  66.3 4.2 %collective-permute-start.19 = (bf16[112,128]{1,0:T(8,128)(2,1)S(1)}, bf16[112,128]{1,0:T(8,128)(2,1)S(1)}, u32[]{:S(2)}, u32[]{:S(2)}) collective-permute-start(bf16[112,128]{1,0:T(8,128)(2,1)S(1)} %get-tuple-element.106), channel_id=1, source_target_pairs={{0,2},{4,6},{2,0},{6,4},{1,3},{5,7},{3,1},{7,5},{8,10},{12,14},{10... | collective-permute-start | bytes 86024 | tf_op jit(solution)/shard_map/ppermute | solution.py:525
  70.5 4.2 %collective-permute-start.20 = (bf16[208,128]{1,0:T(8,128)(2,1)S(1)}, bf16[208,128]{1,0:T(8,128)(2,1)S(1)}, u32[]{:S(2)}, u32[]{:S(2)}) collective-permute-start(bf16[208,128]{1,0:T(8,128)(2,1)S(1)} %shard_map.86), channel_id=1, source_target_pairs={{0,1},{1,0},{2,3},{3,2},{4,5},{5,4},{6,7},{7,6},{8,9},{9,8},{10,11... | collective-permute-start | bytes 159752 | tf_op jit(solution)/shard_map/ppermute | solution.py:570

commit v4 on v3

--- a/solution.py
+++ b/solution.py
@@ -515,14 +515,30 @@
 
 
 def swap_faces(axis, one, two):
-    count = lax.axis_size(axis)
-    pairs = []
-    for low in (1, 0):
-        lows = range(low, count - 1, 2)
-        pair = [(i, i + 1) for i in lows] + [(i + 1, i) for i in lows]
-        alone = sorted(set(range(count)) - {source for source, _ in pair})
-        pairs.append(pair + list(zip(alone, alone[::-1])))
-    return lax.ppermute(one, axis, pairs[0]), lax.ppermute(two, axis, pairs[1])
+    axes = ("gx", "gy")
+    wide, deep = lax.axis_size("gx"), lax.axis_size("gy")
+    count = wide if axis == "gx" else deep
+
+    def partner(i, j, low):
+        at = i if axis == "gx" else j
+        to = at + 1 if at % 2 == low else at - 1
+        if 0 <= to < count:
+            return (to, j) if axis == "gx" else (i, to)
+        if axis == "gy" and wide % 2 == 0:
+            return (i ^ 1, j)
+        ends = sorted({k for k in range(count) if not 0 <= k + (1 if k % 2 == low else -1) < count})
+        to = ends[::-1][ends.index(at)]
+        return (to, j) if axis == "gx" else (i, to)
+
+    out = []
+    for face, low in ((one, 1), (two, 0)):
+        pairs = []
+        for i in range(wide):
+            for j in range(deep):
+                to = partner(i, j, low)
+                pairs.append((i * deep + j, to[0] * deep + to[1]))
+        out.append(lax.ppermute(face, axes, pairs))
+    return out
 
 
 def local(parts, cell_matrix, cell_potential, projectors, slot_atom, slot_cells, coupling):

time: 75.9 us -> 70.4 us (0.928)
  waiting for transfers between devices: 39.1 us -> 26.7 us
  starting transfers between devices: 19.4 us -> 26.2 us
    ppermute x16, waiting for transfers between devices: 21.9 us -> 12.6 us  [swap_faces(): out.append(lax.ppermute(face, axes, pairs))]
    ppermute x16, starting transfers between devices: 15.1 us -> 18.6 us  [swap_faces(): out.append(lax.ppermute(face, axes, pairs))]
    ppermute x3, waiting for transfers between devices: 13.7 us -> 11.4 us  [local(): lax.ppermute(m, 'gz', ring[s + 1])]
    ppermute x3, starting transfers between devices: 2.02 us -> 4.4 us  [local(): lax.ppermute(m, 'gz', ring[s + 1])]
    ppermute x1, waiting for transfers between devices: 3.48 us -> 2.62 us  [local(): zr = [lax.ppermute(f, 'gz', ring[s]) for f, s in zip(sent, link_shifts(sz))]]
    ppermute x1, starting transfers between devices: 0.72 us -> 1.58 us  [local(): zr = [lax.ppermute(f, 'gz', ring[s]) for f, s in zip(sent, link_shifts(sz))]]
  transfers between devices with their start and end apart: 21 -> 21, of which waited for: 15 -> 11; matrix products, arithmetic and copies ran while one was open for 0% -> 0% of each run, Pallas kernels for 7% -> 7%
where the time goes in v4:
time: 70.4 us; the launch traced here: 70.2 us
  waiting for transfers between devices  26.7 us (38%)
  starting transfers between devices  26.2 us (37%)
  Pallas kernels  14 us (20%)
  local copies, waits for them, and re-layouts  3.08 us (4%)
    ppermute x16, starting transfers between devices, swap_faces(): out.append(lax.ppermute(face, axes, pairs))  18.6 us
    pallas_call x15, Pallas kernels, kernel_call(): pl.pallas_call(body, out_shape=outs, in_specs=[VMEM] * len(arrays), out_s...  14 us
    ppermute x16, waiting for transfers between devices, swap_faces(): out.append(lax.ppermute(face, axes, pairs))  12.6 us
    ppermute x3, waiting for transfers between devices, local(): lax.ppermute(m, 'gz', ring[s + 1])  11.4 us
    ppermute x3, starting transfers between devices, local(): lax.ppermute(m, 'gz', ring[s + 1])  4.4 us
    unnamed x14, local copies, waits for them, and re-layouts  3.04 us
    ppermute x1, waiting for transfers between devices, local(): zr = [lax.ppermute(f, 'gz', ring[s]) for f, s in zip(sent, link_shifts(sz))]  2.62 us
    ppermute x1, starting transfers between devices, local(): qfaces.append(lax.ppermute(face_rows[j], 'gz', back))  1.58 us
  transfers between devices with their start and end apart: 21, of which 11 were waited for; matrix products, arithmetic and copies ran while one was open for 0% of the time, Pallas kernels for 7%

profile of v4, /device:TPU:0, one launch (start us, length us, event | category | flops | bytes accessed | tf_op | source)
XLA Modules:
  0.0 70.2 jit_solution(8259176325492007838)
XLA Ops:
  0.0 0.0 copy-start
  0.0 0.0 copy-start.1
  0.0 1.1 %copy-done.1 = f32[13,13,7,128]{3,2,1,0:T(8,128)S(1)} copy-done((f32[13,13,7,128]{3,2,1,0:T(8,128)S(1)}, f32[13,13,7,128]{3,2,1,0:T(8,128)}, u32[]{:S(2)}) %copy-start.1) | copy-done | bytes 605720
  1.1 0.1 shard_map.73
  1.2 2.4 %collective-permute-start = (bf16[112,128]{1,0:T(8,128)(2,1)S(1)}, bf16[112,128]{1,0:T(8,128)(2,1)S(1)}, u32[]{:S(2)}, u32[]{:S(2)}) collective-permute-start(bf16[112,128]{1,0:T(8,128)(2,1)S(1)} %get-tuple-element.57), channel_id=1, source_target_pairs={{0,24},{2,26},{4,28},{6,30},{8,16},{10,18},{12,20},{14,22},{16,8},... | collective-permute-start | bytes 86024 | tf_op jit(solution)/shard_map/ppermute | solution.py:540
  3.7 0.7 collective-permute-start.1
  4.4 0.0 copy-start.2
  4.4 1.2 %copy-done.2 = bf16[1,1,1,343,1536]{4,3,2,1,0:T(8,128)(2,1)S(1)} copy-done((bf16[1,1,1,343,1536]{4,3,2,1,0:T(8,128)(2,1)S(1)}, bf16[1,1,1,343,1536]{4,3,2,1,0:T(8,128)(2,1)}, u32[]{:S(2)}) %copy-start.2) | copy-done | bytes 1053720
  5.6 0.0 copy-start.5
  5.6 0.7 copy-done.5
  6.3 3.1 %shard_map.75 = (bf16[1664,384]{1,0:T(8,128)(2,1)S(1)}, bf16[384,256]{1,0:T(8,128)(2,1)S(1)}) custom-call(bf16[343,1536]{1,0:T(8,128)(2,1)S(1)} %bitcast.10, s32[4,32]{1,0:T(4,128)S(1)} %bitcast.12), custom_call_target="tpu_custom_call" | custom-call | flops 3000000000 | bytes 2528768 | tf_op jit(solution)/shard_map/pallas_call | solution.py:57
  9.4 1.6 %collective-permute-start.4 = (bf16[384,256]{1,0:T(8,128)(2,1)S(1)}, bf16[384,256]{1,0:T(8,128)(2,1)S(1)}, u32[]{:S(2)}, u32[]{:S(2)}) collective-permute-start(bf16[384,256]{1,0:T(8,128)(2,1)S(1)} %get-tuple-element.65), channel_id=1, source_target_pairs={{1,0},{0,1},{3,2},{2,3},{5,4},{4,5},{7,6},{6,7},{9,8},{8,9},{11,10... | collective-permute-start | bytes 589832 | tf_op jit(solution)/shard_map/ppermute | solution.py:566
  11.0 0.0 copy-done
  11.0 0.0 collective-permute-done.xr_one.refs_1_
  11.0 0.0 collective-permute-done.1.xr_two.refs_2_
  11.1 0.1 collective-permute-start.2
  11.2 3.1 %collective-permute-start.3 = (bf16[112,128]{1,0:T(8,128)(2,1)S(1)}, bf16[112,128]{1,0:T(8,128)(2,1)S(1)}, u32[]{:S(2)}, u32[]{:S(2)}) collective-permute-start(bf16[112,128]{1,0:T(8,128)(2,1)S(1)} %get-tuple-element.62), channel_id=1, source_target_pairs={{0,2},{2,0},{4,6},{6,4},{8,10},{10,8},{12,14},{14,12},{16,18},{18,... | collective-permute-start | bytes 86024 | tf_op jit(solution)/shard_map/ppermute | solution.py:540
  14.3 0.0 copy-done.3
  14.3 0.0 copy-done.4
  14.3 0.0 copy-done.6
  14.3 1.8 %shard_map.76 = (bf16[384,1664]{1,0:T(8,128)(2,1)S(1)}, bf16[400,400]{1,0:T(8,128)(2,1)S(1)}, f32[1600,128]{1,0:T(8,128)S(1)}, bf16[384,768]{1,0:T(8,128)(2,1)S(...) custom-call(bf16[1664,384]{1,0:T(8,128)(2,1)S(1)} %get-tuple-element.63.qt.refs_5_.refs, ...), custom_call_target="tpu_custom_call" | custom-call | flops 1000000000 | bytes 5447570 | tf_op jit(solution)/shard_map/pallas_call | solution.py:57
  16.1 0.0 collective-permute-done.2.refs_3_
  16.1 0.0 collective-permute-done.3.refs_4_
  16.1 0.1 collective-permute-done.4.refs_6_.refs_7_
  16.2 1.4 %shard_map.77 = (f32[1352,128]{1,0:T(8,128)S(1)}, f32[384,128]{1,0:T(8,128)S(1)}, bf16[592,128]{1,0:T(8,128)(2,1)S(1)}) custom-call(f32[1352,128]{1,0:T(8,128)S(1)} %bitcast.9, bf16[112,128]{1,0:T(8,128)(2,1)S(1)} %collective-permute-done.xr_one.refs_1_, bf16[112,128]{1,0:T(8,128)(2,1)S(1)} %collective-permute-done.1.xr_two.refs_2_, ...), custom_call_target="tpu_custom_call" | custom-call | flops 400000000 | bytes 4206592 | tf_op jit(solution)/shard_map/pallas_call | solution.py:57
  17.6 1.6 %collective-permute-start.5 = (bf16[592,128]{1,0:T(8,128)(2,1)S(1)}, bf16[592,128]{1,0:T(8,128)(2,1)S(1)}, u32[]{:S(2)}, u32[]{:S(2)}) collective-permute-start(bf16[592,128]{1,0:T(8,128)(2,1)S(1)} %get-tuple-element.70), channel_id=1, source_target_pairs={{0,1},{1,0},{2,3},{3,2},{4,5},{5,4},{6,7},{7,6},{8,9},{9,8},{10,11... | collective-permute-start | bytes 454664 | tf_op jit(solution)/shard_map/ppermute | solution.py:581
  19.2 3.7 %collective-permute-done.5.refs_2_ = bf16[592,128]{1,0:T(8,128)(2,1)S(1)} collective-permute-done((bf16[592,128]{1,0:T(8,128)(2,1)S(1)}, bf16[592,128]{1,0:T(8,128)(2,1)S(1)}, u32[]{:S(2)}, u32[]{:S(2)}) %collective-permute-start.5) | collective-permute-done | bytes 151584 | tf_op jit(solution)/shard_map/ppermute | solution.py:581
  22.9 1.2 %shard_map.78 = (f32[1352,128]{1,0:T(8,128)S(1)}, f32[1352,128]{1,0:T(8,128)S(1)}, f32[1352,128]{1,0:T(8,128)S(1)}, bf16[112,128]{1,0:T(8,128)(2,1)S(1)}, bf16[1...) custom-call(f32[1352,128]{1,0:T(8,128)S(1)} %get-tuple-element.68.refs_0_, ...), custom_call_target="tpu_custom_call" | custom-call | flops 600000000 | bytes 6296064 | tf_op jit(solution)/shard_map/pallas_call | solution.py:57
  24.1 0.1 collective-permute-start.6
  24.1 0.9 %collective-permute-start.7 = (bf16[112,128]{1,0:T(8,128)(2,1)S(1)}, bf16[112,128]{1,0:T(8,128)(2,1)S(1)}, u32[]{:S(2)}, u32[]{:S(2)}) collective-permute-start(bf16[112,128]{1,0:T(8,128)(2,1)S(1)} %get-tuple-element.78), channel_id=1, source_target_pairs={{0,8},{2,10},{4,12},{6,14},{8,0},{10,2},{12,4},{14,6},{16,24},{18,... | collective-permute-start | bytes 86024 | tf_op jit(solution)/shard_map/ppermute | solution.py:540
  25.0 2.4 %collective-permute-done.6.xr_one.refs_2_ = bf16[112,128]{1,0:T(8,128)(2,1)S(1)} collective-permute-done((bf16[112,128]{1,0:T(8,128)(2,1)S(1)}, bf16[112,128]{1,0:T(8,128)(2,1)S(1)}, u32[]{:S(2)}, u32[]{:S(2)}) %collective-permute-start.6) | collective-permute-done | bytes 28704 | tf_op jit(solution)/shard_map/ppermute | solution.py:540
  27.4 0.0 collective-permute-done.7.xr_two.refs_3_
  27.5 0.1 collective-permute-start.8
  27.5 3.1 %collective-permute-start.9 = (bf16[112,128]{1,0:T(8,128)(2,1)S(1)}, bf16[112,128]{1,0:T(8,128)(2,1)S(1)}, u32[]{:S(2)}, u32[]{:S(2)}) collective-permute-start(bf16[112,128]{1,0:T(8,128)(2,1)S(1)} %get-tuple-element.82), channel_id=1, source_target_pairs={{0,2},{2,0},{4,6},{6,4},{8,10},{10,8},{12,14},{14,12},{16,18},{18,... | collective-permute-start | bytes 86024 | tf_op jit(solution)/shard_map/ppermute | solution.py:540
  30.7 0.0 collective-permute-done.8.refs_4_
  30.7 1.8 %collective-permute-done.9.refs_5_ = bf16[112,128]{1,0:T(8,128)(2,1)S(1)} collective-permute-done((bf16[112,128]{1,0:T(8,128)(2,1)S(1)}, bf16[112,128]{1,0:T(8,128)(2,1)S(1)}, u32[]{:S(2)}, u32[]{:S(2)}) %collective-permute-start.9) | collective-permute-done | bytes 28704 | tf_op jit(solution)/shard_map/ppermute | solution.py:540
  32.5 1.4 %shard_map.80 = (f32[1352,128]{1,0:T(8,128)S(1)}, f32[384,128]{1,0:T(8,128)S(1)}, bf16[592,128]{1,0:T(8,128)(2,1)S(1)}) custom-call(f32[1352,128]{1,0:T(8,128)S(1)} %get-tuple-element.75.refs_0_, f32[1352,128]{1,0:T(8,128)S(1)} %get-tuple-element.76.refs_1_, bf16[112,128]{1,0:T(8,128)(2,1)S(1)} %collective-permute-done.6.xr_one.refs_2_, ...), custom_call_target="tpu_custom_call" | custom-call | flops 400000000 | bytes 4898816 | tf_op jit(solution)/shard_map/pallas_call | solution.py:57
  33.9 1.6 %collective-permute-start.10 = (bf16[592,128]{1,0:T(8,128)(2,1)S(1)}, bf16[592,128]{1,0:T(8,128)(2,1)S(1)}, u32[]{:S(2)}, u32[]{:S(2)}) collective-permute-start(bf16[592,128]{1,0:T(8,128)(2,1)S(1)} %get-tuple-element.86), channel_id=1, source_target_pairs={{0,1},{1,0},{2,3},{3,2},{4,5},{5,4},{6,7},{7,6},{8,9},{9,8},{10,11... | collective-permute-start | bytes 454664 | tf_op jit(solution)/shard_map/ppermute | solution.py:581
  35.5 3.7 %collective-permute-done.10.refs_3_ = bf16[592,128]{1,0:T(8,128)(2,1)S(1)} collective-permute-done((bf16[592,128]{1,0:T(8,128)(2,1)S(1)}, bf16[592,128]{1,0:T(8,128)(2,1)S(1)}, u32[]{:S(2)}, u32[]{:S(2)}) %collective-permute-start.10) | collective-permute-done | bytes 151584 | tf_op jit(solution)/shard_map/ppermute | solution.py:581
  39.2 1.2 %shard_map.81 = (f32[1352,128]{1,0:T(8,128)S(1)}, f32[1352,128]{1,0:T(8,128)S(1)}, f32[1352,128]{1,0:T(8,128)S(1)}, bf16[112,128]{1,0:T(8,128)(2,1)S(1)}, bf16[1...) custom-call(f32[1352,128]{1,0:T(8,128)S(1)} %get-tuple-element.83.refs_0_, ...), custom_call_target="tpu_custom_call" | custom-call | flops 600000000 | bytes 6988288 | tf_op jit(solution)/shard_map/pallas_call | solution.py:57
  40.4 0.1 collective-permute-start.11
  40.4 0.9 %collective-permute-start.12 = (bf16[112,128]{1,0:T(8,128)(2,1)S(1)}, bf16[112,128]{1,0:T(8,128)(2,1)S(1)}, u32[]{:S(2)}, u32[]{:S(2)}) collective-permute-start(bf16[112,128]{1,0:T(8,128)(2,1)S(1)} %get-tuple-element.90), channel_id=1, source_target_pairs={{0,8},{2,10},{4,12},{6,14},{8,0},{10,2},{12,4},{14,6},{16,24},{18,... | collective-permute-start | bytes 86024 | tf_op jit(solution)/shard_map/ppermute | solution.py:540
  41.3 2.4 %collective-permute-done.11.xr_one.refs_2_ = bf16[112,128]{1,0:T(8,128)(2,1)S(1)} collective-permute-done((bf16[112,128]{1,0:T(8,128)(2,1)S(1)}, bf16[112,128]{1,0:T(8,128)(2,1)S(1)}, u32[]{:S(2)}, u32[]{:S(2)}) %collective-permute-start.11) | collective-permute-done | bytes 28704 | tf_op jit(solution)/shard_map/ppermute | solution.py:540
  43.7 0.0 collective-permute-done.12.xr_two.refs_3_
  43.7 0.1 collective-permute-start.13
  43.8 2.8 %collective-permute-start.14 = (bf16[112,128]{1,0:T(8,128)(2,1)S(1)}, bf16[112,128]{1,0:T(8,128)(2,1)S(1)}, u32[]{:S(2)}, u32[]{:S(2)}) collective-permute-start(bf16[112,128]{1,0:T(8,128)(2,1)S(1)} %get-tuple-element.94), channel_id=1, source_target_pairs={{0,2},{2,0},{4,6},{6,4},{8,10},{10,8},{12,14},{14,12},{16,18},{18,... | collective-permute-start | bytes 86024 | tf_op jit(solution)/shard_map/ppermute | solution.py:540
  46.6 0.0 collective-permute-done.13.refs_4_
  46.6 1.8 %collective-permute-done.14.refs_5_ = bf16[112,128]{1,0:T(8,128)(2,1)S(1)} collective-permute-done((bf16[112,128]{1,0:T(8,128)(2,1)S(1)}, bf16[112,128]{1,0:T(8,128)(2,1)S(1)}, u32[]{:S(2)}, u32[]{:S(2)}) %collective-permute-start.14) | collective-permute-done | bytes 28704 | tf_op jit(solution)/shard_map/ppermute | solution.py:540
  48.5 1.4 %shard_map.83 = (f32[1352,128]{1,0:T(8,128)S(1)}, f32[384,128]{1,0:T(8,128)S(1)}, bf16[592,128]{1,0:T(8,128)(2,1)S(1)}) custom-call(f32[1352,128]{1,0:T(8,128)S(1)} %get-tuple-element.87.refs_0_, f32[1352,128]{1,0:T(8,128)S(1)} %get-tuple-element.88.refs_1_, bf16[112,128]{1,0:T(8,128)(2,1)S(1)} %collective-permute-done.11.xr_one.refs_2_, ...), custom_call_target="tpu_custom_call" | custom-call | flops 400000000 | bytes 4898816 | tf_op jit(solution)/shard_map/pallas_call | solution.py:57
  49.9 1.2 %collective-permute-start.15 = (bf16[592,128]{1,0:T(8,128)(2,1)S(1)}, bf16[592,128]{1,0:T(8,128)(2,1)S(1)}, u32[]{:S(2)}, u32[]{:S(2)}) collective-permute-start(bf16[592,128]{1,0:T(8,128)(2,1)S(1)} %get-tuple-element.98), channel_id=1, source_target_pairs={{0,1},{1,0},{2,3},{3,2},{4,5},{5,4},{6,7},{7,6},{8,9},{9,8},{10,11... | collective-permute-start | bytes 454664 | tf_op jit(solution)/shard_map/ppermute | solution.py:581
  51.1 4.0 %collective-permute-done.15.refs_3_ = bf16[592,128]{1,0:T(8,128)(2,1)S(1)} collective-permute-done((bf16[592,128]{1,0:T(8,128)(2,1)S(1)}, bf16[592,128]{1,0:T(8,128)(2,1)S(1)}, u32[]{:S(2)}, u32[]{:S(2)}) %collective-permute-start.15) | collective-permute-done | bytes 151584 | tf_op jit(solution)/shard_map/ppermute | solution.py:581
  55.1 1.3 %shard_map.84 = (f32[1352,128]{1,0:T(8,128)S(1)}, f32[1352,128]{1,0:T(8,128)S(1)}, f32[1352,128]{1,0:T(8,128)}, bf16[112,128]{1,0:T(8,128)(2,1)S(1)}, bf16[112,1...) custom-call(f32[1352,128]{1,0:T(8,128)S(1)} %get-tuple-element.95.refs_0_, ...), custom_call_target="tpu_custom_call" | custom-call | flops 600000000 | bytes 6988288 | tf_op jit(solution)/shard_map/pallas_call | solution.py:57
  56.4 0.0 collective-permute-start.16
  56.4 1.0 %collective-permute-start.17 = (bf16[112,128]{1,0:T(8,128)(2,1)S(1)}, bf16[112,128]{1,0:T(8,128)(2,1)S(1)}, u32[]{:S(2)}, u32[]{:S(2)}) collective-permute-start(bf16[112,128]{1,0:T(8,128)(2,1)S(1)} %get-tuple-element.102), channel_id=1, source_target_pairs={{0,8},{2,10},{4,12},{6,14},{8,0},{10,2},{12,4},{14,6},{16,24},{18,... | collective-permute-start | bytes 86024 | tf_op jit(solution)/shard_map/ppermute | solution.py:540
  57.4 2.3 %collective-permute-done.16.xr_one.refs_1_.refs_2_ = bf16[112,128]{1,0:T(8,128)(2,1)S(1)} collective-permute-done((bf16[112,128]{1,0:T(8,128)(2,1)S(1)}, bf16[112,128]{1,0:T(8,128)(2,1)S(1)}, u32[]{:S(2)}, u32[]{:S(2)}) %collective-permute-start.16) | collective-permute-done | bytes 28704 | tf_op jit(solution)/shard_map/ppermute | solution.py:540
  59.7 0.0 collective-permute-done.17.xr_two.refs_2_.refs_3_
  59.7 0.1 collective-permute-start.18
  59.8 3.3 %collective-permute-start.19 = (bf16[112,128]{1,0:T(8,128)(2,1)S(1)}, bf16[112,128]{1,0:T(8,128)(2,1)S(1)}, u32[]{:S(2)}, u32[]{:S(2)}) collective-permute-start(bf16[112,128]{1,0:T(8,128)(2,1)S(1)} %get-tuple-element.106), channel_id=1, source_target_pairs={{0,2},{2,0},{4,6},{6,4},{8,10},{10,8},{12,14},{14,12},{16,18},{18,... | collective-permute-start | bytes 86024 | tf_op jit(solution)/shard_map/ppermute | solution.py:540
  63.1 0.0 collective-permute-done.18.refs_3_.refs_4_
  63.1 1.8 %collective-permute-done.19.refs_4_.refs_5_ = bf16[112,128]{1,0:T(8,128)(2,1)S(1)} collective-permute-done((bf16[112,128]{1,0:T(8,128)(2,1)S(1)}, bf16[112,128]{1,0:T(8,128)(2,1)S(1)}, u32[]{:S(2)}, u32[]{:S(2)}) %collective-permute-start.19) | collective-permute-done | bytes 28704 | tf_op jit(solution)/shard_map/ppermute | solution.py:540
  64.9 0.1 shard_map.86
  65.0 1.6 %collective-permute-start.20 = (bf16[208,128]{1,0:T(8,128)(2,1)S(1)}, bf16[208,128]{1,0:T(8,128)(2,1)S(1)}, u32[]{:S(2)}, u32[]{:S(2)}) collective-permute-start(bf16[208,128]{1,0:T(8,128)(2,1)S(1)} %shard_map.86), channel_id=1, source_target_pairs={{0,1},{1,0},{2,3},{3,2},{4,5},{5,4},{6,7},{7,6},{8,9},{9,8},{10,11... | collective-permute-start | bytes 159752 | tf_op jit(solution)/shard_map/ppermute | solution.py:586
  66.6 2.6 %collective-permute-done.20.refs_6_ = bf16[208,128]{1,0:T(8,128)(2,1)S(1)} collective-permute-done((bf16[208,128]{1,0:T(8,128)(2,1)S(1)}, bf16[208,128]{1,0:T(8,128)(2,1)S(1)}, u32[]{:S(2)}, u32[]{:S(2)}) %collective-permute-start.20) | collective-permute-done | bytes 53280 | tf_op jit(solution)/shard_map/ppermute | solution.py:586
  69.2 1.0 %shard_map.87 = f32[13,13,7,128]{3,2,1,0:T(8,128)} custom-call(f32[1352,128]{1,0:T(8,128)S(1)} %get-tuple-element.99.refs_0_, f32[1352,128]{1,0:T(8,128)S(1)} %get-tuple-element.100.refs_1_, bf16[112,128]{1,0:T(8,128)(2,1)S(1)} %collective-permute-done.16.xr_one.refs_1_.refs_2_, bf16[112,128]{1,0:T(8,128)(2,1)S(1)} %collective-permute-done.17.xr_two.refs_2_.refs_3_, ...), custom_call_target="tpu_custom_call" | custom-call | bytes 2158080 | tf_op jit(solution)/shard_map/pallas_call | solution.py:57
  (9 shorter events, 0.2 us)
Async XLA Ops:
  0.0 11.0 %copy-start = (f32[343,2,2,1]{0,3,2,1:T(1,128)S(1)}, f32[343,2,2,1]{0,3,2,1:T(1,128)}, u32[]{:S(2)}) copy-start(f32[343,2,2,1]{0,3,2,1:T(1,128)} %param.9) | copy-start | bytes 16468
  0.0 1.1 %copy-start.1 = (f32[13,13,7,128]{3,2,1,0:T(8,128)S(1)}, f32[13,13,7,128]{3,2,1,0:T(8,128)}, u32[]{:S(2)}) copy-start(f32[13,13,7,128]{3,2,1,0:T(8,128)} %parts.1) | copy-start | bytes 1817092
  1.2 9.8 %collective-permute-start = (bf16[112,128]{1,0:T(8,128)(2,1)S(1)}, bf16[112,128]{1,0:T(8,128)(2,1)S(1)}, u32[]{:S(2)}, u32[]{:S(2)}) collective-permute-start(bf16[112,128]{1,0:T(8,128)(2,1)S(1)} %get-tuple-element.57), channel_id=1, source_target_pairs={{0,24},{2,26},{4,28},{6,30},{8,16},{10,18},{12,20},{14,22},{16,8},... | collective-permute-start | bytes 86024 | tf_op jit(solution)/shard_map/ppermute | solution.py:540
  3.7 7.4 %collective-permute-start.1 = (bf16[112,128]{1,0:T(8,128)(2,1)S(1)}, bf16[112,128]{1,0:T(8,128)(2,1)S(1)}, u32[]{:S(2)}, u32[]{:S(2)}) collective-permute-start(bf16[112,128]{1,0:T(8,128)(2,1)S(1)} %get-tuple-element.58), channel_id=1, source_target_pairs={{0,8},{2,10},{4,12},{6,14},{8,0},{10,2},{12,4},{14,6},{16,24},{18,... | collective-permute-start | bytes 86024 | tf_op jit(solution)/shard_map/ppermute | solution.py:540
  4.4 1.2 %copy-start.2 = (bf16[1,1,1,343,1536]{4,3,2,1,0:T(8,128)(2,1)S(1)}, bf16[1,1,1,343,1536]{4,3,2,1,0:T(8,128)(2,1)}, u32[]{:S(2)}) copy-start(bf16[1,1,1,343,1536]{4,3,2,1,0:T(8,128)(2,1)} %param.10) | copy-start | bytes 3161092
  5.6 0.7 copy-start.5
  6.3 8.0 %copy-start.3 = (bf16[343,343]{1,0:T(8,128)(2,1)S(1)}, bf16[343,343]{1,0:T(8,128)(2,1)}, u32[]{:S(2)}) copy-start(bf16[343,343]{1,0:T(8,128)(2,1)} %kin.1) | copy-start | bytes 705898
  6.3 8.0 %copy-start.4 = (f32[64,12,12]{0,2,1:T(8,128)S(1)}, f32[64,12,12]{0,2,1:T(8,128)}, u32[]{:S(2)}) copy-start(f32[64,12,12]{0,2,1:T(8,128)} %param.13) | copy-start | bytes 110596
  6.3 8.0 %copy-start.6 = (s32[1,1,2,32]{3,2,1,0:T(2,128)S(1)}, s32[1,1,2,32]{3,2,1,0:T(2,128)}, u32[]{:S(2)}) copy-start(s32[1,1,2,32]{3,2,1,0:T(2,128)} %param.11) | copy-start | bytes 772
  9.4 6.9 %collective-permute-start.4 = (bf16[384,256]{1,0:T(8,128)(2,1)S(1)}, bf16[384,256]{1,0:T(8,128)(2,1)S(1)}, u32[]{:S(2)}, u32[]{:S(2)}) collective-permute-start(bf16[384,256]{1,0:T(8,128)(2,1)S(1)} %get-tuple-element.65), channel_id=1, source_target_pairs={{1,0},{0,1},{3,2},{2,3},{5,4},{4,5},{7,6},{6,7},{9,8},{8,9},{11,10... | collective-permute-start | bytes 589832 | tf_op jit(solution)/shard_map/ppermute | solution.py:566
  11.1 5.1 %collective-permute-start.2 = (bf16[112,128]{1,0:T(8,128)(2,1)S(1)}, bf16[112,128]{1,0:T(8,128)(2,1)S(1)}, u32[]{:S(2)}, u32[]{:S(2)}) collective-permute-start(bf16[112,128]{1,0:T(8,128)(2,1)S(1)} %get-tuple-element.61), channel_id=1, source_target_pairs={{0,8},{2,4},{4,2},{6,14},{8,0},{10,12},{12,10},{14,6},{16,24},{18,... | collective-permute-start | bytes 86024 | tf_op jit(solution)/shard_map/ppermute | solution.py:540
  11.2 5.0 %collective-permute-start.3 = (bf16[112,128]{1,0:T(8,128)(2,1)S(1)}, bf16[112,128]{1,0:T(8,128)(2,1)S(1)}, u32[]{:S(2)}, u32[]{:S(2)}) collective-permute-start(bf16[112,128]{1,0:T(8,128)(2,1)S(1)} %get-tuple-element.62), channel_id=1, source_target_pairs={{0,2},{2,0},{4,6},{6,4},{8,10},{10,8},{12,14},{14,12},{16,18},{18,... | collective-permute-start | bytes 86024 | tf_op jit(solution)/shard_map/ppermute | solution.py:540
  17.6 5.3 %collective-permute-start.5 = (bf16[592,128]{1,0:T(8,128)(2,1)S(1)}, bf16[592,128]{1,0:T(8,128)(2,1)S(1)}, u32[]{:S(2)}, u32[]{:S(2)}) collective-permute-start(bf16[592,128]{1,0:T(8,128)(2,1)S(1)} %get-tuple-element.70), channel_id=1, source_target_pairs={{0,1},{1,0},{2,3},{3,2},{4,5},{5,4},{6,7},{7,6},{8,9},{9,8},{10,11... | collective-permute-start | bytes 454664 | tf_op jit(solution)/shard_map/ppermute | solution.py:581
  24.1 3.4 %collective-permute-start.6 = (bf16[112,128]{1,0:T(8,128)(2,1)S(1)}, bf16[112,128]{1,0:T(8,128)(2,1)S(1)}, u32[]{:S(2)}, u32[]{:S(2)}) collective-permute-start(bf16[112,128]{1,0:T(8,128)(2,1)S(1)} %get-tuple-element.77), channel_id=1, source_target_pairs={{0,24},{2,26},{4,28},{6,30},{8,16},{10,18},{12,20},{14,22},{16,8},... | collective-permute-start | bytes 86024 | tf_op jit(solution)/shard_map/ppermute | solution.py:540
  24.1 3.3 %collective-permute-start.7 = (bf16[112,128]{1,0:T(8,128)(2,1)S(1)}, bf16[112,128]{1,0:T(8,128)(2,1)S(1)}, u32[]{:S(2)}, u32[]{:S(2)}) collective-permute-start(bf16[112,128]{1,0:T(8,128)(2,1)S(1)} %get-tuple-element.78), channel_id=1, source_target_pairs={{0,8},{2,10},{4,12},{6,14},{8,0},{10,2},{12,4},{14,6},{16,24},{18,... | collective-permute-start | bytes 86024 | tf_op jit(solution)/shard_map/ppermute | solution.py:540
  27.5 3.2 %collective-permute-start.8 = (bf16[112,128]{1,0:T(8,128)(2,1)S(1)}, bf16[112,128]{1,0:T(8,128)(2,1)S(1)}, u32[]{:S(2)}, u32[]{:S(2)}) collective-permute-start(bf16[112,128]{1,0:T(8,128)(2,1)S(1)} %get-tuple-element.81), channel_id=1, source_target_pairs={{0,8},{2,4},{4,2},{6,14},{8,0},{10,12},{12,10},{14,6},{16,24},{18,... | collective-permute-start | bytes 86024 | tf_op jit(solution)/shard_map/ppermute | solution.py:540
  27.5 5.0 %collective-permute-start.9 = (bf16[112,128]{1,0:T(8,128)(2,1)S(1)}, bf16[112,128]{1,0:T(8,128)(2,1)S(1)}, u32[]{:S(2)}, u32[]{:S(2)}) collective-permute-start(bf16[112,128]{1,0:T(8,128)(2,1)S(1)} %get-tuple-element.82), channel_id=1, source_target_pairs={{0,2},{2,0},{4,6},{6,4},{8,10},{10,8},{12,14},{14,12},{16,18},{18,... | collective-permute-start | bytes 86024 | tf_op jit(solution)/shard_map/ppermute | solution.py:540
  33.9 5.3 %collective-permute-start.10 = (bf16[592,128]{1,0:T(8,128)(2,1)S(1)}, bf16[592,128]{1,0:T(8,128)(2,1)S(1)}, u32[]{:S(2)}, u32[]{:S(2)}) collective-permute-start(bf16[592,128]{1,0:T(8,128)(2,1)S(1)} %get-tuple-element.86), channel_id=1, source_target_pairs={{0,1},{1,0},{2,3},{3,2},{4,5},{5,4},{6,7},{7,6},{8,9},{9,8},{10,11... | collective-permute-start | bytes 454664 | tf_op jit(solution)/shard_map/ppermute | solution.py:581
  40.4 3.4 %collective-permute-start.11 = (bf16[112,128]{1,0:T(8,128)(2,1)S(1)}, bf16[112,128]{1,0:T(8,128)(2,1)S(1)}, u32[]{:S(2)}, u32[]{:S(2)}) collective-permute-start(bf16[112,128]{1,0:T(8,128)(2,1)S(1)} %get-tuple-element.89), channel_id=1, source_target_pairs={{0,24},{2,26},{4,28},{6,30},{8,16},{10,18},{12,20},{14,22},{16,8},... | collective-permute-start | bytes 86024 | tf_op jit(solution)/shard_map/ppermute | solution.py:540
  40.4 3.3 %collective-permute-start.12 = (bf16[112,128]{1,0:T(8,128)(2,1)S(1)}, bf16[112,128]{1,0:T(8,128)(2,1)S(1)}, u32[]{:S(2)}, u32[]{:S(2)}) collective-permute-start(bf16[112,128]{1,0:T(8,128)(2,1)S(1)} %get-tuple-element.90), channel_id=1, source_target_pairs={{0,8},{2,10},{4,12},{6,14},{8,0},{10,2},{12,4},{14,6},{16,24},{18,... | collective-permute-start | bytes 86024 | tf_op jit(solution)/shard_map/ppermute | solution.py:540
  43.7 2.9 %collective-permute-start.13 = (bf16[112,128]{1,0:T(8,128)(2,1)S(1)}, bf16[112,128]{1,0:T(8,128)(2,1)S(1)}, u32[]{:S(2)}, u32[]{:S(2)}) collective-permute-start(bf16[112,128]{1,0:T(8,128)(2,1)S(1)} %get-tuple-element.93), channel_id=1, source_target_pairs={{0,8},{2,4},{4,2},{6,14},{8,0},{10,12},{12,10},{14,6},{16,24},{18,... | collective-permute-start | bytes 86024 | tf_op jit(solution)/shard_map/ppermute | solution.py:540
  43.8 4.6 %collective-permute-start.14 = (bf16[112,128]{1,0:T(8,128)(2,1)S(1)}, bf16[112,128]{1,0:T(8,128)(2,1)S(1)}, u32[]{:S(2)}, u32[]{:S(2)}) collective-permute-start(bf16[112,128]{1,0:T(8,128)(2,1)S(1)} %get-tuple-element.94), channel_id=1, source_target_pairs={{0,2},{2,0},{4,6},{6,4},{8,10},{10,8},{12,14},{14,12},{16,18},{18,... | collective-permute-start | bytes 86024 | tf_op jit(solution)/shard_map/ppermute | solution.py:540
  49.9 5.3 %collective-permute-start.15 = (bf16[592,128]{1,0:T(8,128)(2,1)S(1)}, bf16[592,128]{1,0:T(8,128)(2,1)S(1)}, u32[]{:S(2)}, u32[]{:S(2)}) collective-permute-start(bf16[592,128]{1,0:T(8,128)(2,1)S(1)} %get-tuple-element.98), channel_id=1, source_target_pairs={{0,1},{1,0},{2,3},{3,2},{4,5},{5,4},{6,7},{7,6},{8,9},{9,8},{10,11... | collective-permute-start | bytes 454664 | tf_op jit(solution)/shard_map/ppermute | solution.py:581
  56.4 3.3 %collective-permute-start.16 = (bf16[112,128]{1,0:T(8,128)(2,1)S(1)}, bf16[112,128]{1,0:T(8,128)(2,1)S(1)}, u32[]{:S(2)}, u32[]{:S(2)}) collective-permute-start(bf16[112,128]{1,0:T(8,128)(2,1)S(1)} %get-tuple-element.101), channel_id=1, source_target_pairs={{0,24},{2,26},{4,28},{6,30},{8,16},{10,18},{12,20},{14,22},{16,8},... | collective-permute-start | bytes 86024 | tf_op jit(solution)/shard_map/ppermute | solution.py:540
  56.4 3.3 %collective-permute-start.17 = (bf16[112,128]{1,0:T(8,128)(2,1)S(1)}, bf16[112,128]{1,0:T(8,128)(2,1)S(1)}, u32[]{:S(2)}, u32[]{:S(2)}) collective-permute-start(bf16[112,128]{1,0:T(8,128)(2,1)S(1)} %get-tuple-element.102), channel_id=1, source_target_pairs={{0,8},{2,10},{4,12},{6,14},{8,0},{10,2},{12,4},{14,6},{16,24},{18,... | collective-permute-start | bytes 86024 | tf_op jit(solution)/shard_map/ppermute | solution.py:540
  59.7 3.3 %collective-permute-start.18 = (bf16[112,128]{1,0:T(8,128)(2,1)S(1)}, bf16[112,128]{1,0:T(8,128)(2,1)S(1)}, u32[]{:S(2)}, u32[]{:S(2)}) collective-permute-start(bf16[112,128]{1,0:T(8,128)(2,1)S(1)} %get-tuple-element.105), channel_id=1, source_target_pairs={{0,8},{2,4},{4,2},{6,14},{8,0},{10,12},{12,10},{14,6},{16,24},{18,... | collective-permute-start | bytes 86024 | tf_op jit(solution)/shard_map/ppermute | solution.py:540
  59.8 5.1 %collective-permute-start.19 = (bf16[112,128]{1,0:T(8,128)(2,1)S(1)}, bf16[112,128]{1,0:T(8,128)(2,1)S(1)}, u32[]{:S(2)}, u32[]{:S(2)}) collective-permute-start(bf16[112,128]{1,0:T(8,128)(2,1)S(1)} %get-tuple-element.106), channel_id=1, source_target_pairs={{0,2},{2,0},{4,6},{6,4},{8,10},{10,8},{12,14},{14,12},{16,18},{18,... | collective-permute-start | bytes 86024 | tf_op jit(solution)/shard_map/ppermute | solution.py:540
  65.0 4.2 %collective-permute-start.20 = (bf16[208,128]{1,0:T(8,128)(2,1)S(1)}, bf16[208,128]{1,0:T(8,128)(2,1)S(1)}, u32[]{:S(2)}, u32[]{:S(2)}) collective-permute-start(bf16[208,128]{1,0:T(8,128)(2,1)S(1)} %shard_map.86), channel_id=1, source_target_pairs={{0,1},{1,0},{2,3},{3,2},{4,5},{5,4},{6,7},{7,6},{8,9},{9,8},{10,11... | collective-permute-start | bytes 159752 | tf_op jit(solution)/shard_map/ppermute | solution.py:586

commit v5 on v4

--- a/solution.py
+++ b/solution.py
@@ -46,7 +46,7 @@
         self.fcell = EDGE * PAD
         self.fall = up(self.fcell * len(self.cells), 256)
         self.shifts, self.links = shifts, min(2, shifts)
-        self.spill = 2 * PAD * PAD
+        self.rows_all = self.rows + (self.face_b - ny + 1) * PAD
 
 
 VMEM = pl.BlockSpec(memory_space=pltpu.VMEM)
@@ -125,7 +125,7 @@
     i = iota(cols, POS, 0)
     first = iota(cols, POS, 1) * (BLK * PA)
     in_slot = ((i >= first) & (i < first + BLK * PA)).astype(BF16)
-    of_block = dot_last(in_slot, cells[...].astype(F32).astype(BF16))
+    of_block = dot_last(in_slot, cells[...].astype(BF16))
     i = iota(cols, BLK, 0)
     block = twelfth(i)
     cell = jnp.sum(
@@ -300,17 +300,20 @@
     return [shape(sz.xface, sz.orb, HALO)] * 2 + [shape(sz.yface, sz.orb, F32)] * 2
 
 
-def start_body(sz, parts, r4, *faces):
+def start_body(sz, parts, r, *faces):
     nz = parts.shape[2]
-    r4[...] = jnp.zeros(r4.shape, F32)
-    r4[:, :, :nz, :] = parts[...]
-    write_faces(sz, r4.reshape(sz.rows, sz.orb), *faces)
+    r[...] = jnp.zeros(r.shape, F32)
+    for a in range(sz.nx):
+        for b in range(sz.ny):
+            at = a * sz.line_x + b * PAD
+            r[at : at + nz, :] = parts[a, b]
+    write_faces(sz, r, *faces)
 
 
 def start_faces(sz, parts):
-    outs = [jax.ShapeDtypeStruct((sz.nx, sz.ny, PAD, sz.orb), F32)] + face_outs(sz)
-    r4, *faces = kernel_call(functools.partial(start_body, sz), outs, [parts])
-    return r4.reshape(sz.rows, sz.orb), faces
+    outs = [shape(sz.rows_all, sz.orb, F32)] + face_outs(sz)
+    r, *faces = kernel_call(functools.partial(start_body, sz), outs, [parts])
+    return r, faces
 
 
 def cross_body(sz, xr_one, xr_two, ry_lo, ry_hi, sy_one, sy_two):
@@ -334,8 +337,7 @@
     return kernel_call(functools.partial(cross_body, sz), outs, list(faces))
 
 
-def add_xy(sz, ra, r, xr_one, xr_two, yr_one, yr_two):
-    ra[0 : sz.rows, :] = r[...]
+def add_xy(sz, ra, xr_one, xr_two, yr_one, yr_two):
     last = (sz.nx - 1) * sz.line_x
     low, high = read_pair("gx", xr_one, xr_two)
     ra[0 : sz.line_x, :] += low[: sz.line_x]
@@ -346,11 +348,21 @@
             ra[at : at + PAD, :] += value[a * PAD : (a + 1) * PAD]
 
 
-def pack_z(sz, ra, j):
+def local_term(weight, fields, at):
+    value = weight * fields[0][at, :]
+    return value - fields[1][at, :] if len(fields) > 1 else value
+
+
+def layer_rows(y, weight, fields, at):
+    rows = pl.ds(at, PAD, stride=PAD)
+    return y[rows, :] - local_term(weight, fields, rows) if fields else y[rows, :]
+
+
+def pack_z(sz, y, weight, fields, j):
     rows, c = [], layer_sent(sz, j)
     for a in range(sz.nx):
         for b in range(0, sz.face_b, PAD):
-            rows.append(ra[pl.ds(a * sz.line_x + b * PAD + c, PAD, stride=PAD), :])
+            rows.append(layer_rows(y, weight, fields, a * sz.line_x + b * PAD + c))
     rest = sz.zface - sz.nx * sz.face_b
     if rest:
         rows.append(jnp.zeros((rest, sz.orb), F32))
@@ -367,73 +379,70 @@
             y[at, :] = y[at, :] + face[a * sz.face_b + b : a * sz.face_b + b + n]
 
 
-def face_cells(sz, ra, j):
+def face_cells(sz, y, weight, fields, j):
     rows, c = [], layer_sent(sz, j)
     for p, q in sz.cells:
         for a in range(EDGE):
             at = (ORDER * p + a) * sz.line_x + ORDER * q * PAD
-            rows.append(ra[pl.ds(at + c, PAD, stride=PAD), :])
+            rows.append(layer_rows(y, weight, fields, at + c))
         rows.append(jnp.zeros((PAD, sz.orb), F32))
     return jnp.concatenate(rows, axis=0).astype(BF16)
 
 
-def project_body(sz, has_local, refs):
+def project_body(sz, weight, past, refs):
     take = iter(refs)
     r = next(take)
-    loc = next(take) if has_local else None
+    fields = [next(take) for _ in range(past)]
     halos = [next(take) for _ in range(4)]
     q = next(take)
     qfaces = [next(take) for _ in range(sz.links)]
     maps, back = next(take), next(take)
     y, own = next(take), next(take)
     messages = [next(take) for _ in range(sz.shifts)]
-    ra = next(take)
-    ra[sz.rows :, :] = jnp.zeros((sz.spill, sz.orb), F32)
-    add_xy(sz, ra, r, *halos)
-    y[...] = ra[0 : sz.rows, :] + loc[...] if has_local else ra[0 : sz.rows, :]
+    everything = slice(0, sz.rows_all)
+    y[...] = r[...] + local_term(weight, fields, everything) if past else r[...]
+    add_xy(sz, y, *halos)
     blocks = [cell_block(sz, y, cell).astype(BF16) for cell in sz.cells]
     rest = sz.all_pad - sz.cell_pad * len(sz.cells)
     if rest:
         blocks.append(jnp.zeros((rest, sz.orb), BF16))
-    beside = [dot(f[...], face_cells(sz, ra, j)).astype(BF16) for j, f in enumerate(qfaces)]
+    beside = []
+    for j, matrix in enumerate(qfaces):
+        beside.append(dot(matrix[...], face_cells(sz, y, weight, fields, j)).astype(BF16))
     sums = dot(q[...], jnp.concatenate(blocks, axis=0))
     mapped = dot(maps[...], jnp.concatenate([sums.astype(BF16)] + beside, axis=0))
     for s, message in enumerate(messages):
         message[0:SLOTS, :] = mapped[s * SLOTS : (s + 1) * SLOTS].astype(HALO)
         for j, shift in enumerate(link_shifts(sz)):
             if shift == s + 1:
-                message[SLOTS : SLOTS + sz.zface, :] = pack_z(sz, ra, j)
+                message[SLOTS : SLOTS + sz.zface, :] = pack_z(sz, y, weight, fields, j)
     own[...] = sums + dot(back[...], jnp.concatenate(beside, axis=0))
 
 
-def project(sz, r, loc, halos, q, qfaces, maps, back):
-    outs = [shape(sz.rows, sz.orb, F32), shape(SLOTS, sz.orb, F32)]
+def project(sz, r, weight, fields, halos, q, qfaces, maps, back):
+    outs = [shape(sz.rows_all, sz.orb, F32), shape(SLOTS, sz.orb, F32)]
     for s in range(1, sz.shifts + 1):
         outs.append(shape(SLOTS + (sz.zface if s in link_shifts(sz) else 0), sz.orb, HALO))
-    arrays = [r] + ([loc] if loc is not None else []) + list(halos) + [q, *qfaces, maps, back]
 
     def body(*refs):
-        project_body(sz, loc is not None, refs)
+        project_body(sz, weight, len(fields), refs)
 
     y, own, *messages = kernel_call(
         body,
         outs,
-        arrays,
-        scratch=[pltpu.VMEM((sz.rows + sz.spill, sz.orb), F32)],
+        [r, *fields, *halos, q, *qfaces, maps, back],
         flops=4 * 10**8,
         limit=(32 << 20) if sz.shifts < 8 else (56 << 20),
     )
     return y, own, messages
 
 
-def apply_body(sz, has_previous, scale, refs):
+def apply_body(sz, scale, refs):
     take = iter(refs)
-    yin = next(take)
-    previous = next(take) if has_previous else None
-    own = next(take)
+    yin, own = next(take), next(take)
     messages = [next(take) for _ in range(sz.shifts)]
     c_hi, c_lo, qt, kin, pot = [next(take) for _ in range(5)]
-    r, loc, y = next(take), next(take), next(take)
+    r, y = next(take), next(take)
     faces = [next(take) for _ in range(4)]
     totals = own[...]
     for message in messages:
@@ -446,72 +455,74 @@
         add_z(sz, y, j, messages[shift - 1][SLOTS : SLOTS + sz.zface, :].astype(F32))
     blocks = [cell_block(sz, y, cell) for cell in sz.cells]
     stiff = dot(kin[...], jnp.concatenate([b.astype(BF16) for b in blocks], axis=1))
-    r[...] = jnp.zeros(r.shape, F32)
     for g, (p, q) in enumerate(sz.cells):
         rows = slice(g * sz.cell_pad, (g + 1) * sz.cell_pad)
         value = stiff[:, g * sz.orb : (g + 1) * sz.orb] + pot[rows, :] * blocks[g]
         value = (value + dot(qt[rows, :], coef)) * scale
         for a in range(EDGE):
             start = (ORDER * p + a) * sz.line_x + ORDER * q * PAD
-            r[start : start + EDGE * PAD, :] += value[a * EDGE * PAD : (a + 1) * EDGE * PAD]
-    local = (-center_value * scale) * y[...]
-    loc[...] = local - previous[...] if has_previous else local
+            line = value[a * EDGE * PAD : (a + 1) * EDGE * PAD]
+            shared = EDGE * PAD if p and a == 0 else PAD if q else 0
+            if shared:
+                r[start : start + shared, :] += line[:shared]
+            if shared < EDGE * PAD:
+                r[start + shared : start + EDGE * PAD, :] = line[shared:]
+    r[sz.rows :, :] = jnp.zeros((sz.rows_all - sz.rows, sz.orb), F32)
     write_faces(sz, r, *faces)
 
 
-def apply(sz, y, previous, own, messages, c_hi, c_lo, qt, kin, pot, scale):
-    outs = [shape(sz.rows, sz.orb, F32)] * 3 + face_outs(sz)
-    arrays = [y] + ([previous] if previous is not None else [])
-    arrays += [own, *messages, c_hi, c_lo, qt, kin, pot]
+def apply(sz, y, own, messages, c_hi, c_lo, qt, kin, pot, scale):
+    outs = [shape(sz.rows_all, sz.orb, F32)] * 2 + face_outs(sz)
+    arrays = [y, own, *messages, c_hi, c_lo, qt, kin, pot]
 
     def body(*refs):
-        apply_body(sz, previous is not None, scale, refs)
-
-    r, loc, y, *faces = kernel_call(body, outs, arrays, flops=6 * 10**8, limit=32 << 20)
-    return r, loc, y, faces
+        apply_body(sz, scale, refs)
+
+    r, y, *faces = kernel_call(body, outs, arrays, flops=6 * 10**8, limit=32 << 20)
+    return r, y, faces
 
 
 def last_faces_body(sz, refs):
     take = iter(refs)
     r = next(take)
     halos = [next(take) for _ in range(4)]
+    ra = next(take)
     outs = [next(take) for _ in range(sz.links)]
-    ra = next(take)
-    ra[sz.rows :, :] = jnp.zeros((sz.spill, sz.orb), F32)
-    add_xy(sz, ra, r, *halos)
+    ra[...] = r[...]
+    add_xy(sz, ra, *halos)
     for j, out in enumerate(outs):
-        out[...] = pack_z(sz, ra, j)
+        out[...] = pack_z(sz, ra, None, [], j)
 
 
 def last_faces(sz, r, halos):
     def body(*refs):
         last_faces_body(sz, refs)
 
-    outs = [shape(sz.zface, sz.orb, HALO)] * sz.links
-    scratch = [pltpu.VMEM((sz.rows + sz.spill, sz.orb), F32)]
-    return kernel_call(body, outs, [r, *halos], scratch=scratch)
-
-
-def finish_body(sz, refs):
+    outs = [shape(sz.rows_all, sz.orb, F32)] + [shape(sz.zface, sz.orb, HALO)] * sz.links
+    ra, *sent = kernel_call(body, outs, [r, *halos])
+    return ra, sent
+
+
+def finish_body(sz, weight, past, refs):
     take = iter(refs)
-    r, loc = next(take), next(take)
-    halos = [next(take) for _ in range(4)]
+    r = next(take)
+    fields = [next(take) for _ in range(past)]
     zr = [next(take) for _ in range(sz.links)]
     out, ra = next(take), next(take)
-    add_xy(sz, ra, r, *halos)
+    ra[...] = r[...] + local_term(weight, fields, slice(0, sz.rows_all))
     for j, face in enumerate(zr):
         add_z(sz, ra, j, face[...].astype(F32))
-    value = ra[0 : sz.rows, :] + loc[...]
+    value = ra[0 : sz.rows, :]
     out[...] = value.reshape(sz.nx, sz.ny, PAD, sz.orb)[:, :, : out.shape[2], :]
 
 
-def finish(sz, r, loc, halos, zr, nz):
+def finish(sz, r, weight, fields, zr, nz):
     def body(*refs):
-        finish_body(sz, refs)
+        finish_body(sz, weight, len(fields), refs)
 
     outs = [jax.ShapeDtypeStruct((sz.nx, sz.ny, nz, sz.orb), F32)]
-    scratch = [pltpu.VMEM((sz.rows + sz.spill, sz.orb), F32)]
-    return kernel_call(body, outs, [r, loc, *halos, *zr], scratch=scratch)[0]
+    scratch = [pltpu.VMEM((sz.rows_all, sz.orb), F32)]
+    return kernel_call(body, outs, [r, *fields, *zr], scratch=scratch)[0]
 
 
 def swap_faces(axis, one, two):
@@ -549,7 +560,8 @@
     ring = [[(i, (i + s) % devices) for i in range(devices)] for s in range(devices)]
 
     proj = projectors.reshape(nodes, POS * BLK * PA)
-    cells = jnp.transpose(slot_cells.reshape(POS, BLK))
+    proj = jnp.pad(proj, ((0, up(nodes, 16) - nodes), (0, 0)))
+    cells = jnp.transpose(slot_cells.reshape(POS, BLK)).astype(F32)
     r, faces = start_faces(sz, parts)
 
     def exchange_xy(sx_one, sx_two, sy_lo, sy_hi):
@@ -574,17 +586,18 @@
         jnp.transpose(coupling, (1, 2, 0)),
     )
 
-    loc = previous = None
-    scale = 1.0 / half_width
+    fields, scale = [], 1.0 / half_width
+    weight = 0.0
     for step in range(STEPS):
-        y, own, messages = project(sz, r, loc, halos, q, qfaces, maps, back)
+        y, own, messages = project(sz, r, weight, fields, halos, q, qfaces, maps, back)
         received = [lax.ppermute(m, "gz", ring[s + 1]) for s, m in enumerate(messages)]
-        r, loc, y, faces = apply(sz, y, previous, own, received, c_hi, c_lo, qt, kin, pot, scale)
-        previous, scale = y, 2.0 / half_width
+        r, y, faces = apply(sz, y, own, received, c_hi, c_lo, qt, kin, pot, scale)
+        fields, weight = [y] + fields[:1], -center_value * scale
+        scale = 2.0 / half_width
         halos = exchange_xy(*faces)
-    sent = last_faces(sz, r, halos)
+    r, sent = last_faces(sz, r, halos)
     zr = [lax.ppermute(f, "gz", ring[s]) for f, s in zip(sent, link_shifts(sz))]
-    return finish(sz, r, loc, halos, zr, nz)
+    return finish(sz, r, weight, fields, zr, nz)
 
 
 def solution(mesh):

time: 70.4 us -> 70.5 us (level)
    unnamed x14 -> x10, local copies, waits for them, and re-layouts: 3.04 us -> 1.14 us
    pad x0 -> x1, local copies, waits for them, and re-layouts: none -> 1.3 us  [local(): proj = jnp.pad(proj, ((0, up(nodes, 16) - nodes), (0, 0)))]
  transfers between devices with their start and end apart: 21 -> 21, of which waited for: 11 -> 11; matrix products, arithmetic and copies ran while one was open for 0% -> 3% of each run, Pallas kernels for 7% -> 7%
where the time goes in v5:
time: 70.5 us; the launch traced here: 70.3 us
  waiting for transfers between devices  26.7 us (38%)
  starting transfers between devices  26.3 us (37%)
  Pallas kernels  14 us (20%)
  local copies, waits for them, and re-layouts  2.48 us (4%)
    ppermute x16, starting transfers between devices, swap_faces(): out.append(lax.ppermute(face, axes, pairs))  18.7 us
    pallas_call x15, Pallas kernels, kernel_call(): pl.pallas_call(body, out_shape=outs, in_specs=[VMEM] * len(arrays), out_s...  14 us
    ppermute x16, waiting for transfers between devices, swap_faces(): out.append(lax.ppermute(face, axes, pairs))  12.6 us
    ppermute x3, waiting for transfers between devices, local(): lax.ppermute(m, 'gz', ring[s + 1])  11.3 us
    ppermute x3, starting transfers between devices, local(): lax.ppermute(m, 'gz', ring[s + 1])  4.41 us
    ppermute x1, waiting for transfers between devices, local(): zr = [lax.ppermute(f, 'gz', ring[s]) for f, s in zip(sent, link_shifts(sz))]  2.62 us
    ppermute x1, starting transfers between devices, local(): qfaces.append(lax.ppermute(face_rows[j], 'gz', back))  1.58 us
    ppermute x1, starting transfers between devices, local(): zr = [lax.ppermute(f, 'gz', ring[s]) for f, s in zip(sent, link_shifts(sz))]  1.58 us
  transfers between devices with their start and end apart: 21, of which 11 were waited for; matrix products, arithmetic and copies ran while one was open for 3% of the time, Pallas kernels for 7%

profile of v5, /device:TPU:0, one launch (start us, length us, event | category | flops | bytes accessed | tf_op | source)
XLA Modules:
  0.0 70.3 jit_solution(7278356490795600852)
XLA Ops:
  0.0 0.0 copy-start
  0.0 1.1 %copy-done.1 = f32[13,13,7,128]{3,2,1,0:T(8,128)S(1)} copy-done((f32[13,13,7,128]{3,2,1,0:T(8,128)S(1)}, f32[13,13,7,128]{3,2,1,0:T(8,128)}, u32[]{:S(2)}) %copy-start.1) | copy-done | bytes 605720
  1.1 0.1 shard_map.73
  1.2 2.4 %collective-permute-start = (bf16[112,128]{1,0:T(8,128)(2,1)S(1)}, bf16[112,128]{1,0:T(8,128)(2,1)S(1)}, u32[]{:S(2)}, u32[]{:S(2)}) collective-permute-start(bf16[112,128]{1,0:T(8,128)(2,1)S(1)} %get-tuple-element.57), channel_id=1, source_target_pairs={{0,24},{2,26},{4,28},{6,30},{8,16},{10,18},{12,20},{14,22},{16,8},... | collective-permute-start | bytes 86024 | tf_op jit(solution)/shard_map/ppermute | solution.py:551
  3.7 0.7 collective-permute-start.1
  4.4 0.7 convert_bitcast_fusion.cells
  5.0 1.3 %pad.4.proj = bf16[352,1536]{1,0:T(8,128)(2,1)S(1)} pad(bf16[343,1536]{1,0:T(8,128)(2,1)} %bitcast.11, bf16[]{:T(256)} %constant.2.clone.1), padding=0_9x0_0 | pad | bytes 2135042 | tf_op jit(solution)/shard_map/jit(_pad)/pad | solution.py:563
  6.3 0.0 copy-start.2
  6.4 0.0 copy-start.3
  6.4 0.0 copy-start.4
  6.4 3.1 %shard_map.75 = (bf16[1664,384]{1,0:T(8,128)(2,1)S(1)}, bf16[384,256]{1,0:T(8,128)(2,1)S(1)}) custom-call(bf16[352,1536]{1,0:T(8,128)(2,1)S(1)} %pad.4.proj, f32[4,32]{1,0:T(4,128)S(1)} %convert_bitcast_fusion.cells), custom_call_target="tpu_custom_call" | custom-call | flops 3000000000 | bytes 2556416 | tf_op jit(solution)/shard_map/pallas_call | solution.py:57
  9.5 1.6 %collective-permute-start.4 = (bf16[384,256]{1,0:T(8,128)(2,1)S(1)}, bf16[384,256]{1,0:T(8,128)(2,1)S(1)}, u32[]{:S(2)}, u32[]{:S(2)}) collective-permute-start(bf16[384,256]{1,0:T(8,128)(2,1)S(1)} %get-tuple-element.65), channel_id=1, source_target_pairs={{1,0},{0,1},{3,2},{2,3},{5,4},{4,5},{7,6},{6,7},{9,8},{8,9},{11,10... | collective-permute-start | bytes 589832 | tf_op jit(solution)/shard_map/ppermute | solution.py:578
  11.1 0.0 copy-done
  11.1 0.0 collective-permute-done.xr_one.refs_1_
  11.1 0.0 collective-permute-done.1.xr_two.refs_2_
  11.2 0.1 collective-permute-start.2
  11.2 3.1 %collective-permute-start.3 = (bf16[112,128]{1,0:T(8,128)(2,1)S(1)}, bf16[112,128]{1,0:T(8,128)(2,1)S(1)}, u32[]{:S(2)}, u32[]{:S(2)}) collective-permute-start(bf16[112,128]{1,0:T(8,128)(2,1)S(1)} %get-tuple-element.62), channel_id=1, source_target_pairs={{0,2},{2,0},{4,6},{6,4},{8,10},{10,8},{12,14},{14,12},{16,18},{18,... | collective-permute-start | bytes 86024 | tf_op jit(solution)/shard_map/ppermute | solution.py:551
  14.4 0.0 copy-done.2
  14.4 0.0 copy-done.3
  14.4 0.0 copy-done.4
  14.4 1.8 %shard_map.76 = (bf16[384,1664]{1,0:T(8,128)(2,1)S(1)}, bf16[400,400]{1,0:T(8,128)(2,1)S(1)}, f32[1600,128]{1,0:T(8,128)S(1)}, bf16[384,768]{1,0:T(8,128)(2,1)S(...) custom-call(bf16[1664,384]{1,0:T(8,128)(2,1)S(1)} %get-tuple-element.63.qt.refs_5_, ...), custom_call_target="tpu_custom_call" | custom-call | flops 1000000000 | bytes 5447570 | tf_op jit(solution)/shard_map/pallas_call | solution.py:57
  16.2 0.0 collective-permute-done.2.refs_3_
  16.2 0.0 collective-permute-done.3.refs_4_
  16.2 0.1 collective-permute-done.4.refs_6_.refs_7_.refs_8_
  16.3 1.4 %shard_map.77 = (f32[1384,128]{1,0:T(8,128)S(1)}, f32[384,128]{1,0:T(8,128)S(1)}, bf16[592,128]{1,0:T(8,128)(2,1)S(1)}) custom-call(f32[1384,128]{1,0:T(8,128)S(1)} %get-tuple-element.56.refs_0_, bf16[112,128]{1,0:T(8,128)(2,1)S(1)} %collective-permute-done.xr_one.refs_1_, bf16[112,128]{1,0:T(8,128)(2,1)S(1)} %collective-permute-done.1.xr_two.refs_2_, ...), custom_call_target="tpu_custom_call" | custom-call | flops 400000000 | bytes 4239360 | tf_op jit(solution)/shard_map/pallas_call | solution.py:57
  17.7 1.6 %collective-permute-start.5 = (bf16[592,128]{1,0:T(8,128)(2,1)S(1)}, bf16[592,128]{1,0:T(8,128)(2,1)S(1)}, u32[]{:S(2)}, u32[]{:S(2)}) collective-permute-start(bf16[592,128]{1,0:T(8,128)(2,1)S(1)} %get-tuple-element.70), channel_id=1, source_target_pairs={{0,1},{1,0},{2,3},{3,2},{4,5},{5,4},{6,7},{7,6},{8,9},{9,8},{10,11... | collective-permute-start | bytes 454664 | tf_op jit(solution)/shard_map/ppermute | solution.py:593
  19.3 3.7 %collective-permute-done.5.refs_2_ = bf16[592,128]{1,0:T(8,128)(2,1)S(1)} collective-permute-done((bf16[592,128]{1,0:T(8,128)(2,1)S(1)}, bf16[592,128]{1,0:T(8,128)(2,1)S(1)}, u32[]{:S(2)}, u32[]{:S(2)}) %collective-permute-start.5) | collective-permute-done | bytes 151584 | tf_op jit(solution)/shard_map/ppermute | solution.py:593
  23.0 1.1 %shard_map.78 = (f32[1384,128]{1,0:T(8,128)S(1)}, f32[1384,128]{1,0:T(8,128)S(1)}, bf16[112,128]{1,0:T(8,128)(2,1)S(1)}, bf16[112,128]{1,0:T(8,128)(2,1)S(1)}, f...) custom-call(f32[1384,128]{1,0:T(8,128)S(1)} %get-tuple-element.68.refs_0_, f32[384,128]{1,0:T(8,128)S(1)} %get-tuple-element.69.refs_1_, ...), custom_call_target="tpu_custom_call" | custom-call | flops 600000000 | bytes 5652992 | tf_op jit(solution)/shard_map/pallas_call | solution.py:57
  24.1 0.1 collective-permute-start.6
  24.2 0.9 %collective-permute-start.7 = (bf16[112,128]{1,0:T(8,128)(2,1)S(1)}, bf16[112,128]{1,0:T(8,128)(2,1)S(1)}, u32[]{:S(2)}, u32[]{:S(2)}) collective-permute-start(bf16[112,128]{1,0:T(8,128)(2,1)S(1)} %get-tuple-element.78), channel_id=1, source_target_pairs={{0,8},{2,10},{4,12},{6,14},{8,0},{10,2},{12,4},{14,6},{16,24},{18,... | collective-permute-start | bytes 86024 | tf_op jit(solution)/shard_map/ppermute | solution.py:551
  25.1 2.4 %collective-permute-done.6.xr_one.refs_2_ = bf16[112,128]{1,0:T(8,128)(2,1)S(1)} collective-permute-done((bf16[112,128]{1,0:T(8,128)(2,1)S(1)}, bf16[112,128]{1,0:T(8,128)(2,1)S(1)}, u32[]{:S(2)}, u32[]{:S(2)}) %collective-permute-start.6) | collective-permute-done | bytes 28704 | tf_op jit(solution)/shard_map/ppermute | solution.py:551
  27.5 0.0 collective-permute-done.7.xr_two.refs_3_
  27.5 0.1 collective-permute-start.8
  27.6 3.1 %collective-permute-start.9 = (bf16[112,128]{1,0:T(8,128)(2,1)S(1)}, bf16[112,128]{1,0:T(8,128)(2,1)S(1)}, u32[]{:S(2)}, u32[]{:S(2)}) collective-permute-start(bf16[112,128]{1,0:T(8,128)(2,1)S(1)} %get-tuple-element.82), channel_id=1, source_target_pairs={{0,2},{2,0},{4,6},{6,4},{8,10},{10,8},{12,14},{14,12},{16,18},{18,... | collective-permute-start | bytes 86024 | tf_op jit(solution)/shard_map/ppermute | solution.py:551
  30.7 0.0 collective-permute-done.8.refs_4_
  30.7 1.8 %collective-permute-done.9.refs_5_ = bf16[112,128]{1,0:T(8,128)(2,1)S(1)} collective-permute-done((bf16[112,128]{1,0:T(8,128)(2,1)S(1)}, bf16[112,128]{1,0:T(8,128)(2,1)S(1)}, u32[]{:S(2)}, u32[]{:S(2)}) %collective-permute-start.9) | collective-permute-done | bytes 28704 | tf_op jit(solution)/shard_map/ppermute | solution.py:551
  32.6 1.4 %shard_map.80 = (f32[1384,128]{1,0:T(8,128)S(1)}, f32[384,128]{1,0:T(8,128)S(1)}, bf16[592,128]{1,0:T(8,128)(2,1)S(1)}) custom-call(f32[1384,128]{1,0:T(8,128)S(1)} %get-tuple-element.75.refs_0_, f32[1384,128]{1,0:T(8,128)S(1)} %get-tuple-element.76.refs_1_.refs_2_, bf16[112,128]{1,0:T(8,128)(2,1)S(1)} %collective-permute-done.6.xr_one.refs_2_, ...), custom_call_target="tpu_custom_call" | custom-call | flops 400000000 | bytes 4947968 | tf_op jit(solution)/shard_map/pallas_call | solution.py:57
  34.0 1.6 %collective-permute-start.10 = (bf16[592,128]{1,0:T(8,128)(2,1)S(1)}, bf16[592,128]{1,0:T(8,128)(2,1)S(1)}, u32[]{:S(2)}, u32[]{:S(2)}) collective-permute-start(bf16[592,128]{1,0:T(8,128)(2,1)S(1)} %get-tuple-element.85), channel_id=1, source_target_pairs={{0,1},{1,0},{2,3},{3,2},{4,5},{5,4},{6,7},{7,6},{8,9},{9,8},{10,11... | collective-permute-start | bytes 454664 | tf_op jit(solution)/shard_map/ppermute | solution.py:593
  35.6 3.7 %collective-permute-done.10.refs_2_ = bf16[592,128]{1,0:T(8,128)(2,1)S(1)} collective-permute-done((bf16[592,128]{1,0:T(8,128)(2,1)S(1)}, bf16[592,128]{1,0:T(8,128)(2,1)S(1)}, u32[]{:S(2)}, u32[]{:S(2)}) %collective-permute-start.10) | collective-permute-done | bytes 151584 | tf_op jit(solution)/shard_map/ppermute | solution.py:593
  39.2 1.1 %shard_map.81 = (f32[1384,128]{1,0:T(8,128)S(1)}, f32[1384,128]{1,0:T(8,128)S(1)}, bf16[112,128]{1,0:T(8,128)(2,1)S(1)}, bf16[112,128]{1,0:T(8,128)(2,1)S(1)}, f...) custom-call(f32[1384,128]{1,0:T(8,128)S(1)} %get-tuple-element.83.refs_0_, f32[384,128]{1,0:T(8,128)S(1)} %get-tuple-element.84.refs_1_, ...), custom_call_target="tpu_custom_call" | custom-call | flops 600000000 | bytes 5652992 | tf_op jit(solution)/shard_map/pallas_call | solution.py:57
  40.4 0.1 collective-permute-start.11
  40.4 0.9 %collective-permute-start.12 = (bf16[112,128]{1,0:T(8,128)(2,1)S(1)}, bf16[112,128]{1,0:T(8,128)(2,1)S(1)}, u32[]{:S(2)}, u32[]{:S(2)}) collective-permute-start(bf16[112,128]{1,0:T(8,128)(2,1)S(1)} %get-tuple-element.89), channel_id=1, source_target_pairs={{0,8},{2,10},{4,12},{6,14},{8,0},{10,2},{12,4},{14,6},{16,24},{18,... | collective-permute-start | bytes 86024 | tf_op jit(solution)/shard_map/ppermute | solution.py:551
  41.3 2.4 %collective-permute-done.11.xr_one.refs_3_ = bf16[112,128]{1,0:T(8,128)(2,1)S(1)} collective-permute-done((bf16[112,128]{1,0:T(8,128)(2,1)S(1)}, bf16[112,128]{1,0:T(8,128)(2,1)S(1)}, u32[]{:S(2)}, u32[]{:S(2)}) %collective-permute-start.11) | collective-permute-done | bytes 28704 | tf_op jit(solution)/shard_map/ppermute | solution.py:551
  43.7 0.0 collective-permute-done.12.xr_two.refs_4_
  43.8 0.1 collective-permute-start.13
  43.8 2.8 %collective-permute-start.14 = (bf16[112,128]{1,0:T(8,128)(2,1)S(1)}, bf16[112,128]{1,0:T(8,128)(2,1)S(1)}, u32[]{:S(2)}, u32[]{:S(2)}) collective-permute-start(bf16[112,128]{1,0:T(8,128)(2,1)S(1)} %get-tuple-element.93), channel_id=1, source_target_pairs={{0,2},{2,0},{4,6},{6,4},{8,10},{10,8},{12,14},{14,12},{16,18},{18,... | collective-permute-start | bytes 86024 | tf_op jit(solution)/shard_map/ppermute | solution.py:551
  46.6 0.0 collective-permute-done.13.refs_5_
  46.6 1.8 %collective-permute-done.14.refs_6_ = bf16[112,128]{1,0:T(8,128)(2,1)S(1)} collective-permute-done((bf16[112,128]{1,0:T(8,128)(2,1)S(1)}, bf16[112,128]{1,0:T(8,128)(2,1)S(1)}, u32[]{:S(2)}, u32[]{:S(2)}) %collective-permute-start.14) | collective-permute-done | bytes 28704 | tf_op jit(solution)/shard_map/ppermute | solution.py:551
  48.5 1.4 %shard_map.83 = (f32[1384,128]{1,0:T(8,128)S(1)}, f32[384,128]{1,0:T(8,128)S(1)}, bf16[592,128]{1,0:T(8,128)(2,1)S(1)}) custom-call(f32[1384,128]{1,0:T(8,128)S(1)} %get-tuple-element.86.refs_0_, f32[1384,128]{1,0:T(8,128)S(1)} %get-tuple-element.87.refs_1_.refs_2_, f32[1384,128]{1,0:T(8,128)S(1)} %get-tuple-element.76.refs_1_.refs_2_, ...), custom_call_target="tpu_custom_call" | custom-call | flops 400000000 | bytes 5656576 | tf_op jit(solution)/shard_map/pallas_call | solution.py:57
  49.9 1.2 %collective-permute-start.15 = (bf16[592,128]{1,0:T(8,128)(2,1)S(1)}, bf16[592,128]{1,0:T(8,128)(2,1)S(1)}, u32[]{:S(2)}, u32[]{:S(2)}) collective-permute-start(bf16[592,128]{1,0:T(8,128)(2,1)S(1)} %get-tuple-element.96), channel_id=1, source_target_pairs={{0,1},{1,0},{2,3},{3,2},{4,5},{5,4},{6,7},{7,6},{8,9},{9,8},{10,11... | collective-permute-start | bytes 454664 | tf_op jit(solution)/shard_map/ppermute | solution.py:593
  51.2 4.0 %collective-permute-done.15.refs_2_ = bf16[592,128]{1,0:T(8,128)(2,1)S(1)} collective-permute-done((bf16[592,128]{1,0:T(8,128)(2,1)S(1)}, bf16[592,128]{1,0:T(8,128)(2,1)S(1)}, u32[]{:S(2)}, u32[]{:S(2)}) %collective-permute-start.15) | collective-permute-done | bytes 151584 | tf_op jit(solution)/shard_map/ppermute | solution.py:593
  55.2 1.2 %shard_map.84 = (f32[1384,128]{1,0:T(8,128)S(1)}, f32[1384,128]{1,0:T(8,128)S(1)}, bf16[112,128]{1,0:T(8,128)(2,1)S(1)}, bf16[112,128]{1,0:T(8,128)(2,1)S(1)}, f...) custom-call(f32[1384,128]{1,0:T(8,128)S(1)} %get-tuple-element.94.refs_0_, f32[384,128]{1,0:T(8,128)S(1)} %get-tuple-element.95.refs_1_, ...), custom_call_target="tpu_custom_call" | custom-call | flops 600000000 | bytes 5652992 | tf_op jit(solution)/shard_map/pallas_call | solution.py:57
  56.3 0.1 collective-permute-start.16
  56.4 1.0 %collective-permute-start.17 = (bf16[112,128]{1,0:T(8,128)(2,1)S(1)}, bf16[112,128]{1,0:T(8,128)(2,1)S(1)}, u32[]{:S(2)}, u32[]{:S(2)}) collective-permute-start(bf16[112,128]{1,0:T(8,128)(2,1)S(1)} %get-tuple-element.99), channel_id=1, source_target_pairs={{0,8},{2,10},{4,12},{6,14},{8,0},{10,2},{12,4},{14,6},{16,24},{18,... | collective-permute-start | bytes 86024 | tf_op jit(solution)/shard_map/ppermute | solution.py:551
  57.4 2.3 %collective-permute-done.16.xr_one.refs_1_ = bf16[112,128]{1,0:T(8,128)(2,1)S(1)} collective-permute-done((bf16[112,128]{1,0:T(8,128)(2,1)S(1)}, bf16[112,128]{1,0:T(8,128)(2,1)S(1)}, u32[]{:S(2)}, u32[]{:S(2)}) %collective-permute-start.16) | collective-permute-done | bytes 28704 | tf_op jit(solution)/shard_map/ppermute | solution.py:551
  59.7 0.0 collective-permute-done.17.xr_two.refs_2_
  59.7 0.1 collective-permute-start.18
  59.8 3.2 %collective-permute-start.19 = (bf16[112,128]{1,0:T(8,128)(2,1)S(1)}, bf16[112,128]{1,0:T(8,128)(2,1)S(1)}, u32[]{:S(2)}, u32[]{:S(2)}) collective-permute-start(bf16[112,128]{1,0:T(8,128)(2,1)S(1)} %get-tuple-element.103), channel_id=1, source_target_pairs={{0,2},{2,0},{4,6},{6,4},{8,10},{10,8},{12,14},{14,12},{16,18},{18,... | collective-permute-start | bytes 86024 | tf_op jit(solution)/shard_map/ppermute | solution.py:551
  63.0 0.0 collective-permute-done.18.refs_3_
  63.1 1.8 %collective-permute-done.19.refs_4_ = bf16[112,128]{1,0:T(8,128)(2,1)S(1)} collective-permute-done((bf16[112,128]{1,0:T(8,128)(2,1)S(1)}, bf16[112,128]{1,0:T(8,128)(2,1)S(1)}, u32[]{:S(2)}, u32[]{:S(2)}) %collective-permute-start.19) | collective-permute-done | bytes 28704 | tf_op jit(solution)/shard_map/ppermute | solution.py:551
  64.9 0.1 shard_map.86
  65.0 1.6 %collective-permute-start.20 = (bf16[208,128]{1,0:T(8,128)(2,1)S(1)}, bf16[208,128]{1,0:T(8,128)(2,1)S(1)}, u32[]{:S(2)}, u32[]{:S(2)}) collective-permute-start(bf16[208,128]{1,0:T(8,128)(2,1)S(1)} %get-tuple-element.106), channel_id=1, source_target_pairs={{0,1},{1,0},{2,3},{3,2},{4,5},{5,4},{6,7},{7,6},{8,9},{9,8},{10,11... | collective-permute-start | bytes 159752 | tf_op jit(solution)/shard_map/ppermute | solution.py:599
  66.6 2.6 %collective-permute-done.20.refs_3_ = bf16[208,128]{1,0:T(8,128)(2,1)S(1)} collective-permute-done((bf16[208,128]{1,0:T(8,128)(2,1)S(1)}, bf16[208,128]{1,0:T(8,128)(2,1)S(1)}, u32[]{:S(2)}, u32[]{:S(2)}) %collective-permute-start.20) | collective-permute-done | bytes 53280 | tf_op jit(solution)/shard_map/ppermute | solution.py:599
  69.2 1.1 %shard_map.87 = f32[13,13,7,128]{3,2,1,0:T(8,128)} custom-call(f32[1384,128]{1,0:T(8,128)S(1)} %get-tuple-element.104.refs_0_, f32[1384,128]{1,0:T(8,128)S(1)} %get-tuple-element.105.refs_1_, f32[1384,128]{1,0:T(8,128)S(1)} %get-tuple-element.87.refs_1_.refs_2_, bf16[208,128]{1,0:T(8,128)(2,1)S(1)} %collective-permute-done.20.refs_3_), custom_call_target="tpu_custom_call" | custom-call | bytes 2784768 | tf_op jit(solution)/shard_map/pallas_call | solution.py:57
  (7 shorter events, 0.1 us)
Async XLA Ops:
  0.0 11.1 %copy-start = (f32[343,2,2,1]{0,3,2,1:T(1,128)S(1)}, f32[343,2,2,1]{0,3,2,1:T(1,128)}, u32[]{:S(2)}) copy-start(f32[343,2,2,1]{0,3,2,1:T(1,128)} %param.9) | copy-start | bytes 16468
  0.0 1.1 %copy-start.1 = (f32[13,13,7,128]{3,2,1,0:T(8,128)S(1)}, f32[13,13,7,128]{3,2,1,0:T(8,128)}, u32[]{:S(2)}) copy-start(f32[13,13,7,128]{3,2,1,0:T(8,128)} %parts.1) | copy-start | bytes 1817092
  1.2 9.9 %collective-permute-start = (bf16[112,128]{1,0:T(8,128)(2,1)S(1)}, bf16[112,128]{1,0:T(8,128)(2,1)S(1)}, u32[]{:S(2)}, u32[]{:S(2)}) collective-permute-start(bf16[112,128]{1,0:T(8,128)(2,1)S(1)} %get-tuple-element.57), channel_id=1, source_target_pairs={{0,24},{2,26},{4,28},{6,30},{8,16},{10,18},{12,20},{14,22},{16,8},... | collective-permute-start | bytes 86024 | tf_op jit(solution)/shard_map/ppermute | solution.py:551
  3.7 7.4 %collective-permute-start.1 = (bf16[112,128]{1,0:T(8,128)(2,1)S(1)}, bf16[112,128]{1,0:T(8,128)(2,1)S(1)}, u32[]{:S(2)}, u32[]{:S(2)}) collective-permute-start(bf16[112,128]{1,0:T(8,128)(2,1)S(1)} %get-tuple-element.58), channel_id=1, source_target_pairs={{0,8},{2,10},{4,12},{6,14},{8,0},{10,2},{12,4},{14,6},{16,24},{18,... | collective-permute-start | bytes 86024 | tf_op jit(solution)/shard_map/ppermute | solution.py:551
  6.3 8.0 %copy-start.2 = (bf16[343,343]{1,0:T(8,128)(2,1)S(1)}, bf16[343,343]{1,0:T(8,128)(2,1)}, u32[]{:S(2)}) copy-start(bf16[343,343]{1,0:T(8,128)(2,1)} %kin.1) | copy-start | bytes 705898
  6.4 8.0 %copy-start.3 = (f32[64,12,12]{0,2,1:T(8,128)S(1)}, f32[64,12,12]{0,2,1:T(8,128)}, u32[]{:S(2)}) copy-start(f32[64,12,12]{0,2,1:T(8,128)} %param.13) | copy-start | bytes 110596
  6.4 8.0 %copy-start.4 = (s32[1,1,2,32]{3,2,1,0:T(2,128)S(1)}, s32[1,1,2,32]{3,2,1,0:T(2,128)}, u32[]{:S(2)}) copy-start(s32[1,1,2,32]{3,2,1,0:T(2,128)} %param.11) | copy-start | bytes 772
  9.5 6.9 %collective-permute-start.4 = (bf16[384,256]{1,0:T(8,128)(2,1)S(1)}, bf16[384,256]{1,0:T(8,128)(2,1)S(1)}, u32[]{:S(2)}, u32[]{:S(2)}) collective-permute-start(bf16[384,256]{1,0:T(8,128)(2,1)S(1)} %get-tuple-element.65), channel_id=1, source_target_pairs={{1,0},{0,1},{3,2},{2,3},{5,4},{4,5},{7,6},{6,7},{9,8},{8,9},{11,10... | collective-permute-start | bytes 589832 | tf_op jit(solution)/shard_map/ppermute | solution.py:578
  11.2 5.1 %collective-permute-start.2 = (bf16[112,128]{1,0:T(8,128)(2,1)S(1)}, bf16[112,128]{1,0:T(8,128)(2,1)S(1)}, u32[]{:S(2)}, u32[]{:S(2)}) collective-permute-start(bf16[112,128]{1,0:T(8,128)(2,1)S(1)} %get-tuple-element.61), channel_id=1, source_target_pairs={{0,8},{2,4},{4,2},{6,14},{8,0},{10,12},{12,10},{14,6},{16,24},{18,... | collective-permute-start | bytes 86024 | tf_op jit(solution)/shard_map/ppermute | solution.py:551
  11.2 5.0 %collective-permute-start.3 = (bf16[112,128]{1,0:T(8,128)(2,1)S(1)}, bf16[112,128]{1,0:T(8,128)(2,1)S(1)}, u32[]{:S(2)}, u32[]{:S(2)}) collective-permute-start(bf16[112,128]{1,0:T(8,128)(2,1)S(1)} %get-tuple-element.62), channel_id=1, source_target_pairs={{0,2},{2,0},{4,6},{6,4},{8,10},{10,8},{12,14},{14,12},{16,18},{18,... | collective-permute-start | bytes 86024 | tf_op jit(solution)/shard_map/ppermute | solution.py:551
  17.7 5.3 %collective-permute-start.5 = (bf16[592,128]{1,0:T(8,128)(2,1)S(1)}, bf16[592,128]{1,0:T(8,128)(2,1)S(1)}, u32[]{:S(2)}, u32[]{:S(2)}) collective-permute-start(bf16[592,128]{1,0:T(8,128)(2,1)S(1)} %get-tuple-element.70), channel_id=1, source_target_pairs={{0,1},{1,0},{2,3},{3,2},{4,5},{5,4},{6,7},{7,6},{8,9},{9,8},{10,11... | collective-permute-start | bytes 454664 | tf_op jit(solution)/shard_map/ppermute | solution.py:593
  24.1 3.4 %collective-permute-start.6 = (bf16[112,128]{1,0:T(8,128)(2,1)S(1)}, bf16[112,128]{1,0:T(8,128)(2,1)S(1)}, u32[]{:S(2)}, u32[]{:S(2)}) collective-permute-start(bf16[112,128]{1,0:T(8,128)(2,1)S(1)} %get-tuple-element.77), channel_id=1, source_target_pairs={{0,24},{2,26},{4,28},{6,30},{8,16},{10,18},{12,20},{14,22},{16,8},... | collective-permute-start | bytes 86024 | tf_op jit(solution)/shard_map/ppermute | solution.py:551
  24.2 3.3 %collective-permute-start.7 = (bf16[112,128]{1,0:T(8,128)(2,1)S(1)}, bf16[112,128]{1,0:T(8,128)(2,1)S(1)}, u32[]{:S(2)}, u32[]{:S(2)}) collective-permute-start(bf16[112,128]{1,0:T(8,128)(2,1)S(1)} %get-tuple-element.78), channel_id=1, source_target_pairs={{0,8},{2,10},{4,12},{6,14},{8,0},{10,2},{12,4},{14,6},{16,24},{18,... | collective-permute-start | bytes 86024 | tf_op jit(solution)/shard_map/ppermute | solution.py:551
  27.5 3.2 %collective-permute-start.8 = (bf16[112,128]{1,0:T(8,128)(2,1)S(1)}, bf16[112,128]{1,0:T(8,128)(2,1)S(1)}, u32[]{:S(2)}, u32[]{:S(2)}) collective-permute-start(bf16[112,128]{1,0:T(8,128)(2,1)S(1)} %get-tuple-element.81), channel_id=1, source_target_pairs={{0,8},{2,4},{4,2},{6,14},{8,0},{10,12},{12,10},{14,6},{16,24},{18,... | collective-permute-start | bytes 86024 | tf_op jit(solution)/shard_map/ppermute | solution.py:551
  27.6 5.0 %collective-permute-start.9 = (bf16[112,128]{1,0:T(8,128)(2,1)S(1)}, bf16[112,128]{1,0:T(8,128)(2,1)S(1)}, u32[]{:S(2)}, u32[]{:S(2)}) collective-permute-start(bf16[112,128]{1,0:T(8,128)(2,1)S(1)} %get-tuple-element.82), channel_id=1, source_target_pairs={{0,2},{2,0},{4,6},{6,4},{8,10},{10,8},{12,14},{14,12},{16,18},{18,... | collective-permute-start | bytes 86024 | tf_op jit(solution)/shard_map/ppermute | solution.py:551
  34.0 5.3 %collective-permute-start.10 = (bf16[592,128]{1,0:T(8,128)(2,1)S(1)}, bf16[592,128]{1,0:T(8,128)(2,1)S(1)}, u32[]{:S(2)}, u32[]{:S(2)}) collective-permute-start(bf16[592,128]{1,0:T(8,128)(2,1)S(1)} %get-tuple-element.85), channel_id=1, source_target_pairs={{0,1},{1,0},{2,3},{3,2},{4,5},{5,4},{6,7},{7,6},{8,9},{9,8},{10,11... | collective-permute-start | bytes 454664 | tf_op jit(solution)/shard_map/ppermute | solution.py:593
  40.4 3.4 %collective-permute-start.11 = (bf16[112,128]{1,0:T(8,128)(2,1)S(1)}, bf16[112,128]{1,0:T(8,128)(2,1)S(1)}, u32[]{:S(2)}, u32[]{:S(2)}) collective-permute-start(bf16[112,128]{1,0:T(8,128)(2,1)S(1)} %get-tuple-element.88), channel_id=1, source_target_pairs={{0,24},{2,26},{4,28},{6,30},{8,16},{10,18},{12,20},{14,22},{16,8},... | collective-permute-start | bytes 86024 | tf_op jit(solution)/shard_map/ppermute | solution.py:551
  40.4 3.3 %collective-permute-start.12 = (bf16[112,128]{1,0:T(8,128)(2,1)S(1)}, bf16[112,128]{1,0:T(8,128)(2,1)S(1)}, u32[]{:S(2)}, u32[]{:S(2)}) collective-permute-start(bf16[112,128]{1,0:T(8,128)(2,1)S(1)} %get-tuple-element.89), channel_id=1, source_target_pairs={{0,8},{2,10},{4,12},{6,14},{8,0},{10,2},{12,4},{14,6},{16,24},{18,... | collective-permute-start | bytes 86024 | tf_op jit(solution)/shard_map/ppermute | solution.py:551
  43.8 2.9 %collective-permute-start.13 = (bf16[112,128]{1,0:T(8,128)(2,1)S(1)}, bf16[112,128]{1,0:T(8,128)(2,1)S(1)}, u32[]{:S(2)}, u32[]{:S(2)}) collective-permute-start(bf16[112,128]{1,0:T(8,128)(2,1)S(1)} %get-tuple-element.92), channel_id=1, source_target_pairs={{0,8},{2,4},{4,2},{6,14},{8,0},{10,12},{12,10},{14,6},{16,24},{18,... | collective-permute-start | bytes 86024 | tf_op jit(solution)/shard_map/ppermute | solution.py:551
  43.8 4.6 %collective-permute-start.14 = (bf16[112,128]{1,0:T(8,128)(2,1)S(1)}, bf16[112,128]{1,0:T(8,128)(2,1)S(1)}, u32[]{:S(2)}, u32[]{:S(2)}) collective-permute-start(bf16[112,128]{1,0:T(8,128)(2,1)S(1)} %get-tuple-element.93), channel_id=1, source_target_pairs={{0,2},{2,0},{4,6},{6,4},{8,10},{10,8},{12,14},{14,12},{16,18},{18,... | collective-permute-start | bytes 86024 | tf_op jit(solution)/shard_map/ppermute | solution.py:551
  49.9 5.3 %collective-permute-start.15 = (bf16[592,128]{1,0:T(8,128)(2,1)S(1)}, bf16[592,128]{1,0:T(8,128)(2,1)S(1)}, u32[]{:S(2)}, u32[]{:S(2)}) collective-permute-start(bf16[592,128]{1,0:T(8,128)(2,1)S(1)} %get-tuple-element.96), channel_id=1, source_target_pairs={{0,1},{1,0},{2,3},{3,2},{4,5},{5,4},{6,7},{7,6},{8,9},{9,8},{10,11... | collective-permute-start | bytes 454664 | tf_op jit(solution)/shard_map/ppermute | solution.py:593
  56.3 3.4 %collective-permute-start.16 = (bf16[112,128]{1,0:T(8,128)(2,1)S(1)}, bf16[112,128]{1,0:T(8,128)(2,1)S(1)}, u32[]{:S(2)}, u32[]{:S(2)}) collective-permute-start(bf16[112,128]{1,0:T(8,128)(2,1)S(1)} %get-tuple-element.98), channel_id=1, source_target_pairs={{0,24},{2,26},{4,28},{6,30},{8,16},{10,18},{12,20},{14,22},{16,8},... | collective-permute-start | bytes 86024 | tf_op jit(solution)/shard_map/ppermute | solution.py:551
  56.4 3.3 %collective-permute-start.17 = (bf16[112,128]{1,0:T(8,128)(2,1)S(1)}, bf16[112,128]{1,0:T(8,128)(2,1)S(1)}, u32[]{:S(2)}, u32[]{:S(2)}) collective-permute-start(bf16[112,128]{1,0:T(8,128)(2,1)S(1)} %get-tuple-element.99), channel_id=1, source_target_pairs={{0,8},{2,10},{4,12},{6,14},{8,0},{10,2},{12,4},{14,6},{16,24},{18,... | collective-permute-start | bytes 86024 | tf_op jit(solution)/shard_map/ppermute | solution.py:551
  59.7 3.3 %collective-permute-start.18 = (bf16[112,128]{1,0:T(8,128)(2,1)S(1)}, bf16[112,128]{1,0:T(8,128)(2,1)S(1)}, u32[]{:S(2)}, u32[]{:S(2)}) collective-permute-start(bf16[112,128]{1,0:T(8,128)(2,1)S(1)} %get-tuple-element.102), channel_id=1, source_target_pairs={{0,8},{2,4},{4,2},{6,14},{8,0},{10,12},{12,10},{14,6},{16,24},{18,... | collective-permute-start | bytes 86024 | tf_op jit(solution)/shard_map/ppermute | solution.py:551
  59.8 5.1 %collective-permute-start.19 = (bf16[112,128]{1,0:T(8,128)(2,1)S(1)}, bf16[112,128]{1,0:T(8,128)(2,1)S(1)}, u32[]{:S(2)}, u32[]{:S(2)}) collective-permute-start(bf16[112,128]{1,0:T(8,128)(2,1)S(1)} %get-tuple-element.103), channel_id=1, source_target_pairs={{0,2},{2,0},{4,6},{6,4},{8,10},{10,8},{12,14},{14,12},{16,18},{18,... | collective-permute-start | bytes 86024 | tf_op jit(solution)/shard_map/ppermute | solution.py:551
  65.0 4.2 %collective-permute-start.20 = (bf16[208,128]{1,0:T(8,128)(2,1)S(1)}, bf16[208,128]{1,0:T(8,128)(2,1)S(1)}, u32[]{:S(2)}, u32[]{:S(2)}) collective-permute-start(bf16[208,128]{1,0:T(8,128)(2,1)S(1)} %get-tuple-element.106), channel_id=1, source_target_pairs={{0,1},{1,0},{2,3},{3,2},{4,5},{5,4},{6,7},{7,6},{8,9},{9,8},{10,11... | collective-permute-start | bytes 159752 | tf_op jit(solution)/shard_map/ppermute | solution.py:599

commit v6 on v5

--- a/solution.py
+++ b/solution.py
@@ -52,17 +52,22 @@
 VMEM = pl.BlockSpec(memory_space=pltpu.VMEM)
 
 
-def kernel_call(body, outs, arrays, scratch=(), flops=0, limit=24 << 20):
+def kernel_call(body, outs, arrays, scratch=(), flops=0, limit=24 << 20, after=()):
+    used = len(arrays)
+
+    def with_waits(*refs):
+        body(*refs[:used], *refs[used + len(after) :])
+
     nbytes = sum(int(np.prod(a.shape)) * a.dtype.itemsize for a in list(arrays) + list(outs))
     return pl.pallas_call(
-        body,
+        with_waits,
         out_shape=outs,
-        in_specs=[VMEM] * len(arrays),
+        in_specs=[VMEM] * used + [pl.BlockSpec(memory_space=pl.ANY)] * len(after),
         out_specs=[VMEM] * len(outs),
         scratch_shapes=list(scratch),
         compiler_params=pltpu.CompilerParams(vmem_limit_bytes=limit),
         cost_estimate=pl.CostEstimate(flops=flops, bytes_accessed=nbytes, transcendentals=0),
-    )(*arrays)
+    )(*arrays, *after)
 
 
 def shape(rows, cols, dtype):
@@ -162,11 +167,13 @@
         qf[...] = jnp.concatenate(rows, axis=0).T.astype(BF16)
 
 
-def sum_matrices(sz, proj, cells):
+def sum_matrices(sz, proj, cells, after):
     outs = [shape(sz.all_pad, SLOTS, BF16)]
     outs += [shape(SLOTS, len(sz.cells) * PAD * PAD, BF16)] * sz.links
     body = functools.partial(sum_body, sz)
-    return kernel_call(body, outs, [proj, cells], flops=3 * 10**9, limit=32 << 20)
+    return kernel_call(
+        body, outs, [proj, cells], flops=3 * 10**9, limit=32 << 20, after=after
+    )
 
 
 def slot_keys(sz, table, dim):
@@ -190,11 +197,15 @@
     return keys
 
 
-def turn_body(sz, qt, kin, pot, atoms, coupling, *refs):
-    q, kout, vout, maps = refs[:4]
-    back = refs[4] if sz.links else None
-    c_hi, c_lo, wide = refs[-3:]
+def turn_body(qt, q):
     q[...] = qt[...].T
+
+
+def turn_matrix(sz, qt):
+    return kernel_call(turn_body, [shape(SLOTS, sz.all_pad, BF16)], [qt], flops=10**8)[0]
+
+
+def other_body(sz, kin, pot, atoms, coupling, kout, vout, maps, back, c_hi, c_lo, wide):
     nodes = kin.shape[0]
     expand = (node_key(iota(sz.cell_pad, nodes, 0)) == iota(sz.cell_pad, nodes, 1)).astype(BF16)
     gather = (node_key(iota(nodes, sz.cell_pad, 1)) == iota(nodes, sz.cell_pad, 0)).astype(BF16)
@@ -240,10 +251,9 @@
         out[...] = jnp.where(same, dot(picked, fold), 0.0).astype(BF16)
 
 
-def turn_matrices(sz, qt, kin, pot, atoms, coupling):
+def other_matrices(sz, kin, pot, atoms, coupling):
     known = (1 + sz.links) * SLOTS
     outs = [
-        shape(SLOTS, sz.all_pad, BF16),
         shape(sz.cell_pad, sz.cell_pad, BF16),
         shape(len(sz.cells) * sz.cell_pad, sz.orb, F32),
         shape(sz.shifts * SLOTS, known, BF16),
@@ -253,9 +263,9 @@
     ]
     limit = (32 << 20) if sz.shifts < 8 else (56 << 20)
     return kernel_call(
-        functools.partial(turn_body, sz),
+        functools.partial(other_body, sz),
         outs,
-        [qt, kin, pot, atoms, coupling],
+        [kin, pot, atoms, coupling],
         scratch=[pltpu.VMEM((coupling.shape[0], 16, coupling.shape[2]), F32)],
         flops=10**9,
         limit=limit,
@@ -300,19 +310,35 @@
     return [shape(sz.xface, sz.orb, HALO)] * 2 + [shape(sz.yface, sz.orb, F32)] * 2
 
 
-def start_body(sz, parts, r, *faces):
+def start_body(sz, parts, r, *sends):
     nz = parts.shape[2]
     r[...] = jnp.zeros(r.shape, F32)
     for a in range(sz.nx):
         for b in range(sz.ny):
             at = a * sz.line_x + b * PAD
             r[at : at + nz, :] = parts[a, b]
+    for j, out in enumerate(sends):
+        out[...] = pack_z(sz, r, None, [], j)
+
+
+def start_field(sz, parts):
+    outs = [shape(sz.rows_all, sz.orb, F32)] + [shape(sz.zface, sz.orb, HALO)] * sz.links
+    r, *sends = kernel_call(functools.partial(start_body, sz), outs, [parts])
+    return r, sends
+
+
+def start_faces_body(sz, rin, *refs):
+    zr, r, faces = refs[: sz.links], refs[sz.links], refs[sz.links + 1 :]
+    r[...] = rin[...]
+    for j, face in enumerate(zr):
+        add_z(sz, r, j, face[...].astype(F32))
     write_faces(sz, r, *faces)
 
 
-def start_faces(sz, parts):
+def start_faces(sz, r, zr, after):
     outs = [shape(sz.rows_all, sz.orb, F32)] + face_outs(sz)
-    r, *faces = kernel_call(functools.partial(start_body, sz), outs, [parts])
+    body = functools.partial(start_faces_body, sz)
+    r, *faces = kernel_call(body, outs, [r, *zr], after=after)
     return r, faces
 
 
@@ -332,9 +358,9 @@
     write_pair("gy", *faces, sy_one, sy_two)
 
 
-def cross_faces(sz, *faces):
+def cross_faces(sz, faces, after=()):
     outs = [shape(sz.yface, sz.orb, HALO)] * 2
-    return kernel_call(functools.partial(cross_body, sz), outs, list(faces))
+    return kernel_call(functools.partial(cross_body, sz), outs, faces, after=after)
 
 
 def add_xy(sz, ra, xr_one, xr_two, yr_one, yr_two):
@@ -389,14 +415,15 @@
     return jnp.concatenate(rows, axis=0).astype(BF16)
 
 
-def project_body(sz, weight, past, refs):
+def project_body(sz, weight, past, with_face, refs):
     take = iter(refs)
     r = next(take)
     fields = [next(take) for _ in range(past)]
     halos = [next(take) for _ in range(4)]
     q = next(take)
-    qfaces = [next(take) for _ in range(sz.links)]
-    maps, back = next(take), next(take)
+    maps = next(take)
+    if with_face:
+        back, *qfaces = [next(take) for _ in range(1 + sz.links)]
     y, own = next(take), next(take)
     messages = [next(take) for _ in range(sz.shifts)]
     everything = slice(0, sz.rows_all)
@@ -407,30 +434,36 @@
     if rest:
         blocks.append(jnp.zeros((rest, sz.orb), BF16))
     beside = []
-    for j, matrix in enumerate(qfaces):
-        beside.append(dot(matrix[...], face_cells(sz, y, weight, fields, j)).astype(BF16))
+    if with_face:
+        for j, matrix in enumerate(qfaces):
+            beside.append(dot(matrix[...], face_cells(sz, y, weight, fields, j)).astype(BF16))
     sums = dot(q[...], jnp.concatenate(blocks, axis=0))
-    mapped = dot(maps[...], jnp.concatenate([sums.astype(BF16)] + beside, axis=0))
+    known = jnp.concatenate([sums.astype(BF16)] + beside, axis=0)
+    mapped = dot(maps[:, : known.shape[0]], known)
     for s, message in enumerate(messages):
         message[0:SLOTS, :] = mapped[s * SLOTS : (s + 1) * SLOTS].astype(HALO)
         for j, shift in enumerate(link_shifts(sz)):
-            if shift == s + 1:
+            if with_face and shift == s + 1:
                 message[SLOTS : SLOTS + sz.zface, :] = pack_z(sz, y, weight, fields, j)
-    own[...] = sums + dot(back[...], jnp.concatenate(beside, axis=0))
-
-
-def project(sz, r, weight, fields, halos, q, qfaces, maps, back):
+    if beside:
+        sums = sums + dot(back[...], jnp.concatenate(beside, axis=0))
+    own[...] = sums
+
+
+def project(sz, r, weight, fields, halos, q, maps, back_and_faces):
+    with_face = bool(back_and_faces)
     outs = [shape(sz.rows_all, sz.orb, F32), shape(SLOTS, sz.orb, F32)]
     for s in range(1, sz.shifts + 1):
-        outs.append(shape(SLOTS + (sz.zface if s in link_shifts(sz) else 0), sz.orb, HALO))
+        face = sz.zface if with_face and s in link_shifts(sz) else 0
+        outs.append(shape(SLOTS + face, sz.orb, HALO))
 
     def body(*refs):
-        project_body(sz, weight, len(fields), refs)
+        project_body(sz, weight, len(fields), with_face, refs)
 
     y, own, *messages = kernel_call(
         body,
         outs,
-        [r, *fields, *halos, q, *qfaces, maps, back],
+        [r, *fields, *halos, q, maps, *back_and_faces],
         flops=4 * 10**8,
         limit=(32 << 20) if sz.shifts < 8 else (56 << 20),
     )
@@ -452,6 +485,8 @@
     coef = (dot(c_hi[...], high) + (dot(c_hi[...], low) + dot(c_lo[...], high))).astype(BF16)
     y[...] = yin[...]
     for j, shift in enumerate(link_shifts(sz)):
+        if messages[shift - 1].shape[0] == SLOTS:
+            continue
         add_z(sz, y, j, messages[shift - 1][SLOTS : SLOTS + sz.zface, :].astype(F32))
     blocks = [cell_block(sz, y, cell) for cell in sz.cells]
     stiff = dot(kin[...], jnp.concatenate([b.astype(BF16) for b in blocks], axis=1))
@@ -559,45 +594,47 @@
     sz = Sizes(nx, ny, nz, orbitals, devices - 1)
     ring = [[(i, (i + s) % devices) for i in range(devices)] for s in range(devices)]
 
+    def exchange_z(faces):
+        return [lax.ppermute(f, "gz", ring[s]) for f, s in zip(faces, link_shifts(sz))]
+
+    def exchange_xy(sx_one, sx_two, sy_lo, sy_hi, after=()):
+        xr = swap_faces("gx", sx_one, sx_two)
+        cross = cross_faces(sz, [*xr, sy_lo, sy_hi], after)
+        yr = swap_faces("gy", *cross)
+        return (*xr, *yr), cross
+
+    r, sends = start_field(sz, parts)
+    zr = exchange_z(sends)
+    pot = jnp.transpose(cell_potential, (1, 2, 3, 0)).reshape(len(sz.cells), nodes)
+    kin, pot, maps, back, c_hi, c_lo = other_matrices(
+        sz, cell_matrix, pot, slot_atom.reshape(devices, POS), jnp.transpose(coupling, (1, 2, 0))
+    )
     proj = projectors.reshape(nodes, POS * BLK * PA)
     proj = jnp.pad(proj, ((0, up(nodes, 16) - nodes), (0, 0)))
     cells = jnp.transpose(slot_cells.reshape(POS, BLK)).astype(F32)
-    r, faces = start_faces(sz, parts)
-
-    def exchange_xy(sx_one, sx_two, sy_lo, sy_hi):
-        xr = swap_faces("gx", sx_one, sx_two)
-        cross = cross_faces(sz, *xr, sy_lo, sy_hi)
-        yr = swap_faces("gy", *cross)
-        return (*xr, *yr)
-
-    halos = exchange_xy(*faces)
-    qt, *face_rows = sum_matrices(sz, proj, cells)
+    r, faces = start_faces(sz, r, zr, [c_lo, proj, cells])
+    qt, *face_rows = sum_matrices(sz, proj, cells, [faces[0]])
+    halos, cross = exchange_xy(*faces, after=[qt])
+    q = turn_matrix(sz, qt)
+    face_rows, _ = lax.optimization_barrier((face_rows, cross[0]))
     qfaces = []
     for j, shift in enumerate(link_shifts(sz)):
-        back = [(target, source) for source, target in ring[shift]]
-        qfaces.append(lax.ppermute(face_rows[j], "gz", back))
-    pot = jnp.transpose(cell_potential, (1, 2, 3, 0)).reshape(len(sz.cells), nodes)
-    q, kin, pot, maps, back, c_hi, c_lo = turn_matrices(
-        sz,
-        qt,
-        cell_matrix,
-        pot,
-        slot_atom.reshape(devices, POS),
-        jnp.transpose(coupling, (1, 2, 0)),
-    )
+        home = [(target, source) for source, target in ring[shift]]
+        qfaces.append(lax.ppermute(face_rows[j], "gz", home))
 
     fields, scale = [], 1.0 / half_width
     weight = 0.0
     for step in range(STEPS):
-        y, own, messages = project(sz, r, weight, fields, halos, q, qfaces, maps, back)
+        y, own, messages = project(
+            sz, r, weight, fields, halos, q, maps, [back, *qfaces] if step else []
+        )
         received = [lax.ppermute(m, "gz", ring[s + 1]) for s, m in enumerate(messages)]
         r, y, faces = apply(sz, y, own, received, c_hi, c_lo, qt, kin, pot, scale)
         fields, weight = [y] + fields[:1], -center_value * scale
         scale = 2.0 / half_width
-        halos = exchange_xy(*faces)
+        halos, _ = exchange_xy(*faces)
     r, sent = last_faces(sz, r, halos)
-    zr = [lax.ppermute(f, "gz", ring[s]) for f, s in zip(sent, link_shifts(sz))]
-    return finish(sz, r, weight, fields, zr, nz)
+    return finish(sz, r, weight, fields, exchange_z(sent), nz)
 
 
 def solution(mesh):

time: 70.5 us -> 72.5 us (1.028)
  waiting for transfers between devices: 26.7 us -> 31.1 us
  starting transfers between devices: 26.3 us -> 23.9 us
    ppermute x3, starting transfers between devices: 4.41 us -> 1.88 us  [local(): lax.ppermute(m, 'gz', ring[s + 1])]
    ppermute x16, waiting for transfers between devices: 12.6 us -> 14.8 us  [swap_faces(): out.append(lax.ppermute(face, axes, pairs))]
    ppermute x2 -> x3, starting transfers between devices: 3.16 us -> 5.3 us  [the longest x2 3.78 us: exchange_z(): lax.ppermute(f, 'gz', ring[s])]
    ppermute x16, starting transfers between devices: 18.7 us -> 16.7 us  [swap_faces(): out.append(lax.ppermute(face, axes, pairs))]
    ppermute x3, waiting for transfers between devices: 11.3 us -> 12.9 us  [local(): lax.ppermute(m, 'gz', ring[s + 1])]
    ppermute x2 -> x3, waiting for transfers between devices: 2.72 us -> 3.45 us  [the longest x2 3.45 us: exchange_z(): lax.ppermute(f, 'gz', ring[s])]
    pallas_call x15 -> x17, Pallas kernels: 14 us -> 13.8 us  [kernel_call(): pl.pallas_call(with_waits, out_shape=outs, in_specs=[VMEM] * used + [pl.B...]
  transfers between devices with their start and end apart: 21 -> 22, of which waited for: 11 -> 11; matrix products, arithmetic and copies ran while one was open for 3% -> 3% of each run, Pallas kernels for 7% -> 9%
where the time goes in v6:
time: 72.5 us; the launch traced here: 72.3 us
  waiting for transfers between devices  31.1 us (43%)
  starting transfers between devices  23.9 us (33%)
  Pallas kernels  13.8 us (19%)
  local copies, waits for them, and re-layouts  2.48 us (3%)
    ppermute x16, starting transfers between devices, swap_faces(): out.append(lax.ppermute(face, axes, pairs))  16.7 us
    ppermute x16, waiting for transfers between devices, swap_faces(): out.append(lax.ppermute(face, axes, pairs))  14.8 us
    pallas_call x17, Pallas kernels, kernel_call(): pl.pallas_call(with_waits, out_shape=outs, in_specs=[VMEM] * used + [pl.B...  13.8 us
    ppermute x3, waiting for transfers between devices, local(): lax.ppermute(m, 'gz', ring[s + 1])  12.9 us
    ppermute x2, starting transfers between devices, exchange_z(): lax.ppermute(f, 'gz', ring[s])  3.78 us
    ppermute x2, waiting for transfers between devices, exchange_z(): lax.ppermute(f, 'gz', ring[s])  3.45 us
    ppermute x3, starting transfers between devices, local(): lax.ppermute(m, 'gz', ring[s + 1])  1.88 us
    ppermute x1, starting transfers between devices, local(): qfaces.append(lax.ppermute(face_rows[j], 'gz', home))  1.52 us
  transfers between devices with their start and end apart: 22, of which 11 were waited for; matrix products, arithmetic and copies ran while one was open for 3% of the time, Pallas kernels for 9%

profile of v6, /device:TPU:0, one launch (start us, length us, event | category | flops | bytes accessed | tf_op | source)
XLA Modules:
  0.0 72.3 jit_solution(18016522352665076985)
XLA Ops:
  0.0 0.0 copy-start
  0.0 1.1 %copy-done.1 = f32[13,13,7,128]{3,2,1,0:T(8,128)S(1)} copy-done((f32[13,13,7,128]{3,2,1,0:T(8,128)S(1)}, f32[13,13,7,128]{3,2,1,0:T(8,128)}, u32[]{:S(2)}) %copy-start.1) | copy-done | bytes 605720
  1.1 0.1 shard_map.73
  1.3 3.0 %collective-permute-start = (bf16[208,128]{1,0:T(8,128)(2,1)S(1)}, bf16[208,128]{1,0:T(8,128)(2,1)S(1)}, u32[]{:S(2)}, u32[]{:S(2)}) collective-permute-start(bf16[208,128]{1,0:T(8,128)(2,1)S(1)} %get-tuple-element.59), channel_id=1, source_target_pairs={{0,1},{1,0},{2,3},{3,2},{4,5},{5,4},{6,7},{7,6},{8,9},{9,8},{10,11... | collective-permute-start | bytes 159752 | tf_op jit(solution)/shard_map/ppermute | solution.py:598
  4.3 0.7 convert_bitcast_fusion.refs_4_.refs_1_
  5.0 0.0 copy-done
  5.0 1.3 %pad.4.refs_3_.refs_0_ = bf16[352,1536]{1,0:T(8,128)(2,1)S(1)} pad(bf16[343,1536]{1,0:T(8,128)(2,1)} %bitcast.11, bf16[]{:T(256)} %constant.2.clone.1), padding=0_9x0_0 | pad | bytes 2135042 | tf_op jit(solution)/shard_map/jit(_pad)/pad | solution.py:613
  6.3 0.0 copy-done.2
  6.3 0.0 copy-done.3
  6.4 1.8 %shard_map.74 = (bf16[400,400]{1,0:T(8,128)(2,1)S(1)}, f32[1600,128]{1,0:T(8,128)S(1)}, bf16[384,768]{1,0:T(8,128)(2,1)S(1)}, bf16[384,384]{1,0:T(8,128)(2,1)S(1...) custom-call(bf16[343,343]{1,0:T(8,128)(2,1)S(1)} %copy-done.2, f32[4,343]{1,0:T(4,128)S(1)} %reshape.11.refs_1_, ...), custom_call_target="tpu_custom_call" | custom-call | flops 1000000000 | bytes 2891666 | tf_op jit(solution)/shard_map/pallas_call | solution.py:62
  8.1 0.0 collective-permute-done.refs_1_
  8.2 0.1 shard_map.75
  8.3 0.1 collective-permute-start.2
  8.3 1.6 %collective-permute-start.1 = (bf16[112,128]{1,0:T(8,128)(2,1)S(1)}, bf16[112,128]{1,0:T(8,128)(2,1)S(1)}, u32[]{:S(2)}, u32[]{:S(2)}) collective-permute-start(bf16[112,128]{1,0:T(8,128)(2,1)S(1)} %get-tuple-element.62.refs_2_), channel_id=1, source_target_pairs={{0,24},{2,26},{4,28},{6,30},{8,16},{10,18},{12,20},{14,22},{16,8},... | collective-permute-start | bytes 86024 | tf_op jit(solution)/shard_map/ppermute | solution.py:586
  9.9 3.1 %shard_map.76 = (bf16[1664,384]{1,0:T(8,128)(2,1)S(1)}, bf16[384,256]{1,0:T(8,128)(2,1)S(1)}) custom-call(bf16[352,1536]{1,0:T(8,128)(2,1)S(1)} %pad.4.refs_3_.refs_0_, f32[4,32]{1,0:T(4,128)S(1)} %convert_bitcast_fusion.refs_4_.refs_1_, bf16[112,128]{1,0:T(8,128)(2,1)S(1)} %get-tuple-element.62.refs_2_), custom_call_target="tpu_custom_call" | custom-call | flops 3000000000 | bytes 2556416 | tf_op jit(solution)/shard_map/pallas_call | solution.py:62
  13.0 0.0 collective-permute-done.2.refs_1_.refs_2_
  13.1 0.0 collective-permute-done.1.refs_0_.refs_1_
  13.1 1.6 %collective-permute-start.4 = (bf16[112,128]{1,0:T(8,128)(2,1)S(1)}, bf16[112,128]{1,0:T(8,128)(2,1)S(1)}, u32[]{:S(2)}, u32[]{:S(2)}) collective-permute-start(bf16[112,128]{1,0:T(8,128)(2,1)S(1)} %get-tuple-element.68), channel_id=1, source_target_pairs={{0,2},{2,0},{4,6},{6,4},{8,10},{10,8},{12,14},{14,12},{16,18},{18,... | collective-permute-start | bytes 86024 | tf_op jit(solution)/shard_map/ppermute | solution.py:586
  14.7 0.0 collective-permute-start.3
  14.7 0.4 shard_map.78.refs_5_.refs_6_.refs_7_
  15.1 1.9 %collective-permute-done.4.refs_4_ = bf16[112,128]{1,0:T(8,128)(2,1)S(1)} collective-permute-done((bf16[112,128]{1,0:T(8,128)(2,1)S(1)}, bf16[112,128]{1,0:T(8,128)(2,1)S(1)}, u32[]{:S(2)}, u32[]{:S(2)}) %collective-permute-start.4) | collective-permute-done | bytes 28704 | tf_op jit(solution)/shard_map/ppermute | solution.py:586
  17.0 0.0 collective-permute-done.3.refs_3_
  17.0 0.8 %shard_map.79 = (f32[1384,128]{1,0:T(8,128)S(1)}, f32[384,128]{1,0:T(8,128)S(1)}, bf16[384,128]{1,0:T(8,128)(2,1)S(1)}) custom-call(f32[1384,128]{1,0:T(8,128)S(1)} %get-tuple-element.61.refs_0_, bf16[112,128]{1,0:T(8,128)(2,1)S(1)} %collective-permute-done.1.refs_0_.refs_1_, bf16[112,128]{1,0:T(8,128)(2,1)S(1)} %collective-permute-done.2.refs_1_.refs_2_, ...), custom_call_target="tpu_custom_call" | custom-call | flops 400000000 | bytes 3694592 | tf_op jit(solution)/shard_map/pallas_call | solution.py:62
  17.9 0.6 collective-permute-start.5
  18.4 1.5 %collective-permute-start.10 = (bf16[384,256]{1,0:T(8,128)(2,1)S(1)}, bf16[384,256]{1,0:T(8,128)(2,1)S(1)}, u32[]{:S(2)}, u32[]{:S(2)}) collective-permute-start(bf16[384,256]{1,0:T(8,128)(2,1)S(1)} %get-tuple-element.86), channel_id=1, source_target_pairs={{1,0},{0,1},{3,2},{2,3},{5,4},{4,5},{7,6},{6,7},{9,8},{8,9},{11,10... | collective-permute-start | bytes 589832 | tf_op jit(solution)/shard_map/ppermute | solution.py:623
  20.0 3.7 %collective-permute-done.5.refs_2_ = bf16[384,128]{1,0:T(8,128)(2,1)S(1)} collective-permute-done((bf16[384,128]{1,0:T(8,128)(2,1)S(1)}, bf16[384,128]{1,0:T(8,128)(2,1)S(1)}, u32[]{:S(2)}, u32[]{:S(2)}) %collective-permute-start.5) | collective-permute-done | bytes 98336 | tf_op jit(solution)/shard_map/ppermute | solution.py:631
  23.7 1.1 %shard_map.80 = (f32[1384,128]{1,0:T(8,128)S(1)}, f32[1384,128]{1,0:T(8,128)S(1)}, bf16[112,128]{1,0:T(8,128)(2,1)S(1)}, bf16[112,128]{1,0:T(8,128)(2,1)S(1)}, f...) custom-call(f32[1384,128]{1,0:T(8,128)S(1)} %get-tuple-element.70.refs_0_, f32[384,128]{1,0:T(8,128)S(1)} %get-tuple-element.71.refs_1_, ...), custom_call_target="tpu_custom_call" | custom-call | flops 600000000 | bytes 5599744 | tf_op jit(solution)/shard_map/pallas_call | solution.py:62
  24.8 0.1 collective-permute-start.6
  24.8 0.6 collective-permute-start.7
  25.5 2.6 %collective-permute-done.6.refs_0_.refs_2_ = bf16[112,128]{1,0:T(8,128)(2,1)S(1)} collective-permute-done((bf16[112,128]{1,0:T(8,128)(2,1)S(1)}, bf16[112,128]{1,0:T(8,128)(2,1)S(1)}, u32[]{:S(2)}, u32[]{:S(2)}) %collective-permute-start.6) | collective-permute-done | bytes 28704 | tf_op jit(solution)/shard_map/ppermute | solution.py:586
  28.1 0.0 collective-permute-done.7.refs_1_.refs_3_
  28.2 0.1 collective-permute-start.8
  28.2 4.4 %collective-permute-start.9 = (bf16[112,128]{1,0:T(8,128)(2,1)S(1)}, bf16[112,128]{1,0:T(8,128)(2,1)S(1)}, u32[]{:S(2)}, u32[]{:S(2)}) collective-permute-start(bf16[112,128]{1,0:T(8,128)(2,1)S(1)} %get-tuple-element.83), channel_id=1, source_target_pairs={{0,2},{2,0},{4,6},{6,4},{8,10},{10,8},{12,14},{14,12},{16,18},{18,... | collective-permute-start | bytes 86024 | tf_op jit(solution)/shard_map/ppermute | solution.py:586
  32.7 0.0 collective-permute-done.8.refs_4_
  32.7 1.8 %collective-permute-done.9.refs_5_ = bf16[112,128]{1,0:T(8,128)(2,1)S(1)} collective-permute-done((bf16[112,128]{1,0:T(8,128)(2,1)S(1)}, bf16[112,128]{1,0:T(8,128)(2,1)S(1)}, u32[]{:S(2)}, u32[]{:S(2)}) %collective-permute-start.9) | collective-permute-done | bytes 28704 | tf_op jit(solution)/shard_map/ppermute | solution.py:586
  34.5 0.0 collective-permute-done.10.refs_9_.refs_10_
  34.5 1.4 %shard_map.82 = (f32[1384,128]{1,0:T(8,128)S(1)}, f32[384,128]{1,0:T(8,128)S(1)}, bf16[592,128]{1,0:T(8,128)(2,1)S(1)}) custom-call(f32[1384,128]{1,0:T(8,128)S(1)} %get-tuple-element.76.refs_0_, f32[1384,128]{1,0:T(8,128)S(1)} %get-tuple-element.77.refs_1_.refs_2_, bf16[112,128]{1,0:T(8,128)(2,1)S(1)} %collective-permute-done.6.refs_0_.refs_2_, ...), custom_call_target="tpu_custom_call" | custom-call | flops 400000000 | bytes 4947968 | tf_op jit(solution)/shard_map/pallas_call | solution.py:62
  35.9 0.8 %collective-permute-start.11 = (bf16[592,128]{1,0:T(8,128)(2,1)S(1)}, bf16[592,128]{1,0:T(8,128)(2,1)S(1)}, u32[]{:S(2)}, u32[]{:S(2)}) collective-permute-start(bf16[592,128]{1,0:T(8,128)(2,1)S(1)} %get-tuple-element.89), channel_id=1, source_target_pairs={{0,1},{1,0},{2,3},{3,2},{4,5},{5,4},{6,7},{7,6},{8,9},{9,8},{10,11... | collective-permute-start | bytes 454664 | tf_op jit(solution)/shard_map/ppermute | solution.py:631
  36.7 4.5 %collective-permute-done.11.refs_2_ = bf16[592,128]{1,0:T(8,128)(2,1)S(1)} collective-permute-done((bf16[592,128]{1,0:T(8,128)(2,1)S(1)}, bf16[592,128]{1,0:T(8,128)(2,1)S(1)}, u32[]{:S(2)}, u32[]{:S(2)}) %collective-permute-start.11) | collective-permute-done | bytes 151584 | tf_op jit(solution)/shard_map/ppermute | solution.py:631
  41.2 1.1 %shard_map.83 = (f32[1384,128]{1,0:T(8,128)S(1)}, f32[1384,128]{1,0:T(8,128)S(1)}, bf16[112,128]{1,0:T(8,128)(2,1)S(1)}, bf16[112,128]{1,0:T(8,128)(2,1)S(1)}, f...) custom-call(f32[1384,128]{1,0:T(8,128)S(1)} %get-tuple-element.87.refs_0_, f32[384,128]{1,0:T(8,128)S(1)} %get-tuple-element.88.refs_1_, ...), custom_call_target="tpu_custom_call" | custom-call | flops 600000000 | bytes 5652992 | tf_op jit(solution)/shard_map/pallas_call | solution.py:62
  42.3 0.1 collective-permute-start.12
  42.4 0.9 %collective-permute-start.13 = (bf16[112,128]{1,0:T(8,128)(2,1)S(1)}, bf16[112,128]{1,0:T(8,128)(2,1)S(1)}, u32[]{:S(2)}, u32[]{:S(2)}) collective-permute-start(bf16[112,128]{1,0:T(8,128)(2,1)S(1)} %get-tuple-element.93), channel_id=1, source_target_pairs={{0,8},{2,10},{4,12},{6,14},{8,0},{10,2},{12,4},{14,6},{16,24},{18,... | collective-permute-start | bytes 86024 | tf_op jit(solution)/shard_map/ppermute | solution.py:586
  43.3 2.4 %collective-permute-done.12.refs_0_.refs_3_ = bf16[112,128]{1,0:T(8,128)(2,1)S(1)} collective-permute-done((bf16[112,128]{1,0:T(8,128)(2,1)S(1)}, bf16[112,128]{1,0:T(8,128)(2,1)S(1)}, u32[]{:S(2)}, u32[]{:S(2)}) %collective-permute-start.12) | collective-permute-done | bytes 28704 | tf_op jit(solution)/shard_map/ppermute | solution.py:586
  45.7 0.0 collective-permute-done.13.refs_1_.refs_4_
  45.7 0.1 collective-permute-start.14
  45.8 2.3 %collective-permute-start.15 = (bf16[112,128]{1,0:T(8,128)(2,1)S(1)}, bf16[112,128]{1,0:T(8,128)(2,1)S(1)}, u32[]{:S(2)}, u32[]{:S(2)}) collective-permute-start(bf16[112,128]{1,0:T(8,128)(2,1)S(1)} %get-tuple-element.97), channel_id=1, source_target_pairs={{0,2},{2,0},{4,6},{6,4},{8,10},{10,8},{12,14},{14,12},{16,18},{18,... | collective-permute-start | bytes 86024 | tf_op jit(solution)/shard_map/ppermute | solution.py:586
  48.1 0.0 collective-permute-done.14.refs_5_
  48.1 1.8 %collective-permute-done.15.refs_6_ = bf16[112,128]{1,0:T(8,128)(2,1)S(1)} collective-permute-done((bf16[112,128]{1,0:T(8,128)(2,1)S(1)}, bf16[112,128]{1,0:T(8,128)(2,1)S(1)}, u32[]{:S(2)}, u32[]{:S(2)}) %collective-permute-start.15) | collective-permute-done | bytes 28704 | tf_op jit(solution)/shard_map/ppermute | solution.py:586
  49.9 1.4 %shard_map.85 = (f32[1384,128]{1,0:T(8,128)S(1)}, f32[384,128]{1,0:T(8,128)S(1)}, bf16[592,128]{1,0:T(8,128)(2,1)S(1)}) custom-call(f32[1384,128]{1,0:T(8,128)S(1)} %get-tuple-element.90.refs_0_, f32[1384,128]{1,0:T(8,128)S(1)} %get-tuple-element.91.refs_1_.refs_2_, f32[1384,128]{1,0:T(8,128)S(1)} %get-tuple-element.77.refs_1_.refs_2_, ...), custom_call_target="tpu_custom_call" | custom-call | flops 400000000 | bytes 5656576 | tf_op jit(solution)/shard_map/pallas_call | solution.py:62
  51.4 0.5 collective-permute-start.16
  51.9 4.7 %collective-permute-done.16.refs_2_ = bf16[592,128]{1,0:T(8,128)(2,1)S(1)} collective-permute-done((bf16[592,128]{1,0:T(8,128)(2,1)S(1)}, bf16[592,128]{1,0:T(8,128)(2,1)S(1)}, u32[]{:S(2)}, u32[]{:S(2)}) %collective-permute-start.16) | collective-permute-done | bytes 151584 | tf_op jit(solution)/shard_map/ppermute | solution.py:631
  56.6 1.2 %shard_map.86 = (f32[1384,128]{1,0:T(8,128)S(1)}, f32[1384,128]{1,0:T(8,128)S(1)}, bf16[112,128]{1,0:T(8,128)(2,1)S(1)}, bf16[112,128]{1,0:T(8,128)(2,1)S(1)}, f...) custom-call(f32[1384,128]{1,0:T(8,128)S(1)} %get-tuple-element.98.refs_0_, f32[384,128]{1,0:T(8,128)S(1)} %get-tuple-element.99.refs_1_, ...), custom_call_target="tpu_custom_call" | custom-call | flops 600000000 | bytes 5652992 | tf_op jit(solution)/shard_map/pallas_call | solution.py:62
  57.8 0.1 collective-permute-start.17
  57.9 1.0 %collective-permute-start.18 = (bf16[112,128]{1,0:T(8,128)(2,1)S(1)}, bf16[112,128]{1,0:T(8,128)(2,1)S(1)}, u32[]{:S(2)}, u32[]{:S(2)}) collective-permute-start(bf16[112,128]{1,0:T(8,128)(2,1)S(1)} %get-tuple-element.103), channel_id=1, source_target_pairs={{0,8},{2,10},{4,12},{6,14},{8,0},{10,2},{12,4},{14,6},{16,24},{18,... | collective-permute-start | bytes 86024 | tf_op jit(solution)/shard_map/ppermute | solution.py:586
  58.9 2.3 %collective-permute-done.17.refs_0_.refs_1_ = bf16[112,128]{1,0:T(8,128)(2,1)S(1)} collective-permute-done((bf16[112,128]{1,0:T(8,128)(2,1)S(1)}, bf16[112,128]{1,0:T(8,128)(2,1)S(1)}, u32[]{:S(2)}, u32[]{:S(2)}) %collective-permute-start.17) | collective-permute-done | bytes 28704 | tf_op jit(solution)/shard_map/ppermute | solution.py:586
  61.1 0.0 collective-permute-done.18.refs_1_.refs_2_
  61.2 0.1 collective-permute-start.19
  61.3 3.8 %collective-permute-start.20 = (bf16[112,128]{1,0:T(8,128)(2,1)S(1)}, bf16[112,128]{1,0:T(8,128)(2,1)S(1)}, u32[]{:S(2)}, u32[]{:S(2)}) collective-permute-start(bf16[112,128]{1,0:T(8,128)(2,1)S(1)} %get-tuple-element.107), channel_id=1, source_target_pairs={{0,2},{2,0},{4,6},{6,4},{8,10},{10,8},{12,14},{14,12},{16,18},{18,... | collective-permute-start | bytes 86024 | tf_op jit(solution)/shard_map/ppermute | solution.py:586
  65.0 0.0 collective-permute-done.19.refs_3_
  65.0 1.8 %collective-permute-done.20.refs_4_ = bf16[112,128]{1,0:T(8,128)(2,1)S(1)} collective-permute-done((bf16[112,128]{1,0:T(8,128)(2,1)S(1)}, bf16[112,128]{1,0:T(8,128)(2,1)S(1)}, u32[]{:S(2)}, u32[]{:S(2)}) %collective-permute-start.20) | collective-permute-done | bytes 28704 | tf_op jit(solution)/shard_map/ppermute | solution.py:586
  66.9 0.1 shard_map.88
  67.0 0.8 %collective-permute-start.21 = (bf16[208,128]{1,0:T(8,128)(2,1)S(1)}, bf16[208,128]{1,0:T(8,128)(2,1)S(1)}, u32[]{:S(2)}, u32[]{:S(2)}) collective-permute-start(bf16[208,128]{1,0:T(8,128)(2,1)S(1)} %get-tuple-element.110), channel_id=1, source_target_pairs={{0,1},{1,0},{2,3},{3,2},{4,5},{5,4},{6,7},{7,6},{8,9},{9,8},{10,11... | collective-permute-start | bytes 159752 | tf_op jit(solution)/shard_map/ppermute | solution.py:598
  67.7 3.4 %collective-permute-done.21.refs_3_ = bf16[208,128]{1,0:T(8,128)(2,1)S(1)} collective-permute-done((bf16[208,128]{1,0:T(8,128)(2,1)S(1)}, bf16[208,128]{1,0:T(8,128)(2,1)S(1)}, u32[]{:S(2)}, u32[]{:S(2)}) %collective-permute-start.21) | collective-permute-done | bytes 53280 | tf_op jit(solution)/shard_map/ppermute | solution.py:598
  71.2 1.1 %shard_map.89 = f32[13,13,7,128]{3,2,1,0:T(8,128)} custom-call(f32[1384,128]{1,0:T(8,128)S(1)} %get-tuple-element.108.refs_0_, f32[1384,128]{1,0:T(8,128)S(1)} %get-tuple-element.109.refs_1_, f32[1384,128]{1,0:T(8,128)S(1)} %get-tuple-element.91.refs_1_.refs_2_, bf16[208,128]{1,0:T(8,128)(2,1)S(1)} %collective-permute-done.21.refs_3_), custom_call_target="tpu_custom_call" | custom-call | bytes 2784768 | tf_op jit(solution)/shard_map/pallas_call | solution.py:62
  (11 shorter events, 0.2 us)
Async XLA Ops:
  0.0 5.0 %copy-start = (f32[343,2,2,1]{0,3,2,1:T(1,128)S(1)}, f32[343,2,2,1]{0,3,2,1:T(1,128)}, u32[]{:S(2)}) copy-start(f32[343,2,2,1]{0,3,2,1:T(1,128)} %param.9) | copy-start | bytes 16468
  0.0 1.1 %copy-start.1 = (f32[13,13,7,128]{3,2,1,0:T(8,128)S(1)}, f32[13,13,7,128]{3,2,1,0:T(8,128)}, u32[]{:S(2)}) copy-start(f32[13,13,7,128]{3,2,1,0:T(8,128)} %refs_0_.2) | copy-start | bytes 1817092
  1.1 5.2 %copy-start.2 = (bf16[343,343]{1,0:T(8,128)(2,1)S(1)}, bf16[343,343]{1,0:T(8,128)(2,1)}, u32[]{:S(2)}) copy-start(bf16[343,343]{1,0:T(8,128)(2,1)} %refs_0_.3) | copy-start | bytes 705898
  1.1 5.2 %copy-start.3 = (f32[64,12,12]{0,2,1:T(8,128)S(1)}, f32[64,12,12]{0,2,1:T(8,128)}, u32[]{:S(2)}) copy-start(f32[64,12,12]{0,2,1:T(8,128)} %param.13) | copy-start | bytes 110596
  1.1 5.2 %copy-start.4 = (s32[1,1,2,32]{3,2,1,0:T(2,128)S(1)}, s32[1,1,2,32]{3,2,1,0:T(2,128)}, u32[]{:S(2)}) copy-start(s32[1,1,2,32]{3,2,1,0:T(2,128)} %param.11) | copy-start | bytes 772
  1.3 6.9 %collective-permute-start = (bf16[208,128]{1,0:T(8,128)(2,1)S(1)}, bf16[208,128]{1,0:T(8,128)(2,1)S(1)}, u32[]{:S(2)}, u32[]{:S(2)}) collective-permute-start(bf16[208,128]{1,0:T(8,128)(2,1)S(1)} %get-tuple-element.59), channel_id=1, source_target_pairs={{0,1},{1,0},{2,3},{3,2},{4,5},{5,4},{6,7},{7,6},{8,9},{9,8},{10,11... | collective-permute-start | bytes 159752 | tf_op jit(solution)/shard_map/ppermute | solution.py:598
  8.3 4.8 %collective-permute-start.2 = (bf16[112,128]{1,0:T(8,128)(2,1)S(1)}, bf16[112,128]{1,0:T(8,128)(2,1)S(1)}, u32[]{:S(2)}, u32[]{:S(2)}) collective-permute-start(bf16[112,128]{1,0:T(8,128)(2,1)S(1)} %get-tuple-element.63), channel_id=1, source_target_pairs={{0,8},{2,10},{4,12},{6,14},{8,0},{10,2},{12,4},{14,6},{16,24},{18,... | collective-permute-start | bytes 86024 | tf_op jit(solution)/shard_map/ppermute | solution.py:586
  8.3 4.7 %collective-permute-start.1 = (bf16[112,128]{1,0:T(8,128)(2,1)S(1)}, bf16[112,128]{1,0:T(8,128)(2,1)S(1)}, u32[]{:S(2)}, u32[]{:S(2)}) collective-permute-start(bf16[112,128]{1,0:T(8,128)(2,1)S(1)} %get-tuple-element.62.refs_2_), channel_id=1, source_target_pairs={{0,24},{2,26},{4,28},{6,30},{8,16},{10,18},{12,20},{14,22},{16,8},... | collective-permute-start | bytes 86024 | tf_op jit(solution)/shard_map/ppermute | solution.py:586
  13.1 3.9 %collective-permute-start.4 = (bf16[112,128]{1,0:T(8,128)(2,1)S(1)}, bf16[112,128]{1,0:T(8,128)(2,1)S(1)}, u32[]{:S(2)}, u32[]{:S(2)}) collective-permute-start(bf16[112,128]{1,0:T(8,128)(2,1)S(1)} %get-tuple-element.68), channel_id=1, source_target_pairs={{0,2},{2,0},{4,6},{6,4},{8,10},{10,8},{12,14},{14,12},{16,18},{18,... | collective-permute-start | bytes 86024 | tf_op jit(solution)/shard_map/ppermute | solution.py:586
  14.7 2.3 %collective-permute-start.3 = (bf16[112,128]{1,0:T(8,128)(2,1)S(1)}, bf16[112,128]{1,0:T(8,128)(2,1)S(1)}, u32[]{:S(2)}, u32[]{:S(2)}) collective-permute-start(bf16[112,128]{1,0:T(8,128)(2,1)S(1)} %get-tuple-element.67), channel_id=1, source_target_pairs={{0,8},{2,4},{4,2},{6,14},{8,0},{10,12},{12,10},{14,6},{16,24},{18,... | collective-permute-start | bytes 86024 | tf_op jit(solution)/shard_map/ppermute | solution.py:586
  17.9 5.8 %collective-permute-start.5 = (bf16[384,128]{1,0:T(8,128)(2,1)S(1)}, bf16[384,128]{1,0:T(8,128)(2,1)S(1)}, u32[]{:S(2)}, u32[]{:S(2)}) collective-permute-start(bf16[384,128]{1,0:T(8,128)(2,1)S(1)} %get-tuple-element.72), channel_id=1, source_target_pairs={{0,1},{1,0},{2,3},{3,2},{4,5},{5,4},{6,7},{7,6},{8,9},{9,8},{10,11... | collective-permute-start | bytes 294920 | tf_op jit(solution)/shard_map/ppermute | solution.py:631
  18.4 16.1 %collective-permute-start.10 = (bf16[384,256]{1,0:T(8,128)(2,1)S(1)}, bf16[384,256]{1,0:T(8,128)(2,1)S(1)}, u32[]{:S(2)}, u32[]{:S(2)}) collective-permute-start(bf16[384,256]{1,0:T(8,128)(2,1)S(1)} %get-tuple-element.86), channel_id=1, source_target_pairs={{1,0},{0,1},{3,2},{2,3},{5,4},{4,5},{7,6},{6,7},{9,8},{8,9},{11,10... | collective-permute-start | bytes 589832 | tf_op jit(solution)/shard_map/ppermute | solution.py:623
  24.8 3.4 %collective-permute-start.6 = (bf16[112,128]{1,0:T(8,128)(2,1)S(1)}, bf16[112,128]{1,0:T(8,128)(2,1)S(1)}, u32[]{:S(2)}, u32[]{:S(2)}) collective-permute-start(bf16[112,128]{1,0:T(8,128)(2,1)S(1)} %get-tuple-element.78), channel_id=1, source_target_pairs={{0,24},{2,26},{4,28},{6,30},{8,16},{10,18},{12,20},{14,22},{16,8},... | collective-permute-start | bytes 86024 | tf_op jit(solution)/shard_map/ppermute | solution.py:586
  24.8 3.3 %collective-permute-start.7 = (bf16[112,128]{1,0:T(8,128)(2,1)S(1)}, bf16[112,128]{1,0:T(8,128)(2,1)S(1)}, u32[]{:S(2)}, u32[]{:S(2)}) collective-permute-start(bf16[112,128]{1,0:T(8,128)(2,1)S(1)} %get-tuple-element.79), channel_id=1, source_target_pairs={{0,8},{2,10},{4,12},{6,14},{8,0},{10,2},{12,4},{14,6},{16,24},{18,... | collective-permute-start | bytes 86024 | tf_op jit(solution)/shard_map/ppermute | solution.py:586
  28.2 4.5 %collective-permute-start.8 = (bf16[112,128]{1,0:T(8,128)(2,1)S(1)}, bf16[112,128]{1,0:T(8,128)(2,1)S(1)}, u32[]{:S(2)}, u32[]{:S(2)}) collective-permute-start(bf16[112,128]{1,0:T(8,128)(2,1)S(1)} %get-tuple-element.82), channel_id=1, source_target_pairs={{0,8},{2,4},{4,2},{6,14},{8,0},{10,12},{12,10},{14,6},{16,24},{18,... | collective-permute-start | bytes 86024 | tf_op jit(solution)/shard_map/ppermute | solution.py:586
  28.2 6.3 %collective-permute-start.9 = (bf16[112,128]{1,0:T(8,128)(2,1)S(1)}, bf16[112,128]{1,0:T(8,128)(2,1)S(1)}, u32[]{:S(2)}, u32[]{:S(2)}) collective-permute-start(bf16[112,128]{1,0:T(8,128)(2,1)S(1)} %get-tuple-element.83), channel_id=1, source_target_pairs={{0,2},{2,0},{4,6},{6,4},{8,10},{10,8},{12,14},{14,12},{16,18},{18,... | collective-permute-start | bytes 86024 | tf_op jit(solution)/shard_map/ppermute | solution.py:586
  35.9 5.3 %collective-permute-start.11 = (bf16[592,128]{1,0:T(8,128)(2,1)S(1)}, bf16[592,128]{1,0:T(8,128)(2,1)S(1)}, u32[]{:S(2)}, u32[]{:S(2)}) collective-permute-start(bf16[592,128]{1,0:T(8,128)(2,1)S(1)} %get-tuple-element.89), channel_id=1, source_target_pairs={{0,1},{1,0},{2,3},{3,2},{4,5},{5,4},{6,7},{7,6},{8,9},{9,8},{10,11... | collective-permute-start | bytes 454664 | tf_op jit(solution)/shard_map/ppermute | solution.py:631
  42.3 3.4 %collective-permute-start.12 = (bf16[112,128]{1,0:T(8,128)(2,1)S(1)}, bf16[112,128]{1,0:T(8,128)(2,1)S(1)}, u32[]{:S(2)}, u32[]{:S(2)}) collective-permute-start(bf16[112,128]{1,0:T(8,128)(2,1)S(1)} %get-tuple-element.92), channel_id=1, source_target_pairs={{0,24},{2,26},{4,28},{6,30},{8,16},{10,18},{12,20},{14,22},{16,8},... | collective-permute-start | bytes 86024 | tf_op jit(solution)/shard_map/ppermute | solution.py:586
  42.4 3.3 %collective-permute-start.13 = (bf16[112,128]{1,0:T(8,128)(2,1)S(1)}, bf16[112,128]{1,0:T(8,128)(2,1)S(1)}, u32[]{:S(2)}, u32[]{:S(2)}) collective-permute-start(bf16[112,128]{1,0:T(8,128)(2,1)S(1)} %get-tuple-element.93), channel_id=1, source_target_pairs={{0,8},{2,10},{4,12},{6,14},{8,0},{10,2},{12,4},{14,6},{16,24},{18,... | collective-permute-start | bytes 86024 | tf_op jit(solution)/shard_map/ppermute | solution.py:586
  45.7 2.4 %collective-permute-start.14 = (bf16[112,128]{1,0:T(8,128)(2,1)S(1)}, bf16[112,128]{1,0:T(8,128)(2,1)S(1)}, u32[]{:S(2)}, u32[]{:S(2)}) collective-permute-start(bf16[112,128]{1,0:T(8,128)(2,1)S(1)} %get-tuple-element.96), channel_id=1, source_target_pairs={{0,8},{2,4},{4,2},{6,14},{8,0},{10,12},{12,10},{14,6},{16,24},{18,... | collective-permute-start | bytes 86024 | tf_op jit(solution)/shard_map/ppermute | solution.py:586
  45.8 4.1 %collective-permute-start.15 = (bf16[112,128]{1,0:T(8,128)(2,1)S(1)}, bf16[112,128]{1,0:T(8,128)(2,1)S(1)}, u32[]{:S(2)}, u32[]{:S(2)}) collective-permute-start(bf16[112,128]{1,0:T(8,128)(2,1)S(1)} %get-tuple-element.97), channel_id=1, source_target_pairs={{0,2},{2,0},{4,6},{6,4},{8,10},{10,8},{12,14},{14,12},{16,18},{18,... | collective-permute-start | bytes 86024 | tf_op jit(solution)/shard_map/ppermute | solution.py:586
  51.4 5.3 %collective-permute-start.16 = (bf16[592,128]{1,0:T(8,128)(2,1)S(1)}, bf16[592,128]{1,0:T(8,128)(2,1)S(1)}, u32[]{:S(2)}, u32[]{:S(2)}) collective-permute-start(bf16[592,128]{1,0:T(8,128)(2,1)S(1)} %get-tuple-element.100), channel_id=1, source_target_pairs={{0,1},{1,0},{2,3},{3,2},{4,5},{5,4},{6,7},{7,6},{8,9},{9,8},{10,11... | collective-permute-start | bytes 454664 | tf_op jit(solution)/shard_map/ppermute | solution.py:631
  57.8 3.4 %collective-permute-start.17 = (bf16[112,128]{1,0:T(8,128)(2,1)S(1)}, bf16[112,128]{1,0:T(8,128)(2,1)S(1)}, u32[]{:S(2)}, u32[]{:S(2)}) collective-permute-start(bf16[112,128]{1,0:T(8,128)(2,1)S(1)} %get-tuple-element.102), channel_id=1, source_target_pairs={{0,24},{2,26},{4,28},{6,30},{8,16},{10,18},{12,20},{14,22},{16,8},... | collective-permute-start | bytes 86024 | tf_op jit(solution)/shard_map/ppermute | solution.py:586
  57.9 3.3 %collective-permute-start.18 = (bf16[112,128]{1,0:T(8,128)(2,1)S(1)}, bf16[112,128]{1,0:T(8,128)(2,1)S(1)}, u32[]{:S(2)}, u32[]{:S(2)}) collective-permute-start(bf16[112,128]{1,0:T(8,128)(2,1)S(1)} %get-tuple-element.103), channel_id=1, source_target_pairs={{0,8},{2,10},{4,12},{6,14},{8,0},{10,2},{12,4},{14,6},{16,24},{18,... | collective-permute-start | bytes 86024 | tf_op jit(solution)/shard_map/ppermute | solution.py:586
  61.2 3.8 %collective-permute-start.19 = (bf16[112,128]{1,0:T(8,128)(2,1)S(1)}, bf16[112,128]{1,0:T(8,128)(2,1)S(1)}, u32[]{:S(2)}, u32[]{:S(2)}) collective-permute-start(bf16[112,128]{1,0:T(8,128)(2,1)S(1)} %get-tuple-element.106), channel_id=1, source_target_pairs={{0,8},{2,4},{4,2},{6,14},{8,0},{10,12},{12,10},{14,6},{16,24},{18,... | collective-permute-start | bytes 86024 | tf_op jit(solution)/shard_map/ppermute | solution.py:586
  61.3 5.6 %collective-permute-start.20 = (bf16[112,128]{1,0:T(8,128)(2,1)S(1)}, bf16[112,128]{1,0:T(8,128)(2,1)S(1)}, u32[]{:S(2)}, u32[]{:S(2)}) collective-permute-start(bf16[112,128]{1,0:T(8,128)(2,1)S(1)} %get-tuple-element.107), channel_id=1, source_target_pairs={{0,2},{2,0},{4,6},{6,4},{8,10},{10,8},{12,14},{14,12},{16,18},{18,... | collective-permute-start | bytes 86024 | tf_op jit(solution)/shard_map/ppermute | solution.py:586
  67.0 4.2 %collective-permute-start.21 = (bf16[208,128]{1,0:T(8,128)(2,1)S(1)}, bf16[208,128]{1,0:T(8,128)(2,1)S(1)}, u32[]{:S(2)}, u32[]{:S(2)}) collective-permute-start(bf16[208,128]{1,0:T(8,128)(2,1)S(1)} %get-tuple-element.110), channel_id=1, source_target_pairs={{0,1},{1,0},{2,3},{3,2},{4,5},{5,4},{6,7},{7,6},{8,9},{9,8},{10,11... | collective-permute-start | bytes 159752 | tf_op jit(solution)/shard_map/ppermute | solution.py:598

commit v7 on v5

--- a/solution.py
+++ b/solution.py
@@ -52,17 +52,22 @@
 VMEM = pl.BlockSpec(memory_space=pltpu.VMEM)
 
 
-def kernel_call(body, outs, arrays, scratch=(), flops=0, limit=24 << 20):
+def kernel_call(body, outs, arrays, scratch=(), flops=0, limit=24 << 20, after=(), out_specs=None):
+    used = len(arrays)
+
+    def with_waits(*refs):
+        body(*refs[:used], *refs[used + len(after) :])
+
     nbytes = sum(int(np.prod(a.shape)) * a.dtype.itemsize for a in list(arrays) + list(outs))
     return pl.pallas_call(
-        body,
+        with_waits,
         out_shape=outs,
-        in_specs=[VMEM] * len(arrays),
-        out_specs=[VMEM] * len(outs),
+        in_specs=[VMEM] * used + [pl.BlockSpec(memory_space=pl.ANY)] * len(after),
+        out_specs=out_specs or [VMEM] * len(outs),
         scratch_shapes=list(scratch),
         compiler_params=pltpu.CompilerParams(vmem_limit_bytes=limit),
         cost_estimate=pl.CostEstimate(flops=flops, bytes_accessed=nbytes, transcendentals=0),
-    )(*arrays)
+    )(*arrays, *after)
 
 
 def shape(rows, cols, dtype):
@@ -310,9 +315,9 @@
     write_faces(sz, r, *faces)
 
 
-def start_faces(sz, parts):
+def start_faces(sz, parts, after):
     outs = [shape(sz.rows_all, sz.orb, F32)] + face_outs(sz)
-    r, *faces = kernel_call(functools.partial(start_body, sz), outs, [parts])
+    r, *faces = kernel_call(functools.partial(start_body, sz), outs, [parts], after=after)
     return r, faces
 
 
@@ -396,8 +401,9 @@
     halos = [next(take) for _ in range(4)]
     q = next(take)
     qfaces = [next(take) for _ in range(sz.links)]
-    maps, back = next(take), next(take)
+    maps = next(take)
     y, own = next(take), next(take)
+    beside = [next(take) for _ in range(sz.links)]
     messages = [next(take) for _ in range(sz.shifts)]
     everything = slice(0, sz.rows_all)
     y[...] = r[...] + local_term(weight, fields, everything) if past else r[...]
@@ -406,35 +412,63 @@
     rest = sz.all_pad - sz.cell_pad * len(sz.cells)
     if rest:
         blocks.append(jnp.zeros((rest, sz.orb), BF16))
-    beside = []
+    sums = dot(q[...], jnp.concatenate(blocks, axis=0))
+    own[...] = sums
+    known = [sums.astype(BF16)]
     for j, matrix in enumerate(qfaces):
-        beside.append(dot(matrix[...], face_cells(sz, y, weight, fields, j)).astype(BF16))
-    sums = dot(q[...], jnp.concatenate(blocks, axis=0))
-    mapped = dot(maps[...], jnp.concatenate([sums.astype(BF16)] + beside, axis=0))
+        value, valid = dot(matrix[...], face_cells(sz, y, weight, fields, j)), link_valid(sz, j)
+        beside[j][...] = (value if valid is None else value * valid.astype(F32)).astype(BF16)
+        known.append(beside[j][...])
+    shift_of = link_shifts(sz)
     for s, message in enumerate(messages):
-        message[0:SLOTS, :] = mapped[s * SLOTS : (s + 1) * SLOTS].astype(HALO)
-        for j, shift in enumerate(link_shifts(sz)):
-            if shift == s + 1:
-                message[SLOTS : SLOTS + sz.zface, :] = pack_z(sz, y, weight, fields, j)
-    own[...] = sums + dot(back[...], jnp.concatenate(beside, axis=0))
-
-
-def project(sz, r, weight, fields, halos, q, qfaces, maps, back):
+        rows = slice(s * SLOTS, (s + 1) * SLOTS)
+        mapped = [0] + [j + 1 for j, shift in enumerate(shift_of) if shift != s + 1]
+        direct = [j for j, shift in enumerate(shift_of) if shift == s + 1]
+        total = sum(dot(maps[rows, k * SLOTS : (k + 1) * SLOTS], known[k]) for k in mapped)
+        for j in direct:
+            total = total + known[j + 1].astype(F32)
+            message[SLOTS : SLOTS + sz.zface, :] = pack_z(sz, y, weight, fields, j)
+        message[0:SLOTS, :] = total.astype(HALO)
+
+
+def project(sz, r, weight, fields, halos, q, qfaces, maps):
     outs = [shape(sz.rows_all, sz.orb, F32), shape(SLOTS, sz.orb, F32)]
+    outs += [shape(SLOTS, sz.orb, BF16)] * sz.links
     for s in range(1, sz.shifts + 1):
         outs.append(shape(SLOTS + (sz.zface if s in link_shifts(sz) else 0), sz.orb, HALO))
 
     def body(*refs):
         project_body(sz, weight, len(fields), refs)
 
-    y, own, *messages = kernel_call(
+    y, own, *rest = kernel_call(
         body,
         outs,
-        [r, *fields, *halos, q, *qfaces, maps, back],
+        [r, *fields, *halos, q, *qfaces, maps],
         flops=4 * 10**8,
         limit=(32 << 20) if sz.shifts < 8 else (56 << 20),
     )
-    return y, own, messages
+    return y, [own, *rest[: sz.links]], rest[sz.links :]
+
+
+def couple(c_hi, c_lo, totals):
+    high = totals.astype(BF16)
+    low = (totals - high.astype(F32)).astype(BF16)
+    return dot(c_hi[...], high) + (dot(c_hi[...], low) + dot(c_lo[...], high))
+
+
+def couple_body(sz, own, *refs):
+    beside = refs[: sz.links]
+    back, c_hi, c_lo, coupled = refs[sz.links :]
+    totals = own[...]
+    for j, part in enumerate(beside):
+        totals = totals + dot(back[:, j * SLOTS : (j + 1) * SLOTS], part[...])
+    coupled[...] = couple(c_hi, c_lo, totals)
+
+
+def couple_own(sz, own, back, c_hi, c_lo):
+    outs = [shape(SLOTS, sz.orb, F32)]
+    body = functools.partial(couple_body, sz)
+    return kernel_call(body, outs, [*own, back, c_hi, c_lo], flops=2 * 10**8)[0]
 
 
 def apply_body(sz, scale, refs):
@@ -444,12 +478,13 @@
     c_hi, c_lo, qt, kin, pot = [next(take) for _ in range(5)]
     r, y = next(take), next(take)
     faces = [next(take) for _ in range(4)]
-    totals = own[...]
-    for message in messages:
-        totals = totals + message[0:SLOTS, :].astype(F32)
-    high = totals.astype(BF16)
-    low = (totals - high.astype(F32)).astype(BF16)
-    coef = (dot(c_hi[...], high) + (dot(c_hi[...], low) + dot(c_lo[...], high))).astype(BF16)
+    if len(messages) == 1:
+        high = messages[0][0:SLOTS, :].astype(BF16)
+        coef = own[...] + (dot(c_hi[...], high) + dot(c_lo[...], high))
+    else:
+        totals = sum(message[0:SLOTS, :].astype(F32) for message in messages)
+        coef = own[...] + couple(c_hi, c_lo, totals)
+    coef = coef.astype(BF16)
     y[...] = yin[...]
     for j, shift in enumerate(link_shifts(sz)):
         add_z(sz, y, j, messages[shift - 1][SLOTS : SLOTS + sz.zface, :].astype(F32))
@@ -503,26 +538,46 @@
     return ra, sent
 
 
-def finish_body(sz, weight, past, refs):
-    take = iter(refs)
-    r = next(take)
-    fields = [next(take) for _ in range(past)]
-    zr = [next(take) for _ in range(sz.links)]
-    out, ra = next(take), next(take)
-    ra[...] = r[...] + local_term(weight, fields, slice(0, sz.rows_all))
+def add_local_body(weight, past, r, *refs):
+    fields, out = refs[:past], refs[past]
+    out[...] = r[...] + local_term(weight, fields, slice(0, out.shape[0]))
+
+
+def add_local(sz, r, weight, fields):
+    body = functools.partial(add_local_body, weight, len(fields))
+    return kernel_call(body, [shape(sz.rows_all, sz.orb, F32)], [r, *fields])[0]
+
+
+def finish_body(sz, r, *refs):
+    zr = refs[: sz.links]
+    out, ra, block, sent = refs[sz.links :]
+    ra[...] = r[...]
     for j, face in enumerate(zr):
         add_z(sz, ra, j, face[...].astype(F32))
-    value = ra[0 : sz.rows, :]
-    out[...] = value.reshape(sz.nx, sz.ny, PAD, sz.orb)[:, :, : out.shape[2], :]
-
-
-def finish(sz, r, weight, fields, zr, nz):
-    def body(*refs):
-        finish_body(sz, weight, len(fields), refs)
-
+    nz = block.shape[2]
+    pieces, copies = 3, []
+    for k in range(pieces):
+        first, last = k * sz.nx // pieces, (k + 1) * sz.nx // pieces
+        value = ra[first * sz.line_x : last * sz.line_x, :]
+        value = value.reshape(last - first, sz.ny, PAD, sz.orb)[:, :, :nz, :]
+        block[first:last] = value
+        copy = pltpu.make_async_copy(block.at[first:last], out.at[first:last], sent.at[k])
+        copy.start()
+        copies.append(copy)
+    for copy in copies:
+        copy.wait()
+
+
+def finish(sz, r, zr, nz):
     outs = [jax.ShapeDtypeStruct((sz.nx, sz.ny, nz, sz.orb), F32)]
-    scratch = [pltpu.VMEM((sz.rows_all, sz.orb), F32)]
-    return kernel_call(body, outs, [r, *fields, *zr], scratch=scratch)[0]
+    scratch = [
+        pltpu.VMEM((sz.rows_all, sz.orb), F32),
+        pltpu.VMEM((sz.nx, sz.ny, nz, sz.orb), F32),
+        pltpu.SemaphoreType.DMA((3,)),
+    ]
+    body = functools.partial(finish_body, sz)
+    anywhere = [pl.BlockSpec(memory_space=pl.ANY)]
+    return kernel_call(body, outs, [r, *zr], scratch=scratch, out_specs=anywhere)[0]
 
 
 def swap_faces(axis, one, two):
@@ -562,7 +617,7 @@
     proj = projectors.reshape(nodes, POS * BLK * PA)
     proj = jnp.pad(proj, ((0, up(nodes, 16) - nodes), (0, 0)))
     cells = jnp.transpose(slot_cells.reshape(POS, BLK)).astype(F32)
-    r, faces = start_faces(sz, parts)
+    r, faces = start_faces(sz, parts, [cells, proj])
 
     def exchange_xy(sx_one, sx_two, sy_lo, sy_hi):
         xr = swap_faces("gx", sx_one, sx_two)
@@ -589,15 +644,16 @@
     fields, scale = [], 1.0 / half_width
     weight = 0.0
     for step in range(STEPS):
-        y, own, messages = project(sz, r, weight, fields, halos, q, qfaces, maps, back)
+        y, own, messages = project(sz, r, weight, fields, halos, q, qfaces, maps)
         received = [lax.ppermute(m, "gz", ring[s + 1]) for s, m in enumerate(messages)]
+        own = couple_own(sz, own, back, c_hi, c_lo)
         r, y, faces = apply(sz, y, own, received, c_hi, c_lo, qt, kin, pot, scale)
         fields, weight = [y] + fields[:1], -center_value * scale
         scale = 2.0 / half_width
         halos = exchange_xy(*faces)
     r, sent = last_faces(sz, r, halos)
     zr = [lax.ppermute(f, "gz", ring[s]) for f, s in zip(sent, link_shifts(sz))]
-    return finish(sz, r, weight, fields, zr, nz)
+    return finish(sz, add_local(sz, r, weight, fields), zr, nz)
 
 
 def solution(mesh):

time: 70.5 us -> 67.7 us (0.960)
  waiting for transfers between devices: 26.7 us -> 24.6 us
  local copies, waits for them, and re-layouts: 2.48 us -> 1.37 us
    ppermute x3, waiting for transfers between devices: 11.3 us -> 9.51 us  [local(): lax.ppermute(m, 'gz', ring[s + 1])]
    unnamed x10, local copies, waits for them, and re-layouts: 1.14 us -> 0.02 us
    pallas_call x15 -> x19, Pallas kernels: 14 us -> 14.2 us  [kernel_call(): pl.pallas_call(with_waits, out_shape=outs, in_specs=[VMEM] * used + [pl.B...]
  transfers between devices with their start and end apart: 21 -> 21, of which waited for: 11 -> 11; matrix products, arithmetic and copies ran while one was open for 3% -> 0% of each run, Pallas kernels for 7% -> 10%
where the time goes in v7:
time: 67.7 us; the launch traced here: 67.5 us
  starting transfers between devices  26.3 us (39%)
  waiting for transfers between devices  24.6 us (36%)
  Pallas kernels  14.2 us (21%)
  local copies, waits for them, and re-layouts  1.37 us (2%)
  other arithmetic  0.75 us (1%)
    ppermute x16, starting transfers between devices, swap_faces(): out.append(lax.ppermute(face, axes, pairs))  18.8 us
    pallas_call x19, Pallas kernels, kernel_call(): pl.pallas_call(with_waits, out_shape=outs, in_specs=[VMEM] * used + [pl.B...  14.2 us
    ppermute x16, waiting for transfers between devices, swap_faces(): out.append(lax.ppermute(face, axes, pairs))  12.6 us
    ppermute x3, waiting for transfers between devices, local(): lax.ppermute(m, 'gz', ring[s + 1])  9.51 us
    ppermute x3, starting transfers between devices, local(): lax.ppermute(m, 'gz', ring[s + 1])  4.42 us
    ppermute x1, waiting for transfers between devices, local(): zr = [lax.ppermute(f, 'gz', ring[s]) for f, s in zip(sent, link_shifts(sz))]  2.44 us
    ppermute x1, starting transfers between devices, local(): qfaces.append(lax.ppermute(face_rows[j], 'gz', back))  1.58 us
    ppermute x1, starting transfers between devices, local(): zr = [lax.ppermute(f, 'gz', ring[s]) for f, s in zip(sent, link_shifts(sz))]  1.58 us
  transfers between devices with their start and end apart: 21, of which 11 were waited for; matrix products, arithmetic and copies ran while one was open for 0% of the time, Pallas kernels for 10%

profile of v7, /device:TPU:0, one launch (start us, length us, event | category | flops | bytes accessed | tf_op | source)
XLA Modules:
  0.0 67.5 jit_solution(6267581775527327208)
XLA Ops:
  0.0 0.0 copy-start
  0.0 0.8 %convert_bitcast_fusion.refs_1_ = f32[4,32]{1,0:T(4,128)S(1)} fusion(s32[1,1,1,32,4]{3,4,2,1,0:T(4,128)} %param.12), kind=kLoop, calls=%fused_computation.1 | loop fusion | flops 128 | bytes 1024 | tf_op jit(solution)/shard_map/convert_element_type | solution.py:619
  0.8 1.3 %pad.4.refs_2_.refs_0_ = bf16[352,1536]{1,0:T(8,128)(2,1)S(1)} pad(bf16[343,1536]{1,0:T(8,128)(2,1)} %bitcast.11, bf16[]{:T(256)} %constant.2.clone.1), padding=0_9x0_0 | pad | bytes 2135042 | tf_op jit(solution)/shard_map/jit(_pad)/pad | solution.py:618
  2.1 0.0 copy-done.1
  2.1 0.1 shard_map.73
  2.2 2.4 %collective-permute-start = (bf16[112,128]{1,0:T(8,128)(2,1)S(1)}, bf16[112,128]{1,0:T(8,128)(2,1)S(1)}, u32[]{:S(2)}, u32[]{:S(2)}) collective-permute-start(bf16[112,128]{1,0:T(8,128)(2,1)S(1)} %get-tuple-element.60), channel_id=1, source_target_pairs={{0,24},{2,26},{4,28},{6,30},{8,16},{10,18},{12,20},{14,22},{16,8},... | collective-permute-start | bytes 86024 | tf_op jit(solution)/shard_map/ppermute | solution.py:606
  4.6 0.7 %collective-permute-start.1 = (bf16[112,128]{1,0:T(8,128)(2,1)S(1)}, bf16[112,128]{1,0:T(8,128)(2,1)S(1)}, u32[]{:S(2)}, u32[]{:S(2)}) collective-permute-start(bf16[112,128]{1,0:T(8,128)(2,1)S(1)} %get-tuple-element.61), channel_id=1, source_target_pairs={{0,8},{2,10},{4,12},{6,14},{8,0},{10,2},{12,4},{14,6},{16,24},{18,... | collective-permute-start | bytes 86024 | tf_op jit(solution)/shard_map/ppermute | solution.py:606
  5.3 3.1 %shard_map.75 = (bf16[1664,384]{1,0:T(8,128)(2,1)S(1)}, bf16[384,256]{1,0:T(8,128)(2,1)S(1)}) custom-call(bf16[352,1536]{1,0:T(8,128)(2,1)S(1)} %pad.4.refs_2_.refs_0_, f32[4,32]{1,0:T(4,128)S(1)} %convert_bitcast_fusion.refs_1_), custom_call_target="tpu_custom_call" | custom-call | flops 3000000000 | bytes 2556416 | tf_op jit(solution)/shard_map/pallas_call | solution.py:62
  8.4 1.6 %collective-permute-start.4 = (bf16[384,256]{1,0:T(8,128)(2,1)S(1)}, bf16[384,256]{1,0:T(8,128)(2,1)S(1)}, u32[]{:S(2)}, u32[]{:S(2)}) collective-permute-start(bf16[384,256]{1,0:T(8,128)(2,1)S(1)} %get-tuple-element.68), channel_id=1, source_target_pairs={{1,0},{0,1},{3,2},{2,3},{5,4},{4,5},{7,6},{6,7},{9,8},{8,9},{11,10... | collective-permute-start | bytes 589832 | tf_op jit(solution)/shard_map/ppermute | solution.py:633
  10.0 0.0 copy-done
  10.1 0.0 collective-permute-done.refs_0_.refs_1_
  10.1 0.0 collective-permute-done.1.refs_1_.refs_2_
  10.1 0.1 collective-permute-start.2
  10.2 3.1 %collective-permute-start.3 = (bf16[112,128]{1,0:T(8,128)(2,1)S(1)}, bf16[112,128]{1,0:T(8,128)(2,1)S(1)}, u32[]{:S(2)}, u32[]{:S(2)}) collective-permute-start(bf16[112,128]{1,0:T(8,128)(2,1)S(1)} %get-tuple-element.65), channel_id=1, source_target_pairs={{0,2},{2,0},{4,6},{6,4},{8,10},{10,8},{12,14},{14,12},{16,18},{18,... | collective-permute-start | bytes 86024 | tf_op jit(solution)/shard_map/ppermute | solution.py:606
  13.4 0.0 copy-done.2
  13.4 0.0 copy-done.3
  13.4 1.8 %shard_map.76 = (bf16[384,1664]{1,0:T(8,128)(2,1)S(1)}, bf16[400,400]{1,0:T(8,128)(2,1)S(1)}, f32[1600,128]{1,0:T(8,128)S(1)}, bf16[384,768]{1,0:T(8,128)(2,1)S(...) custom-call(bf16[1664,384]{1,0:T(8,128)(2,1)S(1)} %get-tuple-element.66.refs_0_.refs_5_, ...), custom_call_target="tpu_custom_call" | custom-call | flops 1000000000 | bytes 5447570 | tf_op jit(solution)/shard_map/pallas_call | solution.py:62
  15.2 0.0 collective-permute-done.2.refs_3_
  15.2 0.0 collective-permute-done.3.refs_4_
  15.2 0.1 collective-permute-done.4.refs_6_.refs_7_.refs_8_
  15.3 0.9 %shard_map.77 = (f32[1384,128]{1,0:T(8,128)S(1)}, f32[384,128]{1,0:T(8,128)S(1)}, bf16[384,128]{1,0:T(8,128)(2,1)S(1)}, bf16[592,128]{1,0:T(8,128)(2,1)S(1)}) custom-call(f32[1384,128]{1,0:T(8,128)S(1)} %get-tuple-element.59.refs_0_, bf16[112,128]{1,0:T(8,128)(2,1)S(1)} %collective-permute-done.refs_0_.refs_1_, ...), custom_call_target="tpu_custom_call" | custom-call | flops 400000000 | bytes 4042752 | tf_op jit(solution)/shard_map/pallas_call | solution.py:62
  16.2 1.6 %collective-permute-start.5 = (bf16[592,128]{1,0:T(8,128)(2,1)S(1)}, bf16[592,128]{1,0:T(8,128)(2,1)S(1)}, u32[]{:S(2)}, u32[]{:S(2)}) collective-permute-start(bf16[592,128]{1,0:T(8,128)(2,1)S(1)} %get-tuple-element.76), channel_id=1, source_target_pairs={{0,1},{1,0},{2,3},{3,2},{4,5},{5,4},{6,7},{7,6},{8,9},{9,8},{10,11... | collective-permute-start | bytes 454664 | tf_op jit(solution)/shard_map/ppermute | solution.py:648
  17.8 0.6 shard_map.78.refs_1_
  18.4 3.1 %collective-permute-done.5.refs_2_ = bf16[592,128]{1,0:T(8,128)(2,1)S(1)} collective-permute-done((bf16[592,128]{1,0:T(8,128)(2,1)S(1)}, bf16[592,128]{1,0:T(8,128)(2,1)S(1)}, u32[]{:S(2)}, u32[]{:S(2)}) %collective-permute-start.5) | collective-permute-done | bytes 151584 | tf_op jit(solution)/shard_map/ppermute | solution.py:648
  21.5 1.1 %shard_map.79 = (f32[1384,128]{1,0:T(8,128)S(1)}, f32[1384,128]{1,0:T(8,128)S(1)}, bf16[112,128]{1,0:T(8,128)(2,1)S(1)}, bf16[112,128]{1,0:T(8,128)(2,1)S(1)}, f...) custom-call(f32[1384,128]{1,0:T(8,128)S(1)} %get-tuple-element.70.refs_0_, f32[384,128]{1,0:T(8,128)S(1)} %shard_map.78.refs_1_, ...), custom_call_target="tpu_custom_call" | custom-call | flops 600000000 | bytes 5652992 | tf_op jit(solution)/shard_map/pallas_call | solution.py:62
  22.6 0.1 collective-permute-start.6
  22.6 0.9 %collective-permute-start.7 = (bf16[112,128]{1,0:T(8,128)(2,1)S(1)}, bf16[112,128]{1,0:T(8,128)(2,1)S(1)}, u32[]{:S(2)}, u32[]{:S(2)}) collective-permute-start(bf16[112,128]{1,0:T(8,128)(2,1)S(1)} %get-tuple-element.82), channel_id=1, source_target_pairs={{0,8},{2,10},{4,12},{6,14},{8,0},{10,2},{12,4},{14,6},{16,24},{18,... | collective-permute-start | bytes 86024 | tf_op jit(solution)/shard_map/ppermute | solution.py:606
  23.5 2.4 %collective-permute-done.6.refs_0_.refs_2_ = bf16[112,128]{1,0:T(8,128)(2,1)S(1)} collective-permute-done((bf16[112,128]{1,0:T(8,128)(2,1)S(1)}, bf16[112,128]{1,0:T(8,128)(2,1)S(1)}, u32[]{:S(2)}, u32[]{:S(2)}) %collective-permute-start.6) | collective-permute-done | bytes 28704 | tf_op jit(solution)/shard_map/ppermute | solution.py:606
  25.9 0.0 collective-permute-done.7.refs_1_.refs_3_
  25.9 0.1 collective-permute-start.8
  26.0 3.1 %collective-permute-start.9 = (bf16[112,128]{1,0:T(8,128)(2,1)S(1)}, bf16[112,128]{1,0:T(8,128)(2,1)S(1)}, u32[]{:S(2)}, u32[]{:S(2)}) collective-permute-start(bf16[112,128]{1,0:T(8,128)(2,1)S(1)} %get-tuple-element.86), channel_id=1, source_target_pairs={{0,2},{2,0},{4,6},{6,4},{8,10},{10,8},{12,14},{14,12},{16,18},{18,... | collective-permute-start | bytes 86024 | tf_op jit(solution)/shard_map/ppermute | solution.py:606
  29.2 0.0 collective-permute-done.8.refs_4_
  29.2 1.8 %collective-permute-done.9.refs_5_ = bf16[112,128]{1,0:T(8,128)(2,1)S(1)} collective-permute-done((bf16[112,128]{1,0:T(8,128)(2,1)S(1)}, bf16[112,128]{1,0:T(8,128)(2,1)S(1)}, u32[]{:S(2)}, u32[]{:S(2)}) %collective-permute-start.9) | collective-permute-done | bytes 28704 | tf_op jit(solution)/shard_map/ppermute | solution.py:606
  31.0 0.9 %shard_map.81 = (f32[1384,128]{1,0:T(8,128)S(1)}, f32[384,128]{1,0:T(8,128)S(1)}, bf16[384,128]{1,0:T(8,128)(2,1)S(1)}, bf16[592,128]{1,0:T(8,128)(2,1)S(1)}) custom-call(f32[1384,128]{1,0:T(8,128)S(1)} %get-tuple-element.79.refs_0_, f32[1384,128]{1,0:T(8,128)S(1)} %get-tuple-element.80.refs_1_.refs_2_, ...), custom_call_target="tpu_custom_call" | custom-call | flops 400000000 | bytes 4751360 | tf_op jit(solution)/shard_map/pallas_call | solution.py:62
  31.9 1.6 %collective-permute-start.10 = (bf16[592,128]{1,0:T(8,128)(2,1)S(1)}, bf16[592,128]{1,0:T(8,128)(2,1)S(1)}, u32[]{:S(2)}, u32[]{:S(2)}) collective-permute-start(bf16[592,128]{1,0:T(8,128)(2,1)S(1)} %get-tuple-element.90), channel_id=1, source_target_pairs={{0,1},{1,0},{2,3},{3,2},{4,5},{5,4},{6,7},{7,6},{8,9},{9,8},{10,11... | collective-permute-start | bytes 454664 | tf_op jit(solution)/shard_map/ppermute | solution.py:648
  33.5 0.6 shard_map.82.refs_1_
  34.1 3.1 %collective-permute-done.10.refs_2_ = bf16[592,128]{1,0:T(8,128)(2,1)S(1)} collective-permute-done((bf16[592,128]{1,0:T(8,128)(2,1)S(1)}, bf16[592,128]{1,0:T(8,128)(2,1)S(1)}, u32[]{:S(2)}, u32[]{:S(2)}) %collective-permute-start.10) | collective-permute-done | bytes 151584 | tf_op jit(solution)/shard_map/ppermute | solution.py:648
  37.2 1.1 %shard_map.83 = (f32[1384,128]{1,0:T(8,128)S(1)}, f32[1384,128]{1,0:T(8,128)S(1)}, bf16[112,128]{1,0:T(8,128)(2,1)S(1)}, bf16[112,128]{1,0:T(8,128)(2,1)S(1)}, f...) custom-call(f32[1384,128]{1,0:T(8,128)S(1)} %get-tuple-element.87.refs_0_, f32[384,128]{1,0:T(8,128)S(1)} %shard_map.82.refs_1_, ...), custom_call_target="tpu_custom_call" | custom-call | flops 600000000 | bytes 5652992 | tf_op jit(solution)/shard_map/pallas_call | solution.py:62
  38.3 0.1 collective-permute-start.11
  38.4 0.9 %collective-permute-start.12 = (bf16[112,128]{1,0:T(8,128)(2,1)S(1)}, bf16[112,128]{1,0:T(8,128)(2,1)S(1)}, u32[]{:S(2)}, u32[]{:S(2)}) collective-permute-start(bf16[112,128]{1,0:T(8,128)(2,1)S(1)} %get-tuple-element.94), channel_id=1, source_target_pairs={{0,8},{2,10},{4,12},{6,14},{8,0},{10,2},{12,4},{14,6},{16,24},{18,... | collective-permute-start | bytes 86024 | tf_op jit(solution)/shard_map/ppermute | solution.py:606
  39.3 2.4 %collective-permute-done.11.refs_0_.refs_3_ = bf16[112,128]{1,0:T(8,128)(2,1)S(1)} collective-permute-done((bf16[112,128]{1,0:T(8,128)(2,1)S(1)}, bf16[112,128]{1,0:T(8,128)(2,1)S(1)}, u32[]{:S(2)}, u32[]{:S(2)}) %collective-permute-start.11) | collective-permute-done | bytes 28704 | tf_op jit(solution)/shard_map/ppermute | solution.py:606
  41.6 0.0 collective-permute-done.12.refs_1_.refs_4_
  41.7 0.1 collective-permute-start.13
  41.8 2.8 %collective-permute-start.14 = (bf16[112,128]{1,0:T(8,128)(2,1)S(1)}, bf16[112,128]{1,0:T(8,128)(2,1)S(1)}, u32[]{:S(2)}, u32[]{:S(2)}) collective-permute-start(bf16[112,128]{1,0:T(8,128)(2,1)S(1)} %get-tuple-element.98), channel_id=1, source_target_pairs={{0,2},{2,0},{4,6},{6,4},{8,10},{10,8},{12,14},{14,12},{16,18},{18,... | collective-permute-start | bytes 86024 | tf_op jit(solution)/shard_map/ppermute | solution.py:606
  44.5 0.0 collective-permute-done.13.refs_5_
  44.5 1.8 %collective-permute-done.14.refs_6_ = bf16[112,128]{1,0:T(8,128)(2,1)S(1)} collective-permute-done((bf16[112,128]{1,0:T(8,128)(2,1)S(1)}, bf16[112,128]{1,0:T(8,128)(2,1)S(1)}, u32[]{:S(2)}, u32[]{:S(2)}) %collective-permute-start.14) | collective-permute-done | bytes 28704 | tf_op jit(solution)/shard_map/ppermute | solution.py:606
  46.4 1.0 %shard_map.85 = (f32[1384,128]{1,0:T(8,128)S(1)}, f32[384,128]{1,0:T(8,128)S(1)}, bf16[384,128]{1,0:T(8,128)(2,1)S(1)}, bf16[592,128]{1,0:T(8,128)(2,1)S(1)}) custom-call(f32[1384,128]{1,0:T(8,128)S(1)} %get-tuple-element.91.refs_0_, f32[1384,128]{1,0:T(8,128)S(1)} %get-tuple-element.92.refs_1_.refs_2_, f32[1384,128]{1,0:T(8,128)S(1)} %get-tuple-element.80.refs_1_.refs_2_, ...), custom_call_target="tpu_custom_call" | custom-call | flops 400000000 | bytes 5459968 | tf_op jit(solution)/shard_map/pallas_call | solution.py:62
  47.4 1.3 %collective-permute-start.15 = (bf16[592,128]{1,0:T(8,128)(2,1)S(1)}, bf16[592,128]{1,0:T(8,128)(2,1)S(1)}, u32[]{:S(2)}, u32[]{:S(2)}) collective-permute-start(bf16[592,128]{1,0:T(8,128)(2,1)S(1)} %get-tuple-element.102), channel_id=1, source_target_pairs={{0,1},{1,0},{2,3},{3,2},{4,5},{5,4},{6,7},{7,6},{8,9},{9,8},{10,11... | collective-permute-start | bytes 454664 | tf_op jit(solution)/shard_map/ppermute | solution.py:648
  48.6 0.6 shard_map.86.refs_1_
  49.2 3.4 %collective-permute-done.15.refs_2_ = bf16[592,128]{1,0:T(8,128)(2,1)S(1)} collective-permute-done((bf16[592,128]{1,0:T(8,128)(2,1)S(1)}, bf16[592,128]{1,0:T(8,128)(2,1)S(1)}, u32[]{:S(2)}, u32[]{:S(2)}) %collective-permute-start.15) | collective-permute-done | bytes 151584 | tf_op jit(solution)/shard_map/ppermute | solution.py:648
  52.6 1.1 %shard_map.87 = (f32[1384,128]{1,0:T(8,128)S(1)}, f32[1384,128]{1,0:T(8,128)S(1)}, bf16[112,128]{1,0:T(8,128)(2,1)S(1)}, bf16[112,128]{1,0:T(8,128)(2,1)S(1)}, f...) custom-call(f32[1384,128]{1,0:T(8,128)S(1)} %get-tuple-element.99.refs_0_, f32[384,128]{1,0:T(8,128)S(1)} %shard_map.86.refs_1_, ...), custom_call_target="tpu_custom_call" | custom-call | flops 600000000 | bytes 5652992 | tf_op jit(solution)/shard_map/pallas_call | solution.py:62
  53.7 0.1 collective-permute-start.16
  53.8 1.0 %collective-permute-start.17 = (bf16[112,128]{1,0:T(8,128)(2,1)S(1)}, bf16[112,128]{1,0:T(8,128)(2,1)S(1)}, u32[]{:S(2)}, u32[]{:S(2)}) collective-permute-start(bf16[112,128]{1,0:T(8,128)(2,1)S(1)} %get-tuple-element.105), channel_id=1, source_target_pairs={{0,8},{2,10},{4,12},{6,14},{8,0},{10,2},{12,4},{14,6},{16,24},{18,... | collective-permute-start | bytes 86024 | tf_op jit(solution)/shard_map/ppermute | solution.py:606
  54.8 2.3 %collective-permute-done.16.refs_0_.refs_1_ = bf16[112,128]{1,0:T(8,128)(2,1)S(1)} collective-permute-done((bf16[112,128]{1,0:T(8,128)(2,1)S(1)}, bf16[112,128]{1,0:T(8,128)(2,1)S(1)}, u32[]{:S(2)}, u32[]{:S(2)}) %collective-permute-start.16) | collective-permute-done | bytes 28704 | tf_op jit(solution)/shard_map/ppermute | solution.py:606
  57.1 0.0 collective-permute-done.17.refs_1_.refs_2_
  57.1 0.1 collective-permute-start.18
  57.2 3.3 %collective-permute-start.19 = (bf16[112,128]{1,0:T(8,128)(2,1)S(1)}, bf16[112,128]{1,0:T(8,128)(2,1)S(1)}, u32[]{:S(2)}, u32[]{:S(2)}) collective-permute-start(bf16[112,128]{1,0:T(8,128)(2,1)S(1)} %get-tuple-element.109), channel_id=1, source_target_pairs={{0,2},{2,0},{4,6},{6,4},{8,10},{10,8},{12,14},{14,12},{16,18},{18,... | collective-permute-start | bytes 86024 | tf_op jit(solution)/shard_map/ppermute | solution.py:606
  60.5 0.0 collective-permute-done.18.refs_3_
  60.5 1.8 %collective-permute-done.19.refs_4_ = bf16[112,128]{1,0:T(8,128)(2,1)S(1)} collective-permute-done((bf16[112,128]{1,0:T(8,128)(2,1)S(1)}, bf16[112,128]{1,0:T(8,128)(2,1)S(1)}, u32[]{:S(2)}, u32[]{:S(2)}) %collective-permute-start.19) | collective-permute-done | bytes 28704 | tf_op jit(solution)/shard_map/ppermute | solution.py:606
  62.3 0.1 shard_map.89
  62.4 1.6 %collective-permute-start.20 = (bf16[208,128]{1,0:T(8,128)(2,1)S(1)}, bf16[208,128]{1,0:T(8,128)(2,1)S(1)}, u32[]{:S(2)}, u32[]{:S(2)}) collective-permute-start(bf16[208,128]{1,0:T(8,128)(2,1)S(1)} %get-tuple-element.112), channel_id=1, source_target_pairs={{0,1},{1,0},{2,3},{3,2},{4,5},{5,4},{6,7},{7,6},{8,9},{9,8},{10,11... | collective-permute-start | bytes 159752 | tf_op jit(solution)/shard_map/ppermute | solution.py:655
  64.0 0.2 shard_map.90.refs_0_
  64.2 2.4 %collective-permute-done.20.refs_1_ = bf16[208,128]{1,0:T(8,128)(2,1)S(1)} collective-permute-done((bf16[208,128]{1,0:T(8,128)(2,1)S(1)}, bf16[208,128]{1,0:T(8,128)(2,1)S(1)}, u32[]{:S(2)}, u32[]{:S(2)}) %collective-permute-start.20) | collective-permute-done | bytes 53280 | tf_op jit(solution)/shard_map/ppermute | solution.py:655
  66.6 0.9 %shard_map.91 = f32[13,13,7,128]{3,2,1,0:T(8,128)} custom-call(f32[1384,128]{1,0:T(8,128)S(1)} %shard_map.90.refs_0_, bf16[208,128]{1,0:T(8,128)(2,1)S(1)} %collective-permute-done.20.refs_1_), custom_call_target="tpu_custom_call" | custom-call | bytes 1367552 | tf_op jit(solution)/shard_map/pallas_call | solution.py:62
  (11 shorter events, 0.2 us)
Async XLA Ops:
  0.0 10.0 %copy-start = (f32[343,2,2,1]{0,3,2,1:T(1,128)S(1)}, f32[343,2,2,1]{0,3,2,1:T(1,128)}, u32[]{:S(2)}) copy-start(f32[343,2,2,1]{0,3,2,1:T(1,128)} %param.9) | copy-start | bytes 16468
  0.0 2.1 %copy-start.1 = (f32[13,13,7,128]{3,2,1,0:T(8,128)S(1)}, f32[13,13,7,128]{3,2,1,0:T(8,128)}, u32[]{:S(2)}) copy-start(f32[13,13,7,128]{3,2,1,0:T(8,128)} %refs_0_.1) | copy-start | bytes 1817092
  2.2 7.9 %collective-permute-start = (bf16[112,128]{1,0:T(8,128)(2,1)S(1)}, bf16[112,128]{1,0:T(8,128)(2,1)S(1)}, u32[]{:S(2)}, u32[]{:S(2)}) collective-permute-start(bf16[112,128]{1,0:T(8,128)(2,1)S(1)} %get-tuple-element.60), channel_id=1, source_target_pairs={{0,24},{2,26},{4,28},{6,30},{8,16},{10,18},{12,20},{14,22},{16,8},... | collective-permute-start | bytes 86024 | tf_op jit(solution)/shard_map/ppermute | solution.py:606
  4.6 8.7 %copy-start.2 = (bf16[343,343]{1,0:T(8,128)(2,1)S(1)}, bf16[343,343]{1,0:T(8,128)(2,1)}, u32[]{:S(2)}) copy-start(bf16[343,343]{1,0:T(8,128)(2,1)} %refs_1_.1) | copy-start | bytes 705898
  4.6 8.7 %copy-start.3 = (f32[64,12,12]{0,2,1:T(8,128)S(1)}, f32[64,12,12]{0,2,1:T(8,128)}, u32[]{:S(2)}) copy-start(f32[64,12,12]{0,2,1:T(8,128)} %param.13) | copy-start | bytes 110596
  4.6 8.7 %copy-start.4 = (s32[1,1,2,32]{3,2,1,0:T(2,128)S(1)}, s32[1,1,2,32]{3,2,1,0:T(2,128)}, u32[]{:S(2)}) copy-start(s32[1,1,2,32]{3,2,1,0:T(2,128)} %param.11) | copy-start | bytes 772
  4.6 5.4 %collective-permute-start.1 = (bf16[112,128]{1,0:T(8,128)(2,1)S(1)}, bf16[112,128]{1,0:T(8,128)(2,1)S(1)}, u32[]{:S(2)}, u32[]{:S(2)}) collective-permute-start(bf16[112,128]{1,0:T(8,128)(2,1)S(1)} %get-tuple-element.61), channel_id=1, source_target_pairs={{0,8},{2,10},{4,12},{6,14},{8,0},{10,2},{12,4},{14,6},{16,24},{18,... | collective-permute-start | bytes 86024 | tf_op jit(solution)/shard_map/ppermute | solution.py:606
  8.4 6.9 %collective-permute-start.4 = (bf16[384,256]{1,0:T(8,128)(2,1)S(1)}, bf16[384,256]{1,0:T(8,128)(2,1)S(1)}, u32[]{:S(2)}, u32[]{:S(2)}) collective-permute-start(bf16[384,256]{1,0:T(8,128)(2,1)S(1)} %get-tuple-element.68), channel_id=1, source_target_pairs={{1,0},{0,1},{3,2},{2,3},{5,4},{4,5},{7,6},{6,7},{9,8},{8,9},{11,10... | collective-permute-start | bytes 589832 | tf_op jit(solution)/shard_map/ppermute | solution.py:633
  10.1 5.1 %collective-permute-start.2 = (bf16[112,128]{1,0:T(8,128)(2,1)S(1)}, bf16[112,128]{1,0:T(8,128)(2,1)S(1)}, u32[]{:S(2)}, u32[]{:S(2)}) collective-permute-start(bf16[112,128]{1,0:T(8,128)(2,1)S(1)} %get-tuple-element.64), channel_id=1, source_target_pairs={{0,8},{2,4},{4,2},{6,14},{8,0},{10,12},{12,10},{14,6},{16,24},{18,... | collective-permute-start | bytes 86024 | tf_op jit(solution)/shard_map/ppermute | solution.py:606
  10.2 5.0 %collective-permute-start.3 = (bf16[112,128]{1,0:T(8,128)(2,1)S(1)}, bf16[112,128]{1,0:T(8,128)(2,1)S(1)}, u32[]{:S(2)}, u32[]{:S(2)}) collective-permute-start(bf16[112,128]{1,0:T(8,128)(2,1)S(1)} %get-tuple-element.65), channel_id=1, source_target_pairs={{0,2},{2,0},{4,6},{6,4},{8,10},{10,8},{12,14},{14,12},{16,18},{18,... | collective-permute-start | bytes 86024 | tf_op jit(solution)/shard_map/ppermute | solution.py:606
  16.2 5.3 %collective-permute-start.5 = (bf16[592,128]{1,0:T(8,128)(2,1)S(1)}, bf16[592,128]{1,0:T(8,128)(2,1)S(1)}, u32[]{:S(2)}, u32[]{:S(2)}) collective-permute-start(bf16[592,128]{1,0:T(8,128)(2,1)S(1)} %get-tuple-element.76), channel_id=1, source_target_pairs={{0,1},{1,0},{2,3},{3,2},{4,5},{5,4},{6,7},{7,6},{8,9},{9,8},{10,11... | collective-permute-start | bytes 454664 | tf_op jit(solution)/shard_map/ppermute | solution.py:648
  22.6 3.4 %collective-permute-start.6 = (bf16[112,128]{1,0:T(8,128)(2,1)S(1)}, bf16[112,128]{1,0:T(8,128)(2,1)S(1)}, u32[]{:S(2)}, u32[]{:S(2)}) collective-permute-start(bf16[112,128]{1,0:T(8,128)(2,1)S(1)} %get-tuple-element.81), channel_id=1, source_target_pairs={{0,24},{2,26},{4,28},{6,30},{8,16},{10,18},{12,20},{14,22},{16,8},... | collective-permute-start | bytes 86024 | tf_op jit(solution)/shard_map/ppermute | solution.py:606
  22.6 3.3 %collective-permute-start.7 = (bf16[112,128]{1,0:T(8,128)(2,1)S(1)}, bf16[112,128]{1,0:T(8,128)(2,1)S(1)}, u32[]{:S(2)}, u32[]{:S(2)}) collective-permute-start(bf16[112,128]{1,0:T(8,128)(2,1)S(1)} %get-tuple-element.82), channel_id=1, source_target_pairs={{0,8},{2,10},{4,12},{6,14},{8,0},{10,2},{12,4},{14,6},{16,24},{18,... | collective-permute-start | bytes 86024 | tf_op jit(solution)/shard_map/ppermute | solution.py:606
  25.9 3.2 %collective-permute-start.8 = (bf16[112,128]{1,0:T(8,128)(2,1)S(1)}, bf16[112,128]{1,0:T(8,128)(2,1)S(1)}, u32[]{:S(2)}, u32[]{:S(2)}) collective-permute-start(bf16[112,128]{1,0:T(8,128)(2,1)S(1)} %get-tuple-element.85), channel_id=1, source_target_pairs={{0,8},{2,4},{4,2},{6,14},{8,0},{10,12},{12,10},{14,6},{16,24},{18,... | collective-permute-start | bytes 86024 | tf_op jit(solution)/shard_map/ppermute | solution.py:606
  26.0 5.0 %collective-permute-start.9 = (bf16[112,128]{1,0:T(8,128)(2,1)S(1)}, bf16[112,128]{1,0:T(8,128)(2,1)S(1)}, u32[]{:S(2)}, u32[]{:S(2)}) collective-permute-start(bf16[112,128]{1,0:T(8,128)(2,1)S(1)} %get-tuple-element.86), channel_id=1, source_target_pairs={{0,2},{2,0},{4,6},{6,4},{8,10},{10,8},{12,14},{14,12},{16,18},{18,... | collective-permute-start | bytes 86024 | tf_op jit(solution)/shard_map/ppermute | solution.py:606
  31.9 5.3 %collective-permute-start.10 = (bf16[592,128]{1,0:T(8,128)(2,1)S(1)}, bf16[592,128]{1,0:T(8,128)(2,1)S(1)}, u32[]{:S(2)}, u32[]{:S(2)}) collective-permute-start(bf16[592,128]{1,0:T(8,128)(2,1)S(1)} %get-tuple-element.90), channel_id=1, source_target_pairs={{0,1},{1,0},{2,3},{3,2},{4,5},{5,4},{6,7},{7,6},{8,9},{9,8},{10,11... | collective-permute-start | bytes 454664 | tf_op jit(solution)/shard_map/ppermute | solution.py:648
  38.3 3.4 %collective-permute-start.11 = (bf16[112,128]{1,0:T(8,128)(2,1)S(1)}, bf16[112,128]{1,0:T(8,128)(2,1)S(1)}, u32[]{:S(2)}, u32[]{:S(2)}) collective-permute-start(bf16[112,128]{1,0:T(8,128)(2,1)S(1)} %get-tuple-element.93), channel_id=1, source_target_pairs={{0,24},{2,26},{4,28},{6,30},{8,16},{10,18},{12,20},{14,22},{16,8},... | collective-permute-start | bytes 86024 | tf_op jit(solution)/shard_map/ppermute | solution.py:606
  38.4 3.3 %collective-permute-start.12 = (bf16[112,128]{1,0:T(8,128)(2,1)S(1)}, bf16[112,128]{1,0:T(8,128)(2,1)S(1)}, u32[]{:S(2)}, u32[]{:S(2)}) collective-permute-start(bf16[112,128]{1,0:T(8,128)(2,1)S(1)} %get-tuple-element.94), channel_id=1, source_target_pairs={{0,8},{2,10},{4,12},{6,14},{8,0},{10,2},{12,4},{14,6},{16,24},{18,... | collective-permute-start | bytes 86024 | tf_op jit(solution)/shard_map/ppermute | solution.py:606
  41.7 2.9 %collective-permute-start.13 = (bf16[112,128]{1,0:T(8,128)(2,1)S(1)}, bf16[112,128]{1,0:T(8,128)(2,1)S(1)}, u32[]{:S(2)}, u32[]{:S(2)}) collective-permute-start(bf16[112,128]{1,0:T(8,128)(2,1)S(1)} %get-tuple-element.97), channel_id=1, source_target_pairs={{0,8},{2,4},{4,2},{6,14},{8,0},{10,12},{12,10},{14,6},{16,24},{18,... | collective-permute-start | bytes 86024 | tf_op jit(solution)/shard_map/ppermute | solution.py:606
  41.8 4.6 %collective-permute-start.14 = (bf16[112,128]{1,0:T(8,128)(2,1)S(1)}, bf16[112,128]{1,0:T(8,128)(2,1)S(1)}, u32[]{:S(2)}, u32[]{:S(2)}) collective-permute-start(bf16[112,128]{1,0:T(8,128)(2,1)S(1)} %get-tuple-element.98), channel_id=1, source_target_pairs={{0,2},{2,0},{4,6},{6,4},{8,10},{10,8},{12,14},{14,12},{16,18},{18,... | collective-permute-start | bytes 86024 | tf_op jit(solution)/shard_map/ppermute | solution.py:606
  47.4 5.3 %collective-permute-start.15 = (bf16[592,128]{1,0:T(8,128)(2,1)S(1)}, bf16[592,128]{1,0:T(8,128)(2,1)S(1)}, u32[]{:S(2)}, u32[]{:S(2)}) collective-permute-start(bf16[592,128]{1,0:T(8,128)(2,1)S(1)} %get-tuple-element.102), channel_id=1, source_target_pairs={{0,1},{1,0},{2,3},{3,2},{4,5},{5,4},{6,7},{7,6},{8,9},{9,8},{10,11... | collective-permute-start | bytes 454664 | tf_op jit(solution)/shard_map/ppermute | solution.py:648
  53.7 3.4 %collective-permute-start.16 = (bf16[112,128]{1,0:T(8,128)(2,1)S(1)}, bf16[112,128]{1,0:T(8,128)(2,1)S(1)}, u32[]{:S(2)}, u32[]{:S(2)}) collective-permute-start(bf16[112,128]{1,0:T(8,128)(2,1)S(1)} %get-tuple-element.104), channel_id=1, source_target_pairs={{0,24},{2,26},{4,28},{6,30},{8,16},{10,18},{12,20},{14,22},{16,8},... | collective-permute-start | bytes 86024 | tf_op jit(solution)/shard_map/ppermute | solution.py:606
  53.8 3.3 %collective-permute-start.17 = (bf16[112,128]{1,0:T(8,128)(2,1)S(1)}, bf16[112,128]{1,0:T(8,128)(2,1)S(1)}, u32[]{:S(2)}, u32[]{:S(2)}) collective-permute-start(bf16[112,128]{1,0:T(8,128)(2,1)S(1)} %get-tuple-element.105), channel_id=1, source_target_pairs={{0,8},{2,10},{4,12},{6,14},{8,0},{10,2},{12,4},{14,6},{16,24},{18,... | collective-permute-start | bytes 86024 | tf_op jit(solution)/shard_map/ppermute | solution.py:606
  57.1 3.3 %collective-permute-start.18 = (bf16[112,128]{1,0:T(8,128)(2,1)S(1)}, bf16[112,128]{1,0:T(8,128)(2,1)S(1)}, u32[]{:S(2)}, u32[]{:S(2)}) collective-permute-start(bf16[112,128]{1,0:T(8,128)(2,1)S(1)} %get-tuple-element.108), channel_id=1, source_target_pairs={{0,8},{2,4},{4,2},{6,14},{8,0},{10,12},{12,10},{14,6},{16,24},{18,... | collective-permute-start | bytes 86024 | tf_op jit(solution)/shard_map/ppermute | solution.py:606
  57.2 5.1 %collective-permute-start.19 = (bf16[112,128]{1,0:T(8,128)(2,1)S(1)}, bf16[112,128]{1,0:T(8,128)(2,1)S(1)}, u32[]{:S(2)}, u32[]{:S(2)}) collective-permute-start(bf16[112,128]{1,0:T(8,128)(2,1)S(1)} %get-tuple-element.109), channel_id=1, source_target_pairs={{0,2},{2,0},{4,6},{6,4},{8,10},{10,8},{12,14},{14,12},{16,18},{18,... | collective-permute-start | bytes 86024 | tf_op jit(solution)/shard_map/ppermute | solution.py:606
  62.4 4.2 %collective-permute-start.20 = (bf16[208,128]{1,0:T(8,128)(2,1)S(1)}, bf16[208,128]{1,0:T(8,128)(2,1)S(1)}, u32[]{:S(2)}, u32[]{:S(2)}) collective-permute-start(bf16[208,128]{1,0:T(8,128)(2,1)S(1)} %get-tuple-element.112), channel_id=1, source_target_pairs={{0,1},{1,0},{2,3},{3,2},{4,5},{5,4},{6,7},{7,6},{8,9},{9,8},{10,11... | collective-permute-start | bytes 159752 | tf_op jit(solution)/shard_map/ppermute | solution.py:655

commit v8 on v7

--- a/solution.py
+++ b/solution.py
@@ -138,9 +138,17 @@
     )
     i, block = i[:, :1], block[:, :1]
     row = (block >> (BLK.bit_length() - 1)) * PA + (i - block * PA)
-    key = cell.astype(jnp.int32) * SLOTS + row
-    targets = len(sz.cells) * SLOTS
-    pick = (key == iota(cols, targets, 1)).astype(BF16)
+    halves, group, width = [], cols // 2, SLOTS // 2
+    targets = len(sz.cells) * width
+    for h in range(2):
+        mine = slice(h * group, (h + 1) * group)
+        key = cell[mine].astype(jnp.int32) * width + (row[mine] - h * width)
+        pick = (key == iota(group, targets, 1)).astype(BF16)
+        halves.append(dot(proj[:, mine], pick))
+    parts = []
+    for g in range(len(sz.cells)):
+        parts += [half[:, g * width : (g + 1) * width] for half in halves]
+    summed = jnp.concatenate(parts, axis=1).astype(BF16)
     keys = [node_key(iota(sz.cell_pad, nodes, 0))]
     for j in range(sz.links):
         keys.append(
@@ -153,7 +161,6 @@
         low = iota(PAD * PAD, nodes, 0) & (PAD - 1)
         keys[-1] = jnp.where(low < EDGE, keys[-1], -1)
     expand = (jnp.concatenate(keys, axis=0) == iota(sz.cell_pad + sz.links * PAD * PAD, nodes, 1))
-    summed = dot(proj[...], pick).astype(BF16)
     full = dot(expand.astype(BF16), summed)
     for g in range(len(sz.cells)):
         value = full[:, g * SLOTS : (g + 1) * SLOTS]

time: 67.7 us -> 66.9 us (0.988)
  Pallas kernels: 14.2 us -> 13.4 us
    pallas_call x19, Pallas kernels: 14.2 us -> 13.4 us  [kernel_call(): pl.pallas_call(with_waits, out_shape=outs, in_specs=[VMEM] * used + [pl.B...]
  transfers between devices with their start and end apart: 21 -> 21, of which waited for: 11 -> 11; matrix products, arithmetic and copies ran while one was open for 0% -> 0% of each run, Pallas kernels for 10% -> 9%
where the time goes in v8:
time: 66.9 us; the launch traced here: 66.7 us
  starting transfers between devices  26.4 us (39%)
  waiting for transfers between devices  24.6 us (37%)
  Pallas kernels  13.4 us (20%)
  local copies, waits for them, and re-layouts  1.37 us (2%)
  other arithmetic  0.75 us (1%)
    ppermute x16, starting transfers between devices, swap_faces(): out.append(lax.ppermute(face, axes, pairs))  18.8 us
    pallas_call x19, Pallas kernels, kernel_call(): pl.pallas_call(with_waits, out_shape=outs, in_specs=[VMEM] * used + [pl.B...  13.4 us
    ppermute x16, waiting for transfers between devices, swap_faces(): out.append(lax.ppermute(face, axes, pairs))  12.6 us
    ppermute x3, waiting for transfers between devices, local(): lax.ppermute(m, 'gz', ring[s + 1])  9.5 us
    ppermute x3, starting transfers between devices, local(): lax.ppermute(m, 'gz', ring[s + 1])  4.43 us
    ppermute x1, waiting for transfers between devices, local(): zr = [lax.ppermute(f, 'gz', ring[s]) for f, s in zip(sent, link_shifts(sz))]  2.43 us
    ppermute x1, starting transfers between devices, local(): zr = [lax.ppermute(f, 'gz', ring[s]) for f, s in zip(sent, link_shifts(sz))]  1.58 us
    ppermute x1, starting transfers between devices, local(): qfaces.append(lax.ppermute(face_rows[j], 'gz', back))  1.58 us
  transfers between devices with their start and end apart: 21, of which 11 were waited for; matrix products, arithmetic and copies ran while one was open for 0% of the time, Pallas kernels for 9%

profile of v8, /device:TPU:0, one launch (start us, length us, event | category | flops | bytes accessed | tf_op | source)
XLA Modules:
  0.0 66.7 jit_solution(46446804844564893)
XLA Ops:
  0.0 0.0 copy-start
  0.0 0.8 %convert_bitcast_fusion.refs_1_ = f32[4,32]{1,0:T(4,128)S(1)} fusion(s32[1,1,1,32,4]{3,4,2,1,0:T(4,128)} %param.12), kind=kLoop, calls=%fused_computation.1 | loop fusion | flops 128 | bytes 1024 | tf_op jit(solution)/shard_map/convert_element_type | solution.py:626
  0.8 1.3 %pad.4.refs_2_.refs_0_ = bf16[352,1536]{1,0:T(8,128)(2,1)S(1)} pad(bf16[343,1536]{1,0:T(8,128)(2,1)} %bitcast.11, bf16[]{:T(256)} %constant.2.clone.1), padding=0_9x0_0 | pad | bytes 2135042 | tf_op jit(solution)/shard_map/jit(_pad)/pad | solution.py:625
  2.1 0.0 copy-done.1
  2.1 0.1 shard_map.73
  2.2 2.4 %collective-permute-start = (bf16[112,128]{1,0:T(8,128)(2,1)S(1)}, bf16[112,128]{1,0:T(8,128)(2,1)S(1)}, u32[]{:S(2)}, u32[]{:S(2)}) collective-permute-start(bf16[112,128]{1,0:T(8,128)(2,1)S(1)} %get-tuple-element.60), channel_id=1, source_target_pairs={{0,24},{2,26},{4,28},{6,30},{8,16},{10,18},{12,20},{14,22},{16,8},... | collective-permute-start | bytes 86024 | tf_op jit(solution)/shard_map/ppermute | solution.py:613
  4.6 0.7 %collective-permute-start.1 = (bf16[112,128]{1,0:T(8,128)(2,1)S(1)}, bf16[112,128]{1,0:T(8,128)(2,1)S(1)}, u32[]{:S(2)}, u32[]{:S(2)}) collective-permute-start(bf16[112,128]{1,0:T(8,128)(2,1)S(1)} %get-tuple-element.61), channel_id=1, source_target_pairs={{0,8},{2,10},{4,12},{6,14},{8,0},{10,2},{12,4},{14,6},{16,24},{18,... | collective-permute-start | bytes 86024 | tf_op jit(solution)/shard_map/ppermute | solution.py:613
  5.3 2.3 %shard_map.75 = (bf16[1664,384]{1,0:T(8,128)(2,1)S(1)}, bf16[384,256]{1,0:T(8,128)(2,1)S(1)}) custom-call(bf16[352,1536]{1,0:T(8,128)(2,1)S(1)} %pad.4.refs_2_.refs_0_, f32[4,32]{1,0:T(4,128)S(1)} %convert_bitcast_fusion.refs_1_), custom_call_target="tpu_custom_call" | custom-call | flops 3000000000 | bytes 2556416 | tf_op jit(solution)/shard_map/pallas_call | solution.py:62
  7.6 1.6 %collective-permute-start.4 = (bf16[384,256]{1,0:T(8,128)(2,1)S(1)}, bf16[384,256]{1,0:T(8,128)(2,1)S(1)}, u32[]{:S(2)}, u32[]{:S(2)}) collective-permute-start(bf16[384,256]{1,0:T(8,128)(2,1)S(1)} %get-tuple-element.68), channel_id=1, source_target_pairs={{1,0},{0,1},{3,2},{2,3},{5,4},{4,5},{7,6},{6,7},{9,8},{8,9},{11,10... | collective-permute-start | bytes 589832 | tf_op jit(solution)/shard_map/ppermute | solution.py:640
  9.2 0.0 copy-done
  9.3 0.0 collective-permute-done.refs_0_.refs_1_
  9.3 0.0 collective-permute-done.1.refs_1_.refs_2_
  9.3 0.1 collective-permute-start.2
  9.4 3.1 %collective-permute-start.3 = (bf16[112,128]{1,0:T(8,128)(2,1)S(1)}, bf16[112,128]{1,0:T(8,128)(2,1)S(1)}, u32[]{:S(2)}, u32[]{:S(2)}) collective-permute-start(bf16[112,128]{1,0:T(8,128)(2,1)S(1)} %get-tuple-element.65), channel_id=1, source_target_pairs={{0,2},{2,0},{4,6},{6,4},{8,10},{10,8},{12,14},{14,12},{16,18},{18,... | collective-permute-start | bytes 86024 | tf_op jit(solution)/shard_map/ppermute | solution.py:613
  12.6 0.0 copy-done.2
  12.6 0.0 copy-done.3
  12.6 1.8 %shard_map.76 = (bf16[384,1664]{1,0:T(8,128)(2,1)S(1)}, bf16[400,400]{1,0:T(8,128)(2,1)S(1)}, f32[1600,128]{1,0:T(8,128)S(1)}, bf16[384,768]{1,0:T(8,128)(2,1)S(...) custom-call(bf16[1664,384]{1,0:T(8,128)(2,1)S(1)} %get-tuple-element.66.refs_0_.refs_5_, ...), custom_call_target="tpu_custom_call" | custom-call | flops 1000000000 | bytes 5447570 | tf_op jit(solution)/shard_map/pallas_call | solution.py:62
  14.4 0.0 collective-permute-done.2.refs_3_
  14.4 0.0 collective-permute-done.3.refs_4_
  14.4 0.1 collective-permute-done.4.refs_6_.refs_7_.refs_8_
  14.5 0.9 %shard_map.77 = (f32[1384,128]{1,0:T(8,128)S(1)}, f32[384,128]{1,0:T(8,128)S(1)}, bf16[384,128]{1,0:T(8,128)(2,1)S(1)}, bf16[592,128]{1,0:T(8,128)(2,1)S(1)}) custom-call(f32[1384,128]{1,0:T(8,128)S(1)} %get-tuple-element.59.refs_0_, bf16[112,128]{1,0:T(8,128)(2,1)S(1)} %collective-permute-done.refs_0_.refs_1_, ...), custom_call_target="tpu_custom_call" | custom-call | flops 400000000 | bytes 4042752 | tf_op jit(solution)/shard_map/pallas_call | solution.py:62
  15.4 1.6 %collective-permute-start.5 = (bf16[592,128]{1,0:T(8,128)(2,1)S(1)}, bf16[592,128]{1,0:T(8,128)(2,1)S(1)}, u32[]{:S(2)}, u32[]{:S(2)}) collective-permute-start(bf16[592,128]{1,0:T(8,128)(2,1)S(1)} %get-tuple-element.76), channel_id=1, source_target_pairs={{0,1},{1,0},{2,3},{3,2},{4,5},{5,4},{6,7},{7,6},{8,9},{9,8},{10,11... | collective-permute-start | bytes 454664 | tf_op jit(solution)/shard_map/ppermute | solution.py:655
  17.0 0.6 shard_map.78.refs_1_
  17.6 3.1 %collective-permute-done.5.refs_2_ = bf16[592,128]{1,0:T(8,128)(2,1)S(1)} collective-permute-done((bf16[592,128]{1,0:T(8,128)(2,1)S(1)}, bf16[592,128]{1,0:T(8,128)(2,1)S(1)}, u32[]{:S(2)}, u32[]{:S(2)}) %collective-permute-start.5) | collective-permute-done | bytes 151584 | tf_op jit(solution)/shard_map/ppermute | solution.py:655
  20.7 1.1 %shard_map.79 = (f32[1384,128]{1,0:T(8,128)S(1)}, f32[1384,128]{1,0:T(8,128)S(1)}, bf16[112,128]{1,0:T(8,128)(2,1)S(1)}, bf16[112,128]{1,0:T(8,128)(2,1)S(1)}, f...) custom-call(f32[1384,128]{1,0:T(8,128)S(1)} %get-tuple-element.70.refs_0_, f32[384,128]{1,0:T(8,128)S(1)} %shard_map.78.refs_1_, ...), custom_call_target="tpu_custom_call" | custom-call | flops 600000000 | bytes 5652992 | tf_op jit(solution)/shard_map/pallas_call | solution.py:62
  21.8 0.1 collective-permute-start.6
  21.8 0.9 %collective-permute-start.7 = (bf16[112,128]{1,0:T(8,128)(2,1)S(1)}, bf16[112,128]{1,0:T(8,128)(2,1)S(1)}, u32[]{:S(2)}, u32[]{:S(2)}) collective-permute-start(bf16[112,128]{1,0:T(8,128)(2,1)S(1)} %get-tuple-element.82), channel_id=1, source_target_pairs={{0,8},{2,10},{4,12},{6,14},{8,0},{10,2},{12,4},{14,6},{16,24},{18,... | collective-permute-start | bytes 86024 | tf_op jit(solution)/shard_map/ppermute | solution.py:613
  22.7 2.4 %collective-permute-done.6.refs_0_.refs_2_ = bf16[112,128]{1,0:T(8,128)(2,1)S(1)} collective-permute-done((bf16[112,128]{1,0:T(8,128)(2,1)S(1)}, bf16[112,128]{1,0:T(8,128)(2,1)S(1)}, u32[]{:S(2)}, u32[]{:S(2)}) %collective-permute-start.6) | collective-permute-done | bytes 28704 | tf_op jit(solution)/shard_map/ppermute | solution.py:613
  25.1 0.0 collective-permute-done.7.refs_1_.refs_3_
  25.1 0.1 collective-permute-start.8
  25.2 3.1 %collective-permute-start.9 = (bf16[112,128]{1,0:T(8,128)(2,1)S(1)}, bf16[112,128]{1,0:T(8,128)(2,1)S(1)}, u32[]{:S(2)}, u32[]{:S(2)}) collective-permute-start(bf16[112,128]{1,0:T(8,128)(2,1)S(1)} %get-tuple-element.86), channel_id=1, source_target_pairs={{0,2},{2,0},{4,6},{6,4},{8,10},{10,8},{12,14},{14,12},{16,18},{18,... | collective-permute-start | bytes 86024 | tf_op jit(solution)/shard_map/ppermute | solution.py:613
  28.4 0.0 collective-permute-done.8.refs_4_
  28.4 1.8 %collective-permute-done.9.refs_5_ = bf16[112,128]{1,0:T(8,128)(2,1)S(1)} collective-permute-done((bf16[112,128]{1,0:T(8,128)(2,1)S(1)}, bf16[112,128]{1,0:T(8,128)(2,1)S(1)}, u32[]{:S(2)}, u32[]{:S(2)}) %collective-permute-start.9) | collective-permute-done | bytes 28704 | tf_op jit(solution)/shard_map/ppermute | solution.py:613
  30.2 0.9 %shard_map.81 = (f32[1384,128]{1,0:T(8,128)S(1)}, f32[384,128]{1,0:T(8,128)S(1)}, bf16[384,128]{1,0:T(8,128)(2,1)S(1)}, bf16[592,128]{1,0:T(8,128)(2,1)S(1)}) custom-call(f32[1384,128]{1,0:T(8,128)S(1)} %get-tuple-element.79.refs_0_, f32[1384,128]{1,0:T(8,128)S(1)} %get-tuple-element.80.refs_1_.refs_2_, ...), custom_call_target="tpu_custom_call" | custom-call | flops 400000000 | bytes 4751360 | tf_op jit(solution)/shard_map/pallas_call | solution.py:62
  31.1 1.6 %collective-permute-start.10 = (bf16[592,128]{1,0:T(8,128)(2,1)S(1)}, bf16[592,128]{1,0:T(8,128)(2,1)S(1)}, u32[]{:S(2)}, u32[]{:S(2)}) collective-permute-start(bf16[592,128]{1,0:T(8,128)(2,1)S(1)} %get-tuple-element.90), channel_id=1, source_target_pairs={{0,1},{1,0},{2,3},{3,2},{4,5},{5,4},{6,7},{7,6},{8,9},{9,8},{10,11... | collective-permute-start | bytes 454664 | tf_op jit(solution)/shard_map/ppermute | solution.py:655
  32.7 0.6 shard_map.82.refs_1_
  33.3 3.1 %collective-permute-done.10.refs_2_ = bf16[592,128]{1,0:T(8,128)(2,1)S(1)} collective-permute-done((bf16[592,128]{1,0:T(8,128)(2,1)S(1)}, bf16[592,128]{1,0:T(8,128)(2,1)S(1)}, u32[]{:S(2)}, u32[]{:S(2)}) %collective-permute-start.10) | collective-permute-done | bytes 151584 | tf_op jit(solution)/shard_map/ppermute | solution.py:655
  36.4 1.1 %shard_map.83 = (f32[1384,128]{1,0:T(8,128)S(1)}, f32[1384,128]{1,0:T(8,128)S(1)}, bf16[112,128]{1,0:T(8,128)(2,1)S(1)}, bf16[112,128]{1,0:T(8,128)(2,1)S(1)}, f...) custom-call(f32[1384,128]{1,0:T(8,128)S(1)} %get-tuple-element.87.refs_0_, f32[384,128]{1,0:T(8,128)S(1)} %shard_map.82.refs_1_, ...), custom_call_target="tpu_custom_call" | custom-call | flops 600000000 | bytes 5652992 | tf_op jit(solution)/shard_map/pallas_call | solution.py:62
  37.5 0.1 collective-permute-start.11
  37.6 0.9 %collective-permute-start.12 = (bf16[112,128]{1,0:T(8,128)(2,1)S(1)}, bf16[112,128]{1,0:T(8,128)(2,1)S(1)}, u32[]{:S(2)}, u32[]{:S(2)}) collective-permute-start(bf16[112,128]{1,0:T(8,128)(2,1)S(1)} %get-tuple-element.94), channel_id=1, source_target_pairs={{0,8},{2,10},{4,12},{6,14},{8,0},{10,2},{12,4},{14,6},{16,24},{18,... | collective-permute-start | bytes 86024 | tf_op jit(solution)/shard_map/ppermute | solution.py:613
  38.5 2.4 %collective-permute-done.11.refs_0_.refs_3_ = bf16[112,128]{1,0:T(8,128)(2,1)S(1)} collective-permute-done((bf16[112,128]{1,0:T(8,128)(2,1)S(1)}, bf16[112,128]{1,0:T(8,128)(2,1)S(1)}, u32[]{:S(2)}, u32[]{:S(2)}) %collective-permute-start.11) | collective-permute-done | bytes 28704 | tf_op jit(solution)/shard_map/ppermute | solution.py:613
  40.8 0.0 collective-permute-done.12.refs_1_.refs_4_
  40.9 0.1 collective-permute-start.13
  41.0 2.8 %collective-permute-start.14 = (bf16[112,128]{1,0:T(8,128)(2,1)S(1)}, bf16[112,128]{1,0:T(8,128)(2,1)S(1)}, u32[]{:S(2)}, u32[]{:S(2)}) collective-permute-start(bf16[112,128]{1,0:T(8,128)(2,1)S(1)} %get-tuple-element.98), channel_id=1, source_target_pairs={{0,2},{2,0},{4,6},{6,4},{8,10},{10,8},{12,14},{14,12},{16,18},{18,... | collective-permute-start | bytes 86024 | tf_op jit(solution)/shard_map/ppermute | solution.py:613
  43.7 0.0 collective-permute-done.13.refs_5_
  43.7 1.8 %collective-permute-done.14.refs_6_ = bf16[112,128]{1,0:T(8,128)(2,1)S(1)} collective-permute-done((bf16[112,128]{1,0:T(8,128)(2,1)S(1)}, bf16[112,128]{1,0:T(8,128)(2,1)S(1)}, u32[]{:S(2)}, u32[]{:S(2)}) %collective-permute-start.14) | collective-permute-done | bytes 28704 | tf_op jit(solution)/shard_map/ppermute | solution.py:613
  45.6 1.0 %shard_map.85 = (f32[1384,128]{1,0:T(8,128)S(1)}, f32[384,128]{1,0:T(8,128)S(1)}, bf16[384,128]{1,0:T(8,128)(2,1)S(1)}, bf16[592,128]{1,0:T(8,128)(2,1)S(1)}) custom-call(f32[1384,128]{1,0:T(8,128)S(1)} %get-tuple-element.91.refs_0_, f32[1384,128]{1,0:T(8,128)S(1)} %get-tuple-element.92.refs_1_.refs_2_, f32[1384,128]{1,0:T(8,128)S(1)} %get-tuple-element.80.refs_1_.refs_2_, ...), custom_call_target="tpu_custom_call" | custom-call | flops 400000000 | bytes 5459968 | tf_op jit(solution)/shard_map/pallas_call | solution.py:62
  46.6 1.3 %collective-permute-start.15 = (bf16[592,128]{1,0:T(8,128)(2,1)S(1)}, bf16[592,128]{1,0:T(8,128)(2,1)S(1)}, u32[]{:S(2)}, u32[]{:S(2)}) collective-permute-start(bf16[592,128]{1,0:T(8,128)(2,1)S(1)} %get-tuple-element.102), channel_id=1, source_target_pairs={{0,1},{1,0},{2,3},{3,2},{4,5},{5,4},{6,7},{7,6},{8,9},{9,8},{10,11... | collective-permute-start | bytes 454664 | tf_op jit(solution)/shard_map/ppermute | solution.py:655
  47.8 0.6 shard_map.86.refs_1_
  48.4 3.4 %collective-permute-done.15.refs_2_ = bf16[592,128]{1,0:T(8,128)(2,1)S(1)} collective-permute-done((bf16[592,128]{1,0:T(8,128)(2,1)S(1)}, bf16[592,128]{1,0:T(8,128)(2,1)S(1)}, u32[]{:S(2)}, u32[]{:S(2)}) %collective-permute-start.15) | collective-permute-done | bytes 151584 | tf_op jit(solution)/shard_map/ppermute | solution.py:655
  51.8 1.1 %shard_map.87 = (f32[1384,128]{1,0:T(8,128)S(1)}, f32[1384,128]{1,0:T(8,128)S(1)}, bf16[112,128]{1,0:T(8,128)(2,1)S(1)}, bf16[112,128]{1,0:T(8,128)(2,1)S(1)}, f...) custom-call(f32[1384,128]{1,0:T(8,128)S(1)} %get-tuple-element.99.refs_0_, f32[384,128]{1,0:T(8,128)S(1)} %shard_map.86.refs_1_, ...), custom_call_target="tpu_custom_call" | custom-call | flops 600000000 | bytes 5652992 | tf_op jit(solution)/shard_map/pallas_call | solution.py:62
  52.9 0.1 collective-permute-start.16
  53.0 1.0 %collective-permute-start.17 = (bf16[112,128]{1,0:T(8,128)(2,1)S(1)}, bf16[112,128]{1,0:T(8,128)(2,1)S(1)}, u32[]{:S(2)}, u32[]{:S(2)}) collective-permute-start(bf16[112,128]{1,0:T(8,128)(2,1)S(1)} %get-tuple-element.105), channel_id=1, source_target_pairs={{0,8},{2,10},{4,12},{6,14},{8,0},{10,2},{12,4},{14,6},{16,24},{18,... | collective-permute-start | bytes 86024 | tf_op jit(solution)/shard_map/ppermute | solution.py:613
  54.0 2.3 %collective-permute-done.16.refs_0_.refs_1_ = bf16[112,128]{1,0:T(8,128)(2,1)S(1)} collective-permute-done((bf16[112,128]{1,0:T(8,128)(2,1)S(1)}, bf16[112,128]{1,0:T(8,128)(2,1)S(1)}, u32[]{:S(2)}, u32[]{:S(2)}) %collective-permute-start.16) | collective-permute-done | bytes 28704 | tf_op jit(solution)/shard_map/ppermute | solution.py:613
  56.3 0.0 collective-permute-done.17.refs_1_.refs_2_
  56.3 0.1 collective-permute-start.18
  56.4 3.3 %collective-permute-start.19 = (bf16[112,128]{1,0:T(8,128)(2,1)S(1)}, bf16[112,128]{1,0:T(8,128)(2,1)S(1)}, u32[]{:S(2)}, u32[]{:S(2)}) collective-permute-start(bf16[112,128]{1,0:T(8,128)(2,1)S(1)} %get-tuple-element.109), channel_id=1, source_target_pairs={{0,2},{2,0},{4,6},{6,4},{8,10},{10,8},{12,14},{14,12},{16,18},{18,... | collective-permute-start | bytes 86024 | tf_op jit(solution)/shard_map/ppermute | solution.py:613
  59.7 0.0 collective-permute-done.18.refs_3_
  59.7 1.8 %collective-permute-done.19.refs_4_ = bf16[112,128]{1,0:T(8,128)(2,1)S(1)} collective-permute-done((bf16[112,128]{1,0:T(8,128)(2,1)S(1)}, bf16[112,128]{1,0:T(8,128)(2,1)S(1)}, u32[]{:S(2)}, u32[]{:S(2)}) %collective-permute-start.19) | collective-permute-done | bytes 28704 | tf_op jit(solution)/shard_map/ppermute | solution.py:613
  61.5 0.1 shard_map.89
  61.6 1.6 %collective-permute-start.20 = (bf16[208,128]{1,0:T(8,128)(2,1)S(1)}, bf16[208,128]{1,0:T(8,128)(2,1)S(1)}, u32[]{:S(2)}, u32[]{:S(2)}) collective-permute-start(bf16[208,128]{1,0:T(8,128)(2,1)S(1)} %get-tuple-element.112), channel_id=1, source_target_pairs={{0,1},{1,0},{2,3},{3,2},{4,5},{5,4},{6,7},{7,6},{8,9},{9,8},{10,11... | collective-permute-start | bytes 159752 | tf_op jit(solution)/shard_map/ppermute | solution.py:662
  63.2 0.2 shard_map.90.refs_0_
  63.4 2.4 %collective-permute-done.20.refs_1_ = bf16[208,128]{1,0:T(8,128)(2,1)S(1)} collective-permute-done((bf16[208,128]{1,0:T(8,128)(2,1)S(1)}, bf16[208,128]{1,0:T(8,128)(2,1)S(1)}, u32[]{:S(2)}, u32[]{:S(2)}) %collective-permute-start.20) | collective-permute-done | bytes 53280 | tf_op jit(solution)/shard_map/ppermute | solution.py:662
  65.8 0.9 %shard_map.91 = f32[13,13,7,128]{3,2,1,0:T(8,128)} custom-call(f32[1384,128]{1,0:T(8,128)S(1)} %shard_map.90.refs_0_, bf16[208,128]{1,0:T(8,128)(2,1)S(1)} %collective-permute-done.20.refs_1_), custom_call_target="tpu_custom_call" | custom-call | bytes 1367552 | tf_op jit(solution)/shard_map/pallas_call | solution.py:62
  (11 shorter events, 0.2 us)
Async XLA Ops:
  0.0 9.2 %copy-start = (f32[343,2,2,1]{0,3,2,1:T(1,128)S(1)}, f32[343,2,2,1]{0,3,2,1:T(1,128)}, u32[]{:S(2)}) copy-start(f32[343,2,2,1]{0,3,2,1:T(1,128)} %param.9) | copy-start | bytes 16468
  0.0 2.1 %copy-start.1 = (f32[13,13,7,128]{3,2,1,0:T(8,128)S(1)}, f32[13,13,7,128]{3,2,1,0:T(8,128)}, u32[]{:S(2)}) copy-start(f32[13,13,7,128]{3,2,1,0:T(8,128)} %refs_0_.1) | copy-start | bytes 1817092
  2.2 7.1 %collective-permute-start = (bf16[112,128]{1,0:T(8,128)(2,1)S(1)}, bf16[112,128]{1,0:T(8,128)(2,1)S(1)}, u32[]{:S(2)}, u32[]{:S(2)}) collective-permute-start(bf16[112,128]{1,0:T(8,128)(2,1)S(1)} %get-tuple-element.60), channel_id=1, source_target_pairs={{0,24},{2,26},{4,28},{6,30},{8,16},{10,18},{12,20},{14,22},{16,8},... | collective-permute-start | bytes 86024 | tf_op jit(solution)/shard_map/ppermute | solution.py:613
  4.6 7.9 %copy-start.2 = (bf16[343,343]{1,0:T(8,128)(2,1)S(1)}, bf16[343,343]{1,0:T(8,128)(2,1)}, u32[]{:S(2)}) copy-start(bf16[343,343]{1,0:T(8,128)(2,1)} %refs_1_.1) | copy-start | bytes 705898
  4.6 7.9 %copy-start.3 = (f32[64,12,12]{0,2,1:T(8,128)S(1)}, f32[64,12,12]{0,2,1:T(8,128)}, u32[]{:S(2)}) copy-start(f32[64,12,12]{0,2,1:T(8,128)} %param.13) | copy-start | bytes 110596
  4.6 7.9 %copy-start.4 = (s32[1,1,2,32]{3,2,1,0:T(2,128)S(1)}, s32[1,1,2,32]{3,2,1,0:T(2,128)}, u32[]{:S(2)}) copy-start(s32[1,1,2,32]{3,2,1,0:T(2,128)} %param.11) | copy-start | bytes 772
  4.6 4.6 %collective-permute-start.1 = (bf16[112,128]{1,0:T(8,128)(2,1)S(1)}, bf16[112,128]{1,0:T(8,128)(2,1)S(1)}, u32[]{:S(2)}, u32[]{:S(2)}) collective-permute-start(bf16[112,128]{1,0:T(8,128)(2,1)S(1)} %get-tuple-element.61), channel_id=1, source_target_pairs={{0,8},{2,10},{4,12},{6,14},{8,0},{10,2},{12,4},{14,6},{16,24},{18,... | collective-permute-start | bytes 86024 | tf_op jit(solution)/shard_map/ppermute | solution.py:613
  7.6 6.9 %collective-permute-start.4 = (bf16[384,256]{1,0:T(8,128)(2,1)S(1)}, bf16[384,256]{1,0:T(8,128)(2,1)S(1)}, u32[]{:S(2)}, u32[]{:S(2)}) collective-permute-start(bf16[384,256]{1,0:T(8,128)(2,1)S(1)} %get-tuple-element.68), channel_id=1, source_target_pairs={{1,0},{0,1},{3,2},{2,3},{5,4},{4,5},{7,6},{6,7},{9,8},{8,9},{11,10... | collective-permute-start | bytes 589832 | tf_op jit(solution)/shard_map/ppermute | solution.py:640
  9.3 5.1 %collective-permute-start.2 = (bf16[112,128]{1,0:T(8,128)(2,1)S(1)}, bf16[112,128]{1,0:T(8,128)(2,1)S(1)}, u32[]{:S(2)}, u32[]{:S(2)}) collective-permute-start(bf16[112,128]{1,0:T(8,128)(2,1)S(1)} %get-tuple-element.64), channel_id=1, source_target_pairs={{0,8},{2,4},{4,2},{6,14},{8,0},{10,12},{12,10},{14,6},{16,24},{18,... | collective-permute-start | bytes 86024 | tf_op jit(solution)/shard_map/ppermute | solution.py:613
  9.4 5.0 %collective-permute-start.3 = (bf16[112,128]{1,0:T(8,128)(2,1)S(1)}, bf16[112,128]{1,0:T(8,128)(2,1)S(1)}, u32[]{:S(2)}, u32[]{:S(2)}) collective-permute-start(bf16[112,128]{1,0:T(8,128)(2,1)S(1)} %get-tuple-element.65), channel_id=1, source_target_pairs={{0,2},{2,0},{4,6},{6,4},{8,10},{10,8},{12,14},{14,12},{16,18},{18,... | collective-permute-start | bytes 86024 | tf_op jit(solution)/shard_map/ppermute | solution.py:613
  15.4 5.3 %collective-permute-start.5 = (bf16[592,128]{1,0:T(8,128)(2,1)S(1)}, bf16[592,128]{1,0:T(8,128)(2,1)S(1)}, u32[]{:S(2)}, u32[]{:S(2)}) collective-permute-start(bf16[592,128]{1,0:T(8,128)(2,1)S(1)} %get-tuple-element.76), channel_id=1, source_target_pairs={{0,1},{1,0},{2,3},{3,2},{4,5},{5,4},{6,7},{7,6},{8,9},{9,8},{10,11... | collective-permute-start | bytes 454664 | tf_op jit(solution)/shard_map/ppermute | solution.py:655
  21.8 3.4 %collective-permute-start.6 = (bf16[112,128]{1,0:T(8,128)(2,1)S(1)}, bf16[112,128]{1,0:T(8,128)(2,1)S(1)}, u32[]{:S(2)}, u32[]{:S(2)}) collective-permute-start(bf16[112,128]{1,0:T(8,128)(2,1)S(1)} %get-tuple-element.81), channel_id=1, source_target_pairs={{0,24},{2,26},{4,28},{6,30},{8,16},{10,18},{12,20},{14,22},{16,8},... | collective-permute-start | bytes 86024 | tf_op jit(solution)/shard_map/ppermute | solution.py:613
  21.8 3.3 %collective-permute-start.7 = (bf16[112,128]{1,0:T(8,128)(2,1)S(1)}, bf16[112,128]{1,0:T(8,128)(2,1)S(1)}, u32[]{:S(2)}, u32[]{:S(2)}) collective-permute-start(bf16[112,128]{1,0:T(8,128)(2,1)S(1)} %get-tuple-element.82), channel_id=1, source_target_pairs={{0,8},{2,10},{4,12},{6,14},{8,0},{10,2},{12,4},{14,6},{16,24},{18,... | collective-permute-start | bytes 86024 | tf_op jit(solution)/shard_map/ppermute | solution.py:613
  25.1 3.2 %collective-permute-start.8 = (bf16[112,128]{1,0:T(8,128)(2,1)S(1)}, bf16[112,128]{1,0:T(8,128)(2,1)S(1)}, u32[]{:S(2)}, u32[]{:S(2)}) collective-permute-start(bf16[112,128]{1,0:T(8,128)(2,1)S(1)} %get-tuple-element.85), channel_id=1, source_target_pairs={{0,8},{2,4},{4,2},{6,14},{8,0},{10,12},{12,10},{14,6},{16,24},{18,... | collective-permute-start | bytes 86024 | tf_op jit(solution)/shard_map/ppermute | solution.py:613
  25.2 5.0 %collective-permute-start.9 = (bf16[112,128]{1,0:T(8,128)(2,1)S(1)}, bf16[112,128]{1,0:T(8,128)(2,1)S(1)}, u32[]{:S(2)}, u32[]{:S(2)}) collective-permute-start(bf16[112,128]{1,0:T(8,128)(2,1)S(1)} %get-tuple-element.86), channel_id=1, source_target_pairs={{0,2},{2,0},{4,6},{6,4},{8,10},{10,8},{12,14},{14,12},{16,18},{18,... | collective-permute-start | bytes 86024 | tf_op jit(solution)/shard_map/ppermute | solution.py:613
  31.1 5.3 %collective-permute-start.10 = (bf16[592,128]{1,0:T(8,128)(2,1)S(1)}, bf16[592,128]{1,0:T(8,128)(2,1)S(1)}, u32[]{:S(2)}, u32[]{:S(2)}) collective-permute-start(bf16[592,128]{1,0:T(8,128)(2,1)S(1)} %get-tuple-element.90), channel_id=1, source_target_pairs={{0,1},{1,0},{2,3},{3,2},{4,5},{5,4},{6,7},{7,6},{8,9},{9,8},{10,11... | collective-permute-start | bytes 454664 | tf_op jit(solution)/shard_map/ppermute | solution.py:655
  37.5 3.4 %collective-permute-start.11 = (bf16[112,128]{1,0:T(8,128)(2,1)S(1)}, bf16[112,128]{1,0:T(8,128)(2,1)S(1)}, u32[]{:S(2)}, u32[]{:S(2)}) collective-permute-start(bf16[112,128]{1,0:T(8,128)(2,1)S(1)} %get-tuple-element.93), channel_id=1, source_target_pairs={{0,24},{2,26},{4,28},{6,30},{8,16},{10,18},{12,20},{14,22},{16,8},... | collective-permute-start | bytes 86024 | tf_op jit(solution)/shard_map/ppermute | solution.py:613
  37.6 3.3 %collective-permute-start.12 = (bf16[112,128]{1,0:T(8,128)(2,1)S(1)}, bf16[112,128]{1,0:T(8,128)(2,1)S(1)}, u32[]{:S(2)}, u32[]{:S(2)}) collective-permute-start(bf16[112,128]{1,0:T(8,128)(2,1)S(1)} %get-tuple-element.94), channel_id=1, source_target_pairs={{0,8},{2,10},{4,12},{6,14},{8,0},{10,2},{12,4},{14,6},{16,24},{18,... | collective-permute-start | bytes 86024 | tf_op jit(solution)/shard_map/ppermute | solution.py:613
  40.9 2.9 %collective-permute-start.13 = (bf16[112,128]{1,0:T(8,128)(2,1)S(1)}, bf16[112,128]{1,0:T(8,128)(2,1)S(1)}, u32[]{:S(2)}, u32[]{:S(2)}) collective-permute-start(bf16[112,128]{1,0:T(8,128)(2,1)S(1)} %get-tuple-element.97), channel_id=1, source_target_pairs={{0,8},{2,4},{4,2},{6,14},{8,0},{10,12},{12,10},{14,6},{16,24},{18,... | collective-permute-start | bytes 86024 | tf_op jit(solution)/shard_map/ppermute | solution.py:613
  41.0 4.6 %collective-permute-start.14 = (bf16[112,128]{1,0:T(8,128)(2,1)S(1)}, bf16[112,128]{1,0:T(8,128)(2,1)S(1)}, u32[]{:S(2)}, u32[]{:S(2)}) collective-permute-start(bf16[112,128]{1,0:T(8,128)(2,1)S(1)} %get-tuple-element.98), channel_id=1, source_target_pairs={{0,2},{2,0},{4,6},{6,4},{8,10},{10,8},{12,14},{14,12},{16,18},{18,... | collective-permute-start | bytes 86024 | tf_op jit(solution)/shard_map/ppermute | solution.py:613
  46.6 5.3 %collective-permute-start.15 = (bf16[592,128]{1,0:T(8,128)(2,1)S(1)}, bf16[592,128]{1,0:T(8,128)(2,1)S(1)}, u32[]{:S(2)}, u32[]{:S(2)}) collective-permute-start(bf16[592,128]{1,0:T(8,128)(2,1)S(1)} %get-tuple-element.102), channel_id=1, source_target_pairs={{0,1},{1,0},{2,3},{3,2},{4,5},{5,4},{6,7},{7,6},{8,9},{9,8},{10,11... | collective-permute-start | bytes 454664 | tf_op jit(solution)/shard_map/ppermute | solution.py:655
  52.9 3.4 %collective-permute-start.16 = (bf16[112,128]{1,0:T(8,128)(2,1)S(1)}, bf16[112,128]{1,0:T(8,128)(2,1)S(1)}, u32[]{:S(2)}, u32[]{:S(2)}) collective-permute-start(bf16[112,128]{1,0:T(8,128)(2,1)S(1)} %get-tuple-element.104), channel_id=1, source_target_pairs={{0,24},{2,26},{4,28},{6,30},{8,16},{10,18},{12,20},{14,22},{16,8},... | collective-permute-start | bytes 86024 | tf_op jit(solution)/shard_map/ppermute | solution.py:613
  53.0 3.3 %collective-permute-start.17 = (bf16[112,128]{1,0:T(8,128)(2,1)S(1)}, bf16[112,128]{1,0:T(8,128)(2,1)S(1)}, u32[]{:S(2)}, u32[]{:S(2)}) collective-permute-start(bf16[112,128]{1,0:T(8,128)(2,1)S(1)} %get-tuple-element.105), channel_id=1, source_target_pairs={{0,8},{2,10},{4,12},{6,14},{8,0},{10,2},{12,4},{14,6},{16,24},{18,... | collective-permute-start | bytes 86024 | tf_op jit(solution)/shard_map/ppermute | solution.py:613
  56.3 3.3 %collective-permute-start.18 = (bf16[112,128]{1,0:T(8,128)(2,1)S(1)}, bf16[112,128]{1,0:T(8,128)(2,1)S(1)}, u32[]{:S(2)}, u32[]{:S(2)}) collective-permute-start(bf16[112,128]{1,0:T(8,128)(2,1)S(1)} %get-tuple-element.108), channel_id=1, source_target_pairs={{0,8},{2,4},{4,2},{6,14},{8,0},{10,12},{12,10},{14,6},{16,24},{18,... | collective-permute-start | bytes 86024 | tf_op jit(solution)/shard_map/ppermute | solution.py:613
  56.4 5.1 %collective-permute-start.19 = (bf16[112,128]{1,0:T(8,128)(2,1)S(1)}, bf16[112,128]{1,0:T(8,128)(2,1)S(1)}, u32[]{:S(2)}, u32[]{:S(2)}) collective-permute-start(bf16[112,128]{1,0:T(8,128)(2,1)S(1)} %get-tuple-element.109), channel_id=1, source_target_pairs={{0,2},{2,0},{4,6},{6,4},{8,10},{10,8},{12,14},{14,12},{16,18},{18,... | collective-permute-start | bytes 86024 | tf_op jit(solution)/shard_map/ppermute | solution.py:613
  61.6 4.2 %collective-permute-start.20 = (bf16[208,128]{1,0:T(8,128)(2,1)S(1)}, bf16[208,128]{1,0:T(8,128)(2,1)S(1)}, u32[]{:S(2)}, u32[]{:S(2)}) collective-permute-start(bf16[208,128]{1,0:T(8,128)(2,1)S(1)} %get-tuple-element.112), channel_id=1, source_target_pairs={{0,1},{1,0},{2,3},{3,2},{4,5},{5,4},{6,7},{7,6},{8,9},{9,8},{10,11... | collective-permute-start | bytes 159752 | tf_op jit(solution)/shard_map/ppermute | solution.py:662

commit v9 on v8

--- a/solution.py
+++ b/solution.py
@@ -78,12 +78,11 @@
     return jnp.dot(a, b, preferred_element_type=F32)
 
 
-def is_odd(axis):
-    return lax.rem(lax.axis_index(axis), 2) == 1
-
-
-def by_parity(axis, even, odd):
-    return jnp.where(is_odd(axis), odd, even)
+FIRST = {"gx": 1, "gy": 0}
+
+
+def if_first(axis, value, otherwise):
+    return jnp.where(lax.rem(lax.axis_index(axis), 2) == FIRST[axis], value, otherwise)
 
 
 def link_shifts(sz):
@@ -285,13 +284,13 @@
 
 
 def write_pair(axis, low, high, first, second):
-    first[...] = by_parity(axis, low, high).astype(first.dtype)
-    second[...] = by_parity(axis, high, low).astype(second.dtype)
+    first[...] = if_first(axis, high, low).astype(first.dtype)
+    second[...] = if_first(axis, low, high).astype(second.dtype)
 
 
 def read_pair(axis, first, second):
     one, two = first[...].astype(F32), second[...].astype(F32)
-    low, high = by_parity(axis, one, two), by_parity(axis, two, one)
+    low, high = if_first(axis, two, one), if_first(axis, one, two)
     at, last = lax.axis_index(axis), lax.axis_size(axis) - 1
     return jnp.where(at > 0, low, 0.0), jnp.where(at < last, high, 0.0)
 
@@ -604,7 +603,7 @@
         return (to, j) if axis == "gx" else (i, to)
 
     out = []
-    for face, low in ((one, 1), (two, 0)):
+    for face, low in ((one, FIRST[axis]), (two, 1 - FIRST[axis])):
         pairs = []
         for i in range(wide):
             for j in range(deep):

time: 66.9 us -> 64.6 us (0.966)
  starting transfers between devices: 26.4 us -> 22.2 us
  waiting for transfers between devices: 24.6 us -> 26.5 us
    ppermute x16, starting transfers between devices: 18.8 us -> 14.3 us  [swap_faces(): out.append(lax.ppermute(face, axes, pairs))]
    ppermute x1, waiting for transfers between devices: 0.11 us -> 1.26 us  [local(): qfaces.append(lax.ppermute(face_rows[j], 'gz', back))]
    ppermute x16, waiting for transfers between devices: 12.6 us -> 13.5 us  [swap_faces(): out.append(lax.ppermute(face, axes, pairs))]
  transfers between devices with their start and end apart: 21 -> 21, of which waited for: 11 -> 12; matrix products, arithmetic and copies ran while one was open for 0% -> 0% of each run, Pallas kernels for 9% -> 10%
where the time goes in v9:
time: 64.6 us; the launch traced here: 64.4 us
  waiting for transfers between devices  26.5 us (41%)
  starting transfers between devices  22.2 us (34%)
  Pallas kernels  13.4 us (21%)
  local copies, waits for them, and re-layouts  1.37 us (2%)
  other arithmetic  0.75 us (1%)
    ppermute x16, starting transfers between devices, swap_faces(): out.append(lax.ppermute(face, axes, pairs))  14.3 us
    ppermute x16, waiting for transfers between devices, swap_faces(): out.append(lax.ppermute(face, axes, pairs))  13.5 us
    pallas_call x19, Pallas kernels, kernel_call(): pl.pallas_call(with_waits, out_shape=outs, in_specs=[VMEM] * used + [pl.B...  13.4 us
    ppermute x3, waiting for transfers between devices, local(): lax.ppermute(m, 'gz', ring[s + 1])  9.37 us
    ppermute x3, starting transfers between devices, local(): lax.ppermute(m, 'gz', ring[s + 1])  4.73 us
    ppermute x1, waiting for transfers between devices, local(): zr = [lax.ppermute(f, 'gz', ring[s]) for f, s in zip(sent, link_shifts(sz))]  2.45 us
    ppermute x1, starting transfers between devices, local(): qfaces.append(lax.ppermute(face_rows[j], 'gz', back))  1.58 us
    ppermute x1, starting transfers between devices, local(): zr = [lax.ppermute(f, 'gz', ring[s]) for f, s in zip(sent, link_shifts(sz))]  1.57 us
  transfers between devices with their start and end apart: 21, of which 12 were waited for; matrix products, arithmetic and copies ran while one was open for 0% of the time, Pallas kernels for 10%

profile of v9, /device:TPU:0, one launch (start us, length us, event | category | flops | bytes accessed | tf_op | source)
XLA Modules:
  0.0 64.4 jit_solution(8181415337499407057)
XLA Ops:
  0.0 0.0 copy-start
  0.0 0.8 %convert_bitcast_fusion.refs_1_ = f32[4,32]{1,0:T(4,128)S(1)} fusion(s32[1,1,1,32,4]{3,4,2,1,0:T(4,128)} %param.12), kind=kLoop, calls=%fused_computation.1 | loop fusion | flops 128 | bytes 1024 | tf_op jit(solution)/shard_map/convert_element_type | solution.py:625
  0.8 1.3 %pad.4.refs_2_.refs_0_ = bf16[352,1536]{1,0:T(8,128)(2,1)S(1)} pad(bf16[343,1536]{1,0:T(8,128)(2,1)} %bitcast.11, bf16[]{:T(256)} %constant.2.clone.1), padding=0_9x0_0 | pad | bytes 2135042 | tf_op jit(solution)/shard_map/jit(_pad)/pad | solution.py:624
  2.1 0.0 copy-done.1
  2.1 0.1 shard_map.73
  2.2 2.4 %collective-permute-start = (bf16[112,128]{1,0:T(8,128)(2,1)S(1)}, bf16[112,128]{1,0:T(8,128)(2,1)S(1)}, u32[]{:S(2)}, u32[]{:S(2)}) collective-permute-start(bf16[112,128]{1,0:T(8,128)(2,1)S(1)} %get-tuple-element.60), channel_id=1, source_target_pairs={{0,24},{2,26},{4,28},{6,30},{8,16},{10,18},{12,20},{14,22},{16,8},... | collective-permute-start | bytes 86024 | tf_op jit(solution)/shard_map/ppermute | solution.py:612
  4.6 0.7 %collective-permute-start.1 = (bf16[112,128]{1,0:T(8,128)(2,1)S(1)}, bf16[112,128]{1,0:T(8,128)(2,1)S(1)}, u32[]{:S(2)}, u32[]{:S(2)}) collective-permute-start(bf16[112,128]{1,0:T(8,128)(2,1)S(1)} %get-tuple-element.61), channel_id=1, source_target_pairs={{0,8},{2,10},{4,12},{6,14},{8,0},{10,2},{12,4},{14,6},{16,24},{18,... | collective-permute-start | bytes 86024 | tf_op jit(solution)/shard_map/ppermute | solution.py:612
  5.3 2.3 %shard_map.75 = (bf16[1664,384]{1,0:T(8,128)(2,1)S(1)}, bf16[384,256]{1,0:T(8,128)(2,1)S(1)}) custom-call(bf16[352,1536]{1,0:T(8,128)(2,1)S(1)} %pad.4.refs_2_.refs_0_, f32[4,32]{1,0:T(4,128)S(1)} %convert_bitcast_fusion.refs_1_), custom_call_target="tpu_custom_call" | custom-call | flops 3000000000 | bytes 2556416 | tf_op jit(solution)/shard_map/pallas_call | solution.py:62
  7.6 1.6 %collective-permute-start.4 = (bf16[384,256]{1,0:T(8,128)(2,1)S(1)}, bf16[384,256]{1,0:T(8,128)(2,1)S(1)}, u32[]{:S(2)}, u32[]{:S(2)}) collective-permute-start(bf16[384,256]{1,0:T(8,128)(2,1)S(1)} %get-tuple-element.68), channel_id=1, source_target_pairs={{1,0},{0,1},{3,2},{2,3},{5,4},{4,5},{7,6},{6,7},{9,8},{8,9},{11,10... | collective-permute-start | bytes 589832 | tf_op jit(solution)/shard_map/ppermute | solution.py:639
  9.2 0.0 copy-done
  9.3 0.0 collective-permute-done.refs_0_.refs_1_
  9.3 0.0 collective-permute-done.1.refs_1_.refs_2_
  9.3 1.6 %collective-permute-start.2 = (bf16[112,128]{1,0:T(8,128)(2,1)S(1)}, bf16[112,128]{1,0:T(8,128)(2,1)S(1)}, u32[]{:S(2)}, u32[]{:S(2)}) collective-permute-start(bf16[112,128]{1,0:T(8,128)(2,1)S(1)} %get-tuple-element.64), channel_id=1, source_target_pairs={{0,2},{2,0},{4,6},{6,4},{8,10},{10,8},{12,14},{14,12},{16,18},{18,... | collective-permute-start | bytes 86024 | tf_op jit(solution)/shard_map/ppermute | solution.py:612
  11.0 0.0 collective-permute-start.3
  11.0 0.0 copy-done.2
  11.0 0.0 copy-done.3
  11.0 1.8 %shard_map.76 = (bf16[384,1664]{1,0:T(8,128)(2,1)S(1)}, bf16[400,400]{1,0:T(8,128)(2,1)S(1)}, f32[1600,128]{1,0:T(8,128)S(1)}, bf16[384,768]{1,0:T(8,128)(2,1)S(...) custom-call(bf16[1664,384]{1,0:T(8,128)(2,1)S(1)} %get-tuple-element.66.refs_0_.refs_5_, ...), custom_call_target="tpu_custom_call" | custom-call | flops 1000000000 | bytes 5447570 | tf_op jit(solution)/shard_map/pallas_call | solution.py:62
  12.8 0.4 collective-permute-done.2.refs_3_
  13.3 0.0 collective-permute-done.3.refs_4_
  13.3 1.3 %collective-permute-done.4.refs_6_.refs_7_.refs_8_ = bf16[384,256]{1,0:T(8,128)(2,1)S(1)} collective-permute-done((bf16[384,256]{1,0:T(8,128)(2,1)S(1)}, bf16[384,256]{1,0:T(8,128)(2,1)S(1)}, u32[]{:S(2)}, u32[]{:S(2)}) %collective-permute-start.4) | collective-permute-done | bytes 196640 | tf_op jit(solution)/shard_map/ppermute | solution.py:639
  14.5 0.9 %shard_map.77 = (f32[1384,128]{1,0:T(8,128)S(1)}, f32[384,128]{1,0:T(8,128)S(1)}, bf16[384,128]{1,0:T(8,128)(2,1)S(1)}, bf16[592,128]{1,0:T(8,128)(2,1)S(1)}) custom-call(f32[1384,128]{1,0:T(8,128)S(1)} %get-tuple-element.59.refs_0_, bf16[112,128]{1,0:T(8,128)(2,1)S(1)} %collective-permute-done.refs_0_.refs_1_, ...), custom_call_target="tpu_custom_call" | custom-call | flops 400000000 | bytes 4042752 | tf_op jit(solution)/shard_map/pallas_call | solution.py:62
  15.4 1.6 %collective-permute-start.5 = (bf16[592,128]{1,0:T(8,128)(2,1)S(1)}, bf16[592,128]{1,0:T(8,128)(2,1)S(1)}, u32[]{:S(2)}, u32[]{:S(2)}) collective-permute-start(bf16[592,128]{1,0:T(8,128)(2,1)S(1)} %get-tuple-element.76), channel_id=1, source_target_pairs={{0,1},{1,0},{2,3},{3,2},{4,5},{5,4},{6,7},{7,6},{8,9},{9,8},{10,11... | collective-permute-start | bytes 454664 | tf_op jit(solution)/shard_map/ppermute | solution.py:654
  17.0 0.6 shard_map.78.refs_1_
  17.6 3.1 %collective-permute-done.5.refs_2_ = bf16[592,128]{1,0:T(8,128)(2,1)S(1)} collective-permute-done((bf16[592,128]{1,0:T(8,128)(2,1)S(1)}, bf16[592,128]{1,0:T(8,128)(2,1)S(1)}, u32[]{:S(2)}, u32[]{:S(2)}) %collective-permute-start.5) | collective-permute-done | bytes 151584 | tf_op jit(solution)/shard_map/ppermute | solution.py:654
  20.7 1.1 %shard_map.79 = (f32[1384,128]{1,0:T(8,128)S(1)}, f32[1384,128]{1,0:T(8,128)S(1)}, bf16[112,128]{1,0:T(8,128)(2,1)S(1)}, bf16[112,128]{1,0:T(8,128)(2,1)S(1)}, f...) custom-call(f32[1384,128]{1,0:T(8,128)S(1)} %get-tuple-element.70.refs_0_, f32[384,128]{1,0:T(8,128)S(1)} %shard_map.78.refs_1_, ...), custom_call_target="tpu_custom_call" | custom-call | flops 600000000 | bytes 5652992 | tf_op jit(solution)/shard_map/pallas_call | solution.py:62
  21.8 0.1 collective-permute-start.6
  21.8 0.9 %collective-permute-start.7 = (bf16[112,128]{1,0:T(8,128)(2,1)S(1)}, bf16[112,128]{1,0:T(8,128)(2,1)S(1)}, u32[]{:S(2)}, u32[]{:S(2)}) collective-permute-start(bf16[112,128]{1,0:T(8,128)(2,1)S(1)} %get-tuple-element.82), channel_id=1, source_target_pairs={{0,8},{2,10},{4,12},{6,14},{8,0},{10,2},{12,4},{14,6},{16,24},{18,... | collective-permute-start | bytes 86024 | tf_op jit(solution)/shard_map/ppermute | solution.py:612
  22.7 2.4 %collective-permute-done.6.refs_0_.refs_2_ = bf16[112,128]{1,0:T(8,128)(2,1)S(1)} collective-permute-done((bf16[112,128]{1,0:T(8,128)(2,1)S(1)}, bf16[112,128]{1,0:T(8,128)(2,1)S(1)}, u32[]{:S(2)}, u32[]{:S(2)}) %collective-permute-start.6) | collective-permute-done | bytes 28704 | tf_op jit(solution)/shard_map/ppermute | solution.py:612
  25.1 0.0 collective-permute-done.7.refs_1_.refs_3_
  25.1 1.6 %collective-permute-start.8 = (bf16[112,128]{1,0:T(8,128)(2,1)S(1)}, bf16[112,128]{1,0:T(8,128)(2,1)S(1)}, u32[]{:S(2)}, u32[]{:S(2)}) collective-permute-start(bf16[112,128]{1,0:T(8,128)(2,1)S(1)} %get-tuple-element.85), channel_id=1, source_target_pairs={{0,2},{2,0},{4,6},{6,4},{8,10},{10,8},{12,14},{14,12},{16,18},{18,... | collective-permute-start | bytes 86024 | tf_op jit(solution)/shard_map/ppermute | solution.py:612
  26.8 0.0 collective-permute-start.9
  26.8 2.3 %collective-permute-done.8.refs_4_ = bf16[112,128]{1,0:T(8,128)(2,1)S(1)} collective-permute-done((bf16[112,128]{1,0:T(8,128)(2,1)S(1)}, bf16[112,128]{1,0:T(8,128)(2,1)S(1)}, u32[]{:S(2)}, u32[]{:S(2)}) %collective-permute-start.8) | collective-permute-done | bytes 28704 | tf_op jit(solution)/shard_map/ppermute | solution.py:612
  29.1 0.0 collective-permute-done.9.refs_5_
  29.1 0.9 %shard_map.81 = (f32[1384,128]{1,0:T(8,128)S(1)}, f32[384,128]{1,0:T(8,128)S(1)}, bf16[384,128]{1,0:T(8,128)(2,1)S(1)}, bf16[592,128]{1,0:T(8,128)(2,1)S(1)}) custom-call(f32[1384,128]{1,0:T(8,128)S(1)} %get-tuple-element.79.refs_0_, f32[1384,128]{1,0:T(8,128)S(1)} %get-tuple-element.80.refs_1_.refs_2_, ...), custom_call_target="tpu_custom_call" | custom-call | flops 400000000 | bytes 4751360 | tf_op jit(solution)/shard_map/pallas_call | solution.py:62
  30.0 1.6 %collective-permute-start.10 = (bf16[592,128]{1,0:T(8,128)(2,1)S(1)}, bf16[592,128]{1,0:T(8,128)(2,1)S(1)}, u32[]{:S(2)}, u32[]{:S(2)}) collective-permute-start(bf16[592,128]{1,0:T(8,128)(2,1)S(1)} %get-tuple-element.90), channel_id=1, source_target_pairs={{0,1},{1,0},{2,3},{3,2},{4,5},{5,4},{6,7},{7,6},{8,9},{9,8},{10,11... | collective-permute-start | bytes 454664 | tf_op jit(solution)/shard_map/ppermute | solution.py:654
  31.6 0.6 shard_map.82.refs_1_
  32.2 3.1 %collective-permute-done.10.refs_2_ = bf16[592,128]{1,0:T(8,128)(2,1)S(1)} collective-permute-done((bf16[592,128]{1,0:T(8,128)(2,1)S(1)}, bf16[592,128]{1,0:T(8,128)(2,1)S(1)}, u32[]{:S(2)}, u32[]{:S(2)}) %collective-permute-start.10) | collective-permute-done | bytes 151584 | tf_op jit(solution)/shard_map/ppermute | solution.py:654
  35.3 1.1 %shard_map.83 = (f32[1384,128]{1,0:T(8,128)S(1)}, f32[1384,128]{1,0:T(8,128)S(1)}, bf16[112,128]{1,0:T(8,128)(2,1)S(1)}, bf16[112,128]{1,0:T(8,128)(2,1)S(1)}, f...) custom-call(f32[1384,128]{1,0:T(8,128)S(1)} %get-tuple-element.87.refs_0_, f32[384,128]{1,0:T(8,128)S(1)} %shard_map.82.refs_1_, ...), custom_call_target="tpu_custom_call" | custom-call | flops 600000000 | bytes 5652992 | tf_op jit(solution)/shard_map/pallas_call | solution.py:62
  36.4 0.1 collective-permute-start.11
  36.4 1.0 %collective-permute-start.12 = (bf16[112,128]{1,0:T(8,128)(2,1)S(1)}, bf16[112,128]{1,0:T(8,128)(2,1)S(1)}, u32[]{:S(2)}, u32[]{:S(2)}) collective-permute-start(bf16[112,128]{1,0:T(8,128)(2,1)S(1)} %get-tuple-element.94), channel_id=1, source_target_pairs={{0,8},{2,10},{4,12},{6,14},{8,0},{10,2},{12,4},{14,6},{16,24},{18,... | collective-permute-start | bytes 86024 | tf_op jit(solution)/shard_map/ppermute | solution.py:612
  37.4 2.3 %collective-permute-done.11.refs_0_.refs_3_ = bf16[112,128]{1,0:T(8,128)(2,1)S(1)} collective-permute-done((bf16[112,128]{1,0:T(8,128)(2,1)S(1)}, bf16[112,128]{1,0:T(8,128)(2,1)S(1)}, u32[]{:S(2)}, u32[]{:S(2)}) %collective-permute-start.11) | collective-permute-done | bytes 28704 | tf_op jit(solution)/shard_map/ppermute | solution.py:612
  39.7 0.0 collective-permute-done.12.refs_1_.refs_4_
  39.8 2.8 %collective-permute-start.13 = (bf16[112,128]{1,0:T(8,128)(2,1)S(1)}, bf16[112,128]{1,0:T(8,128)(2,1)S(1)}, u32[]{:S(2)}, u32[]{:S(2)}) collective-permute-start(bf16[112,128]{1,0:T(8,128)(2,1)S(1)} %get-tuple-element.97), channel_id=1, source_target_pairs={{0,2},{2,0},{4,6},{6,4},{8,10},{10,8},{12,14},{14,12},{16,18},{18,... | collective-permute-start | bytes 86024 | tf_op jit(solution)/shard_map/ppermute | solution.py:612
  42.5 0.0 collective-permute-start.14
  42.5 1.8 %collective-permute-done.13.refs_5_ = bf16[112,128]{1,0:T(8,128)(2,1)S(1)} collective-permute-done((bf16[112,128]{1,0:T(8,128)(2,1)S(1)}, bf16[112,128]{1,0:T(8,128)(2,1)S(1)}, u32[]{:S(2)}, u32[]{:S(2)}) %collective-permute-start.13) | collective-permute-done | bytes 28704 | tf_op jit(solution)/shard_map/ppermute | solution.py:612
  44.4 0.0 collective-permute-done.14.refs_6_
  44.4 1.0 %shard_map.85 = (f32[1384,128]{1,0:T(8,128)S(1)}, f32[384,128]{1,0:T(8,128)S(1)}, bf16[384,128]{1,0:T(8,128)(2,1)S(1)}, bf16[592,128]{1,0:T(8,128)(2,1)S(1)}) custom-call(f32[1384,128]{1,0:T(8,128)S(1)} %get-tuple-element.91.refs_0_, f32[1384,128]{1,0:T(8,128)S(1)} %get-tuple-element.92.refs_1_.refs_2_, f32[1384,128]{1,0:T(8,128)S(1)} %get-tuple-element.80.refs_1_.refs_2_, ...), custom_call_target="tpu_custom_call" | custom-call | flops 400000000 | bytes 5459968 | tf_op jit(solution)/shard_map/pallas_call | solution.py:62
  45.4 1.6 %collective-permute-start.15 = (bf16[592,128]{1,0:T(8,128)(2,1)S(1)}, bf16[592,128]{1,0:T(8,128)(2,1)S(1)}, u32[]{:S(2)}, u32[]{:S(2)}) collective-permute-start(bf16[592,128]{1,0:T(8,128)(2,1)S(1)} %get-tuple-element.102), channel_id=1, source_target_pairs={{0,1},{1,0},{2,3},{3,2},{4,5},{5,4},{6,7},{7,6},{8,9},{9,8},{10,11... | collective-permute-start | bytes 454664 | tf_op jit(solution)/shard_map/ppermute | solution.py:654
  46.9 0.6 shard_map.86.refs_1_
  47.5 3.2 %collective-permute-done.15.refs_2_ = bf16[592,128]{1,0:T(8,128)(2,1)S(1)} collective-permute-done((bf16[592,128]{1,0:T(8,128)(2,1)S(1)}, bf16[592,128]{1,0:T(8,128)(2,1)S(1)}, u32[]{:S(2)}, u32[]{:S(2)}) %collective-permute-start.15) | collective-permute-done | bytes 151584 | tf_op jit(solution)/shard_map/ppermute | solution.py:654
  50.8 1.1 %shard_map.87 = (f32[1384,128]{1,0:T(8,128)S(1)}, f32[1384,128]{1,0:T(8,128)S(1)}, bf16[112,128]{1,0:T(8,128)(2,1)S(1)}, bf16[112,128]{1,0:T(8,128)(2,1)S(1)}, f...) custom-call(f32[1384,128]{1,0:T(8,128)S(1)} %get-tuple-element.99.refs_0_, f32[384,128]{1,0:T(8,128)S(1)} %shard_map.86.refs_1_, ...), custom_call_target="tpu_custom_call" | custom-call | flops 600000000 | bytes 5652992 | tf_op jit(solution)/shard_map/pallas_call | solution.py:62
  51.9 0.1 collective-permute-start.16
  52.0 1.0 %collective-permute-start.17 = (bf16[112,128]{1,0:T(8,128)(2,1)S(1)}, bf16[112,128]{1,0:T(8,128)(2,1)S(1)}, u32[]{:S(2)}, u32[]{:S(2)}) collective-permute-start(bf16[112,128]{1,0:T(8,128)(2,1)S(1)} %get-tuple-element.105), channel_id=1, source_target_pairs={{0,8},{2,10},{4,12},{6,14},{8,0},{10,2},{12,4},{14,6},{16,24},{18,... | collective-permute-start | bytes 86024 | tf_op jit(solution)/shard_map/ppermute | solution.py:612
  52.9 2.3 %collective-permute-done.16.refs_0_.refs_1_ = bf16[112,128]{1,0:T(8,128)(2,1)S(1)} collective-permute-done((bf16[112,128]{1,0:T(8,128)(2,1)S(1)}, bf16[112,128]{1,0:T(8,128)(2,1)S(1)}, u32[]{:S(2)}, u32[]{:S(2)}) %collective-permute-start.16) | collective-permute-done | bytes 28704 | tf_op jit(solution)/shard_map/ppermute | solution.py:612
  55.2 0.0 collective-permute-done.17.refs_1_.refs_2_
  55.3 2.0 %collective-permute-start.18 = (bf16[112,128]{1,0:T(8,128)(2,1)S(1)}, bf16[112,128]{1,0:T(8,128)(2,1)S(1)}, u32[]{:S(2)}, u32[]{:S(2)}) collective-permute-start(bf16[112,128]{1,0:T(8,128)(2,1)S(1)} %get-tuple-element.108), channel_id=1, source_target_pairs={{0,2},{2,0},{4,6},{6,4},{8,10},{10,8},{12,14},{14,12},{16,18},{18,... | collective-permute-start | bytes 86024 | tf_op jit(solution)/shard_map/ppermute | solution.py:612
  57.3 0.0 collective-permute-start.19
  57.3 1.9 %collective-permute-done.18.refs_3_ = bf16[112,128]{1,0:T(8,128)(2,1)S(1)} collective-permute-done((bf16[112,128]{1,0:T(8,128)(2,1)S(1)}, bf16[112,128]{1,0:T(8,128)(2,1)S(1)}, u32[]{:S(2)}, u32[]{:S(2)}) %collective-permute-start.18) | collective-permute-done | bytes 28704 | tf_op jit(solution)/shard_map/ppermute | solution.py:612
  59.2 0.0 collective-permute-done.19.refs_4_
  59.2 0.1 shard_map.89
  59.3 1.6 %collective-permute-start.20 = (bf16[208,128]{1,0:T(8,128)(2,1)S(1)}, bf16[208,128]{1,0:T(8,128)(2,1)S(1)}, u32[]{:S(2)}, u32[]{:S(2)}) collective-permute-start(bf16[208,128]{1,0:T(8,128)(2,1)S(1)} %get-tuple-element.112), channel_id=1, source_target_pairs={{0,1},{1,0},{2,3},{3,2},{4,5},{5,4},{6,7},{7,6},{8,9},{9,8},{10,11... | collective-permute-start | bytes 159752 | tf_op jit(solution)/shard_map/ppermute | solution.py:661
  60.9 0.2 shard_map.90.refs_0_
  61.1 2.4 %collective-permute-done.20.refs_1_ = bf16[208,128]{1,0:T(8,128)(2,1)S(1)} collective-permute-done((bf16[208,128]{1,0:T(8,128)(2,1)S(1)}, bf16[208,128]{1,0:T(8,128)(2,1)S(1)}, u32[]{:S(2)}, u32[]{:S(2)}) %collective-permute-start.20) | collective-permute-done | bytes 53280 | tf_op jit(solution)/shard_map/ppermute | solution.py:661
  63.5 0.9 %shard_map.91 = f32[13,13,7,128]{3,2,1,0:T(8,128)} custom-call(f32[1384,128]{1,0:T(8,128)S(1)} %shard_map.90.refs_0_, bf16[208,128]{1,0:T(8,128)(2,1)S(1)} %collective-permute-done.20.refs_1_), custom_call_target="tpu_custom_call" | custom-call | bytes 1367552 | tf_op jit(solution)/shard_map/pallas_call | solution.py:62
  (11 shorter events, 0.2 us)
Async XLA Ops:
  0.0 9.2 %copy-start = (f32[343,2,2,1]{0,3,2,1:T(1,128)S(1)}, f32[343,2,2,1]{0,3,2,1:T(1,128)}, u32[]{:S(2)}) copy-start(f32[343,2,2,1]{0,3,2,1:T(1,128)} %param.9) | copy-start | bytes 16468
  0.0 2.1 %copy-start.1 = (f32[13,13,7,128]{3,2,1,0:T(8,128)S(1)}, f32[13,13,7,128]{3,2,1,0:T(8,128)}, u32[]{:S(2)}) copy-start(f32[13,13,7,128]{3,2,1,0:T(8,128)} %refs_0_.1) | copy-start | bytes 1817092
  2.2 7.1 %collective-permute-start = (bf16[112,128]{1,0:T(8,128)(2,1)S(1)}, bf16[112,128]{1,0:T(8,128)(2,1)S(1)}, u32[]{:S(2)}, u32[]{:S(2)}) collective-permute-start(bf16[112,128]{1,0:T(8,128)(2,1)S(1)} %get-tuple-element.60), channel_id=1, source_target_pairs={{0,24},{2,26},{4,28},{6,30},{8,16},{10,18},{12,20},{14,22},{16,8},... | collective-permute-start | bytes 86024 | tf_op jit(solution)/shard_map/ppermute | solution.py:612
  4.6 6.3 %copy-start.2 = (bf16[343,343]{1,0:T(8,128)(2,1)S(1)}, bf16[343,343]{1,0:T(8,128)(2,1)}, u32[]{:S(2)}) copy-start(bf16[343,343]{1,0:T(8,128)(2,1)} %refs_1_.1) | copy-start | bytes 705898
  4.6 6.3 %copy-start.3 = (f32[64,12,12]{0,2,1:T(8,128)S(1)}, f32[64,12,12]{0,2,1:T(8,128)}, u32[]{:S(2)}) copy-start(f32[64,12,12]{0,2,1:T(8,128)} %param.13) | copy-start | bytes 110596
  4.6 6.3 %copy-start.4 = (s32[1,1,2,32]{3,2,1,0:T(2,128)S(1)}, s32[1,1,2,32]{3,2,1,0:T(2,128)}, u32[]{:S(2)}) copy-start(s32[1,1,2,32]{3,2,1,0:T(2,128)} %param.11) | copy-start | bytes 772
  4.6 4.6 %collective-permute-start.1 = (bf16[112,128]{1,0:T(8,128)(2,1)S(1)}, bf16[112,128]{1,0:T(8,128)(2,1)S(1)}, u32[]{:S(2)}, u32[]{:S(2)}) collective-permute-start(bf16[112,128]{1,0:T(8,128)(2,1)S(1)} %get-tuple-element.61), channel_id=1, source_target_pairs={{0,8},{2,10},{4,12},{6,14},{8,0},{10,2},{12,4},{14,6},{16,24},{18,... | collective-permute-start | bytes 86024 | tf_op jit(solution)/shard_map/ppermute | solution.py:612
  7.6 6.9 %collective-permute-start.4 = (bf16[384,256]{1,0:T(8,128)(2,1)S(1)}, bf16[384,256]{1,0:T(8,128)(2,1)S(1)}, u32[]{:S(2)}, u32[]{:S(2)}) collective-permute-start(bf16[384,256]{1,0:T(8,128)(2,1)S(1)} %get-tuple-element.68), channel_id=1, source_target_pairs={{1,0},{0,1},{3,2},{2,3},{5,4},{4,5},{7,6},{6,7},{9,8},{8,9},{11,10... | collective-permute-start | bytes 589832 | tf_op jit(solution)/shard_map/ppermute | solution.py:639
  9.3 3.9 %collective-permute-start.2 = (bf16[112,128]{1,0:T(8,128)(2,1)S(1)}, bf16[112,128]{1,0:T(8,128)(2,1)S(1)}, u32[]{:S(2)}, u32[]{:S(2)}) collective-permute-start(bf16[112,128]{1,0:T(8,128)(2,1)S(1)} %get-tuple-element.64), channel_id=1, source_target_pairs={{0,2},{2,0},{4,6},{6,4},{8,10},{10,8},{12,14},{14,12},{16,18},{18,... | collective-permute-start | bytes 86024 | tf_op jit(solution)/shard_map/ppermute | solution.py:612
  11.0 2.3 %collective-permute-start.3 = (bf16[112,128]{1,0:T(8,128)(2,1)S(1)}, bf16[112,128]{1,0:T(8,128)(2,1)S(1)}, u32[]{:S(2)}, u32[]{:S(2)}) collective-permute-start(bf16[112,128]{1,0:T(8,128)(2,1)S(1)} %get-tuple-element.65), channel_id=1, source_target_pairs={{0,8},{2,4},{4,2},{6,14},{8,0},{10,12},{12,10},{14,6},{16,24},{18,... | collective-permute-start | bytes 86024 | tf_op jit(solution)/shard_map/ppermute | solution.py:612
  15.4 5.3 %collective-permute-start.5 = (bf16[592,128]{1,0:T(8,128)(2,1)S(1)}, bf16[592,128]{1,0:T(8,128)(2,1)S(1)}, u32[]{:S(2)}, u32[]{:S(2)}) collective-permute-start(bf16[592,128]{1,0:T(8,128)(2,1)S(1)} %get-tuple-element.76), channel_id=1, source_target_pairs={{0,1},{1,0},{2,3},{3,2},{4,5},{5,4},{6,7},{7,6},{8,9},{9,8},{10,11... | collective-permute-start | bytes 454664 | tf_op jit(solution)/shard_map/ppermute | solution.py:654
  21.8 3.4 %collective-permute-start.6 = (bf16[112,128]{1,0:T(8,128)(2,1)S(1)}, bf16[112,128]{1,0:T(8,128)(2,1)S(1)}, u32[]{:S(2)}, u32[]{:S(2)}) collective-permute-start(bf16[112,128]{1,0:T(8,128)(2,1)S(1)} %get-tuple-element.81), channel_id=1, source_target_pairs={{0,24},{2,26},{4,28},{6,30},{8,16},{10,18},{12,20},{14,22},{16,8},... | collective-permute-start | bytes 86024 | tf_op jit(solution)/shard_map/ppermute | solution.py:612
  21.8 3.3 %collective-permute-start.7 = (bf16[112,128]{1,0:T(8,128)(2,1)S(1)}, bf16[112,128]{1,0:T(8,128)(2,1)S(1)}, u32[]{:S(2)}, u32[]{:S(2)}) collective-permute-start(bf16[112,128]{1,0:T(8,128)(2,1)S(1)} %get-tuple-element.82), channel_id=1, source_target_pairs={{0,8},{2,10},{4,12},{6,14},{8,0},{10,2},{12,4},{14,6},{16,24},{18,... | collective-permute-start | bytes 86024 | tf_op jit(solution)/shard_map/ppermute | solution.py:612
  25.1 3.9 %collective-permute-start.8 = (bf16[112,128]{1,0:T(8,128)(2,1)S(1)}, bf16[112,128]{1,0:T(8,128)(2,1)S(1)}, u32[]{:S(2)}, u32[]{:S(2)}) collective-permute-start(bf16[112,128]{1,0:T(8,128)(2,1)S(1)} %get-tuple-element.85), channel_id=1, source_target_pairs={{0,2},{2,0},{4,6},{6,4},{8,10},{10,8},{12,14},{14,12},{16,18},{18,... | collective-permute-start | bytes 86024 | tf_op jit(solution)/shard_map/ppermute | solution.py:612
  26.8 2.3 %collective-permute-start.9 = (bf16[112,128]{1,0:T(8,128)(2,1)S(1)}, bf16[112,128]{1,0:T(8,128)(2,1)S(1)}, u32[]{:S(2)}, u32[]{:S(2)}) collective-permute-start(bf16[112,128]{1,0:T(8,128)(2,1)S(1)} %get-tuple-element.86), channel_id=1, source_target_pairs={{0,8},{2,4},{4,2},{6,14},{8,0},{10,12},{12,10},{14,6},{16,24},{18,... | collective-permute-start | bytes 86024 | tf_op jit(solution)/shard_map/ppermute | solution.py:612
  30.0 5.3 %collective-permute-start.10 = (bf16[592,128]{1,0:T(8,128)(2,1)S(1)}, bf16[592,128]{1,0:T(8,128)(2,1)S(1)}, u32[]{:S(2)}, u32[]{:S(2)}) collective-permute-start(bf16[592,128]{1,0:T(8,128)(2,1)S(1)} %get-tuple-element.90), channel_id=1, source_target_pairs={{0,1},{1,0},{2,3},{3,2},{4,5},{5,4},{6,7},{7,6},{8,9},{9,8},{10,11... | collective-permute-start | bytes 454664 | tf_op jit(solution)/shard_map/ppermute | solution.py:654
  36.4 3.4 %collective-permute-start.11 = (bf16[112,128]{1,0:T(8,128)(2,1)S(1)}, bf16[112,128]{1,0:T(8,128)(2,1)S(1)}, u32[]{:S(2)}, u32[]{:S(2)}) collective-permute-start(bf16[112,128]{1,0:T(8,128)(2,1)S(1)} %get-tuple-element.93), channel_id=1, source_target_pairs={{0,24},{2,26},{4,28},{6,30},{8,16},{10,18},{12,20},{14,22},{16,8},... | collective-permute-start | bytes 86024 | tf_op jit(solution)/shard_map/ppermute | solution.py:612
  36.4 3.3 %collective-permute-start.12 = (bf16[112,128]{1,0:T(8,128)(2,1)S(1)}, bf16[112,128]{1,0:T(8,128)(2,1)S(1)}, u32[]{:S(2)}, u32[]{:S(2)}) collective-permute-start(bf16[112,128]{1,0:T(8,128)(2,1)S(1)} %get-tuple-element.94), channel_id=1, source_target_pairs={{0,8},{2,10},{4,12},{6,14},{8,0},{10,2},{12,4},{14,6},{16,24},{18,... | collective-permute-start | bytes 86024 | tf_op jit(solution)/shard_map/ppermute | solution.py:612
  39.8 4.6 %collective-permute-start.13 = (bf16[112,128]{1,0:T(8,128)(2,1)S(1)}, bf16[112,128]{1,0:T(8,128)(2,1)S(1)}, u32[]{:S(2)}, u32[]{:S(2)}) collective-permute-start(bf16[112,128]{1,0:T(8,128)(2,1)S(1)} %get-tuple-element.97), channel_id=1, source_target_pairs={{0,2},{2,0},{4,6},{6,4},{8,10},{10,8},{12,14},{14,12},{16,18},{18,... | collective-permute-start | bytes 86024 | tf_op jit(solution)/shard_map/ppermute | solution.py:612
  42.5 1.9 %collective-permute-start.14 = (bf16[112,128]{1,0:T(8,128)(2,1)S(1)}, bf16[112,128]{1,0:T(8,128)(2,1)S(1)}, u32[]{:S(2)}, u32[]{:S(2)}) collective-permute-start(bf16[112,128]{1,0:T(8,128)(2,1)S(1)} %get-tuple-element.98), channel_id=1, source_target_pairs={{0,8},{2,4},{4,2},{6,14},{8,0},{10,12},{12,10},{14,6},{16,24},{18,... | collective-permute-start | bytes 86024 | tf_op jit(solution)/shard_map/ppermute | solution.py:612
  45.4 5.4 %collective-permute-start.15 = (bf16[592,128]{1,0:T(8,128)(2,1)S(1)}, bf16[592,128]{1,0:T(8,128)(2,1)S(1)}, u32[]{:S(2)}, u32[]{:S(2)}) collective-permute-start(bf16[592,128]{1,0:T(8,128)(2,1)S(1)} %get-tuple-element.102), channel_id=1, source_target_pairs={{0,1},{1,0},{2,3},{3,2},{4,5},{5,4},{6,7},{7,6},{8,9},{9,8},{10,11... | collective-permute-start | bytes 454664 | tf_op jit(solution)/shard_map/ppermute | solution.py:654
  51.9 3.4 %collective-permute-start.16 = (bf16[112,128]{1,0:T(8,128)(2,1)S(1)}, bf16[112,128]{1,0:T(8,128)(2,1)S(1)}, u32[]{:S(2)}, u32[]{:S(2)}) collective-permute-start(bf16[112,128]{1,0:T(8,128)(2,1)S(1)} %get-tuple-element.104), channel_id=1, source_target_pairs={{0,24},{2,26},{4,28},{6,30},{8,16},{10,18},{12,20},{14,22},{16,8},... | collective-permute-start | bytes 86024 | tf_op jit(solution)/shard_map/ppermute | solution.py:612
  52.0 3.3 %collective-permute-start.17 = (bf16[112,128]{1,0:T(8,128)(2,1)S(1)}, bf16[112,128]{1,0:T(8,128)(2,1)S(1)}, u32[]{:S(2)}, u32[]{:S(2)}) collective-permute-start(bf16[112,128]{1,0:T(8,128)(2,1)S(1)} %get-tuple-element.105), channel_id=1, source_target_pairs={{0,8},{2,10},{4,12},{6,14},{8,0},{10,2},{12,4},{14,6},{16,24},{18,... | collective-permute-start | bytes 86024 | tf_op jit(solution)/shard_map/ppermute | solution.py:612
  55.3 3.9 %collective-permute-start.18 = (bf16[112,128]{1,0:T(8,128)(2,1)S(1)}, bf16[112,128]{1,0:T(8,128)(2,1)S(1)}, u32[]{:S(2)}, u32[]{:S(2)}) collective-permute-start(bf16[112,128]{1,0:T(8,128)(2,1)S(1)} %get-tuple-element.108), channel_id=1, source_target_pairs={{0,2},{2,0},{4,6},{6,4},{8,10},{10,8},{12,14},{14,12},{16,18},{18,... | collective-permute-start | bytes 86024 | tf_op jit(solution)/shard_map/ppermute | solution.py:612
  57.3 1.9 %collective-permute-start.19 = (bf16[112,128]{1,0:T(8,128)(2,1)S(1)}, bf16[112,128]{1,0:T(8,128)(2,1)S(1)}, u32[]{:S(2)}, u32[]{:S(2)}) collective-permute-start(bf16[112,128]{1,0:T(8,128)(2,1)S(1)} %get-tuple-element.109), channel_id=1, source_target_pairs={{0,8},{2,4},{4,2},{6,14},{8,0},{10,12},{12,10},{14,6},{16,24},{18,... | collective-permute-start | bytes 86024 | tf_op jit(solution)/shard_map/ppermute | solution.py:612
  59.3 4.2 %collective-permute-start.20 = (bf16[208,128]{1,0:T(8,128)(2,1)S(1)}, bf16[208,128]{1,0:T(8,128)(2,1)S(1)}, u32[]{:S(2)}, u32[]{:S(2)}) collective-permute-start(bf16[208,128]{1,0:T(8,128)(2,1)S(1)} %get-tuple-element.112), channel_id=1, source_target_pairs={{0,1},{1,0},{2,3},{3,2},{4,5},{5,4},{6,7},{7,6},{8,9},{9,8},{10,11... | collective-permute-start | bytes 159752 | tf_op jit(solution)/shard_map/ppermute | solution.py:661

commit v10 on v9

--- a/solution.py
+++ b/solution.py
@@ -311,7 +311,8 @@
     return [shape(sz.xface, sz.orb, HALO)] * 2 + [shape(sz.yface, sz.orb, F32)] * 2
 
 
-def start_body(sz, parts, r, *faces):
+def start_body(sz, parts, cells, r, cells_out, *faces):
+    cells_out[...] = cells[...].astype(F32)
     nz = parts.shape[2]
     r[...] = jnp.zeros(r.shape, F32)
     for a in range(sz.nx):
@@ -321,10 +322,11 @@
     write_faces(sz, r, *faces)
 
 
-def start_faces(sz, parts, after):
-    outs = [shape(sz.rows_all, sz.orb, F32)] + face_outs(sz)
-    r, *faces = kernel_call(functools.partial(start_body, sz), outs, [parts], after=after)
-    return r, faces
+def start_faces(sz, parts, cells, after):
+    outs = [shape(sz.rows_all, sz.orb, F32), shape(*cells.shape, F32)] + face_outs(sz)
+    body = functools.partial(start_body, sz)
+    r, cells, *faces = kernel_call(body, outs, [parts, cells], after=after)
+    return r, cells, faces
 
 
 def cross_body(sz, xr_one, xr_two, ry_lo, ry_hi, sy_one, sy_two):
@@ -496,10 +498,11 @@
         add_z(sz, y, j, messages[shift - 1][SLOTS : SLOTS + sz.zface, :].astype(F32))
     blocks = [cell_block(sz, y, cell) for cell in sz.cells]
     stiff = dot(kin[...], jnp.concatenate([b.astype(BF16) for b in blocks], axis=1))
+    spread = dot(qt[: sz.cell_pad * len(sz.cells), :], coef)
     for g, (p, q) in enumerate(sz.cells):
         rows = slice(g * sz.cell_pad, (g + 1) * sz.cell_pad)
         value = stiff[:, g * sz.orb : (g + 1) * sz.orb] + pot[rows, :] * blocks[g]
-        value = (value + dot(qt[rows, :], coef)) * scale
+        value = (value + spread[rows]) * scale
         for a in range(EDGE):
             start = (ORDER * p + a) * sz.line_x + ORDER * q * PAD
             line = value[a * EDGE * PAD : (a + 1) * EDGE * PAD]
@@ -622,8 +625,8 @@
 
     proj = projectors.reshape(nodes, POS * BLK * PA)
     proj = jnp.pad(proj, ((0, up(nodes, 16) - nodes), (0, 0)))
-    cells = jnp.transpose(slot_cells.reshape(POS, BLK)).astype(F32)
-    r, faces = start_faces(sz, parts, [cells, proj])
+    cells = jnp.transpose(slot_cells.reshape(POS, BLK))
+    r, cells, faces = start_faces(sz, parts, cells, [proj])
 
     def exchange_xy(sx_one, sx_two, sy_lo, sy_hi):
         xr = swap_faces("gx", sx_one, sx_two)

time: 64.6 us -> 63.7 us (0.986)
  other arithmetic: 0.75 us -> 0 us
    convert_element_type x1 -> x0, other arithmetic: 0.75 us -> none  [local(): cells = jnp.transpose(slot_cells.reshape(POS, BLK)).astype(F32)]
where the time goes in v10:
time: 63.7 us; the launch traced here: 63.5 us
  waiting for transfers between devices  26.5 us (42%)
  starting transfers between devices  22.2 us (35%)
  Pallas kernels  13.1 us (21%)
  local copies, waits for them, and re-layouts  1.5 us (2%)
    ppermute x16, starting transfers between devices, swap_faces(): out.append(lax.ppermute(face, axes, pairs))  14.2 us
    ppermute x16, waiting for transfers between devices, swap_faces(): out.append(lax.ppermute(face, axes, pairs))  13.5 us
    pallas_call x19, Pallas kernels, kernel_call(): pl.pallas_call(with_waits, out_shape=outs, in_specs=[VMEM] * used + [pl.B...  13.1 us
    ppermute x3, waiting for transfers between devices, local(): lax.ppermute(m, 'gz', ring[s + 1])  9.34 us
    ppermute x3, starting transfers between devices, local(): lax.ppermute(m, 'gz', ring[s + 1])  4.75 us
    ppermute x1, waiting for transfers between devices, local(): zr = [lax.ppermute(f, 'gz', ring[s]) for f, s in zip(sent, link_shifts(sz))]  2.43 us
    ppermute x1, starting transfers between devices, local(): zr = [lax.ppermute(f, 'gz', ring[s]) for f, s in zip(sent, link_shifts(sz))]  1.59 us
    ppermute x1, starting transfers between devices, local(): qfaces.append(lax.ppermute(face_rows[j], 'gz', back))  1.58 us
  transfers between devices with their start and end apart: 21, of which 12 were waited for; matrix products, arithmetic and copies ran while one was open for 0% of the time, Pallas kernels for 10%

profile of v10, /device:TPU:0, one launch (start us, length us, event | category | flops | bytes accessed | tf_op | source)
XLA Modules:
  0.0 63.5 jit_solution(6519364171692234150)
XLA Ops:
  0.0 0.0 copy-start
  0.0 1.4 %pad.4.refs_2_.refs_0_ = bf16[352,1536]{1,0:T(8,128)(2,1)S(1)} pad(bf16[343,1536]{1,0:T(8,128)(2,1)} %bitcast.11, bf16[]{:T(256)} %constant.2.clone.1), padding=0_9x0_0 | pad | bytes 2135042 | tf_op jit(solution)/shard_map/jit(_pad)/pad | solution.py:627
  1.4 0.0 copy-done.2
  1.4 0.1 copy-done.1
  1.5 0.1 shard_map.73
  1.6 2.4 %collective-permute-start = (bf16[112,128]{1,0:T(8,128)(2,1)S(1)}, bf16[112,128]{1,0:T(8,128)(2,1)S(1)}, u32[]{:S(2)}, u32[]{:S(2)}) collective-permute-start(bf16[112,128]{1,0:T(8,128)(2,1)S(1)} %get-tuple-element.61), channel_id=1, source_target_pairs={{0,24},{2,26},{4,28},{6,30},{8,16},{10,18},{12,20},{14,22},{16,8},... | collective-permute-start | bytes 86024 | tf_op jit(solution)/shard_map/ppermute | solution.py:615
  4.0 0.7 %collective-permute-start.1 = (bf16[112,128]{1,0:T(8,128)(2,1)S(1)}, bf16[112,128]{1,0:T(8,128)(2,1)S(1)}, u32[]{:S(2)}, u32[]{:S(2)}) collective-permute-start(bf16[112,128]{1,0:T(8,128)(2,1)S(1)} %get-tuple-element.62), channel_id=1, source_target_pairs={{0,8},{2,10},{4,12},{6,14},{8,0},{10,2},{12,4},{14,6},{16,24},{18,... | collective-permute-start | bytes 86024 | tf_op jit(solution)/shard_map/ppermute | solution.py:615
  4.7 2.3 %shard_map.75 = (bf16[1664,384]{1,0:T(8,128)(2,1)S(1)}, bf16[384,256]{1,0:T(8,128)(2,1)S(1)}) custom-call(bf16[352,1536]{1,0:T(8,128)(2,1)S(1)} %pad.4.refs_2_.refs_0_, f32[4,32]{1,0:T(4,128)S(1)} %get-tuple-element.67.refs_1_), custom_call_target="tpu_custom_call" | custom-call | flops 3000000000 | bytes 2556416 | tf_op jit(solution)/shard_map/pallas_call | solution.py:62
  7.0 1.6 %collective-permute-start.4 = (bf16[384,256]{1,0:T(8,128)(2,1)S(1)}, bf16[384,256]{1,0:T(8,128)(2,1)S(1)}, u32[]{:S(2)}, u32[]{:S(2)}) collective-permute-start(bf16[384,256]{1,0:T(8,128)(2,1)S(1)} %get-tuple-element.70), channel_id=1, source_target_pairs={{1,0},{0,1},{3,2},{2,3},{5,4},{4,5},{7,6},{6,7},{9,8},{8,9},{11,10... | collective-permute-start | bytes 589832 | tf_op jit(solution)/shard_map/ppermute | solution.py:642
  8.6 0.0 copy-done
  8.7 0.0 collective-permute-done.refs_0_.refs_1_
  8.7 0.0 collective-permute-done.1.refs_1_.refs_2_
  8.7 1.6 %collective-permute-start.2 = (bf16[112,128]{1,0:T(8,128)(2,1)S(1)}, bf16[112,128]{1,0:T(8,128)(2,1)S(1)}, u32[]{:S(2)}, u32[]{:S(2)}) collective-permute-start(bf16[112,128]{1,0:T(8,128)(2,1)S(1)} %get-tuple-element.65), channel_id=1, source_target_pairs={{0,2},{2,0},{4,6},{6,4},{8,10},{10,8},{12,14},{14,12},{16,18},{18,... | collective-permute-start | bytes 86024 | tf_op jit(solution)/shard_map/ppermute | solution.py:615
  10.4 0.0 collective-permute-start.3
  10.4 0.0 copy-done.3
  10.4 0.0 copy-done.4
  10.4 1.8 %shard_map.76 = (bf16[384,1664]{1,0:T(8,128)(2,1)S(1)}, bf16[400,400]{1,0:T(8,128)(2,1)S(1)}, f32[1600,128]{1,0:T(8,128)S(1)}, bf16[384,768]{1,0:T(8,128)(2,1)S(...) custom-call(bf16[1664,384]{1,0:T(8,128)(2,1)S(1)} %get-tuple-element.68.refs_0_.refs_5_, ...), custom_call_target="tpu_custom_call" | custom-call | flops 1000000000 | bytes 5447570 | tf_op jit(solution)/shard_map/pallas_call | solution.py:62
  12.2 0.4 collective-permute-done.2.refs_3_
  12.6 0.0 collective-permute-done.3.refs_4_
  12.6 1.3 %collective-permute-done.4.refs_6_.refs_7_.refs_8_ = bf16[384,256]{1,0:T(8,128)(2,1)S(1)} collective-permute-done((bf16[384,256]{1,0:T(8,128)(2,1)S(1)}, bf16[384,256]{1,0:T(8,128)(2,1)S(1)}, u32[]{:S(2)}, u32[]{:S(2)}) %collective-permute-start.4) | collective-permute-done | bytes 196640 | tf_op jit(solution)/shard_map/ppermute | solution.py:642
  13.9 0.9 %shard_map.77 = (f32[1384,128]{1,0:T(8,128)S(1)}, f32[384,128]{1,0:T(8,128)S(1)}, bf16[384,128]{1,0:T(8,128)(2,1)S(1)}, bf16[592,128]{1,0:T(8,128)(2,1)S(1)}) custom-call(f32[1384,128]{1,0:T(8,128)S(1)} %get-tuple-element.60.refs_0_, bf16[112,128]{1,0:T(8,128)(2,1)S(1)} %collective-permute-done.refs_0_.refs_1_, ...), custom_call_target="tpu_custom_call" | custom-call | flops 400000000 | bytes 4042752 | tf_op jit(solution)/shard_map/pallas_call | solution.py:62
  14.8 1.6 %collective-permute-start.5 = (bf16[592,128]{1,0:T(8,128)(2,1)S(1)}, bf16[592,128]{1,0:T(8,128)(2,1)S(1)}, u32[]{:S(2)}, u32[]{:S(2)}) collective-permute-start(bf16[592,128]{1,0:T(8,128)(2,1)S(1)} %get-tuple-element.78), channel_id=1, source_target_pairs={{0,1},{1,0},{2,3},{3,2},{4,5},{5,4},{6,7},{7,6},{8,9},{9,8},{10,11... | collective-permute-start | bytes 454664 | tf_op jit(solution)/shard_map/ppermute | solution.py:657
  16.4 0.6 shard_map.78.refs_1_
  17.0 3.1 %collective-permute-done.5.refs_2_ = bf16[592,128]{1,0:T(8,128)(2,1)S(1)} collective-permute-done((bf16[592,128]{1,0:T(8,128)(2,1)S(1)}, bf16[592,128]{1,0:T(8,128)(2,1)S(1)}, u32[]{:S(2)}, u32[]{:S(2)}) %collective-permute-start.5) | collective-permute-done | bytes 151584 | tf_op jit(solution)/shard_map/ppermute | solution.py:657
  20.1 1.0 %shard_map.79 = (f32[1384,128]{1,0:T(8,128)S(1)}, f32[1384,128]{1,0:T(8,128)S(1)}, bf16[112,128]{1,0:T(8,128)(2,1)S(1)}, bf16[112,128]{1,0:T(8,128)(2,1)S(1)}, f...) custom-call(f32[1384,128]{1,0:T(8,128)S(1)} %get-tuple-element.72.refs_0_, f32[384,128]{1,0:T(8,128)S(1)} %shard_map.78.refs_1_, ...), custom_call_target="tpu_custom_call" | custom-call | flops 600000000 | bytes 5652992 | tf_op jit(solution)/shard_map/pallas_call | solution.py:62
  21.0 0.1 collective-permute-start.6
  21.1 0.9 %collective-permute-start.7 = (bf16[112,128]{1,0:T(8,128)(2,1)S(1)}, bf16[112,128]{1,0:T(8,128)(2,1)S(1)}, u32[]{:S(2)}, u32[]{:S(2)}) collective-permute-start(bf16[112,128]{1,0:T(8,128)(2,1)S(1)} %get-tuple-element.84), channel_id=1, source_target_pairs={{0,8},{2,10},{4,12},{6,14},{8,0},{10,2},{12,4},{14,6},{16,24},{18,... | collective-permute-start | bytes 86024 | tf_op jit(solution)/shard_map/ppermute | solution.py:615
  22.0 2.4 %collective-permute-done.6.refs_0_.refs_2_ = bf16[112,128]{1,0:T(8,128)(2,1)S(1)} collective-permute-done((bf16[112,128]{1,0:T(8,128)(2,1)S(1)}, bf16[112,128]{1,0:T(8,128)(2,1)S(1)}, u32[]{:S(2)}, u32[]{:S(2)}) %collective-permute-start.6) | collective-permute-done | bytes 28704 | tf_op jit(solution)/shard_map/ppermute | solution.py:615
  24.4 0.0 collective-permute-done.7.refs_1_.refs_3_
  24.4 1.6 %collective-permute-start.8 = (bf16[112,128]{1,0:T(8,128)(2,1)S(1)}, bf16[112,128]{1,0:T(8,128)(2,1)S(1)}, u32[]{:S(2)}, u32[]{:S(2)}) collective-permute-start(bf16[112,128]{1,0:T(8,128)(2,1)S(1)} %get-tuple-element.87), channel_id=1, source_target_pairs={{0,2},{2,0},{4,6},{6,4},{8,10},{10,8},{12,14},{14,12},{16,18},{18,... | collective-permute-start | bytes 86024 | tf_op jit(solution)/shard_map/ppermute | solution.py:615
  26.1 0.0 collective-permute-start.9
  26.1 2.3 %collective-permute-done.8.refs_4_ = bf16[112,128]{1,0:T(8,128)(2,1)S(1)} collective-permute-done((bf16[112,128]{1,0:T(8,128)(2,1)S(1)}, bf16[112,128]{1,0:T(8,128)(2,1)S(1)}, u32[]{:S(2)}, u32[]{:S(2)}) %collective-permute-start.8) | collective-permute-done | bytes 28704 | tf_op jit(solution)/shard_map/ppermute | solution.py:615
  28.4 0.0 collective-permute-done.9.refs_5_
  28.4 0.9 %shard_map.81 = (f32[1384,128]{1,0:T(8,128)S(1)}, f32[384,128]{1,0:T(8,128)S(1)}, bf16[384,128]{1,0:T(8,128)(2,1)S(1)}, bf16[592,128]{1,0:T(8,128)(2,1)S(1)}) custom-call(f32[1384,128]{1,0:T(8,128)S(1)} %get-tuple-element.81.refs_0_, f32[1384,128]{1,0:T(8,128)S(1)} %get-tuple-element.82.refs_1_.refs_2_, ...), custom_call_target="tpu_custom_call" | custom-call | flops 400000000 | bytes 4751360 | tf_op jit(solution)/shard_map/pallas_call | solution.py:62
  29.3 1.6 %collective-permute-start.10 = (bf16[592,128]{1,0:T(8,128)(2,1)S(1)}, bf16[592,128]{1,0:T(8,128)(2,1)S(1)}, u32[]{:S(2)}, u32[]{:S(2)}) collective-permute-start(bf16[592,128]{1,0:T(8,128)(2,1)S(1)} %get-tuple-element.92), channel_id=1, source_target_pairs={{0,1},{1,0},{2,3},{3,2},{4,5},{5,4},{6,7},{7,6},{8,9},{9,8},{10,11... | collective-permute-start | bytes 454664 | tf_op jit(solution)/shard_map/ppermute | solution.py:657
  30.9 0.6 shard_map.82.refs_1_
  31.5 3.1 %collective-permute-done.10.refs_2_ = bf16[592,128]{1,0:T(8,128)(2,1)S(1)} collective-permute-done((bf16[592,128]{1,0:T(8,128)(2,1)S(1)}, bf16[592,128]{1,0:T(8,128)(2,1)S(1)}, u32[]{:S(2)}, u32[]{:S(2)}) %collective-permute-start.10) | collective-permute-done | bytes 151584 | tf_op jit(solution)/shard_map/ppermute | solution.py:657
  34.6 1.0 %shard_map.83 = (f32[1384,128]{1,0:T(8,128)S(1)}, f32[1384,128]{1,0:T(8,128)S(1)}, bf16[112,128]{1,0:T(8,128)(2,1)S(1)}, bf16[112,128]{1,0:T(8,128)(2,1)S(1)}, f...) custom-call(f32[1384,128]{1,0:T(8,128)S(1)} %get-tuple-element.89.refs_0_, f32[384,128]{1,0:T(8,128)S(1)} %shard_map.82.refs_1_, ...), custom_call_target="tpu_custom_call" | custom-call | flops 600000000 | bytes 5652992 | tf_op jit(solution)/shard_map/pallas_call | solution.py:62
  35.5 0.1 collective-permute-start.11
  35.6 1.0 %collective-permute-start.12 = (bf16[112,128]{1,0:T(8,128)(2,1)S(1)}, bf16[112,128]{1,0:T(8,128)(2,1)S(1)}, u32[]{:S(2)}, u32[]{:S(2)}) collective-permute-start(bf16[112,128]{1,0:T(8,128)(2,1)S(1)} %get-tuple-element.96), channel_id=1, source_target_pairs={{0,8},{2,10},{4,12},{6,14},{8,0},{10,2},{12,4},{14,6},{16,24},{18,... | collective-permute-start | bytes 86024 | tf_op jit(solution)/shard_map/ppermute | solution.py:615
  36.6 2.3 %collective-permute-done.11.refs_0_.refs_3_ = bf16[112,128]{1,0:T(8,128)(2,1)S(1)} collective-permute-done((bf16[112,128]{1,0:T(8,128)(2,1)S(1)}, bf16[112,128]{1,0:T(8,128)(2,1)S(1)}, u32[]{:S(2)}, u32[]{:S(2)}) %collective-permute-start.11) | collective-permute-done | bytes 28704 | tf_op jit(solution)/shard_map/ppermute | solution.py:615
  38.9 0.0 collective-permute-done.12.refs_1_.refs_4_
  38.9 2.8 %collective-permute-start.13 = (bf16[112,128]{1,0:T(8,128)(2,1)S(1)}, bf16[112,128]{1,0:T(8,128)(2,1)S(1)}, u32[]{:S(2)}, u32[]{:S(2)}) collective-permute-start(bf16[112,128]{1,0:T(8,128)(2,1)S(1)} %get-tuple-element.99), channel_id=1, source_target_pairs={{0,2},{2,0},{4,6},{6,4},{8,10},{10,8},{12,14},{14,12},{16,18},{18,... | collective-permute-start | bytes 86024 | tf_op jit(solution)/shard_map/ppermute | solution.py:615
  41.7 0.0 collective-permute-start.14
  41.7 1.8 %collective-permute-done.13.refs_5_ = bf16[112,128]{1,0:T(8,128)(2,1)S(1)} collective-permute-done((bf16[112,128]{1,0:T(8,128)(2,1)S(1)}, bf16[112,128]{1,0:T(8,128)(2,1)S(1)}, u32[]{:S(2)}, u32[]{:S(2)}) %collective-permute-start.13) | collective-permute-done | bytes 28704 | tf_op jit(solution)/shard_map/ppermute | solution.py:615
  43.5 0.0 collective-permute-done.14.refs_6_
  43.6 1.0 %shard_map.85 = (f32[1384,128]{1,0:T(8,128)S(1)}, f32[384,128]{1,0:T(8,128)S(1)}, bf16[384,128]{1,0:T(8,128)(2,1)S(1)}, bf16[592,128]{1,0:T(8,128)(2,1)S(1)}) custom-call(f32[1384,128]{1,0:T(8,128)S(1)} %get-tuple-element.93.refs_0_, f32[1384,128]{1,0:T(8,128)S(1)} %get-tuple-element.94.refs_1_.refs_2_, f32[1384,128]{1,0:T(8,128)S(1)} %get-tuple-element.82.refs_1_.refs_2_, ...), custom_call_target="tpu_custom_call" | custom-call | flops 400000000 | bytes 5459968 | tf_op jit(solution)/shard_map/pallas_call | solution.py:62
  44.5 1.6 %collective-permute-start.15 = (bf16[592,128]{1,0:T(8,128)(2,1)S(1)}, bf16[592,128]{1,0:T(8,128)(2,1)S(1)}, u32[]{:S(2)}, u32[]{:S(2)}) collective-permute-start(bf16[592,128]{1,0:T(8,128)(2,1)S(1)} %get-tuple-element.104), channel_id=1, source_target_pairs={{0,1},{1,0},{2,3},{3,2},{4,5},{5,4},{6,7},{7,6},{8,9},{9,8},{10,11... | collective-permute-start | bytes 454664 | tf_op jit(solution)/shard_map/ppermute | solution.py:657
  46.1 0.6 shard_map.86.refs_1_
  46.7 3.2 %collective-permute-done.15.refs_2_ = bf16[592,128]{1,0:T(8,128)(2,1)S(1)} collective-permute-done((bf16[592,128]{1,0:T(8,128)(2,1)S(1)}, bf16[592,128]{1,0:T(8,128)(2,1)S(1)}, u32[]{:S(2)}, u32[]{:S(2)}) %collective-permute-start.15) | collective-permute-done | bytes 151584 | tf_op jit(solution)/shard_map/ppermute | solution.py:657
  50.0 1.0 %shard_map.87 = (f32[1384,128]{1,0:T(8,128)S(1)}, f32[1384,128]{1,0:T(8,128)S(1)}, bf16[112,128]{1,0:T(8,128)(2,1)S(1)}, bf16[112,128]{1,0:T(8,128)(2,1)S(1)}, f...) custom-call(f32[1384,128]{1,0:T(8,128)S(1)} %get-tuple-element.101.refs_0_, f32[384,128]{1,0:T(8,128)S(1)} %shard_map.86.refs_1_, ...), custom_call_target="tpu_custom_call" | custom-call | flops 600000000 | bytes 5652992 | tf_op jit(solution)/shard_map/pallas_call | solution.py:62
  51.0 0.1 collective-permute-start.16
  51.0 1.0 %collective-permute-start.17 = (bf16[112,128]{1,0:T(8,128)(2,1)S(1)}, bf16[112,128]{1,0:T(8,128)(2,1)S(1)}, u32[]{:S(2)}, u32[]{:S(2)}) collective-permute-start(bf16[112,128]{1,0:T(8,128)(2,1)S(1)} %get-tuple-element.107), channel_id=1, source_target_pairs={{0,8},{2,10},{4,12},{6,14},{8,0},{10,2},{12,4},{14,6},{16,24},{18,... | collective-permute-start | bytes 86024 | tf_op jit(solution)/shard_map/ppermute | solution.py:615
  52.0 2.3 %collective-permute-done.16.refs_0_.refs_1_ = bf16[112,128]{1,0:T(8,128)(2,1)S(1)} collective-permute-done((bf16[112,128]{1,0:T(8,128)(2,1)S(1)}, bf16[112,128]{1,0:T(8,128)(2,1)S(1)}, u32[]{:S(2)}, u32[]{:S(2)}) %collective-permute-start.16) | collective-permute-done | bytes 28704 | tf_op jit(solution)/shard_map/ppermute | solution.py:615
  54.3 0.0 collective-permute-done.17.refs_1_.refs_2_
  54.4 2.0 %collective-permute-start.18 = (bf16[112,128]{1,0:T(8,128)(2,1)S(1)}, bf16[112,128]{1,0:T(8,128)(2,1)S(1)}, u32[]{:S(2)}, u32[]{:S(2)}) collective-permute-start(bf16[112,128]{1,0:T(8,128)(2,1)S(1)} %get-tuple-element.110), channel_id=1, source_target_pairs={{0,2},{2,0},{4,6},{6,4},{8,10},{10,8},{12,14},{14,12},{16,18},{18,... | collective-permute-start | bytes 86024 | tf_op jit(solution)/shard_map/ppermute | solution.py:615
  56.4 0.0 collective-permute-start.19
  56.4 1.9 %collective-permute-done.18.refs_3_ = bf16[112,128]{1,0:T(8,128)(2,1)S(1)} collective-permute-done((bf16[112,128]{1,0:T(8,128)(2,1)S(1)}, bf16[112,128]{1,0:T(8,128)(2,1)S(1)}, u32[]{:S(2)}, u32[]{:S(2)}) %collective-permute-start.18) | collective-permute-done | bytes 28704 | tf_op jit(solution)/shard_map/ppermute | solution.py:615
  58.3 0.0 collective-permute-done.19.refs_4_
  58.3 0.1 shard_map.89
  58.4 1.6 %collective-permute-start.20 = (bf16[208,128]{1,0:T(8,128)(2,1)S(1)}, bf16[208,128]{1,0:T(8,128)(2,1)S(1)}, u32[]{:S(2)}, u32[]{:S(2)}) collective-permute-start(bf16[208,128]{1,0:T(8,128)(2,1)S(1)} %get-tuple-element.114), channel_id=1, source_target_pairs={{0,1},{1,0},{2,3},{3,2},{4,5},{5,4},{6,7},{7,6},{8,9},{9,8},{10,11... | collective-permute-start | bytes 159752 | tf_op jit(solution)/shard_map/ppermute | solution.py:664
  60.0 0.2 shard_map.90.refs_0_
  60.2 2.4 %collective-permute-done.20.refs_1_ = bf16[208,128]{1,0:T(8,128)(2,1)S(1)} collective-permute-done((bf16[208,128]{1,0:T(8,128)(2,1)S(1)}, bf16[208,128]{1,0:T(8,128)(2,1)S(1)}, u32[]{:S(2)}, u32[]{:S(2)}) %collective-permute-start.20) | collective-permute-done | bytes 53280 | tf_op jit(solution)/shard_map/ppermute | solution.py:664
  62.6 0.9 %shard_map.91 = f32[13,13,7,128]{3,2,1,0:T(8,128)} custom-call(f32[1384,128]{1,0:T(8,128)S(1)} %shard_map.90.refs_0_, bf16[208,128]{1,0:T(8,128)(2,1)S(1)} %collective-permute-done.20.refs_1_), custom_call_target="tpu_custom_call" | custom-call | bytes 1367552 | tf_op jit(solution)/shard_map/pallas_call | solution.py:62
  (12 shorter events, 0.2 us)
Async XLA Ops:
  0.0 8.6 %copy-start = (f32[343,2,2,1]{0,3,2,1:T(1,128)S(1)}, f32[343,2,2,1]{0,3,2,1:T(1,128)}, u32[]{:S(2)}) copy-start(f32[343,2,2,1]{0,3,2,1:T(1,128)} %param.9) | copy-start | bytes 16468
  0.0 1.4 %copy-start.2 = (s32[1,1,1,32,4]{3,4,2,1,0:T(4,128)S(1)}, s32[1,1,1,32,4]{3,4,2,1,0:T(4,128)}, u32[]{:S(2)}) copy-start(s32[1,1,1,32,4]{3,4,2,1,0:T(4,128)} %param.12) | copy-start | bytes 1540
  0.0 1.4 %copy-start.1 = (f32[13,13,7,128]{3,2,1,0:T(8,128)S(1)}, f32[13,13,7,128]{3,2,1,0:T(8,128)}, u32[]{:S(2)}) copy-start(f32[13,13,7,128]{3,2,1,0:T(8,128)} %refs_0_.1) | copy-start | bytes 1817092
  1.6 7.1 %collective-permute-start = (bf16[112,128]{1,0:T(8,128)(2,1)S(1)}, bf16[112,128]{1,0:T(8,128)(2,1)S(1)}, u32[]{:S(2)}, u32[]{:S(2)}) collective-permute-start(bf16[112,128]{1,0:T(8,128)(2,1)S(1)} %get-tuple-element.61), channel_id=1, source_target_pairs={{0,24},{2,26},{4,28},{6,30},{8,16},{10,18},{12,20},{14,22},{16,8},... | collective-permute-start | bytes 86024 | tf_op jit(solution)/shard_map/ppermute | solution.py:615
  4.0 4.6 %collective-permute-start.1 = (bf16[112,128]{1,0:T(8,128)(2,1)S(1)}, bf16[112,128]{1,0:T(8,128)(2,1)S(1)}, u32[]{:S(2)}, u32[]{:S(2)}) collective-permute-start(bf16[112,128]{1,0:T(8,128)(2,1)S(1)} %get-tuple-element.62), channel_id=1, source_target_pairs={{0,8},{2,10},{4,12},{6,14},{8,0},{10,2},{12,4},{14,6},{16,24},{18,... | collective-permute-start | bytes 86024 | tf_op jit(solution)/shard_map/ppermute | solution.py:615
  4.7 5.7 %copy-start.3 = (bf16[343,343]{1,0:T(8,128)(2,1)S(1)}, bf16[343,343]{1,0:T(8,128)(2,1)}, u32[]{:S(2)}) copy-start(bf16[343,343]{1,0:T(8,128)(2,1)} %refs_1_.1) | copy-start | bytes 705898
  4.7 5.7 %copy-start.4 = (f32[64,12,12]{0,2,1:T(8,128)S(1)}, f32[64,12,12]{0,2,1:T(8,128)}, u32[]{:S(2)}) copy-start(f32[64,12,12]{0,2,1:T(8,128)} %param.13) | copy-start | bytes 110596
  4.7 5.7 %copy-start.5 = (s32[1,1,2,32]{3,2,1,0:T(2,128)S(1)}, s32[1,1,2,32]{3,2,1,0:T(2,128)}, u32[]{:S(2)}) copy-start(s32[1,1,2,32]{3,2,1,0:T(2,128)} %param.11) | copy-start | bytes 772
  7.0 6.9 %collective-permute-start.4 = (bf16[384,256]{1,0:T(8,128)(2,1)S(1)}, bf16[384,256]{1,0:T(8,128)(2,1)S(1)}, u32[]{:S(2)}, u32[]{:S(2)}) collective-permute-start(bf16[384,256]{1,0:T(8,128)(2,1)S(1)} %get-tuple-element.70), channel_id=1, source_target_pairs={{1,0},{0,1},{3,2},{2,3},{5,4},{4,5},{7,6},{6,7},{9,8},{8,9},{11,10... | collective-permute-start | bytes 589832 | tf_op jit(solution)/shard_map/ppermute | solution.py:642
  8.7 3.9 %collective-permute-start.2 = (bf16[112,128]{1,0:T(8,128)(2,1)S(1)}, bf16[112,128]{1,0:T(8,128)(2,1)S(1)}, u32[]{:S(2)}, u32[]{:S(2)}) collective-permute-start(bf16[112,128]{1,0:T(8,128)(2,1)S(1)} %get-tuple-element.65), channel_id=1, source_target_pairs={{0,2},{2,0},{4,6},{6,4},{8,10},{10,8},{12,14},{14,12},{16,18},{18,... | collective-permute-start | bytes 86024 | tf_op jit(solution)/shard_map/ppermute | solution.py:615
  10.4 2.3 %collective-permute-start.3 = (bf16[112,128]{1,0:T(8,128)(2,1)S(1)}, bf16[112,128]{1,0:T(8,128)(2,1)S(1)}, u32[]{:S(2)}, u32[]{:S(2)}) collective-permute-start(bf16[112,128]{1,0:T(8,128)(2,1)S(1)} %get-tuple-element.66), channel_id=1, source_target_pairs={{0,8},{2,4},{4,2},{6,14},{8,0},{10,12},{12,10},{14,6},{16,24},{18,... | collective-permute-start | bytes 86024 | tf_op jit(solution)/shard_map/ppermute | solution.py:615
  14.8 5.3 %collective-permute-start.5 = (bf16[592,128]{1,0:T(8,128)(2,1)S(1)}, bf16[592,128]{1,0:T(8,128)(2,1)S(1)}, u32[]{:S(2)}, u32[]{:S(2)}) collective-permute-start(bf16[592,128]{1,0:T(8,128)(2,1)S(1)} %get-tuple-element.78), channel_id=1, source_target_pairs={{0,1},{1,0},{2,3},{3,2},{4,5},{5,4},{6,7},{7,6},{8,9},{9,8},{10,11... | collective-permute-start | bytes 454664 | tf_op jit(solution)/shard_map/ppermute | solution.py:657
  21.0 3.4 %collective-permute-start.6 = (bf16[112,128]{1,0:T(8,128)(2,1)S(1)}, bf16[112,128]{1,0:T(8,128)(2,1)S(1)}, u32[]{:S(2)}, u32[]{:S(2)}) collective-permute-start(bf16[112,128]{1,0:T(8,128)(2,1)S(1)} %get-tuple-element.83), channel_id=1, source_target_pairs={{0,24},{2,26},{4,28},{6,30},{8,16},{10,18},{12,20},{14,22},{16,8},... | collective-permute-start | bytes 86024 | tf_op jit(solution)/shard_map/ppermute | solution.py:615
  21.1 3.3 %collective-permute-start.7 = (bf16[112,128]{1,0:T(8,128)(2,1)S(1)}, bf16[112,128]{1,0:T(8,128)(2,1)S(1)}, u32[]{:S(2)}, u32[]{:S(2)}) collective-permute-start(bf16[112,128]{1,0:T(8,128)(2,1)S(1)} %get-tuple-element.84), channel_id=1, source_target_pairs={{0,8},{2,10},{4,12},{6,14},{8,0},{10,2},{12,4},{14,6},{16,24},{18,... | collective-permute-start | bytes 86024 | tf_op jit(solution)/shard_map/ppermute | solution.py:615
  24.4 3.9 %collective-permute-start.8 = (bf16[112,128]{1,0:T(8,128)(2,1)S(1)}, bf16[112,128]{1,0:T(8,128)(2,1)S(1)}, u32[]{:S(2)}, u32[]{:S(2)}) collective-permute-start(bf16[112,128]{1,0:T(8,128)(2,1)S(1)} %get-tuple-element.87), channel_id=1, source_target_pairs={{0,2},{2,0},{4,6},{6,4},{8,10},{10,8},{12,14},{14,12},{16,18},{18,... | collective-permute-start | bytes 86024 | tf_op jit(solution)/shard_map/ppermute | solution.py:615
  26.1 2.3 %collective-permute-start.9 = (bf16[112,128]{1,0:T(8,128)(2,1)S(1)}, bf16[112,128]{1,0:T(8,128)(2,1)S(1)}, u32[]{:S(2)}, u32[]{:S(2)}) collective-permute-start(bf16[112,128]{1,0:T(8,128)(2,1)S(1)} %get-tuple-element.88), channel_id=1, source_target_pairs={{0,8},{2,4},{4,2},{6,14},{8,0},{10,12},{12,10},{14,6},{16,24},{18,... | collective-permute-start | bytes 86024 | tf_op jit(solution)/shard_map/ppermute | solution.py:615
  29.3 5.3 %collective-permute-start.10 = (bf16[592,128]{1,0:T(8,128)(2,1)S(1)}, bf16[592,128]{1,0:T(8,128)(2,1)S(1)}, u32[]{:S(2)}, u32[]{:S(2)}) collective-permute-start(bf16[592,128]{1,0:T(8,128)(2,1)S(1)} %get-tuple-element.92), channel_id=1, source_target_pairs={{0,1},{1,0},{2,3},{3,2},{4,5},{5,4},{6,7},{7,6},{8,9},{9,8},{10,11... | collective-permute-start | bytes 454664 | tf_op jit(solution)/shard_map/ppermute | solution.py:657
  35.5 3.4 %collective-permute-start.11 = (bf16[112,128]{1,0:T(8,128)(2,1)S(1)}, bf16[112,128]{1,0:T(8,128)(2,1)S(1)}, u32[]{:S(2)}, u32[]{:S(2)}) collective-permute-start(bf16[112,128]{1,0:T(8,128)(2,1)S(1)} %get-tuple-element.95), channel_id=1, source_target_pairs={{0,24},{2,26},{4,28},{6,30},{8,16},{10,18},{12,20},{14,22},{16,8},... | collective-permute-start | bytes 86024 | tf_op jit(solution)/shard_map/ppermute | solution.py:615
  35.6 3.3 %collective-permute-start.12 = (bf16[112,128]{1,0:T(8,128)(2,1)S(1)}, bf16[112,128]{1,0:T(8,128)(2,1)S(1)}, u32[]{:S(2)}, u32[]{:S(2)}) collective-permute-start(bf16[112,128]{1,0:T(8,128)(2,1)S(1)} %get-tuple-element.96), channel_id=1, source_target_pairs={{0,8},{2,10},{4,12},{6,14},{8,0},{10,2},{12,4},{14,6},{16,24},{18,... | collective-permute-start | bytes 86024 | tf_op jit(solution)/shard_map/ppermute | solution.py:615
  38.9 4.6 %collective-permute-start.13 = (bf16[112,128]{1,0:T(8,128)(2,1)S(1)}, bf16[112,128]{1,0:T(8,128)(2,1)S(1)}, u32[]{:S(2)}, u32[]{:S(2)}) collective-permute-start(bf16[112,128]{1,0:T(8,128)(2,1)S(1)} %get-tuple-element.99), channel_id=1, source_target_pairs={{0,2},{2,0},{4,6},{6,4},{8,10},{10,8},{12,14},{14,12},{16,18},{18,... | collective-permute-start | bytes 86024 | tf_op jit(solution)/shard_map/ppermute | solution.py:615
  41.7 1.9 %collective-permute-start.14 = (bf16[112,128]{1,0:T(8,128)(2,1)S(1)}, bf16[112,128]{1,0:T(8,128)(2,1)S(1)}, u32[]{:S(2)}, u32[]{:S(2)}) collective-permute-start(bf16[112,128]{1,0:T(8,128)(2,1)S(1)} %get-tuple-element.100), channel_id=1, source_target_pairs={{0,8},{2,4},{4,2},{6,14},{8,0},{10,12},{12,10},{14,6},{16,24},{18,... | collective-permute-start | bytes 86024 | tf_op jit(solution)/shard_map/ppermute | solution.py:615
  44.5 5.4 %collective-permute-start.15 = (bf16[592,128]{1,0:T(8,128)(2,1)S(1)}, bf16[592,128]{1,0:T(8,128)(2,1)S(1)}, u32[]{:S(2)}, u32[]{:S(2)}) collective-permute-start(bf16[592,128]{1,0:T(8,128)(2,1)S(1)} %get-tuple-element.104), channel_id=1, source_target_pairs={{0,1},{1,0},{2,3},{3,2},{4,5},{5,4},{6,7},{7,6},{8,9},{9,8},{10,11... | collective-permute-start | bytes 454664 | tf_op jit(solution)/shard_map/ppermute | solution.py:657
  51.0 3.4 %collective-permute-start.16 = (bf16[112,128]{1,0:T(8,128)(2,1)S(1)}, bf16[112,128]{1,0:T(8,128)(2,1)S(1)}, u32[]{:S(2)}, u32[]{:S(2)}) collective-permute-start(bf16[112,128]{1,0:T(8,128)(2,1)S(1)} %get-tuple-element.106), channel_id=1, source_target_pairs={{0,24},{2,26},{4,28},{6,30},{8,16},{10,18},{12,20},{14,22},{16,8},... | collective-permute-start | bytes 86024 | tf_op jit(solution)/shard_map/ppermute | solution.py:615
  51.0 3.3 %collective-permute-start.17 = (bf16[112,128]{1,0:T(8,128)(2,1)S(1)}, bf16[112,128]{1,0:T(8,128)(2,1)S(1)}, u32[]{:S(2)}, u32[]{:S(2)}) collective-permute-start(bf16[112,128]{1,0:T(8,128)(2,1)S(1)} %get-tuple-element.107), channel_id=1, source_target_pairs={{0,8},{2,10},{4,12},{6,14},{8,0},{10,2},{12,4},{14,6},{16,24},{18,... | collective-permute-start | bytes 86024 | tf_op jit(solution)/shard_map/ppermute | solution.py:615
  54.4 3.9 %collective-permute-start.18 = (bf16[112,128]{1,0:T(8,128)(2,1)S(1)}, bf16[112,128]{1,0:T(8,128)(2,1)S(1)}, u32[]{:S(2)}, u32[]{:S(2)}) collective-permute-start(bf16[112,128]{1,0:T(8,128)(2,1)S(1)} %get-tuple-element.110), channel_id=1, source_target_pairs={{0,2},{2,0},{4,6},{6,4},{8,10},{10,8},{12,14},{14,12},{16,18},{18,... | collective-permute-start | bytes 86024 | tf_op jit(solution)/shard_map/ppermute | solution.py:615
  56.4 1.9 %collective-permute-start.19 = (bf16[112,128]{1,0:T(8,128)(2,1)S(1)}, bf16[112,128]{1,0:T(8,128)(2,1)S(1)}, u32[]{:S(2)}, u32[]{:S(2)}) collective-permute-start(bf16[112,128]{1,0:T(8,128)(2,1)S(1)} %get-tuple-element.111), channel_id=1, source_target_pairs={{0,8},{2,4},{4,2},{6,14},{8,0},{10,12},{12,10},{14,6},{16,24},{18,... | collective-permute-start | bytes 86024 | tf_op jit(solution)/shard_map/ppermute | solution.py:615
  58.4 4.2 %collective-permute-start.20 = (bf16[208,128]{1,0:T(8,128)(2,1)S(1)}, bf16[208,128]{1,0:T(8,128)(2,1)S(1)}, u32[]{:S(2)}, u32[]{:S(2)}) collective-permute-start(bf16[208,128]{1,0:T(8,128)(2,1)S(1)} %get-tuple-element.114), channel_id=1, source_target_pairs={{0,1},{1,0},{2,3},{3,2},{4,5},{5,4},{6,7},{7,6},{8,9},{9,8},{10,11... | collective-permute-start | bytes 159752 | tf_op jit(solution)/shard_map/ppermute | solution.py:664

commit v11 on v10

--- a/solution.py
+++ b/solution.py
@@ -46,6 +46,7 @@
         self.fcell = EDGE * PAD
         self.fall = up(self.fcell * len(self.cells), 256)
         self.shifts, self.links = shifts, min(2, shifts)
+        self.pair = shifts == 1
         self.rows_all = self.rows + (self.face_b - ny + 1) * PAD
 
 
@@ -202,9 +203,9 @@
 
 
 def turn_body(sz, qt, kin, pot, atoms, coupling, *refs):
-    q, kout, vout, maps = refs[:4]
-    back = refs[4] if sz.links else None
-    c_hi, c_lo, wide = refs[-3:]
+    own_rows, refs = (refs[0], refs[1:]) if sz.pair else (None, refs)
+    q, kout, vout, back, c_hi, c_lo = refs[:6]
+    *others, wide = refs[6:]
     q[...] = qt[...].T
     nodes = kin.shape[0]
     expand = (node_key(iota(sz.cell_pad, nodes, 0)) == iota(sz.cell_pad, nodes, 1)).astype(BF16)
@@ -227,7 +228,8 @@
         key = jnp.where(cols[shift][1] >= 0, cols[shift][1], -2)
         valid = link_valid(sz, j)
         known.append(key if valid is None else jnp.where(valid == 1, key, -2))
-    for s in range(sz.shifts):
+    for s in range(0 if sz.pair else sz.shifts):
+        maps = others[0]
         for j, key in enumerate(known):
             maps[s * SLOTS : (s + 1) * SLOTS, j * SLOTS : (j + 1) * SLOTS] = (
                 rows[s + 1][1] == key
@@ -249,24 +251,32 @@
         table2 = table2 - part.astype(F32)
         picked = jnp.where(own_row, dot_last(hot, part), 0.0).astype(BF16)
         out[...] = jnp.where(same, dot(picked, fold), 0.0).astype(BF16)
-
-
-def turn_matrices(sz, qt, kin, pot, atoms, coupling):
+    if sz.pair:
+        m_hi, m_lo, c_rows = others
+        m_hi[...] = dot(c_hi[...], back[...]).astype(BF16)
+        m_lo[...] = dot(c_lo[...], back[...]).astype(BF16)
+        c_rows[...] = (dot(c_hi[...], own_rows[...]) + dot(c_lo[...], own_rows[...])).astype(BF16)
+
+
+def turn_matrices(sz, qt, kin, pot, atoms, coupling, face_rows):
     known = (1 + sz.links) * SLOTS
     outs = [
         shape(SLOTS, sz.all_pad, BF16),
         shape(sz.cell_pad, sz.cell_pad, BF16),
         shape(len(sz.cells) * sz.cell_pad, sz.orb, F32),
-        shape(sz.shifts * SLOTS, known, BF16),
         shape(SLOTS, sz.links * SLOTS, BF16),
         shape(SLOTS, SLOTS, BF16),
         shape(SLOTS, SLOTS, BF16),
     ]
+    if sz.pair:
+        outs += [shape(SLOTS, SLOTS, BF16)] * 2 + [shape(*face_rows[0].shape, BF16)]
+    else:
+        outs += [shape(sz.shifts * SLOTS, known, BF16)]
     limit = (32 << 20) if sz.shifts < 8 else (56 << 20)
     return kernel_call(
         functools.partial(turn_body, sz),
         outs,
-        [qt, kin, pot, atoms, coupling],
+        [qt, kin, pot, atoms, coupling] + (face_rows if sz.pair else []),
         scratch=[pltpu.VMEM((coupling.shape[0], 16, coupling.shape[2]), F32)],
         flops=10**9,
         limit=limit,
@@ -402,14 +412,25 @@
     return jnp.concatenate(rows, axis=0).astype(BF16)
 
 
+def message_cells(sz, face):
+    rows = []
+    for p, q in sz.cells:
+        for a in range(EDGE):
+            at = (ORDER * p + a) * sz.face_b + ORDER * q
+            rows.append(face[at : at + PAD])
+        rows.append(jnp.zeros((PAD, sz.orb), F32))
+    return jnp.concatenate(rows, axis=0).astype(BF16)
+
+
 def project_body(sz, weight, past, refs):
     take = iter(refs)
     r = next(take)
     fields = [next(take) for _ in range(past)]
     halos = [next(take) for _ in range(4)]
     q = next(take)
-    qfaces = [next(take) for _ in range(sz.links)]
-    maps = next(take)
+    if not sz.pair:
+        qfaces = [next(take) for _ in range(sz.links)]
+        maps = next(take)
     y, own = next(take), next(take)
     beside = [next(take) for _ in range(sz.links)]
     messages = [next(take) for _ in range(sz.shifts)]
@@ -422,6 +443,11 @@
         blocks.append(jnp.zeros((rest, sz.orb), BF16))
     sums = dot(q[...], jnp.concatenate(blocks, axis=0))
     own[...] = sums
+    if sz.pair:
+        messages[0][0:SLOTS, :] = sums.astype(HALO)
+        messages[0][SLOTS : SLOTS + sz.zface, :] = pack_z(sz, y, weight, fields, 0)
+        beside[0][...] = face_cells(sz, y, weight, fields, 0)
+        return
     known = [sums.astype(BF16)]
     for j, matrix in enumerate(qfaces):
         value, valid = dot(matrix[...], face_cells(sz, y, weight, fields, j)), link_valid(sz, j)
@@ -439,9 +465,9 @@
         message[0:SLOTS, :] = total.astype(HALO)
 
 
-def project(sz, r, weight, fields, halos, q, qfaces, maps):
+def project(sz, r, weight, fields, halos, q, mapping):
     outs = [shape(sz.rows_all, sz.orb, F32), shape(SLOTS, sz.orb, F32)]
-    outs += [shape(SLOTS, sz.orb, BF16)] * sz.links
+    outs += [shape(sz.fall if sz.pair else SLOTS, sz.orb, BF16)] * sz.links
     for s in range(1, sz.shifts + 1):
         outs.append(shape(SLOTS + (sz.zface if s in link_shifts(sz) else 0), sz.orb, HALO))
 
@@ -451,7 +477,7 @@
     y, own, *rest = kernel_call(
         body,
         outs,
-        [r, *fields, *halos, q, *qfaces, maps],
+        [r, *fields, *halos, q, *mapping],
         flops=4 * 10**8,
         limit=(32 << 20) if sz.shifts < 8 else (56 << 20),
     )
@@ -466,32 +492,40 @@
 
 def couple_body(sz, own, *refs):
     beside = refs[: sz.links]
-    back, c_hi, c_lo, coupled = refs[sz.links :]
+    *rows, back, c_hi, c_lo, coupled = refs[sz.links :]
     totals = own[...]
     for j, part in enumerate(beside):
-        totals = totals + dot(back[:, j * SLOTS : (j + 1) * SLOTS], part[...])
+        value = part[...]
+        if sz.pair:
+            value = dot(rows[0][...], value).astype(BF16)
+        totals = totals + dot(back[:, j * SLOTS : (j + 1) * SLOTS], value)
     coupled[...] = couple(c_hi, c_lo, totals)
 
 
-def couple_own(sz, own, back, c_hi, c_lo):
+def couple_own(sz, own, qfaces, back, c_hi, c_lo):
     outs = [shape(SLOTS, sz.orb, F32)]
     body = functools.partial(couple_body, sz)
-    return kernel_call(body, outs, [*own, back, c_hi, c_lo], flops=2 * 10**8)[0]
+    arrays = [*own, *(qfaces if sz.pair else []), back, c_hi, c_lo]
+    return kernel_call(body, outs, arrays, flops=2 * 10**8)[0]
 
 
 def apply_body(sz, scale, refs):
     take = iter(refs)
     yin, own = next(take), next(take)
     messages = [next(take) for _ in range(sz.shifts)]
-    c_hi, c_lo, qt, kin, pot = [next(take) for _ in range(5)]
+    factors = [next(take) for _ in range(3 if sz.pair else 2)]
+    qt, kin, pot = [next(take) for _ in range(3)]
     r, y = next(take), next(take)
     faces = [next(take) for _ in range(4)]
-    if len(messages) == 1:
-        high = messages[0][0:SLOTS, :].astype(BF16)
-        coef = own[...] + (dot(c_hi[...], high) + dot(c_lo[...], high))
+    if sz.pair:
+        m_hi, m_lo, c_rows = factors
+        sums, message = messages[0][0:SLOTS, :].astype(BF16), messages[0]
+        face = message[SLOTS : SLOTS + sz.zface, :].astype(F32)
+        coef = dot(m_hi[...], sums) + dot(m_lo[...], sums)
+        coef = own[...] + (coef + dot(c_rows[...], message_cells(sz, face)))
     else:
         totals = sum(message[0:SLOTS, :].astype(F32) for message in messages)
-        coef = own[...] + couple(c_hi, c_lo, totals)
+        coef = own[...] + couple(*factors, totals)
     coef = coef.astype(BF16)
     y[...] = yin[...]
     for j, shift in enumerate(link_shifts(sz)):
@@ -515,9 +549,9 @@
     write_faces(sz, r, *faces)
 
 
-def apply(sz, y, own, messages, c_hi, c_lo, qt, kin, pot, scale):
+def apply(sz, y, own, messages, factors, qt, kin, pot, scale):
     outs = [shape(sz.rows_all, sz.orb, F32)] * 2 + face_outs(sz)
-    arrays = [y, own, *messages, c_hi, c_lo, qt, kin, pot]
+    arrays = [y, own, *messages, *factors, qt, kin, pot]
 
     def body(*refs):
         apply_body(sz, scale, refs)
@@ -641,22 +675,25 @@
         back = [(target, source) for source, target in ring[shift]]
         qfaces.append(lax.ppermute(face_rows[j], "gz", back))
     pot = jnp.transpose(cell_potential, (1, 2, 3, 0)).reshape(len(sz.cells), nodes)
-    q, kin, pot, maps, back, c_hi, c_lo = turn_matrices(
+    q, kin, pot, back, c_hi, c_lo, *others = turn_matrices(
         sz,
         qt,
         cell_matrix,
         pot,
         slot_atom.reshape(devices, POS),
         jnp.transpose(coupling, (1, 2, 0)),
+        face_rows,
     )
+    factors = others if sz.pair else [c_hi, c_lo]
+    mapping = [] if sz.pair else [*qfaces, *others]
 
     fields, scale = [], 1.0 / half_width
     weight = 0.0
     for step in range(STEPS):
-        y, own, messages = project(sz, r, weight, fields, halos, q, qfaces, maps)
+        y, own, messages = project(sz, r, weight, fields, halos, q, mapping)
         received = [lax.ppermute(m, "gz", ring[s + 1]) for s, m in enumerate(messages)]
-        own = couple_own(sz, own, back, c_hi, c_lo)
-        r, y, faces = apply(sz, y, own, received, c_hi, c_lo, qt, kin, pot, scale)
+        own = couple_own(sz, own, qfaces, back, c_hi, c_lo)
+        r, y, faces = apply(sz, y, own, received, factors, qt, kin, pot, scale)
         fields, weight = [y] + fields[:1], -center_value * scale
         scale = 2.0 / half_width
         halos = exchange_xy(*faces)

time: 63.7 us -> 62.3 us (0.978)
  starting transfers between devices: 22.2 us -> 17.3 us
  waiting for transfers between devices: 26.5 us -> 29.9 us
    ppermute x3, waiting for transfers between devices: 9.34 us -> 13 us  [local(): lax.ppermute(m, 'gz', ring[s + 1])]
    ppermute x3, starting transfers between devices: 4.75 us -> 1.72 us  [local(): lax.ppermute(m, 'gz', ring[s + 1])]
    ppermute x1, waiting for transfers between devices: 1.26 us -> 0.01 us  [local(): qfaces.append(lax.ppermute(face_rows[j], 'gz', back))]
    ppermute x1, starting transfers between devices: 1.59 us -> 0.57 us  [local(): zr = [lax.ppermute(f, 'gz', ring[s]) for f, s in zip(sent, link_shifts(sz))]]
    ppermute x1, waiting for transfers between devices: 2.43 us -> 3.44 us  [local(): zr = [lax.ppermute(f, 'gz', ring[s]) for f, s in zip(sent, link_shifts(sz))]]
    ppermute x16, starting transfers between devices: 14.2 us -> 13.4 us  [swap_faces(): out.append(lax.ppermute(face, axes, pairs))]
  transfers between devices with their start and end apart: 21 -> 21, of which waited for: 12 -> 10; matrix products, arithmetic and copies ran while one was open for 0% -> 0% of each run, Pallas kernels for 10% -> 13%
where the time goes in v11:
time: 62.3 us; the launch traced here: 62.2 us
  waiting for transfers between devices  29.9 us (48%)
  starting transfers between devices  17.3 us (28%)
  Pallas kernels  13.3 us (21%)
  local copies, waits for them, and re-layouts  1.5 us (2%)
    ppermute x16, waiting for transfers between devices, swap_faces(): out.append(lax.ppermute(face, axes, pairs))  13.5 us
    ppermute x16, starting transfers between devices, swap_faces(): out.append(lax.ppermute(face, axes, pairs))  13.4 us
    pallas_call x19, Pallas kernels, kernel_call(): pl.pallas_call(with_waits, out_shape=outs, in_specs=[VMEM] * used + [pl.B...  13.3 us
    ppermute x3, waiting for transfers between devices, local(): lax.ppermute(m, 'gz', ring[s + 1])  13 us
    ppermute x1, waiting for transfers between devices, local(): zr = [lax.ppermute(f, 'gz', ring[s]) for f, s in zip(sent, link_shifts(sz))]  3.44 us
    ppermute x3, starting transfers between devices, local(): lax.ppermute(m, 'gz', ring[s + 1])  1.72 us
    ppermute x1, starting transfers between devices, local(): qfaces.append(lax.ppermute(face_rows[j], 'gz', back))  1.58 us
    pad x1, local copies, waits for them, and re-layouts, local(): proj = jnp.pad(proj, ((0, up(nodes, 16) - nodes), (0, 0)))  1.37 us
  transfers between devices with their start and end apart: 21, of which 10 were waited for; matrix products, arithmetic and copies ran while one was open for 0% of the time, Pallas kernels for 13%

profile of v11, /device:TPU:0, one launch (start us, length us, event | category | flops | bytes accessed | tf_op | source)
XLA Modules:
  0.0 62.2 jit_solution(17490196150229346299)
XLA Ops:
  0.0 0.0 copy-start
  0.0 1.4 %pad.4.refs_2_.refs_0_ = bf16[352,1536]{1,0:T(8,128)(2,1)S(1)} pad(bf16[343,1536]{1,0:T(8,128)(2,1)} %bitcast.11, bf16[]{:T(256)} %constant.2.clone.1), padding=0_9x0_0 | pad | bytes 2135042 | tf_op jit(solution)/shard_map/jit(_pad)/pad | solution.py:661
  1.4 0.0 copy-done.2
  1.4 0.1 copy-done.1
  1.5 0.1 shard_map.73
  1.6 2.4 %collective-permute-start = (bf16[112,128]{1,0:T(8,128)(2,1)S(1)}, bf16[112,128]{1,0:T(8,128)(2,1)S(1)}, u32[]{:S(2)}, u32[]{:S(2)}) collective-permute-start(bf16[112,128]{1,0:T(8,128)(2,1)S(1)} %get-tuple-element.63), channel_id=1, source_target_pairs={{0,24},{2,26},{4,28},{6,30},{8,16},{10,18},{12,20},{14,22},{16,8},... | collective-permute-start | bytes 86024 | tf_op jit(solution)/shard_map/ppermute | solution.py:649
  4.0 0.7 %collective-permute-start.1 = (bf16[112,128]{1,0:T(8,128)(2,1)S(1)}, bf16[112,128]{1,0:T(8,128)(2,1)S(1)}, u32[]{:S(2)}, u32[]{:S(2)}) collective-permute-start(bf16[112,128]{1,0:T(8,128)(2,1)S(1)} %get-tuple-element.64), channel_id=1, source_target_pairs={{0,8},{2,10},{4,12},{6,14},{8,0},{10,2},{12,4},{14,6},{16,24},{18,... | collective-permute-start | bytes 86024 | tf_op jit(solution)/shard_map/ppermute | solution.py:649
  4.7 2.3 %shard_map.75 = (bf16[1664,384]{1,0:T(8,128)(2,1)S(1)}, bf16[384,256]{1,0:T(8,128)(2,1)S(1)}) custom-call(bf16[352,1536]{1,0:T(8,128)(2,1)S(1)} %pad.4.refs_2_.refs_0_, f32[4,32]{1,0:T(4,128)S(1)} %get-tuple-element.69.refs_1_), custom_call_target="tpu_custom_call" | custom-call | flops 3000000000 | bytes 2556416 | tf_op jit(solution)/shard_map/pallas_call | solution.py:63
  7.0 1.6 %collective-permute-start.4 = (bf16[384,256]{1,0:T(8,128)(2,1)S(1)}, bf16[384,256]{1,0:T(8,128)(2,1)S(1)}, u32[]{:S(2)}, u32[]{:S(2)}) collective-permute-start(bf16[384,256]{1,0:T(8,128)(2,1)S(1)} %get-tuple-element.71.refs_5_), channel_id=1, source_target_pairs={{1,0},{0,1},{3,2},{2,3},{5,4},{4,5},{7,6},{6,7},{9,8},{8,9},{11,10... | collective-permute-start | bytes 589832 | tf_op jit(solution)/shard_map/ppermute | solution.py:676
  8.6 0.0 copy-done
  8.7 0.0 collective-permute-done.refs_0_.refs_1_
  8.7 0.0 collective-permute-done.1.refs_1_.refs_2_
  8.7 1.6 %collective-permute-start.2 = (bf16[112,128]{1,0:T(8,128)(2,1)S(1)}, bf16[112,128]{1,0:T(8,128)(2,1)S(1)}, u32[]{:S(2)}, u32[]{:S(2)}) collective-permute-start(bf16[112,128]{1,0:T(8,128)(2,1)S(1)} %get-tuple-element.67), channel_id=1, source_target_pairs={{0,2},{2,0},{4,6},{6,4},{8,10},{10,8},{12,14},{14,12},{16,18},{18,... | collective-permute-start | bytes 86024 | tf_op jit(solution)/shard_map/ppermute | solution.py:649
  10.4 0.0 collective-permute-start.3
  10.4 0.0 copy-done.3
  10.4 0.0 copy-done.4
  10.4 2.5 %shard_map.76 = (bf16[384,1664]{1,0:T(8,128)(2,1)S(1)}, bf16[400,400]{1,0:T(8,128)(2,1)S(1)}, f32[1600,128]{1,0:T(8,128)S(1)}, bf16[384,384]{1,0:T(8,128)(2,1)S(...) custom-call(bf16[1664,384]{1,0:T(8,128)(2,1)S(1)} %get-tuple-element, ...), custom_call_target="tpu_custom_call" | custom-call | flops 1000000000 | bytes 5840786 | tf_op jit(solution)/shard_map/pallas_call | solution.py:63
  12.9 0.0 collective-permute-done.2.refs_3_
  12.9 0.0 collective-permute-done.3.refs_4_
  12.9 0.6 shard_map.77
  13.5 0.6 collective-permute-start.5
  14.0 0.0 collective-permute-done.4.refs_2_
  14.0 0.8 %shard_map.78.refs_1_ = f32[384,128]{1,0:T(8,128)S(1)} custom-call(f32[384,128]{1,0:T(8,128)S(1)} %get-tuple-element.74.refs_0_, bf16[256,128]{1,0:T(8,128)(2,1)S(1)} %get-tuple-element.75.refs_1_, bf16[384,256]{1,0:T(8,128)(2,1)S(1)} %collective-permute-done.4.refs_2_, bf16[384,384]{1,0:T(8,128)(2,1)S(1)} %get-tuple-element.76.refs_3_, ...), custom_call_target="tpu_custom_call" | custom-call | flops 200000000 | bytes 1540096 | tf_op jit(solution)/shard_map/pallas_call | solution.py:63
  14.8 5.0 %collective-permute-done.5.refs_2_ = bf16[592,128]{1,0:T(8,128)(2,1)S(1)} collective-permute-done((bf16[592,128]{1,0:T(8,128)(2,1)S(1)}, bf16[592,128]{1,0:T(8,128)(2,1)S(1)}, u32[]{:S(2)}, u32[]{:S(2)}) %collective-permute-start.5) | collective-permute-done | bytes 151584 | tf_op jit(solution)/shard_map/ppermute | solution.py:694
  19.9 1.0 %shard_map.79 = (f32[1384,128]{1,0:T(8,128)S(1)}, f32[1384,128]{1,0:T(8,128)S(1)}, bf16[112,128]{1,0:T(8,128)(2,1)S(1)}, bf16[112,128]{1,0:T(8,128)(2,1)S(1)}, f...) custom-call(f32[1384,128]{1,0:T(8,128)S(1)} %get-tuple-element.73.refs_0_, f32[384,128]{1,0:T(8,128)S(1)} %shard_map.78.refs_1_, ...), custom_call_target="tpu_custom_call" | custom-call | flops 600000000 | bytes 5849600 | tf_op jit(solution)/shard_map/pallas_call | solution.py:63
  20.8 0.1 collective-permute-start.6
  20.9 0.6 %collective-permute-start.7 = (bf16[112,128]{1,0:T(8,128)(2,1)S(1)}, bf16[112,128]{1,0:T(8,128)(2,1)S(1)}, u32[]{:S(2)}, u32[]{:S(2)}) collective-permute-start(bf16[112,128]{1,0:T(8,128)(2,1)S(1)} %get-tuple-element.88), channel_id=1, source_target_pairs={{0,8},{2,10},{4,12},{6,14},{8,0},{10,2},{12,4},{14,6},{16,24},{18,... | collective-permute-start | bytes 86024 | tf_op jit(solution)/shard_map/ppermute | solution.py:649
  21.6 2.8 %collective-permute-done.6.refs_0_.refs_2_ = bf16[112,128]{1,0:T(8,128)(2,1)S(1)} collective-permute-done((bf16[112,128]{1,0:T(8,128)(2,1)S(1)}, bf16[112,128]{1,0:T(8,128)(2,1)S(1)}, u32[]{:S(2)}, u32[]{:S(2)}) %collective-permute-start.6) | collective-permute-done | bytes 28704 | tf_op jit(solution)/shard_map/ppermute | solution.py:649
  24.4 0.0 collective-permute-done.7.refs_1_.refs_3_
  24.4 1.9 %collective-permute-start.8 = (bf16[112,128]{1,0:T(8,128)(2,1)S(1)}, bf16[112,128]{1,0:T(8,128)(2,1)S(1)}, u32[]{:S(2)}, u32[]{:S(2)}) collective-permute-start(bf16[112,128]{1,0:T(8,128)(2,1)S(1)} %get-tuple-element.91), channel_id=1, source_target_pairs={{0,2},{2,0},{4,6},{6,4},{8,10},{10,8},{12,14},{14,12},{16,18},{18,... | collective-permute-start | bytes 86024 | tf_op jit(solution)/shard_map/ppermute | solution.py:649
  26.3 0.0 collective-permute-start.9
  26.3 2.1 %collective-permute-done.8.refs_4_ = bf16[112,128]{1,0:T(8,128)(2,1)S(1)} collective-permute-done((bf16[112,128]{1,0:T(8,128)(2,1)S(1)}, bf16[112,128]{1,0:T(8,128)(2,1)S(1)}, u32[]{:S(2)}, u32[]{:S(2)}) %collective-permute-start.8) | collective-permute-done | bytes 28704 | tf_op jit(solution)/shard_map/ppermute | solution.py:649
  28.4 0.0 collective-permute-done.9.refs_5_
  28.4 0.6 shard_map.81
  29.0 0.6 collective-permute-start.10
  29.6 0.8 %shard_map.82.refs_1_ = f32[384,128]{1,0:T(8,128)S(1)} custom-call(f32[384,128]{1,0:T(8,128)S(1)} %get-tuple-element.94.refs_0_, bf16[256,128]{1,0:T(8,128)(2,1)S(1)} %get-tuple-element.95.refs_1_, bf16[384,256]{1,0:T(8,128)(2,1)S(1)} %collective-permute-done.4.refs_2_, bf16[384,384]{1,0:T(8,128)(2,1)S(1)} %get-tuple-element.76.refs_3_, ...), custom_call_target="tpu_custom_call" | custom-call | flops 200000000 | bytes 1540096 | tf_op jit(solution)/shard_map/pallas_call | solution.py:63
  30.3 3.9 %collective-permute-done.10.refs_2_ = bf16[592,128]{1,0:T(8,128)(2,1)S(1)} collective-permute-done((bf16[592,128]{1,0:T(8,128)(2,1)S(1)}, bf16[592,128]{1,0:T(8,128)(2,1)S(1)}, u32[]{:S(2)}, u32[]{:S(2)}) %collective-permute-start.10) | collective-permute-done | bytes 151584 | tf_op jit(solution)/shard_map/ppermute | solution.py:694
  34.2 1.0 %shard_map.83 = (f32[1384,128]{1,0:T(8,128)S(1)}, f32[1384,128]{1,0:T(8,128)S(1)}, bf16[112,128]{1,0:T(8,128)(2,1)S(1)}, bf16[112,128]{1,0:T(8,128)(2,1)S(1)}, f...) custom-call(f32[1384,128]{1,0:T(8,128)S(1)} %get-tuple-element.93.refs_0_, f32[384,128]{1,0:T(8,128)S(1)} %shard_map.82.refs_1_, ...), custom_call_target="tpu_custom_call" | custom-call | flops 600000000 | bytes 5849600 | tf_op jit(solution)/shard_map/pallas_call | solution.py:63
  35.2 0.1 collective-permute-start.11
  35.3 0.8 %collective-permute-start.12 = (bf16[112,128]{1,0:T(8,128)(2,1)S(1)}, bf16[112,128]{1,0:T(8,128)(2,1)S(1)}, u32[]{:S(2)}, u32[]{:S(2)}) collective-permute-start(bf16[112,128]{1,0:T(8,128)(2,1)S(1)} %get-tuple-element.100), channel_id=1, source_target_pairs={{0,8},{2,10},{4,12},{6,14},{8,0},{10,2},{12,4},{14,6},{16,24},{18,... | collective-permute-start | bytes 86024 | tf_op jit(solution)/shard_map/ppermute | solution.py:649
  36.2 2.4 %collective-permute-done.11.refs_0_.refs_3_ = bf16[112,128]{1,0:T(8,128)(2,1)S(1)} collective-permute-done((bf16[112,128]{1,0:T(8,128)(2,1)S(1)}, bf16[112,128]{1,0:T(8,128)(2,1)S(1)}, u32[]{:S(2)}, u32[]{:S(2)}) %collective-permute-start.11) | collective-permute-done | bytes 28704 | tf_op jit(solution)/shard_map/ppermute | solution.py:649
  38.6 0.0 collective-permute-done.12.refs_1_.refs_4_
  38.6 2.1 %collective-permute-start.13 = (bf16[112,128]{1,0:T(8,128)(2,1)S(1)}, bf16[112,128]{1,0:T(8,128)(2,1)S(1)}, u32[]{:S(2)}, u32[]{:S(2)}) collective-permute-start(bf16[112,128]{1,0:T(8,128)(2,1)S(1)} %get-tuple-element.103), channel_id=1, source_target_pairs={{0,2},{2,0},{4,6},{6,4},{8,10},{10,8},{12,14},{14,12},{16,18},{18,... | collective-permute-start | bytes 86024 | tf_op jit(solution)/shard_map/ppermute | solution.py:649
  40.7 0.0 collective-permute-start.14
  40.7 1.8 %collective-permute-done.13.refs_5_ = bf16[112,128]{1,0:T(8,128)(2,1)S(1)} collective-permute-done((bf16[112,128]{1,0:T(8,128)(2,1)S(1)}, bf16[112,128]{1,0:T(8,128)(2,1)S(1)}, u32[]{:S(2)}, u32[]{:S(2)}) %collective-permute-start.13) | collective-permute-done | bytes 28704 | tf_op jit(solution)/shard_map/ppermute | solution.py:649
  42.6 0.0 collective-permute-done.14.refs_6_
  42.6 0.6 %shard_map.85 = (f32[1384,128]{1,0:T(8,128)S(1)}, f32[384,128]{1,0:T(8,128)S(1)}, bf16[256,128]{1,0:T(8,128)(2,1)S(1)}, bf16[592,128]{1,0:T(8,128)(2,1)S(1)}) custom-call(f32[1384,128]{1,0:T(8,128)S(1)} %get-tuple-element.97.refs_0_, f32[1384,128]{1,0:T(8,128)S(1)} %get-tuple-element.98.refs_1_.refs_2_, f32[1384,128]{1,0:T(8,128)S(1)} %get-tuple-element.86.refs_1_.refs_2_, ...), custom_call_target="tpu_custom_call" | custom-call | flops 400000000 | bytes 4640768 | tf_op jit(solution)/shard_map/pallas_call | solution.py:63
  43.2 0.6 collective-permute-start.15
  43.8 0.8 %shard_map.86.refs_1_ = f32[384,128]{1,0:T(8,128)S(1)} custom-call(f32[384,128]{1,0:T(8,128)S(1)} %get-tuple-element.106.refs_0_, bf16[256,128]{1,0:T(8,128)(2,1)S(1)} %get-tuple-element.107.refs_1_, bf16[384,256]{1,0:T(8,128)(2,1)S(1)} %collective-permute-done.4.refs_2_, bf16[384,384]{1,0:T(8,128)(2,1)S(1)} %get-tuple-element.76.refs_3_, ...), custom_call_target="tpu_custom_call" | custom-call | flops 200000000 | bytes 1540096 | tf_op jit(solution)/shard_map/pallas_call | solution.py:63
  44.6 4.1 %collective-permute-done.15.refs_2_ = bf16[592,128]{1,0:T(8,128)(2,1)S(1)} collective-permute-done((bf16[592,128]{1,0:T(8,128)(2,1)S(1)}, bf16[592,128]{1,0:T(8,128)(2,1)S(1)}, u32[]{:S(2)}, u32[]{:S(2)}) %collective-permute-start.15) | collective-permute-done | bytes 151584 | tf_op jit(solution)/shard_map/ppermute | solution.py:694
  48.6 1.0 %shard_map.87 = (f32[1384,128]{1,0:T(8,128)S(1)}, f32[1384,128]{1,0:T(8,128)S(1)}, bf16[112,128]{1,0:T(8,128)(2,1)S(1)}, bf16[112,128]{1,0:T(8,128)(2,1)S(1)}, f...) custom-call(f32[1384,128]{1,0:T(8,128)S(1)} %get-tuple-element.105.refs_0_, f32[384,128]{1,0:T(8,128)S(1)} %shard_map.86.refs_1_, ...), custom_call_target="tpu_custom_call" | custom-call | flops 600000000 | bytes 5849600 | tf_op jit(solution)/shard_map/pallas_call | solution.py:63
  49.6 0.1 collective-permute-start.16
  49.7 1.0 %collective-permute-start.17 = (bf16[112,128]{1,0:T(8,128)(2,1)S(1)}, bf16[112,128]{1,0:T(8,128)(2,1)S(1)}, u32[]{:S(2)}, u32[]{:S(2)}) collective-permute-start(bf16[112,128]{1,0:T(8,128)(2,1)S(1)} %get-tuple-element.111), channel_id=1, source_target_pairs={{0,8},{2,10},{4,12},{6,14},{8,0},{10,2},{12,4},{14,6},{16,24},{18,... | collective-permute-start | bytes 86024 | tf_op jit(solution)/shard_map/ppermute | solution.py:649
  50.7 2.3 %collective-permute-done.16.refs_0_.refs_1_ = bf16[112,128]{1,0:T(8,128)(2,1)S(1)} collective-permute-done((bf16[112,128]{1,0:T(8,128)(2,1)S(1)}, bf16[112,128]{1,0:T(8,128)(2,1)S(1)}, u32[]{:S(2)}, u32[]{:S(2)}) %collective-permute-start.16) | collective-permute-done | bytes 28704 | tf_op jit(solution)/shard_map/ppermute | solution.py:649
  53.0 0.0 collective-permute-done.17.refs_1_.refs_2_
  53.0 2.0 %collective-permute-start.18 = (bf16[112,128]{1,0:T(8,128)(2,1)S(1)}, bf16[112,128]{1,0:T(8,128)(2,1)S(1)}, u32[]{:S(2)}, u32[]{:S(2)}) collective-permute-start(bf16[112,128]{1,0:T(8,128)(2,1)S(1)} %get-tuple-element.114), channel_id=1, source_target_pairs={{0,2},{2,0},{4,6},{6,4},{8,10},{10,8},{12,14},{14,12},{16,18},{18,... | collective-permute-start | bytes 86024 | tf_op jit(solution)/shard_map/ppermute | solution.py:649
  55.0 0.0 collective-permute-start.19
  55.0 1.9 %collective-permute-done.18.refs_3_ = bf16[112,128]{1,0:T(8,128)(2,1)S(1)} collective-permute-done((bf16[112,128]{1,0:T(8,128)(2,1)S(1)}, bf16[112,128]{1,0:T(8,128)(2,1)S(1)}, u32[]{:S(2)}, u32[]{:S(2)}) %collective-permute-start.18) | collective-permute-done | bytes 28704 | tf_op jit(solution)/shard_map/ppermute | solution.py:649
  57.0 0.0 collective-permute-done.19.refs_4_
  57.0 0.1 shard_map.89
  57.1 0.6 collective-permute-start.20
  57.6 0.2 shard_map.90.refs_0_
  57.8 3.4 %collective-permute-done.20.refs_1_ = bf16[208,128]{1,0:T(8,128)(2,1)S(1)} collective-permute-done((bf16[208,128]{1,0:T(8,128)(2,1)S(1)}, bf16[208,128]{1,0:T(8,128)(2,1)S(1)}, u32[]{:S(2)}, u32[]{:S(2)}) %collective-permute-start.20) | collective-permute-done | bytes 53280 | tf_op jit(solution)/shard_map/ppermute | solution.py:701
  61.3 0.9 %shard_map.91 = f32[13,13,7,128]{3,2,1,0:T(8,128)} custom-call(f32[1384,128]{1,0:T(8,128)S(1)} %shard_map.90.refs_0_, bf16[208,128]{1,0:T(8,128)(2,1)S(1)} %collective-permute-done.20.refs_1_), custom_call_target="tpu_custom_call" | custom-call | bytes 1367552 | tf_op jit(solution)/shard_map/pallas_call | solution.py:63
  (12 shorter events, 0.2 us)
Async XLA Ops:
  0.0 8.6 %copy-start = (f32[343,2,2,1]{0,3,2,1:T(1,128)S(1)}, f32[343,2,2,1]{0,3,2,1:T(1,128)}, u32[]{:S(2)}) copy-start(f32[343,2,2,1]{0,3,2,1:T(1,128)} %param.9) | copy-start | bytes 16468
  0.0 1.4 %copy-start.2 = (s32[1,1,1,32,4]{3,4,2,1,0:T(4,128)S(1)}, s32[1,1,1,32,4]{3,4,2,1,0:T(4,128)}, u32[]{:S(2)}) copy-start(s32[1,1,1,32,4]{3,4,2,1,0:T(4,128)} %param.12) | copy-start | bytes 1540
  0.0 1.4 %copy-start.1 = (f32[13,13,7,128]{3,2,1,0:T(8,128)S(1)}, f32[13,13,7,128]{3,2,1,0:T(8,128)}, u32[]{:S(2)}) copy-start(f32[13,13,7,128]{3,2,1,0:T(8,128)} %refs_0_.1) | copy-start | bytes 1817092
  1.6 7.1 %collective-permute-start = (bf16[112,128]{1,0:T(8,128)(2,1)S(1)}, bf16[112,128]{1,0:T(8,128)(2,1)S(1)}, u32[]{:S(2)}, u32[]{:S(2)}) collective-permute-start(bf16[112,128]{1,0:T(8,128)(2,1)S(1)} %get-tuple-element.63), channel_id=1, source_target_pairs={{0,24},{2,26},{4,28},{6,30},{8,16},{10,18},{12,20},{14,22},{16,8},... | collective-permute-start | bytes 86024 | tf_op jit(solution)/shard_map/ppermute | solution.py:649
  4.0 4.6 %collective-permute-start.1 = (bf16[112,128]{1,0:T(8,128)(2,1)S(1)}, bf16[112,128]{1,0:T(8,128)(2,1)S(1)}, u32[]{:S(2)}, u32[]{:S(2)}) collective-permute-start(bf16[112,128]{1,0:T(8,128)(2,1)S(1)} %get-tuple-element.64), channel_id=1, source_target_pairs={{0,8},{2,10},{4,12},{6,14},{8,0},{10,2},{12,4},{14,6},{16,24},{18,... | collective-permute-start | bytes 86024 | tf_op jit(solution)/shard_map/ppermute | solution.py:649
  4.7 5.7 %copy-start.3 = (bf16[343,343]{1,0:T(8,128)(2,1)S(1)}, bf16[343,343]{1,0:T(8,128)(2,1)}, u32[]{:S(2)}) copy-start(bf16[343,343]{1,0:T(8,128)(2,1)} %refs_1_.1) | copy-start | bytes 705898
  4.7 5.7 %copy-start.4 = (f32[64,12,12]{0,2,1:T(8,128)S(1)}, f32[64,12,12]{0,2,1:T(8,128)}, u32[]{:S(2)}) copy-start(f32[64,12,12]{0,2,1:T(8,128)} %param.13) | copy-start | bytes 110596
  4.7 5.7 %copy-start.5 = (s32[1,1,2,32]{3,2,1,0:T(2,128)S(1)}, s32[1,1,2,32]{3,2,1,0:T(2,128)}, u32[]{:S(2)}) copy-start(s32[1,1,2,32]{3,2,1,0:T(2,128)} %param.11) | copy-start | bytes 772
  7.0 7.0 %collective-permute-start.4 = (bf16[384,256]{1,0:T(8,128)(2,1)S(1)}, bf16[384,256]{1,0:T(8,128)(2,1)S(1)}, u32[]{:S(2)}, u32[]{:S(2)}) collective-permute-start(bf16[384,256]{1,0:T(8,128)(2,1)S(1)} %get-tuple-element.71.refs_5_), channel_id=1, source_target_pairs={{1,0},{0,1},{3,2},{2,3},{5,4},{4,5},{7,6},{6,7},{9,8},{8,9},{11,10... | collective-permute-start | bytes 589832 | tf_op jit(solution)/shard_map/ppermute | solution.py:676
  8.7 4.2 %collective-permute-start.2 = (bf16[112,128]{1,0:T(8,128)(2,1)S(1)}, bf16[112,128]{1,0:T(8,128)(2,1)S(1)}, u32[]{:S(2)}, u32[]{:S(2)}) collective-permute-start(bf16[112,128]{1,0:T(8,128)(2,1)S(1)} %get-tuple-element.67), channel_id=1, source_target_pairs={{0,2},{2,0},{4,6},{6,4},{8,10},{10,8},{12,14},{14,12},{16,18},{18,... | collective-permute-start | bytes 86024 | tf_op jit(solution)/shard_map/ppermute | solution.py:649
  10.4 2.5 %collective-permute-start.3 = (bf16[112,128]{1,0:T(8,128)(2,1)S(1)}, bf16[112,128]{1,0:T(8,128)(2,1)S(1)}, u32[]{:S(2)}, u32[]{:S(2)}) collective-permute-start(bf16[112,128]{1,0:T(8,128)(2,1)S(1)} %get-tuple-element.68), channel_id=1, source_target_pairs={{0,8},{2,4},{4,2},{6,14},{8,0},{10,12},{12,10},{14,6},{16,24},{18,... | collective-permute-start | bytes 86024 | tf_op jit(solution)/shard_map/ppermute | solution.py:649
  13.5 6.4 %collective-permute-start.5 = (bf16[592,128]{1,0:T(8,128)(2,1)S(1)}, bf16[592,128]{1,0:T(8,128)(2,1)S(1)}, u32[]{:S(2)}, u32[]{:S(2)}) collective-permute-start(bf16[592,128]{1,0:T(8,128)(2,1)S(1)} %get-tuple-element.79), channel_id=1, source_target_pairs={{0,1},{1,0},{2,3},{3,2},{4,5},{5,4},{6,7},{7,6},{8,9},{9,8},{10,11... | collective-permute-start | bytes 454664 | tf_op jit(solution)/shard_map/ppermute | solution.py:694
  20.8 3.6 %collective-permute-start.6 = (bf16[112,128]{1,0:T(8,128)(2,1)S(1)}, bf16[112,128]{1,0:T(8,128)(2,1)S(1)}, u32[]{:S(2)}, u32[]{:S(2)}) collective-permute-start(bf16[112,128]{1,0:T(8,128)(2,1)S(1)} %get-tuple-element.87), channel_id=1, source_target_pairs={{0,24},{2,26},{4,28},{6,30},{8,16},{10,18},{12,20},{14,22},{16,8},... | collective-permute-start | bytes 86024 | tf_op jit(solution)/shard_map/ppermute | solution.py:649
  20.9 3.5 %collective-permute-start.7 = (bf16[112,128]{1,0:T(8,128)(2,1)S(1)}, bf16[112,128]{1,0:T(8,128)(2,1)S(1)}, u32[]{:S(2)}, u32[]{:S(2)}) collective-permute-start(bf16[112,128]{1,0:T(8,128)(2,1)S(1)} %get-tuple-element.88), channel_id=1, source_target_pairs={{0,8},{2,10},{4,12},{6,14},{8,0},{10,2},{12,4},{14,6},{16,24},{18,... | collective-permute-start | bytes 86024 | tf_op jit(solution)/shard_map/ppermute | solution.py:649
  24.4 3.9 %collective-permute-start.8 = (bf16[112,128]{1,0:T(8,128)(2,1)S(1)}, bf16[112,128]{1,0:T(8,128)(2,1)S(1)}, u32[]{:S(2)}, u32[]{:S(2)}) collective-permute-start(bf16[112,128]{1,0:T(8,128)(2,1)S(1)} %get-tuple-element.91), channel_id=1, source_target_pairs={{0,2},{2,0},{4,6},{6,4},{8,10},{10,8},{12,14},{14,12},{16,18},{18,... | collective-permute-start | bytes 86024 | tf_op jit(solution)/shard_map/ppermute | solution.py:649
  26.3 2.1 %collective-permute-start.9 = (bf16[112,128]{1,0:T(8,128)(2,1)S(1)}, bf16[112,128]{1,0:T(8,128)(2,1)S(1)}, u32[]{:S(2)}, u32[]{:S(2)}) collective-permute-start(bf16[112,128]{1,0:T(8,128)(2,1)S(1)} %get-tuple-element.92), channel_id=1, source_target_pairs={{0,8},{2,4},{4,2},{6,14},{8,0},{10,12},{12,10},{14,6},{16,24},{18,... | collective-permute-start | bytes 86024 | tf_op jit(solution)/shard_map/ppermute | solution.py:649
  29.0 5.3 %collective-permute-start.10 = (bf16[592,128]{1,0:T(8,128)(2,1)S(1)}, bf16[592,128]{1,0:T(8,128)(2,1)S(1)}, u32[]{:S(2)}, u32[]{:S(2)}) collective-permute-start(bf16[592,128]{1,0:T(8,128)(2,1)S(1)} %get-tuple-element.96), channel_id=1, source_target_pairs={{0,1},{1,0},{2,3},{3,2},{4,5},{5,4},{6,7},{7,6},{8,9},{9,8},{10,11... | collective-permute-start | bytes 454664 | tf_op jit(solution)/shard_map/ppermute | solution.py:694
  35.2 3.4 %collective-permute-start.11 = (bf16[112,128]{1,0:T(8,128)(2,1)S(1)}, bf16[112,128]{1,0:T(8,128)(2,1)S(1)}, u32[]{:S(2)}, u32[]{:S(2)}) collective-permute-start(bf16[112,128]{1,0:T(8,128)(2,1)S(1)} %get-tuple-element.99), channel_id=1, source_target_pairs={{0,24},{2,26},{4,28},{6,30},{8,16},{10,18},{12,20},{14,22},{16,8},... | collective-permute-start | bytes 86024 | tf_op jit(solution)/shard_map/ppermute | solution.py:649
  35.3 3.3 %collective-permute-start.12 = (bf16[112,128]{1,0:T(8,128)(2,1)S(1)}, bf16[112,128]{1,0:T(8,128)(2,1)S(1)}, u32[]{:S(2)}, u32[]{:S(2)}) collective-permute-start(bf16[112,128]{1,0:T(8,128)(2,1)S(1)} %get-tuple-element.100), channel_id=1, source_target_pairs={{0,8},{2,10},{4,12},{6,14},{8,0},{10,2},{12,4},{14,6},{16,24},{18,... | collective-permute-start | bytes 86024 | tf_op jit(solution)/shard_map/ppermute | solution.py:649
  38.6 3.9 %collective-permute-start.13 = (bf16[112,128]{1,0:T(8,128)(2,1)S(1)}, bf16[112,128]{1,0:T(8,128)(2,1)S(1)}, u32[]{:S(2)}, u32[]{:S(2)}) collective-permute-start(bf16[112,128]{1,0:T(8,128)(2,1)S(1)} %get-tuple-element.103), channel_id=1, source_target_pairs={{0,2},{2,0},{4,6},{6,4},{8,10},{10,8},{12,14},{14,12},{16,18},{18,... | collective-permute-start | bytes 86024 | tf_op jit(solution)/shard_map/ppermute | solution.py:649
  40.7 1.9 %collective-permute-start.14 = (bf16[112,128]{1,0:T(8,128)(2,1)S(1)}, bf16[112,128]{1,0:T(8,128)(2,1)S(1)}, u32[]{:S(2)}, u32[]{:S(2)}) collective-permute-start(bf16[112,128]{1,0:T(8,128)(2,1)S(1)} %get-tuple-element.104), channel_id=1, source_target_pairs={{0,8},{2,4},{4,2},{6,14},{8,0},{10,12},{12,10},{14,6},{16,24},{18,... | collective-permute-start | bytes 86024 | tf_op jit(solution)/shard_map/ppermute | solution.py:649
  43.2 5.4 %collective-permute-start.15 = (bf16[592,128]{1,0:T(8,128)(2,1)S(1)}, bf16[592,128]{1,0:T(8,128)(2,1)S(1)}, u32[]{:S(2)}, u32[]{:S(2)}) collective-permute-start(bf16[592,128]{1,0:T(8,128)(2,1)S(1)} %get-tuple-element.108), channel_id=1, source_target_pairs={{0,1},{1,0},{2,3},{3,2},{4,5},{5,4},{6,7},{7,6},{8,9},{9,8},{10,11... | collective-permute-start | bytes 454664 | tf_op jit(solution)/shard_map/ppermute | solution.py:694
  49.6 3.4 %collective-permute-start.16 = (bf16[112,128]{1,0:T(8,128)(2,1)S(1)}, bf16[112,128]{1,0:T(8,128)(2,1)S(1)}, u32[]{:S(2)}, u32[]{:S(2)}) collective-permute-start(bf16[112,128]{1,0:T(8,128)(2,1)S(1)} %get-tuple-element.110), channel_id=1, source_target_pairs={{0,24},{2,26},{4,28},{6,30},{8,16},{10,18},{12,20},{14,22},{16,8},... | collective-permute-start | bytes 86024 | tf_op jit(solution)/shard_map/ppermute | solution.py:649
  49.7 3.3 %collective-permute-start.17 = (bf16[112,128]{1,0:T(8,128)(2,1)S(1)}, bf16[112,128]{1,0:T(8,128)(2,1)S(1)}, u32[]{:S(2)}, u32[]{:S(2)}) collective-permute-start(bf16[112,128]{1,0:T(8,128)(2,1)S(1)} %get-tuple-element.111), channel_id=1, source_target_pairs={{0,8},{2,10},{4,12},{6,14},{8,0},{10,2},{12,4},{14,6},{16,24},{18,... | collective-permute-start | bytes 86024 | tf_op jit(solution)/shard_map/ppermute | solution.py:649
  53.0 3.9 %collective-permute-start.18 = (bf16[112,128]{1,0:T(8,128)(2,1)S(1)}, bf16[112,128]{1,0:T(8,128)(2,1)S(1)}, u32[]{:S(2)}, u32[]{:S(2)}) collective-permute-start(bf16[112,128]{1,0:T(8,128)(2,1)S(1)} %get-tuple-element.114), channel_id=1, source_target_pairs={{0,2},{2,0},{4,6},{6,4},{8,10},{10,8},{12,14},{14,12},{16,18},{18,... | collective-permute-start | bytes 86024 | tf_op jit(solution)/shard_map/ppermute | solution.py:649
  55.0 1.9 %collective-permute-start.19 = (bf16[112,128]{1,0:T(8,128)(2,1)S(1)}, bf16[112,128]{1,0:T(8,128)(2,1)S(1)}, u32[]{:S(2)}, u32[]{:S(2)}) collective-permute-start(bf16[112,128]{1,0:T(8,128)(2,1)S(1)} %get-tuple-element.115), channel_id=1, source_target_pairs={{0,8},{2,4},{4,2},{6,14},{8,0},{10,12},{12,10},{14,6},{16,24},{18,... | collective-permute-start | bytes 86024 | tf_op jit(solution)/shard_map/ppermute | solution.py:649
  57.1 4.2 %collective-permute-start.20 = (bf16[208,128]{1,0:T(8,128)(2,1)S(1)}, bf16[208,128]{1,0:T(8,128)(2,1)S(1)}, u32[]{:S(2)}, u32[]{:S(2)}) collective-permute-start(bf16[208,128]{1,0:T(8,128)(2,1)S(1)} %get-tuple-element.118), channel_id=1, source_target_pairs={{0,1},{1,0},{2,3},{3,2},{4,5},{5,4},{6,7},{7,6},{8,9},{9,8},{10,11... | collective-permute-start | bytes 159752 | tf_op jit(solution)/shard_map/ppermute | solution.py:701

commit v12 on v11

--- a/solution.py
+++ b/solution.py
@@ -202,11 +202,24 @@
     return keys
 
 
-def turn_body(sz, qt, kin, pot, atoms, coupling, *refs):
+def flip_body(sz, qt, *refs):
+    rows, q, leaving = refs[: sz.links], refs[sz.links], refs[sz.links + 1 :]
+    q[...] = qt[...].T
+    for source, out in zip(rows, leaving):
+        out[...] = source[...]
+
+
+def flip_matrix(sz, qt, face_rows, after):
+    outs = [shape(SLOTS, sz.all_pad, BF16)] + [shape(*f.shape, BF16) for f in face_rows]
+    body = functools.partial(flip_body, sz)
+    q, *leaving = kernel_call(body, outs, [qt, *face_rows], flops=10**8, after=after)
+    return q, leaving
+
+
+def turn_body(sz, kin, pot, atoms, coupling, *refs):
     own_rows, refs = (refs[0], refs[1:]) if sz.pair else (None, refs)
-    q, kout, vout, back, c_hi, c_lo = refs[:6]
-    *others, wide = refs[6:]
-    q[...] = qt[...].T
+    kout, vout, back, c_hi, c_lo = refs[:5]
+    *others, wide = refs[5:]
     nodes = kin.shape[0]
     expand = (node_key(iota(sz.cell_pad, nodes, 0)) == iota(sz.cell_pad, nodes, 1)).astype(BF16)
     gather = (node_key(iota(nodes, sz.cell_pad, 1)) == iota(nodes, sz.cell_pad, 0)).astype(BF16)
@@ -258,10 +271,9 @@
         c_rows[...] = (dot(c_hi[...], own_rows[...]) + dot(c_lo[...], own_rows[...])).astype(BF16)
 
 
-def turn_matrices(sz, qt, kin, pot, atoms, coupling, face_rows):
+def turn_matrices(sz, kin, pot, atoms, coupling, face_rows, after):
     known = (1 + sz.links) * SLOTS
     outs = [
-        shape(SLOTS, sz.all_pad, BF16),
         shape(sz.cell_pad, sz.cell_pad, BF16),
         shape(len(sz.cells) * sz.cell_pad, sz.orb, F32),
         shape(SLOTS, sz.links * SLOTS, BF16),
@@ -276,10 +288,11 @@
     return kernel_call(
         functools.partial(turn_body, sz),
         outs,
-        [qt, kin, pot, atoms, coupling] + (face_rows if sz.pair else []),
+        [kin, pot, atoms, coupling] + (face_rows if sz.pair else []),
         scratch=[pltpu.VMEM((coupling.shape[0], 16, coupling.shape[2]), F32)],
         flops=10**9,
         limit=limit,
+        after=after,
     )
 
 
@@ -355,9 +368,9 @@
     write_pair("gy", *faces, sy_one, sy_two)
 
 
-def cross_faces(sz, *faces):
+def cross_faces(sz, *faces, after=()):
     outs = [shape(sz.yface, sz.orb, HALO)] * 2
-    return kernel_call(functools.partial(cross_body, sz), outs, list(faces))
+    return kernel_call(functools.partial(cross_body, sz), outs, list(faces), after=after)
 
 
 def add_xy(sz, ra, xr_one, xr_two, yr_one, yr_two):
@@ -662,41 +675,48 @@
     cells = jnp.transpose(slot_cells.reshape(POS, BLK))
     r, cells, faces = start_faces(sz, parts, cells, [proj])
 
-    def exchange_xy(sx_one, sx_two, sy_lo, sy_hi):
+    def exchange_xy(sx_one, sx_two, sy_lo, sy_hi, after=()):
         xr = swap_faces("gx", sx_one, sx_two)
-        cross = cross_faces(sz, *xr, sy_lo, sy_hi)
+        cross = cross_faces(sz, *xr, sy_lo, sy_hi, after=after)
         yr = swap_faces("gy", *cross)
-        return (*xr, *yr)
-
-    halos = exchange_xy(*faces)
+        return [*xr, *yr], cross
+
     qt, *face_rows = sum_matrices(sz, proj, cells)
+    halos, cross = exchange_xy(*faces, after=[qt])
+    q, leaving = flip_matrix(sz, qt, face_rows, [cross[0]])
     qfaces = []
     for j, shift in enumerate(link_shifts(sz)):
-        back = [(target, source) for source, target in ring[shift]]
-        qfaces.append(lax.ppermute(face_rows[j], "gz", back))
-    pot = jnp.transpose(cell_potential, (1, 2, 3, 0)).reshape(len(sz.cells), nodes)
-    q, kin, pot, back, c_hi, c_lo, *others = turn_matrices(
-        sz,
-        qt,
-        cell_matrix,
-        pot,
-        slot_atom.reshape(devices, POS),
-        jnp.transpose(coupling, (1, 2, 0)),
-        face_rows,
-    )
-    factors = others if sz.pair else [c_hi, c_lo]
-    mapping = [] if sz.pair else [*qfaces, *others]
+        home = [(target, source) for source, target in ring[shift]]
+        qfaces.append(lax.ppermute(leaving[j], "gz", home))
+
+    def make_matrices(after):
+        return turn_matrices(
+            sz,
+            cell_matrix,
+            jnp.transpose(cell_potential, (1, 2, 3, 0)).reshape(len(sz.cells), nodes),
+            slot_atom.reshape(devices, POS),
+            jnp.transpose(coupling, (1, 2, 0)),
+            face_rows,
+            after,
+        )
+
+    mapping = []
+    if not sz.pair:
+        kin, pot, back, c_hi, c_lo, *others = make_matrices([])
+        factors, mapping = [c_hi, c_lo], [*qfaces, *others]
 
     fields, scale = [], 1.0 / half_width
     weight = 0.0
     for step in range(STEPS):
         y, own, messages = project(sz, r, weight, fields, halos, q, mapping)
         received = [lax.ppermute(m, "gz", ring[s + 1]) for s, m in enumerate(messages)]
+        if sz.pair and step == 0:
+            kin, pot, back, c_hi, c_lo, *factors = make_matrices([own[0]])
         own = couple_own(sz, own, qfaces, back, c_hi, c_lo)
         r, y, faces = apply(sz, y, own, received, factors, qt, kin, pot, scale)
         fields, weight = [y] + fields[:1], -center_value * scale
         scale = 2.0 / half_width
-        halos = exchange_xy(*faces)
+        halos, _ = exchange_xy(*faces)
     r, sent = last_faces(sz, r, halos)
     zr = [lax.ppermute(f, "gz", ring[s]) for f, s in zip(sent, link_shifts(sz))]
     return finish(sz, add_local(sz, r, weight, fields), zr, nz)

time: 62.3 us -> 66 us (1.059)
  waiting for transfers between devices: 29.9 us -> 21.5 us
  starting transfers between devices: 17.3 us -> 22.2 us
  local copies, waits for them, and re-layouts: 1.5 us -> 5.86 us
  Pallas kernels: 13.3 us -> 15.9 us
    ppermute x3, waiting for transfers between devices: 13 us -> 6.8 us  [local(): lax.ppermute(m, 'gz', ring[s + 1])]
    unnamed x12 -> x20, local copies, waits for them, and re-layouts: 0.08 us -> 4.44 us
    ppermute x16, starting transfers between devices: 13.4 us -> 16.3 us  [swap_faces(): out.append(lax.ppermute(face, axes, pairs))]
    pallas_call x19 -> x20, Pallas kernels: 13.3 us -> 15.9 us  [kernel_call(): pl.pallas_call(with_waits, out_shape=outs, in_specs=[VMEM] * used + [pl.B...]
    ppermute x16, waiting for transfers between devices: 13.5 us -> 11.9 us  [swap_faces(): out.append(lax.ppermute(face, axes, pairs))]
    ppermute x3, starting transfers between devices: 1.72 us -> 3.2 us  [local(): lax.ppermute(m, 'gz', ring[s + 1])]
  transfers between devices with their start and end apart: 21 -> 21, of which waited for: 10 -> 9; matrix products, arithmetic and copies ran while one was open for 0% -> 0% of each run, Pallas kernels for 13% -> 14%
where the time goes in v12:
time: 66 us; the launch traced here: 65.8 us
  starting transfers between devices  22.2 us (34%)
  waiting for transfers between devices  21.5 us (33%)
  Pallas kernels  15.9 us (24%)
  local copies, waits for them, and re-layouts  5.86 us (9%)
    ppermute x16, starting transfers between devices, swap_faces(): out.append(lax.ppermute(face, axes, pairs))  16.3 us
    pallas_call x20, Pallas kernels, kernel_call(): pl.pallas_call(with_waits, out_shape=outs, in_specs=[VMEM] * used + [pl.B...  15.9 us
    ppermute x16, waiting for transfers between devices, swap_faces(): out.append(lax.ppermute(face, axes, pairs))  11.9 us
    ppermute x3, waiting for transfers between devices, local(): lax.ppermute(m, 'gz', ring[s + 1])  6.8 us
    unnamed x20, local copies, waits for them, and re-layouts  4.44 us
    ppermute x3, starting transfers between devices, local(): lax.ppermute(m, 'gz', ring[s + 1])  3.2 us
    ppermute x1, waiting for transfers between devices, local(): zr = [lax.ppermute(f, 'gz', ring[s]) for f, s in zip(sent, link_shifts(sz))]  2.82 us
    ppermute x1, starting transfers between devices, local(): qfaces.append(lax.ppermute(leaving[j], 'gz', home))  1.52 us
  transfers between devices with their start and end apart: 21, of which 9 were waited for; matrix products, arithmetic and copies ran while one was open for 0% of the time, Pallas kernels for 14%

profile of v12, /device:TPU:0, one launch (start us, length us, event | category | flops | bytes accessed | tf_op | source)
XLA Modules:
  0.0 65.8 jit_solution(3215152750561424994)
XLA Ops:
  0.0 1.4 %pad.4.refs_2_.refs_0_ = bf16[352,1536]{1,0:T(8,128)(2,1)S(1)} pad(bf16[343,1536]{1,0:T(8,128)(2,1)} %bitcast.11, bf16[]{:T(256)} %constant.2.clone.1), padding=0_9x0_0 | pad | bytes 2135042 | tf_op jit(solution)/shard_map/jit(_pad)/pad | solution.py:674
  1.4 0.1 copy-done.1
  1.5 0.1 shard_map.73
  1.6 2.4 %collective-permute-start = (bf16[112,128]{1,0:T(8,128)(2,1)S(1)}, bf16[112,128]{1,0:T(8,128)(2,1)S(1)}, u32[]{:S(2)}, u32[]{:S(2)}) collective-permute-start(bf16[112,128]{1,0:T(8,128)(2,1)S(1)} %get-tuple-element.64), channel_id=1, source_target_pairs={{0,24},{2,26},{4,28},{6,30},{8,16},{10,18},{12,20},{14,22},{16,8},... | collective-permute-start | bytes 86024 | tf_op jit(solution)/shard_map/ppermute | solution.py:662
  4.0 0.7 %collective-permute-start.1 = (bf16[112,128]{1,0:T(8,128)(2,1)S(1)}, bf16[112,128]{1,0:T(8,128)(2,1)S(1)}, u32[]{:S(2)}, u32[]{:S(2)}) collective-permute-start(bf16[112,128]{1,0:T(8,128)(2,1)S(1)} %get-tuple-element.65), channel_id=1, source_target_pairs={{0,8},{2,10},{4,12},{6,14},{8,0},{10,2},{12,4},{14,6},{16,24},{18,... | collective-permute-start | bytes 86024 | tf_op jit(solution)/shard_map/ppermute | solution.py:662
  4.7 2.3 %shard_map.74 = (bf16[1664,384]{1,0:T(8,128)(2,1)S(1)}, bf16[384,256]{1,0:T(8,128)(2,1)S(1)}) custom-call(bf16[352,1536]{1,0:T(8,128)(2,1)S(1)} %pad.4.refs_2_.refs_0_, f32[4,32]{1,0:T(4,128)S(1)} %get-tuple-element.68.refs_1_), custom_call_target="tpu_custom_call" | custom-call | flops 3000000000 | bytes 2556416 | tf_op jit(solution)/shard_map/pallas_call | solution.py:63
  7.0 0.0 collective-permute-done.refs_0_.refs_1_
  7.0 0.0 collective-permute-done.1.refs_1_.refs_2_
  7.1 0.1 collective-permute-start.3
  7.2 3.1 %collective-permute-start.2 = (bf16[112,128]{1,0:T(8,128)(2,1)S(1)}, bf16[112,128]{1,0:T(8,128)(2,1)S(1)}, u32[]{:S(2)}, u32[]{:S(2)}) collective-permute-start(bf16[112,128]{1,0:T(8,128)(2,1)S(1)} %get-tuple-element.70.refs_2_), channel_id=1, source_target_pairs={{0,2},{2,0},{4,6},{6,4},{8,10},{10,8},{12,14},{14,12},{16,18},{18,... | collective-permute-start | bytes 86024 | tf_op jit(solution)/shard_map/ppermute | solution.py:662
  10.3 1.0 %shard_map.76 = (bf16[384,1664]{1,0:T(8,128)(2,1)S(1)}, bf16[384,256]{1,0:T(8,128)(2,1)}) custom-call(bf16[1664,384]{1,0:T(8,128)(2,1)S(1)} %get-tuple-element.69.refs_4_.refs_0_.refs_6_, bf16[384,256]{1,0:T(8,128)(2,1)S(1)} %get-tuple-element.72.refs_1_.refs_4_, bf16[112,128]{1,0:T(8,128)(2,1)S(1)} %get-tuple-element.70.refs_2_), custom_call_target="tpu_custom_call" | custom-call | flops 100000000 | bytes 2949120 | tf_op jit(solution)/shard_map/pallas_call | solution.py:63
  11.3 1.5 %collective-permute-start.4 = (bf16[384,256]{1,0:T(8,128)(2,1)}, bf16[384,256]{1,0:T(8,128)(2,1)S(1)}, u32[]{:S(2)}, u32[]{:S(2)}) collective-permute-start(bf16[384,256]{1,0:T(8,128)(2,1)} %get-tuple-element.77), channel_id=1, source_target_pairs={{1,0},{0,1},{3,2},{2,3},{5,4},{4,5},{7,6},{6,7},{9,8},{8,9},{11,10... | collective-permute-start | bytes 589832 | tf_op jit(solution)/shard_map/ppermute | solution.py:690
  12.8 0.0 collective-permute-done.3.refs_4_
  12.8 0.0 collective-permute-done.2.refs_3_
  12.8 1.2 %shard_map.77 = (f32[1384,128]{1,0:T(8,128)S(1)}, f32[384,128]{1,0:T(8,128)S(1)}, bf16[256,128]{1,0:T(8,128)(2,1)S(1)}, bf16[592,128]{1,0:T(8,128)(2,1)}) custom-call(f32[1384,128]{1,0:T(8,128)S(1)} %get-tuple-element.63.refs_0_, bf16[112,128]{1,0:T(8,128)(2,1)S(1)} %collective-permute-done.refs_0_.refs_1_, ...), custom_call_target="tpu_custom_call" | custom-call | flops 400000000 | bytes 3223552 | tf_op jit(solution)/shard_map/pallas_call | solution.py:63
  14.1 0.7 %copy-done.2 = f32[384,128]{1,0:T(8,128)} copy-done((f32[384,128]{1,0:T(8,128)}, f32[384,128]{1,0:T(8,128)S(1)}, u32[]{:S(2)}) %copy-start.2) | copy-done | bytes 196632
  14.7 0.8 %collective-permute-start.5 = (bf16[592,128]{1,0:T(8,128)(2,1)}, bf16[592,128]{1,0:T(8,128)(2,1)}, u32[]{:S(2)}, u32[]{:S(2)}) collective-permute-start(bf16[592,128]{1,0:T(8,128)(2,1)} %get-tuple-element.81), channel_id=1, source_target_pairs={{0,1},{1,0},{2,3},{3,2},{4,5},{5,4},{6,7},{7,6},{8,9},{9,8},{10,11... | collective-permute-start | bytes 454664 | tf_op jit(solution)/shard_map/ppermute | solution.py:712
  15.6 0.9 %copy-done.3 = f32[384,128]{1,0:T(8,128)S(1)} copy-done((f32[384,128]{1,0:T(8,128)S(1)}, f32[384,128]{1,0:T(8,128)}, u32[]{:S(2)}) %copy-start.3) | copy-done | bytes 196632
  16.5 0.9 %copy-done.5 = bf16[384,256]{1,0:T(8,128)(2,1)S(1)} copy-done((bf16[384,256]{1,0:T(8,128)(2,1)S(1)}, bf16[384,256]{1,0:T(8,128)(2,1)}, u32[]{:S(2)}) %copy-start.5) | copy-done | bytes 196632
  17.5 0.9 %copy-done.7 = bf16[343,343]{1,0:T(8,128)(2,1)S(1)} copy-done((bf16[343,343]{1,0:T(8,128)(2,1)S(1)}, bf16[343,343]{1,0:T(8,128)(2,1)}, u32[]{:S(2)}) %copy-start.7) | copy-done | bytes 235322
  18.4 0.9 %copy-done.8 = f32[64,12,12]{0,2,1:T(8,128)S(1)} copy-done((f32[64,12,12]{0,2,1:T(8,128)S(1)}, f32[64,12,12]{0,2,1:T(8,128)}, u32[]{:S(2)}) %copy-start.8) | copy-done | bytes 36888
  19.3 2.5 %shard_map.78 = (bf16[400,400]{1,0:T(8,128)(2,1)S(1)}, f32[1600,128]{1,0:T(8,128)S(1)}, bf16[384,384]{1,0:T(8,128)(2,1)S(1)}, bf16[384,384]{1,0:T(8,128)(2,1)S(1...) custom-call(bf16[343,343]{1,0:T(8,128)(2,1)S(1)} %copy-done.7, ...), custom_call_target="tpu_custom_call" | custom-call | flops 1000000000 | bytes 3284882 | tf_op jit(solution)/shard_map/pallas_call | solution.py:63
  21.8 0.0 collective-permute-done.4.refs_2_
  21.8 0.8 %shard_map.79.refs_1_ = f32[384,128]{1,0:T(8,128)S(1)} custom-call(f32[384,128]{1,0:T(8,128)S(1)} %copy-done.3, bf16[256,128]{1,0:T(8,128)(2,1)S(1)} %get-tuple-element.76.refs_1_, bf16[384,256]{1,0:T(8,128)(2,1)S(1)} %collective-permute-done.4.refs_2_, bf16[384,384]{1,0:T(8,128)(2,1)S(1)} %get-tuple-element.78.refs_3_, ...), custom_call_target="tpu_custom_call" | custom-call | flops 200000000 | bytes 1540096 | tf_op jit(solution)/shard_map/pallas_call | solution.py:63
  22.6 0.0 collective-permute-done.5.refs_2_
  22.6 1.9 %shard_map.80 = (f32[1384,128]{1,0:T(8,128)S(1)}, f32[1384,128]{1,0:T(8,128)S(1)}, bf16[112,128]{1,0:T(8,128)(2,1)S(1)}, bf16[112,128]{1,0:T(8,128)(2,1)S(1)}, f...) custom-call(f32[1384,128]{1,0:T(8,128)S(1)} %get-tuple-element.74.refs_0_, f32[384,128]{1,0:T(8,128)S(1)} %shard_map.79.refs_1_, ...), custom_call_target="tpu_custom_call" | custom-call | flops 600000000 | bytes 5849600 | tf_op jit(solution)/shard_map/pallas_call | solution.py:63
  24.5 0.1 collective-permute-start.6
  24.6 1.2 %collective-permute-start.7 = (bf16[112,128]{1,0:T(8,128)(2,1)S(1)}, bf16[112,128]{1,0:T(8,128)(2,1)S(1)}, u32[]{:S(2)}, u32[]{:S(2)}) collective-permute-start(bf16[112,128]{1,0:T(8,128)(2,1)S(1)} %get-tuple-element.90), channel_id=1, source_target_pairs={{0,8},{2,10},{4,12},{6,14},{8,0},{10,2},{12,4},{14,6},{16,24},{18,... | collective-permute-start | bytes 86024 | tf_op jit(solution)/shard_map/ppermute | solution.py:662
  25.8 2.1 %collective-permute-done.6.refs_0_.refs_2_ = bf16[112,128]{1,0:T(8,128)(2,1)S(1)} collective-permute-done((bf16[112,128]{1,0:T(8,128)(2,1)S(1)}, bf16[112,128]{1,0:T(8,128)(2,1)S(1)}, u32[]{:S(2)}, u32[]{:S(2)}) %collective-permute-start.6) | collective-permute-done | bytes 28704 | tf_op jit(solution)/shard_map/ppermute | solution.py:662
  27.9 0.0 collective-permute-done.7.refs_1_.refs_3_
  27.9 2.1 %collective-permute-start.8 = (bf16[112,128]{1,0:T(8,128)(2,1)S(1)}, bf16[112,128]{1,0:T(8,128)(2,1)S(1)}, u32[]{:S(2)}, u32[]{:S(2)}) collective-permute-start(bf16[112,128]{1,0:T(8,128)(2,1)S(1)} %get-tuple-element.93), channel_id=1, source_target_pairs={{0,2},{2,0},{4,6},{6,4},{8,10},{10,8},{12,14},{14,12},{16,18},{18,... | collective-permute-start | bytes 86024 | tf_op jit(solution)/shard_map/ppermute | solution.py:662
  30.0 0.0 collective-permute-start.9
  30.0 1.8 %collective-permute-done.8.refs_4_ = bf16[112,128]{1,0:T(8,128)(2,1)S(1)} collective-permute-done((bf16[112,128]{1,0:T(8,128)(2,1)S(1)}, bf16[112,128]{1,0:T(8,128)(2,1)S(1)}, u32[]{:S(2)}, u32[]{:S(2)}) %collective-permute-start.8) | collective-permute-done | bytes 28704 | tf_op jit(solution)/shard_map/ppermute | solution.py:662
  31.8 0.0 collective-permute-done.9.refs_5_
  31.8 0.6 shard_map.82
  32.4 1.3 %collective-permute-start.10 = (bf16[592,128]{1,0:T(8,128)(2,1)S(1)}, bf16[592,128]{1,0:T(8,128)(2,1)S(1)}, u32[]{:S(2)}, u32[]{:S(2)}) collective-permute-start(bf16[592,128]{1,0:T(8,128)(2,1)S(1)} %get-tuple-element.98), channel_id=1, source_target_pairs={{0,1},{1,0},{2,3},{3,2},{4,5},{5,4},{6,7},{7,6},{8,9},{9,8},{10,11... | collective-permute-start | bytes 454664 | tf_op jit(solution)/shard_map/ppermute | solution.py:712
  33.7 0.8 %shard_map.83.refs_1_ = f32[384,128]{1,0:T(8,128)S(1)} custom-call(f32[384,128]{1,0:T(8,128)S(1)} %get-tuple-element.96.refs_0_, bf16[256,128]{1,0:T(8,128)(2,1)S(1)} %get-tuple-element.97.refs_1_, bf16[384,256]{1,0:T(8,128)(2,1)S(1)} %collective-permute-done.4.refs_2_, bf16[384,384]{1,0:T(8,128)(2,1)S(1)} %get-tuple-element.78.refs_3_, ...), custom_call_target="tpu_custom_call" | custom-call | flops 200000000 | bytes 1540096 | tf_op jit(solution)/shard_map/pallas_call | solution.py:63
  34.5 3.4 %collective-permute-done.10.refs_2_ = bf16[592,128]{1,0:T(8,128)(2,1)S(1)} collective-permute-done((bf16[592,128]{1,0:T(8,128)(2,1)S(1)}, bf16[592,128]{1,0:T(8,128)(2,1)S(1)}, u32[]{:S(2)}, u32[]{:S(2)}) %collective-permute-start.10) | collective-permute-done | bytes 151584 | tf_op jit(solution)/shard_map/ppermute | solution.py:712
  37.9 1.0 %shard_map.84 = (f32[1384,128]{1,0:T(8,128)S(1)}, f32[1384,128]{1,0:T(8,128)S(1)}, bf16[112,128]{1,0:T(8,128)(2,1)S(1)}, bf16[112,128]{1,0:T(8,128)(2,1)S(1)}, f...) custom-call(f32[1384,128]{1,0:T(8,128)S(1)} %get-tuple-element.95.refs_0_, f32[384,128]{1,0:T(8,128)S(1)} %shard_map.83.refs_1_, ...), custom_call_target="tpu_custom_call" | custom-call | flops 600000000 | bytes 5849600 | tf_op jit(solution)/shard_map/pallas_call | solution.py:63
  38.9 0.1 collective-permute-start.11
  38.9 1.2 %collective-permute-start.12 = (bf16[112,128]{1,0:T(8,128)(2,1)S(1)}, bf16[112,128]{1,0:T(8,128)(2,1)S(1)}, u32[]{:S(2)}, u32[]{:S(2)}) collective-permute-start(bf16[112,128]{1,0:T(8,128)(2,1)S(1)} %get-tuple-element.102), channel_id=1, source_target_pairs={{0,8},{2,10},{4,12},{6,14},{8,0},{10,2},{12,4},{14,6},{16,24},{18,... | collective-permute-start | bytes 86024 | tf_op jit(solution)/shard_map/ppermute | solution.py:662
  40.2 2.1 %collective-permute-done.11.refs_0_.refs_3_ = bf16[112,128]{1,0:T(8,128)(2,1)S(1)} collective-permute-done((bf16[112,128]{1,0:T(8,128)(2,1)S(1)}, bf16[112,128]{1,0:T(8,128)(2,1)S(1)}, u32[]{:S(2)}, u32[]{:S(2)}) %collective-permute-start.11) | collective-permute-done | bytes 28704 | tf_op jit(solution)/shard_map/ppermute | solution.py:662
  42.3 2.0 %collective-permute-start.13 = (bf16[112,128]{1,0:T(8,128)(2,1)S(1)}, bf16[112,128]{1,0:T(8,128)(2,1)S(1)}, u32[]{:S(2)}, u32[]{:S(2)}) collective-permute-start(bf16[112,128]{1,0:T(8,128)(2,1)S(1)} %get-tuple-element.105), channel_id=1, source_target_pairs={{0,2},{2,0},{4,6},{6,4},{8,10},{10,8},{12,14},{14,12},{16,18},{18,... | collective-permute-start | bytes 86024 | tf_op jit(solution)/shard_map/ppermute | solution.py:662
  44.3 0.0 collective-permute-start.14
  44.3 1.9 %collective-permute-done.13.refs_5_ = bf16[112,128]{1,0:T(8,128)(2,1)S(1)} collective-permute-done((bf16[112,128]{1,0:T(8,128)(2,1)S(1)}, bf16[112,128]{1,0:T(8,128)(2,1)S(1)}, u32[]{:S(2)}, u32[]{:S(2)}) %collective-permute-start.13) | collective-permute-done | bytes 28704 | tf_op jit(solution)/shard_map/ppermute | solution.py:662
  46.2 0.0 collective-permute-done.14.refs_6_
  46.2 0.6 shard_map.86
  46.8 1.1 %collective-permute-start.15 = (bf16[592,128]{1,0:T(8,128)(2,1)S(1)}, bf16[592,128]{1,0:T(8,128)(2,1)S(1)}, u32[]{:S(2)}, u32[]{:S(2)}) collective-permute-start(bf16[592,128]{1,0:T(8,128)(2,1)S(1)} %get-tuple-element.110), channel_id=1, source_target_pairs={{0,1},{1,0},{2,3},{3,2},{4,5},{5,4},{6,7},{7,6},{8,9},{9,8},{10,11... | collective-permute-start | bytes 454664 | tf_op jit(solution)/shard_map/ppermute | solution.py:712
  47.9 0.8 %shard_map.87.refs_1_ = f32[384,128]{1,0:T(8,128)S(1)} custom-call(f32[384,128]{1,0:T(8,128)S(1)} %get-tuple-element.108.refs_0_, bf16[256,128]{1,0:T(8,128)(2,1)S(1)} %get-tuple-element.109.refs_1_, bf16[384,256]{1,0:T(8,128)(2,1)S(1)} %collective-permute-done.4.refs_2_, bf16[384,384]{1,0:T(8,128)(2,1)S(1)} %get-tuple-element.78.refs_3_, ...), custom_call_target="tpu_custom_call" | custom-call | flops 200000000 | bytes 1540096 | tf_op jit(solution)/shard_map/pallas_call | solution.py:63
  48.7 3.4 %collective-permute-done.15.refs_2_ = bf16[592,128]{1,0:T(8,128)(2,1)S(1)} collective-permute-done((bf16[592,128]{1,0:T(8,128)(2,1)S(1)}, bf16[592,128]{1,0:T(8,128)(2,1)S(1)}, u32[]{:S(2)}, u32[]{:S(2)}) %collective-permute-start.15) | collective-permute-done | bytes 151584 | tf_op jit(solution)/shard_map/ppermute | solution.py:712
  52.2 1.0 %shard_map.88 = (f32[1384,128]{1,0:T(8,128)S(1)}, f32[1384,128]{1,0:T(8,128)S(1)}, bf16[112,128]{1,0:T(8,128)(2,1)S(1)}, bf16[112,128]{1,0:T(8,128)(2,1)S(1)}, f...) custom-call(f32[1384,128]{1,0:T(8,128)S(1)} %get-tuple-element.107.refs_0_, f32[384,128]{1,0:T(8,128)S(1)} %shard_map.87.refs_1_, ...), custom_call_target="tpu_custom_call" | custom-call | flops 600000000 | bytes 5849600 | tf_op jit(solution)/shard_map/pallas_call | solution.py:63
  53.2 0.1 collective-permute-start.16
  53.3 1.2 %collective-permute-start.17 = (bf16[112,128]{1,0:T(8,128)(2,1)S(1)}, bf16[112,128]{1,0:T(8,128)(2,1)S(1)}, u32[]{:S(2)}, u32[]{:S(2)}) collective-permute-start(bf16[112,128]{1,0:T(8,128)(2,1)S(1)} %get-tuple-element.113), channel_id=1, source_target_pairs={{0,8},{2,10},{4,12},{6,14},{8,0},{10,2},{12,4},{14,6},{16,24},{18,... | collective-permute-start | bytes 86024 | tf_op jit(solution)/shard_map/ppermute | solution.py:662
  54.5 2.1 %collective-permute-done.16.refs_0_.refs_1_ = bf16[112,128]{1,0:T(8,128)(2,1)S(1)} collective-permute-done((bf16[112,128]{1,0:T(8,128)(2,1)S(1)}, bf16[112,128]{1,0:T(8,128)(2,1)S(1)}, u32[]{:S(2)}, u32[]{:S(2)}) %collective-permute-start.16) | collective-permute-done | bytes 28704 | tf_op jit(solution)/shard_map/ppermute | solution.py:662
  56.6 0.0 collective-permute-done.17.refs_1_.refs_2_
  56.6 2.0 %collective-permute-start.18 = (bf16[112,128]{1,0:T(8,128)(2,1)S(1)}, bf16[112,128]{1,0:T(8,128)(2,1)S(1)}, u32[]{:S(2)}, u32[]{:S(2)}) collective-permute-start(bf16[112,128]{1,0:T(8,128)(2,1)S(1)} %get-tuple-element.116), channel_id=1, source_target_pairs={{0,2},{2,0},{4,6},{6,4},{8,10},{10,8},{12,14},{14,12},{16,18},{18,... | collective-permute-start | bytes 86024 | tf_op jit(solution)/shard_map/ppermute | solution.py:662
  58.6 0.0 collective-permute-start.19
  58.6 1.9 %collective-permute-done.18.refs_3_ = bf16[112,128]{1,0:T(8,128)(2,1)S(1)} collective-permute-done((bf16[112,128]{1,0:T(8,128)(2,1)S(1)}, bf16[112,128]{1,0:T(8,128)(2,1)S(1)}, u32[]{:S(2)}, u32[]{:S(2)}) %collective-permute-start.18) | collective-permute-done | bytes 28704 | tf_op jit(solution)/shard_map/ppermute | solution.py:662
  60.5 0.0 collective-permute-done.19.refs_4_
  60.5 0.1 shard_map.90
  60.6 1.2 %collective-permute-start.20 = (bf16[208,128]{1,0:T(8,128)(2,1)S(1)}, bf16[208,128]{1,0:T(8,128)(2,1)S(1)}, u32[]{:S(2)}, u32[]{:S(2)}) collective-permute-start(bf16[208,128]{1,0:T(8,128)(2,1)S(1)} %get-tuple-element.120), channel_id=1, source_target_pairs={{0,1},{1,0},{2,3},{3,2},{4,5},{5,4},{6,7},{7,6},{8,9},{9,8},{10,11... | collective-permute-start | bytes 159752 | tf_op jit(solution)/shard_map/ppermute | solution.py:721
  61.8 0.2 shard_map.91.refs_0_
  62.0 2.8 %collective-permute-done.20.refs_1_ = bf16[208,128]{1,0:T(8,128)(2,1)S(1)} collective-permute-done((bf16[208,128]{1,0:T(8,128)(2,1)S(1)}, bf16[208,128]{1,0:T(8,128)(2,1)S(1)}, u32[]{:S(2)}, u32[]{:S(2)}) %collective-permute-start.20) | collective-permute-done | bytes 53280 | tf_op jit(solution)/shard_map/ppermute | solution.py:721
  64.8 0.9 %shard_map.92 = f32[13,13,7,128]{3,2,1,0:T(8,128)} custom-call(f32[1384,128]{1,0:T(8,128)S(1)} %shard_map.91.refs_0_, bf16[208,128]{1,0:T(8,128)(2,1)S(1)} %collective-permute-done.20.refs_1_), custom_call_target="tpu_custom_call" | custom-call | bytes 1367552 | tf_op jit(solution)/shard_map/pallas_call | solution.py:63
  (21 shorter events, 0.2 us)
Async XLA Ops:
  0.0 15.6 %copy-start = (f32[343,2,2,1]{0,3,2,1:T(1,128)S(1)}, f32[343,2,2,1]{0,3,2,1:T(1,128)}, u32[]{:S(2)}) copy-start(f32[343,2,2,1]{0,3,2,1:T(1,128)} %param.9) | copy-start | bytes 16468
  0.0 1.4 %copy-start.6 = (s32[1,1,1,32,4]{3,4,2,1,0:T(4,128)S(1)}, s32[1,1,1,32,4]{3,4,2,1,0:T(4,128)}, u32[]{:S(2)}) copy-start(s32[1,1,1,32,4]{3,4,2,1,0:T(4,128)} %param.12) | copy-start | bytes 1540
  0.0 1.4 %copy-start.1 = (f32[13,13,7,128]{3,2,1,0:T(8,128)S(1)}, f32[13,13,7,128]{3,2,1,0:T(8,128)}, u32[]{:S(2)}) copy-start(f32[13,13,7,128]{3,2,1,0:T(8,128)} %refs_0_.2) | copy-start | bytes 1817092
  1.6 5.5 %collective-permute-start = (bf16[112,128]{1,0:T(8,128)(2,1)S(1)}, bf16[112,128]{1,0:T(8,128)(2,1)S(1)}, u32[]{:S(2)}, u32[]{:S(2)}) collective-permute-start(bf16[112,128]{1,0:T(8,128)(2,1)S(1)} %get-tuple-element.64), channel_id=1, source_target_pairs={{0,24},{2,26},{4,28},{6,30},{8,16},{10,18},{12,20},{14,22},{16,8},... | collective-permute-start | bytes 86024 | tf_op jit(solution)/shard_map/ppermute | solution.py:662
  4.0 3.0 %collective-permute-start.1 = (bf16[112,128]{1,0:T(8,128)(2,1)S(1)}, bf16[112,128]{1,0:T(8,128)(2,1)S(1)}, u32[]{:S(2)}, u32[]{:S(2)}) collective-permute-start(bf16[112,128]{1,0:T(8,128)(2,1)S(1)} %get-tuple-element.65), channel_id=1, source_target_pairs={{0,8},{2,10},{4,12},{6,14},{8,0},{10,2},{12,4},{14,6},{16,24},{18,... | collective-permute-start | bytes 86024 | tf_op jit(solution)/shard_map/ppermute | solution.py:662
  7.0 4.3 %copy-start.4 = (bf16[384,256]{1,0:T(8,128)(2,1)}, bf16[384,256]{1,0:T(8,128)(2,1)S(1)}, u32[]{:S(2)}) copy-start(bf16[384,256]{1,0:T(8,128)(2,1)S(1)} %get-tuple-element.72.refs_1_.refs_4_) | copy-start | bytes 589828
  7.1 5.7 %collective-permute-start.3 = (bf16[112,128]{1,0:T(8,128)(2,1)S(1)}, bf16[112,128]{1,0:T(8,128)(2,1)S(1)}, u32[]{:S(2)}, u32[]{:S(2)}) collective-permute-start(bf16[112,128]{1,0:T(8,128)(2,1)S(1)} %get-tuple-element.71), channel_id=1, source_target_pairs={{0,8},{2,4},{4,2},{6,14},{8,0},{10,12},{12,10},{14,6},{16,24},{18,... | collective-permute-start | bytes 86024 | tf_op jit(solution)/shard_map/ppermute | solution.py:662
  7.2 5.7 %collective-permute-start.2 = (bf16[112,128]{1,0:T(8,128)(2,1)S(1)}, bf16[112,128]{1,0:T(8,128)(2,1)S(1)}, u32[]{:S(2)}, u32[]{:S(2)}) collective-permute-start(bf16[112,128]{1,0:T(8,128)(2,1)S(1)} %get-tuple-element.70.refs_2_), channel_id=1, source_target_pairs={{0,2},{2,0},{4,6},{6,4},{8,10},{10,8},{12,14},{14,12},{16,18},{18,... | collective-permute-start | bytes 86024 | tf_op jit(solution)/shard_map/ppermute | solution.py:662
  11.3 4.3 %copy-start.9 = (s32[1,1,2,32]{3,2,1,0:T(2,128)S(1)}, s32[1,1,2,32]{3,2,1,0:T(2,128)}, u32[]{:S(2)}) copy-start(s32[1,1,2,32]{3,2,1,0:T(2,128)} %param.11) | copy-start | bytes 772
  11.3 10.5 %collective-permute-start.4 = (bf16[384,256]{1,0:T(8,128)(2,1)}, bf16[384,256]{1,0:T(8,128)(2,1)S(1)}, u32[]{:S(2)}, u32[]{:S(2)}) collective-permute-start(bf16[384,256]{1,0:T(8,128)(2,1)} %get-tuple-element.77), channel_id=1, source_target_pairs={{1,0},{0,1},{3,2},{2,3},{5,4},{4,5},{7,6},{6,7},{9,8},{8,9},{11,10... | collective-permute-start | bytes 589832 | tf_op jit(solution)/shard_map/ppermute | solution.py:690
  14.0 0.7 %copy-start.2 = (f32[384,128]{1,0:T(8,128)}, f32[384,128]{1,0:T(8,128)S(1)}, u32[]{:S(2)}) copy-start(f32[384,128]{1,0:T(8,128)S(1)} %get-tuple-element.75.refs_5_.refs_0_) | copy-start | bytes 589828
  14.7 7.9 %collective-permute-start.5 = (bf16[592,128]{1,0:T(8,128)(2,1)}, bf16[592,128]{1,0:T(8,128)(2,1)}, u32[]{:S(2)}, u32[]{:S(2)}) collective-permute-start(bf16[592,128]{1,0:T(8,128)(2,1)} %get-tuple-element.81), channel_id=1, source_target_pairs={{0,1},{1,0},{2,3},{3,2},{4,5},{5,4},{6,7},{7,6},{8,9},{9,8},{10,11... | collective-permute-start | bytes 454664 | tf_op jit(solution)/shard_map/ppermute | solution.py:712
  15.6 0.9 %copy-start.3 = (f32[384,128]{1,0:T(8,128)S(1)}, f32[384,128]{1,0:T(8,128)}, u32[]{:S(2)}) copy-start(f32[384,128]{1,0:T(8,128)} %copy-done.2) | copy-start | bytes 589828
  16.5 0.9 %copy-start.5 = (bf16[384,256]{1,0:T(8,128)(2,1)S(1)}, bf16[384,256]{1,0:T(8,128)(2,1)}, u32[]{:S(2)}) copy-start(bf16[384,256]{1,0:T(8,128)(2,1)} %copy-done.4) | copy-start | bytes 589828
  17.5 1.0 %copy-start.7 = (bf16[343,343]{1,0:T(8,128)(2,1)S(1)}, bf16[343,343]{1,0:T(8,128)(2,1)}, u32[]{:S(2)}) copy-start(bf16[343,343]{1,0:T(8,128)(2,1)} %refs_0_.3) | copy-start | bytes 705898
  18.4 0.9 %copy-start.8 = (f32[64,12,12]{0,2,1:T(8,128)S(1)}, f32[64,12,12]{0,2,1:T(8,128)}, u32[]{:S(2)}) copy-start(f32[64,12,12]{0,2,1:T(8,128)} %param.13) | copy-start | bytes 110596
  24.5 3.4 %collective-permute-start.6 = (bf16[112,128]{1,0:T(8,128)(2,1)S(1)}, bf16[112,128]{1,0:T(8,128)(2,1)S(1)}, u32[]{:S(2)}, u32[]{:S(2)}) collective-permute-start(bf16[112,128]{1,0:T(8,128)(2,1)S(1)} %get-tuple-element.89), channel_id=1, source_target_pairs={{0,24},{2,26},{4,28},{6,30},{8,16},{10,18},{12,20},{14,22},{16,8},... | collective-permute-start | bytes 86024 | tf_op jit(solution)/shard_map/ppermute | solution.py:662
  24.6 3.3 %collective-permute-start.7 = (bf16[112,128]{1,0:T(8,128)(2,1)S(1)}, bf16[112,128]{1,0:T(8,128)(2,1)S(1)}, u32[]{:S(2)}, u32[]{:S(2)}) collective-permute-start(bf16[112,128]{1,0:T(8,128)(2,1)S(1)} %get-tuple-element.90), channel_id=1, source_target_pairs={{0,8},{2,10},{4,12},{6,14},{8,0},{10,2},{12,4},{14,6},{16,24},{18,... | collective-permute-start | bytes 86024 | tf_op jit(solution)/shard_map/ppermute | solution.py:662
  27.9 3.9 %collective-permute-start.8 = (bf16[112,128]{1,0:T(8,128)(2,1)S(1)}, bf16[112,128]{1,0:T(8,128)(2,1)S(1)}, u32[]{:S(2)}, u32[]{:S(2)}) collective-permute-start(bf16[112,128]{1,0:T(8,128)(2,1)S(1)} %get-tuple-element.93), channel_id=1, source_target_pairs={{0,2},{2,0},{4,6},{6,4},{8,10},{10,8},{12,14},{14,12},{16,18},{18,... | collective-permute-start | bytes 86024 | tf_op jit(solution)/shard_map/ppermute | solution.py:662
  30.0 1.9 %collective-permute-start.9 = (bf16[112,128]{1,0:T(8,128)(2,1)S(1)}, bf16[112,128]{1,0:T(8,128)(2,1)S(1)}, u32[]{:S(2)}, u32[]{:S(2)}) collective-permute-start(bf16[112,128]{1,0:T(8,128)(2,1)S(1)} %get-tuple-element.94), channel_id=1, source_target_pairs={{0,8},{2,4},{4,2},{6,14},{8,0},{10,12},{12,10},{14,6},{16,24},{18,... | collective-permute-start | bytes 86024 | tf_op jit(solution)/shard_map/ppermute | solution.py:662
  32.4 5.4 %collective-permute-start.10 = (bf16[592,128]{1,0:T(8,128)(2,1)S(1)}, bf16[592,128]{1,0:T(8,128)(2,1)S(1)}, u32[]{:S(2)}, u32[]{:S(2)}) collective-permute-start(bf16[592,128]{1,0:T(8,128)(2,1)S(1)} %get-tuple-element.98), channel_id=1, source_target_pairs={{0,1},{1,0},{2,3},{3,2},{4,5},{5,4},{6,7},{7,6},{8,9},{9,8},{10,11... | collective-permute-start | bytes 454664 | tf_op jit(solution)/shard_map/ppermute | solution.py:712
  38.9 3.4 %collective-permute-start.11 = (bf16[112,128]{1,0:T(8,128)(2,1)S(1)}, bf16[112,128]{1,0:T(8,128)(2,1)S(1)}, u32[]{:S(2)}, u32[]{:S(2)}) collective-permute-start(bf16[112,128]{1,0:T(8,128)(2,1)S(1)} %get-tuple-element.101), channel_id=1, source_target_pairs={{0,24},{2,26},{4,28},{6,30},{8,16},{10,18},{12,20},{14,22},{16,8},... | collective-permute-start | bytes 86024 | tf_op jit(solution)/shard_map/ppermute | solution.py:662
  38.9 3.3 %collective-permute-start.12 = (bf16[112,128]{1,0:T(8,128)(2,1)S(1)}, bf16[112,128]{1,0:T(8,128)(2,1)S(1)}, u32[]{:S(2)}, u32[]{:S(2)}) collective-permute-start(bf16[112,128]{1,0:T(8,128)(2,1)S(1)} %get-tuple-element.102), channel_id=1, source_target_pairs={{0,8},{2,10},{4,12},{6,14},{8,0},{10,2},{12,4},{14,6},{16,24},{18,... | collective-permute-start | bytes 86024 | tf_op jit(solution)/shard_map/ppermute | solution.py:662
  42.3 3.9 %collective-permute-start.13 = (bf16[112,128]{1,0:T(8,128)(2,1)S(1)}, bf16[112,128]{1,0:T(8,128)(2,1)S(1)}, u32[]{:S(2)}, u32[]{:S(2)}) collective-permute-start(bf16[112,128]{1,0:T(8,128)(2,1)S(1)} %get-tuple-element.105), channel_id=1, source_target_pairs={{0,2},{2,0},{4,6},{6,4},{8,10},{10,8},{12,14},{14,12},{16,18},{18,... | collective-permute-start | bytes 86024 | tf_op jit(solution)/shard_map/ppermute | solution.py:662
  44.3 1.9 %collective-permute-start.14 = (bf16[112,128]{1,0:T(8,128)(2,1)S(1)}, bf16[112,128]{1,0:T(8,128)(2,1)S(1)}, u32[]{:S(2)}, u32[]{:S(2)}) collective-permute-start(bf16[112,128]{1,0:T(8,128)(2,1)S(1)} %get-tuple-element.106), channel_id=1, source_target_pairs={{0,8},{2,4},{4,2},{6,14},{8,0},{10,12},{12,10},{14,6},{16,24},{18,... | collective-permute-start | bytes 86024 | tf_op jit(solution)/shard_map/ppermute | solution.py:662
  46.8 5.3 %collective-permute-start.15 = (bf16[592,128]{1,0:T(8,128)(2,1)S(1)}, bf16[592,128]{1,0:T(8,128)(2,1)S(1)}, u32[]{:S(2)}, u32[]{:S(2)}) collective-permute-start(bf16[592,128]{1,0:T(8,128)(2,1)S(1)} %get-tuple-element.110), channel_id=1, source_target_pairs={{0,1},{1,0},{2,3},{3,2},{4,5},{5,4},{6,7},{7,6},{8,9},{9,8},{10,11... | collective-permute-start | bytes 454664 | tf_op jit(solution)/shard_map/ppermute | solution.py:712
  53.2 3.4 %collective-permute-start.16 = (bf16[112,128]{1,0:T(8,128)(2,1)S(1)}, bf16[112,128]{1,0:T(8,128)(2,1)S(1)}, u32[]{:S(2)}, u32[]{:S(2)}) collective-permute-start(bf16[112,128]{1,0:T(8,128)(2,1)S(1)} %get-tuple-element.112), channel_id=1, source_target_pairs={{0,24},{2,26},{4,28},{6,30},{8,16},{10,18},{12,20},{14,22},{16,8},... | collective-permute-start | bytes 86024 | tf_op jit(solution)/shard_map/ppermute | solution.py:662
  53.3 3.3 %collective-permute-start.17 = (bf16[112,128]{1,0:T(8,128)(2,1)S(1)}, bf16[112,128]{1,0:T(8,128)(2,1)S(1)}, u32[]{:S(2)}, u32[]{:S(2)}) collective-permute-start(bf16[112,128]{1,0:T(8,128)(2,1)S(1)} %get-tuple-element.113), channel_id=1, source_target_pairs={{0,8},{2,10},{4,12},{6,14},{8,0},{10,2},{12,4},{14,6},{16,24},{18,... | collective-permute-start | bytes 86024 | tf_op jit(solution)/shard_map/ppermute | solution.py:662
  56.6 3.9 %collective-permute-start.18 = (bf16[112,128]{1,0:T(8,128)(2,1)S(1)}, bf16[112,128]{1,0:T(8,128)(2,1)S(1)}, u32[]{:S(2)}, u32[]{:S(2)}) collective-permute-start(bf16[112,128]{1,0:T(8,128)(2,1)S(1)} %get-tuple-element.116), channel_id=1, source_target_pairs={{0,2},{2,0},{4,6},{6,4},{8,10},{10,8},{12,14},{14,12},{16,18},{18,... | collective-permute-start | bytes 86024 | tf_op jit(solution)/shard_map/ppermute | solution.py:662
  58.6 1.9 %collective-permute-start.19 = (bf16[112,128]{1,0:T(8,128)(2,1)S(1)}, bf16[112,128]{1,0:T(8,128)(2,1)S(1)}, u32[]{:S(2)}, u32[]{:S(2)}) collective-permute-start(bf16[112,128]{1,0:T(8,128)(2,1)S(1)} %get-tuple-element.117), channel_id=1, source_target_pairs={{0,8},{2,4},{4,2},{6,14},{8,0},{10,12},{12,10},{14,6},{16,24},{18,... | collective-permute-start | bytes 86024 | tf_op jit(solution)/shard_map/ppermute | solution.py:662
  60.6 4.2 %collective-permute-start.20 = (bf16[208,128]{1,0:T(8,128)(2,1)S(1)}, bf16[208,128]{1,0:T(8,128)(2,1)S(1)}, u32[]{:S(2)}, u32[]{:S(2)}) collective-permute-start(bf16[208,128]{1,0:T(8,128)(2,1)S(1)} %get-tuple-element.120), channel_id=1, source_target_pairs={{0,1},{1,0},{2,3},{3,2},{4,5},{5,4},{6,7},{7,6},{8,9},{9,8},{10,11... | collective-permute-start | bytes 159752 | tf_op jit(solution)/shard_map/ppermute | solution.py:721

commit v13 on v11

--- a/solution.py
+++ b/solution.py
@@ -44,7 +44,7 @@
         self.cell_pad = up(self.cell_rows, 16)
         self.all_pad = up(self.cell_pad * len(self.cells), 128)
         self.fcell = EDGE * PAD
-        self.fall = up(self.fcell * len(self.cells), 256)
+        self.fall = up(self.fcell * len(self.cells), 16)
         self.shifts, self.links = shifts, min(2, shifts)
         self.pair = shifts == 1
         self.rows_all = self.rows + (self.face_b - ny + 1) * PAD
@@ -123,6 +123,11 @@
 def dot_last(a, b, precision=None):
     dims = (((1,), (1,)), ((), ()))
     return lax.dot_general(a, b, dims, precision=precision, preferred_element_type=F32)
+
+
+def dot_first(a, b):
+    dims = (((0,), (0,)), ((), ()))
+    return lax.dot_general(a, b, dims, preferred_element_type=F32)
 
 
 def sum_body(sz, proj, cells, qt, *qt_faces):
@@ -170,13 +175,16 @@
         qt[sz.cell_pad * len(sz.cells) :, :] = jnp.zeros((rest, SLOTS), BF16)
     for j, qf in enumerate(qt_faces):
         at = sz.cell_pad + j * PAD * PAD
-        rows = [full[at : at + PAD * PAD, g * SLOTS : (g + 1) * SLOTS] for g in range(len(sz.cells))]
-        qf[...] = jnp.concatenate(rows, axis=0).T.astype(BF16)
+        rows = [full[at : at + sz.fcell, g * SLOTS : (g + 1) * SLOTS] for g in range(len(sz.cells))]
+        rest = sz.fall - sz.fcell * len(sz.cells)
+        if rest:
+            rows.append(jnp.zeros((rest, SLOTS), F32))
+        qf[...] = jnp.concatenate(rows, axis=0).astype(BF16)
 
 
 def sum_matrices(sz, proj, cells):
     outs = [shape(sz.all_pad, SLOTS, BF16)]
-    outs += [shape(SLOTS, len(sz.cells) * PAD * PAD, BF16)] * sz.links
+    outs += [shape(sz.fall, SLOTS, BF16)] * sz.links
     body = functools.partial(sum_body, sz)
     return kernel_call(body, outs, [proj, cells], flops=3 * 10**9, limit=32 << 20)
 
@@ -255,7 +263,7 @@
         m_hi, m_lo, c_rows = others
         m_hi[...] = dot(c_hi[...], back[...]).astype(BF16)
         m_lo[...] = dot(c_lo[...], back[...]).astype(BF16)
-        c_rows[...] = (dot(c_hi[...], own_rows[...]) + dot(c_lo[...], own_rows[...])).astype(BF16)
+        c_rows[...] = (dot_last(c_hi[...], own_rows[...]) + dot_last(c_lo[...], own_rows[...])).astype(BF16)
 
 
 def turn_matrices(sz, qt, kin, pot, atoms, coupling, face_rows):
@@ -269,7 +277,7 @@
         shape(SLOTS, SLOTS, BF16),
     ]
     if sz.pair:
-        outs += [shape(SLOTS, SLOTS, BF16)] * 2 + [shape(*face_rows[0].shape, BF16)]
+        outs += [shape(SLOTS, SLOTS, BF16)] * 2 + [shape(SLOTS, sz.fall, BF16)]
     else:
         outs += [shape(sz.shifts * SLOTS, known, BF16)]
     limit = (32 << 20) if sz.shifts < 8 else (56 << 20)
@@ -408,7 +416,9 @@
         for a in range(EDGE):
             at = (ORDER * p + a) * sz.line_x + ORDER * q * PAD
             rows.append(layer_rows(y, weight, fields, at + c))
-        rows.append(jnp.zeros((PAD, sz.orb), F32))
+    rest = sz.fall - sz.fcell * len(sz.cells)
+    if rest:
+        rows.append(jnp.zeros((rest, sz.orb), F32))
     return jnp.concatenate(rows, axis=0).astype(BF16)
 
 
@@ -418,7 +428,9 @@
         for a in range(EDGE):
             at = (ORDER * p + a) * sz.face_b + ORDER * q
             rows.append(face[at : at + PAD])
-        rows.append(jnp.zeros((PAD, sz.orb), F32))
+    rest = sz.fall - sz.fcell * len(sz.cells)
+    if rest:
+        rows.append(jnp.zeros((rest, sz.orb), F32))
     return jnp.concatenate(rows, axis=0).astype(BF16)
 
 
@@ -450,7 +462,7 @@
         return
     known = [sums.astype(BF16)]
     for j, matrix in enumerate(qfaces):
-        value, valid = dot(matrix[...], face_cells(sz, y, weight, fields, j)), link_valid(sz, j)
+        value, valid = dot_first(matrix[...], face_cells(sz, y, weight, fields, j)), link_valid(sz, j)
         beside[j][...] = (value if valid is None else value * valid.astype(F32)).astype(BF16)
         known.append(beside[j][...])
     shift_of = link_shifts(sz)
@@ -497,7 +509,7 @@
     for j, part in enumerate(beside):
         value = part[...]
         if sz.pair:
-            value = dot(rows[0][...], value).astype(BF16)
+            value = dot_first(rows[0][...], value).astype(BF16)
         totals = totals + dot(back[:, j * SLOTS : (j + 1) * SLOTS], value)
     coupled[...] = couple(c_hi, c_lo, totals)
 

time: 62.3 us -> 62.4 us (level)
  no operation moved by 1% of the time
where the time goes in v13:
time: 62.4 us; the launch traced here: 62.2 us
  waiting for transfers between devices  29.8 us (48%)
  starting transfers between devices  17.3 us (28%)
  Pallas kernels  13.4 us (21%)
  local copies, waits for them, and re-layouts  1.5 us (2%)
    ppermute x16, waiting for transfers between devices, swap_faces(): out.append(lax.ppermute(face, axes, pairs))  13.5 us
    pallas_call x19, Pallas kernels, kernel_call(): pl.pallas_call(with_waits, out_shape=outs, in_specs=[VMEM] * used + [pl.B...  13.4 us
    ppermute x16, starting transfers between devices, swap_faces(): out.append(lax.ppermute(face, axes, pairs))  13.4 us
    ppermute x3, waiting for transfers between devices, local(): lax.ppermute(m, 'gz', ring[s + 1])  12.9 us
    ppermute x1, waiting for transfers between devices, local(): zr = [lax.ppermute(f, 'gz', ring[s]) for f, s in zip(sent, link_shifts(sz))]  3.45 us
    ppermute x3, starting transfers between devices, local(): lax.ppermute(m, 'gz', ring[s + 1])  1.71 us
    ppermute x1, starting transfers between devices, local(): qfaces.append(lax.ppermute(face_rows[j], 'gz', back))  1.58 us
    pad x1, local copies, waits for them, and re-layouts, local(): proj = jnp.pad(proj, ((0, up(nodes, 16) - nodes), (0, 0)))  1.37 us
  transfers between devices with their start and end apart: 21, of which 10 were waited for; matrix products, arithmetic and copies ran while one was open for 0% of the time, Pallas kernels for 13%

profile of v13, /device:TPU:0, one launch (start us, length us, event | category | flops | bytes accessed | tf_op | source)
XLA Modules:
  0.0 62.2 jit_solution(17956096923646651298)
XLA Ops:
  0.0 0.0 copy-start
  0.0 1.4 %pad.4.refs_2_.refs_0_ = bf16[352,1536]{1,0:T(8,128)(2,1)S(1)} pad(bf16[343,1536]{1,0:T(8,128)(2,1)} %bitcast.11, bf16[]{:T(256)} %constant.2.clone.1), padding=0_9x0_0 | pad | bytes 2135042 | tf_op jit(solution)/shard_map/jit(_pad)/pad | solution.py:673
  1.4 0.0 copy-done.2
  1.4 0.1 copy-done.1
  1.5 0.1 shard_map.73
  1.6 2.4 %collective-permute-start = (bf16[112,128]{1,0:T(8,128)(2,1)S(1)}, bf16[112,128]{1,0:T(8,128)(2,1)S(1)}, u32[]{:S(2)}, u32[]{:S(2)}) collective-permute-start(bf16[112,128]{1,0:T(8,128)(2,1)S(1)} %get-tuple-element.63), channel_id=1, source_target_pairs={{0,24},{2,26},{4,28},{6,30},{8,16},{10,18},{12,20},{14,22},{16,8},... | collective-permute-start | bytes 86024 | tf_op jit(solution)/shard_map/ppermute | solution.py:661
  4.0 0.7 %collective-permute-start.1 = (bf16[112,128]{1,0:T(8,128)(2,1)S(1)}, bf16[112,128]{1,0:T(8,128)(2,1)S(1)}, u32[]{:S(2)}, u32[]{:S(2)}) collective-permute-start(bf16[112,128]{1,0:T(8,128)(2,1)S(1)} %get-tuple-element.64), channel_id=1, source_target_pairs={{0,8},{2,10},{4,12},{6,14},{8,0},{10,2},{12,4},{14,6},{16,24},{18,... | collective-permute-start | bytes 86024 | tf_op jit(solution)/shard_map/ppermute | solution.py:661
  4.7 2.2 %shard_map.75 = (bf16[1664,384]{1,0:T(8,128)(2,1)S(1)}, bf16[224,384]{1,0:T(8,128)(2,1)S(1)}) custom-call(bf16[352,1536]{1,0:T(8,128)(2,1)S(1)} %pad.4.refs_2_.refs_0_, f32[4,32]{1,0:T(4,128)S(1)} %get-tuple-element.69.refs_1_), custom_call_target="tpu_custom_call" | custom-call | flops 3000000000 | bytes 2531840 | tf_op jit(solution)/shard_map/pallas_call | solution.py:63
  6.9 1.6 %collective-permute-start.4 = (bf16[224,384]{1,0:T(8,128)(2,1)S(1)}, bf16[224,384]{1,0:T(8,128)(2,1)S(1)}, u32[]{:S(2)}, u32[]{:S(2)}) collective-permute-start(bf16[224,384]{1,0:T(8,128)(2,1)S(1)} %get-tuple-element.71.refs_5_), channel_id=1, source_target_pairs={{1,0},{0,1},{3,2},{2,3},{5,4},{4,5},{7,6},{6,7},{9,8},{8,9},{11,10... | collective-permute-start | bytes 516104 | tf_op jit(solution)/shard_map/ppermute | solution.py:688
  8.5 0.0 copy-done
  8.6 0.0 collective-permute-done.refs_0_.refs_1_
  8.6 0.0 collective-permute-done.1.refs_1_.refs_2_
  8.6 1.6 %collective-permute-start.2 = (bf16[112,128]{1,0:T(8,128)(2,1)S(1)}, bf16[112,128]{1,0:T(8,128)(2,1)S(1)}, u32[]{:S(2)}, u32[]{:S(2)}) collective-permute-start(bf16[112,128]{1,0:T(8,128)(2,1)S(1)} %get-tuple-element.67), channel_id=1, source_target_pairs={{0,2},{2,0},{4,6},{6,4},{8,10},{10,8},{12,14},{14,12},{16,18},{18,... | collective-permute-start | bytes 86024 | tf_op jit(solution)/shard_map/ppermute | solution.py:661
  10.3 0.0 collective-permute-start.3
  10.3 0.0 copy-done.3
  10.3 0.0 copy-done.4
  10.3 2.5 %shard_map.76 = (bf16[384,1664]{1,0:T(8,128)(2,1)S(1)}, bf16[400,400]{1,0:T(8,128)(2,1)S(1)}, f32[1600,128]{1,0:T(8,128)S(1)}, bf16[384,384]{1,0:T(8,128)(2,1)S(...) custom-call(bf16[1664,384]{1,0:T(8,128)(2,1)S(1)} %get-tuple-element, ...), custom_call_target="tpu_custom_call" | custom-call | flops 1000000000 | bytes 5791634 | tf_op jit(solution)/shard_map/pallas_call | solution.py:63
  12.8 0.0 collective-permute-done.2.refs_3_
  12.9 0.0 collective-permute-done.3.refs_4_
  12.9 0.6 shard_map.77
  13.4 0.6 collective-permute-start.5
  14.0 0.0 collective-permute-done.4.refs_2_
  14.0 0.8 %shard_map.78.refs_1_ = f32[384,128]{1,0:T(8,128)S(1)} custom-call(f32[384,128]{1,0:T(8,128)S(1)} %get-tuple-element.74.refs_0_, bf16[224,128]{1,0:T(8,128)(2,1)S(1)} %get-tuple-element.75.refs_1_, bf16[224,384]{1,0:T(8,128)(2,1)S(1)} %collective-permute-done.4.refs_2_, bf16[384,384]{1,0:T(8,128)(2,1)S(1)} %get-tuple-element.76.refs_3_, ...), custom_call_target="tpu_custom_call" | custom-call | flops 200000000 | bytes 1507328 | tf_op jit(solution)/shard_map/pallas_call | solution.py:63
  14.8 5.0 %collective-permute-done.5.refs_2_ = bf16[592,128]{1,0:T(8,128)(2,1)S(1)} collective-permute-done((bf16[592,128]{1,0:T(8,128)(2,1)S(1)}, bf16[592,128]{1,0:T(8,128)(2,1)S(1)}, u32[]{:S(2)}, u32[]{:S(2)}) %collective-permute-start.5) | collective-permute-done | bytes 151584 | tf_op jit(solution)/shard_map/ppermute | solution.py:706
  19.8 1.0 %shard_map.79 = (f32[1384,128]{1,0:T(8,128)S(1)}, f32[1384,128]{1,0:T(8,128)S(1)}, bf16[112,128]{1,0:T(8,128)(2,1)S(1)}, bf16[112,128]{1,0:T(8,128)(2,1)S(1)}, f...) custom-call(f32[1384,128]{1,0:T(8,128)S(1)} %get-tuple-element.73.refs_0_, f32[384,128]{1,0:T(8,128)S(1)} %shard_map.78.refs_1_, ...), custom_call_target="tpu_custom_call" | custom-call | flops 600000000 | bytes 5825024 | tf_op jit(solution)/shard_map/pallas_call | solution.py:63
  20.8 0.1 collective-permute-start.6
  20.9 0.6 %collective-permute-start.7 = (bf16[112,128]{1,0:T(8,128)(2,1)S(1)}, bf16[112,128]{1,0:T(8,128)(2,1)S(1)}, u32[]{:S(2)}, u32[]{:S(2)}) collective-permute-start(bf16[112,128]{1,0:T(8,128)(2,1)S(1)} %get-tuple-element.88), channel_id=1, source_target_pairs={{0,8},{2,10},{4,12},{6,14},{8,0},{10,2},{12,4},{14,6},{16,24},{18,... | collective-permute-start | bytes 86024 | tf_op jit(solution)/shard_map/ppermute | solution.py:661
  21.6 2.8 %collective-permute-done.6.refs_0_.refs_2_ = bf16[112,128]{1,0:T(8,128)(2,1)S(1)} collective-permute-done((bf16[112,128]{1,0:T(8,128)(2,1)S(1)}, bf16[112,128]{1,0:T(8,128)(2,1)S(1)}, u32[]{:S(2)}, u32[]{:S(2)}) %collective-permute-start.6) | collective-permute-done | bytes 28704 | tf_op jit(solution)/shard_map/ppermute | solution.py:661
  24.4 0.0 collective-permute-done.7.refs_1_.refs_3_
  24.4 1.9 %collective-permute-start.8 = (bf16[112,128]{1,0:T(8,128)(2,1)S(1)}, bf16[112,128]{1,0:T(8,128)(2,1)S(1)}, u32[]{:S(2)}, u32[]{:S(2)}) collective-permute-start(bf16[112,128]{1,0:T(8,128)(2,1)S(1)} %get-tuple-element.91), channel_id=1, source_target_pairs={{0,2},{2,0},{4,6},{6,4},{8,10},{10,8},{12,14},{14,12},{16,18},{18,... | collective-permute-start | bytes 86024 | tf_op jit(solution)/shard_map/ppermute | solution.py:661
  26.3 0.0 collective-permute-start.9
  26.3 2.1 %collective-permute-done.8.refs_4_ = bf16[112,128]{1,0:T(8,128)(2,1)S(1)} collective-permute-done((bf16[112,128]{1,0:T(8,128)(2,1)S(1)}, bf16[112,128]{1,0:T(8,128)(2,1)S(1)}, u32[]{:S(2)}, u32[]{:S(2)}) %collective-permute-start.8) | collective-permute-done | bytes 28704 | tf_op jit(solution)/shard_map/ppermute | solution.py:661
  28.4 0.0 collective-permute-done.9.refs_5_
  28.4 0.6 shard_map.81
  29.0 0.6 collective-permute-start.10
  29.5 0.8 %shard_map.82.refs_1_ = f32[384,128]{1,0:T(8,128)S(1)} custom-call(f32[384,128]{1,0:T(8,128)S(1)} %get-tuple-element.94.refs_0_, bf16[224,128]{1,0:T(8,128)(2,1)S(1)} %get-tuple-element.95.refs_1_, bf16[224,384]{1,0:T(8,128)(2,1)S(1)} %collective-permute-done.4.refs_2_, bf16[384,384]{1,0:T(8,128)(2,1)S(1)} %get-tuple-element.76.refs_3_, ...), custom_call_target="tpu_custom_call" | custom-call | flops 200000000 | bytes 1507328 | tf_op jit(solution)/shard_map/pallas_call | solution.py:63
  30.4 3.9 %collective-permute-done.10.refs_2_ = bf16[592,128]{1,0:T(8,128)(2,1)S(1)} collective-permute-done((bf16[592,128]{1,0:T(8,128)(2,1)S(1)}, bf16[592,128]{1,0:T(8,128)(2,1)S(1)}, u32[]{:S(2)}, u32[]{:S(2)}) %collective-permute-start.10) | collective-permute-done | bytes 151584 | tf_op jit(solution)/shard_map/ppermute | solution.py:706
  34.2 1.0 %shard_map.83 = (f32[1384,128]{1,0:T(8,128)S(1)}, f32[1384,128]{1,0:T(8,128)S(1)}, bf16[112,128]{1,0:T(8,128)(2,1)S(1)}, bf16[112,128]{1,0:T(8,128)(2,1)S(1)}, f...) custom-call(f32[1384,128]{1,0:T(8,128)S(1)} %get-tuple-element.93.refs_0_, f32[384,128]{1,0:T(8,128)S(1)} %shard_map.82.refs_1_, ...), custom_call_target="tpu_custom_call" | custom-call | flops 600000000 | bytes 5825024 | tf_op jit(solution)/shard_map/pallas_call | solution.py:63
  35.3 0.1 collective-permute-start.11
  35.3 0.8 %collective-permute-start.12 = (bf16[112,128]{1,0:T(8,128)(2,1)S(1)}, bf16[112,128]{1,0:T(8,128)(2,1)S(1)}, u32[]{:S(2)}, u32[]{:S(2)}) collective-permute-start(bf16[112,128]{1,0:T(8,128)(2,1)S(1)} %get-tuple-element.100), channel_id=1, source_target_pairs={{0,8},{2,10},{4,12},{6,14},{8,0},{10,2},{12,4},{14,6},{16,24},{18,... | collective-permute-start | bytes 86024 | tf_op jit(solution)/shard_map/ppermute | solution.py:661
  36.2 2.4 %collective-permute-done.11.refs_0_.refs_3_ = bf16[112,128]{1,0:T(8,128)(2,1)S(1)} collective-permute-done((bf16[112,128]{1,0:T(8,128)(2,1)S(1)}, bf16[112,128]{1,0:T(8,128)(2,1)S(1)}, u32[]{:S(2)}, u32[]{:S(2)}) %collective-permute-start.11) | collective-permute-done | bytes 28704 | tf_op jit(solution)/shard_map/ppermute | solution.py:661
  38.6 0.0 collective-permute-done.12.refs_1_.refs_4_
  38.6 2.1 %collective-permute-start.13 = (bf16[112,128]{1,0:T(8,128)(2,1)S(1)}, bf16[112,128]{1,0:T(8,128)(2,1)S(1)}, u32[]{:S(2)}, u32[]{:S(2)}) collective-permute-start(bf16[112,128]{1,0:T(8,128)(2,1)S(1)} %get-tuple-element.103), channel_id=1, source_target_pairs={{0,2},{2,0},{4,6},{6,4},{8,10},{10,8},{12,14},{14,12},{16,18},{18,... | collective-permute-start | bytes 86024 | tf_op jit(solution)/shard_map/ppermute | solution.py:661
  40.7 0.0 collective-permute-start.14
  40.7 1.8 %collective-permute-done.13.refs_5_ = bf16[112,128]{1,0:T(8,128)(2,1)S(1)} collective-permute-done((bf16[112,128]{1,0:T(8,128)(2,1)S(1)}, bf16[112,128]{1,0:T(8,128)(2,1)S(1)}, u32[]{:S(2)}, u32[]{:S(2)}) %collective-permute-start.13) | collective-permute-done | bytes 28704 | tf_op jit(solution)/shard_map/ppermute | solution.py:661
  42.6 0.0 collective-permute-done.14.refs_6_
  42.6 0.6 %shard_map.85 = (f32[1384,128]{1,0:T(8,128)S(1)}, f32[384,128]{1,0:T(8,128)S(1)}, bf16[224,128]{1,0:T(8,128)(2,1)S(1)}, bf16[592,128]{1,0:T(8,128)(2,1)S(1)}) custom-call(f32[1384,128]{1,0:T(8,128)S(1)} %get-tuple-element.97.refs_0_, f32[1384,128]{1,0:T(8,128)S(1)} %get-tuple-element.98.refs_1_.refs_2_, f32[1384,128]{1,0:T(8,128)S(1)} %get-tuple-element.86.refs_1_.refs_2_, ...), custom_call_target="tpu_custom_call" | custom-call | flops 400000000 | bytes 4632576 | tf_op jit(solution)/shard_map/pallas_call | solution.py:63
  43.2 0.6 collective-permute-start.15
  43.8 0.8 %shard_map.86.refs_1_ = f32[384,128]{1,0:T(8,128)S(1)} custom-call(f32[384,128]{1,0:T(8,128)S(1)} %get-tuple-element.106.refs_0_, bf16[224,128]{1,0:T(8,128)(2,1)S(1)} %get-tuple-element.107.refs_1_, bf16[224,384]{1,0:T(8,128)(2,1)S(1)} %collective-permute-done.4.refs_2_, bf16[384,384]{1,0:T(8,128)(2,1)S(1)} %get-tuple-element.76.refs_3_, ...), custom_call_target="tpu_custom_call" | custom-call | flops 200000000 | bytes 1507328 | tf_op jit(solution)/shard_map/pallas_call | solution.py:63
  44.6 4.0 %collective-permute-done.15.refs_2_ = bf16[592,128]{1,0:T(8,128)(2,1)S(1)} collective-permute-done((bf16[592,128]{1,0:T(8,128)(2,1)S(1)}, bf16[592,128]{1,0:T(8,128)(2,1)S(1)}, u32[]{:S(2)}, u32[]{:S(2)}) %collective-permute-start.15) | collective-permute-done | bytes 151584 | tf_op jit(solution)/shard_map/ppermute | solution.py:706
  48.6 1.0 %shard_map.87 = (f32[1384,128]{1,0:T(8,128)S(1)}, f32[1384,128]{1,0:T(8,128)S(1)}, bf16[112,128]{1,0:T(8,128)(2,1)S(1)}, bf16[112,128]{1,0:T(8,128)(2,1)S(1)}, f...) custom-call(f32[1384,128]{1,0:T(8,128)S(1)} %get-tuple-element.105.refs_0_, f32[384,128]{1,0:T(8,128)S(1)} %shard_map.86.refs_1_, ...), custom_call_target="tpu_custom_call" | custom-call | flops 600000000 | bytes 5825024 | tf_op jit(solution)/shard_map/pallas_call | solution.py:63
  49.7 0.1 collective-permute-start.16
  49.7 1.0 %collective-permute-start.17 = (bf16[112,128]{1,0:T(8,128)(2,1)S(1)}, bf16[112,128]{1,0:T(8,128)(2,1)S(1)}, u32[]{:S(2)}, u32[]{:S(2)}) collective-permute-start(bf16[112,128]{1,0:T(8,128)(2,1)S(1)} %get-tuple-element.111), channel_id=1, source_target_pairs={{0,8},{2,10},{4,12},{6,14},{8,0},{10,2},{12,4},{14,6},{16,24},{18,... | collective-permute-start | bytes 86024 | tf_op jit(solution)/shard_map/ppermute | solution.py:661
  50.7 2.3 %collective-permute-done.16.refs_0_.refs_1_ = bf16[112,128]{1,0:T(8,128)(2,1)S(1)} collective-permute-done((bf16[112,128]{1,0:T(8,128)(2,1)S(1)}, bf16[112,128]{1,0:T(8,128)(2,1)S(1)}, u32[]{:S(2)}, u32[]{:S(2)}) %collective-permute-start.16) | collective-permute-done | bytes 28704 | tf_op jit(solution)/shard_map/ppermute | solution.py:661
  53.0 0.0 collective-permute-done.17.refs_1_.refs_2_
  53.1 2.0 %collective-permute-start.18 = (bf16[112,128]{1,0:T(8,128)(2,1)S(1)}, bf16[112,128]{1,0:T(8,128)(2,1)S(1)}, u32[]{:S(2)}, u32[]{:S(2)}) collective-permute-start(bf16[112,128]{1,0:T(8,128)(2,1)S(1)} %get-tuple-element.114), channel_id=1, source_target_pairs={{0,2},{2,0},{4,6},{6,4},{8,10},{10,8},{12,14},{14,12},{16,18},{18,... | collective-permute-start | bytes 86024 | tf_op jit(solution)/shard_map/ppermute | solution.py:661
  55.1 0.0 collective-permute-start.19
  55.1 1.9 %collective-permute-done.18.refs_3_ = bf16[112,128]{1,0:T(8,128)(2,1)S(1)} collective-permute-done((bf16[112,128]{1,0:T(8,128)(2,1)S(1)}, bf16[112,128]{1,0:T(8,128)(2,1)S(1)}, u32[]{:S(2)}, u32[]{:S(2)}) %collective-permute-start.18) | collective-permute-done | bytes 28704 | tf_op jit(solution)/shard_map/ppermute | solution.py:661
  57.0 0.0 collective-permute-done.19.refs_4_
  57.0 0.1 shard_map.89
  57.1 0.6 collective-permute-start.20
  57.7 0.2 shard_map.90.refs_0_
  57.9 3.4 %collective-permute-done.20.refs_1_ = bf16[208,128]{1,0:T(8,128)(2,1)S(1)} collective-permute-done((bf16[208,128]{1,0:T(8,128)(2,1)S(1)}, bf16[208,128]{1,0:T(8,128)(2,1)S(1)}, u32[]{:S(2)}, u32[]{:S(2)}) %collective-permute-start.20) | collective-permute-done | bytes 53280 | tf_op jit(solution)/shard_map/ppermute | solution.py:713
  61.3 0.9 %shard_map.91 = f32[13,13,7,128]{3,2,1,0:T(8,128)} custom-call(f32[1384,128]{1,0:T(8,128)S(1)} %shard_map.90.refs_0_, bf16[208,128]{1,0:T(8,128)(2,1)S(1)} %collective-permute-done.20.refs_1_), custom_call_target="tpu_custom_call" | custom-call | bytes 1367552 | tf_op jit(solution)/shard_map/pallas_call | solution.py:63
  (12 shorter events, 0.2 us)
Async XLA Ops:
  0.0 8.5 %copy-start = (f32[343,2,2,1]{0,3,2,1:T(1,128)S(1)}, f32[343,2,2,1]{0,3,2,1:T(1,128)}, u32[]{:S(2)}) copy-start(f32[343,2,2,1]{0,3,2,1:T(1,128)} %param.9) | copy-start | bytes 16468
  0.0 1.4 %copy-start.2 = (s32[1,1,1,32,4]{3,4,2,1,0:T(4,128)S(1)}, s32[1,1,1,32,4]{3,4,2,1,0:T(4,128)}, u32[]{:S(2)}) copy-start(s32[1,1,1,32,4]{3,4,2,1,0:T(4,128)} %param.12) | copy-start | bytes 1540
  0.0 1.4 %copy-start.1 = (f32[13,13,7,128]{3,2,1,0:T(8,128)S(1)}, f32[13,13,7,128]{3,2,1,0:T(8,128)}, u32[]{:S(2)}) copy-start(f32[13,13,7,128]{3,2,1,0:T(8,128)} %refs_0_.1) | copy-start | bytes 1817092
  1.6 7.0 %collective-permute-start = (bf16[112,128]{1,0:T(8,128)(2,1)S(1)}, bf16[112,128]{1,0:T(8,128)(2,1)S(1)}, u32[]{:S(2)}, u32[]{:S(2)}) collective-permute-start(bf16[112,128]{1,0:T(8,128)(2,1)S(1)} %get-tuple-element.63), channel_id=1, source_target_pairs={{0,24},{2,26},{4,28},{6,30},{8,16},{10,18},{12,20},{14,22},{16,8},... | collective-permute-start | bytes 86024 | tf_op jit(solution)/shard_map/ppermute | solution.py:661
  4.0 4.6 %collective-permute-start.1 = (bf16[112,128]{1,0:T(8,128)(2,1)S(1)}, bf16[112,128]{1,0:T(8,128)(2,1)S(1)}, u32[]{:S(2)}, u32[]{:S(2)}) collective-permute-start(bf16[112,128]{1,0:T(8,128)(2,1)S(1)} %get-tuple-element.64), channel_id=1, source_target_pairs={{0,8},{2,10},{4,12},{6,14},{8,0},{10,2},{12,4},{14,6},{16,24},{18,... | collective-permute-start | bytes 86024 | tf_op jit(solution)/shard_map/ppermute | solution.py:661
  4.7 5.6 %copy-start.3 = (bf16[343,343]{1,0:T(8,128)(2,1)S(1)}, bf16[343,343]{1,0:T(8,128)(2,1)}, u32[]{:S(2)}) copy-start(bf16[343,343]{1,0:T(8,128)(2,1)} %refs_1_.1) | copy-start | bytes 705898
  4.7 5.6 %copy-start.4 = (f32[64,12,12]{0,2,1:T(8,128)S(1)}, f32[64,12,12]{0,2,1:T(8,128)}, u32[]{:S(2)}) copy-start(f32[64,12,12]{0,2,1:T(8,128)} %param.13) | copy-start | bytes 110596
  4.7 5.6 %copy-start.5 = (s32[1,1,2,32]{3,2,1,0:T(2,128)S(1)}, s32[1,1,2,32]{3,2,1,0:T(2,128)}, u32[]{:S(2)}) copy-start(s32[1,1,2,32]{3,2,1,0:T(2,128)} %param.11) | copy-start | bytes 772
  6.9 7.1 %collective-permute-start.4 = (bf16[224,384]{1,0:T(8,128)(2,1)S(1)}, bf16[224,384]{1,0:T(8,128)(2,1)S(1)}, u32[]{:S(2)}, u32[]{:S(2)}) collective-permute-start(bf16[224,384]{1,0:T(8,128)(2,1)S(1)} %get-tuple-element.71.refs_5_), channel_id=1, source_target_pairs={{1,0},{0,1},{3,2},{2,3},{5,4},{4,5},{7,6},{6,7},{9,8},{8,9},{11,10... | collective-permute-start | bytes 516104 | tf_op jit(solution)/shard_map/ppermute | solution.py:688
  8.6 4.2 %collective-permute-start.2 = (bf16[112,128]{1,0:T(8,128)(2,1)S(1)}, bf16[112,128]{1,0:T(8,128)(2,1)S(1)}, u32[]{:S(2)}, u32[]{:S(2)}) collective-permute-start(bf16[112,128]{1,0:T(8,128)(2,1)S(1)} %get-tuple-element.67), channel_id=1, source_target_pairs={{0,2},{2,0},{4,6},{6,4},{8,10},{10,8},{12,14},{14,12},{16,18},{18,... | collective-permute-start | bytes 86024 | tf_op jit(solution)/shard_map/ppermute | solution.py:661
  10.3 2.6 %collective-permute-start.3 = (bf16[112,128]{1,0:T(8,128)(2,1)S(1)}, bf16[112,128]{1,0:T(8,128)(2,1)S(1)}, u32[]{:S(2)}, u32[]{:S(2)}) collective-permute-start(bf16[112,128]{1,0:T(8,128)(2,1)S(1)} %get-tuple-element.68), channel_id=1, source_target_pairs={{0,8},{2,4},{4,2},{6,14},{8,0},{10,12},{12,10},{14,6},{16,24},{18,... | collective-permute-start | bytes 86024 | tf_op jit(solution)/shard_map/ppermute | solution.py:661
  13.4 6.4 %collective-permute-start.5 = (bf16[592,128]{1,0:T(8,128)(2,1)S(1)}, bf16[592,128]{1,0:T(8,128)(2,1)S(1)}, u32[]{:S(2)}, u32[]{:S(2)}) collective-permute-start(bf16[592,128]{1,0:T(8,128)(2,1)S(1)} %get-tuple-element.79), channel_id=1, source_target_pairs={{0,1},{1,0},{2,3},{3,2},{4,5},{5,4},{6,7},{7,6},{8,9},{9,8},{10,11... | collective-permute-start | bytes 454664 | tf_op jit(solution)/shard_map/ppermute | solution.py:706
  20.8 3.6 %collective-permute-start.6 = (bf16[112,128]{1,0:T(8,128)(2,1)S(1)}, bf16[112,128]{1,0:T(8,128)(2,1)S(1)}, u32[]{:S(2)}, u32[]{:S(2)}) collective-permute-start(bf16[112,128]{1,0:T(8,128)(2,1)S(1)} %get-tuple-element.87), channel_id=1, source_target_pairs={{0,24},{2,26},{4,28},{6,30},{8,16},{10,18},{12,20},{14,22},{16,8},... | collective-permute-start | bytes 86024 | tf_op jit(solution)/shard_map/ppermute | solution.py:661
  20.9 3.5 %collective-permute-start.7 = (bf16[112,128]{1,0:T(8,128)(2,1)S(1)}, bf16[112,128]{1,0:T(8,128)(2,1)S(1)}, u32[]{:S(2)}, u32[]{:S(2)}) collective-permute-start(bf16[112,128]{1,0:T(8,128)(2,1)S(1)} %get-tuple-element.88), channel_id=1, source_target_pairs={{0,8},{2,10},{4,12},{6,14},{8,0},{10,2},{12,4},{14,6},{16,24},{18,... | collective-permute-start | bytes 86024 | tf_op jit(solution)/shard_map/ppermute | solution.py:661
  24.4 3.9 %collective-permute-start.8 = (bf16[112,128]{1,0:T(8,128)(2,1)S(1)}, bf16[112,128]{1,0:T(8,128)(2,1)S(1)}, u32[]{:S(2)}, u32[]{:S(2)}) collective-permute-start(bf16[112,128]{1,0:T(8,128)(2,1)S(1)} %get-tuple-element.91), channel_id=1, source_target_pairs={{0,2},{2,0},{4,6},{6,4},{8,10},{10,8},{12,14},{14,12},{16,18},{18,... | collective-permute-start | bytes 86024 | tf_op jit(solution)/shard_map/ppermute | solution.py:661
  26.3 2.1 %collective-permute-start.9 = (bf16[112,128]{1,0:T(8,128)(2,1)S(1)}, bf16[112,128]{1,0:T(8,128)(2,1)S(1)}, u32[]{:S(2)}, u32[]{:S(2)}) collective-permute-start(bf16[112,128]{1,0:T(8,128)(2,1)S(1)} %get-tuple-element.92), channel_id=1, source_target_pairs={{0,8},{2,4},{4,2},{6,14},{8,0},{10,12},{12,10},{14,6},{16,24},{18,... | collective-permute-start | bytes 86024 | tf_op jit(solution)/shard_map/ppermute | solution.py:661
  29.0 5.3 %collective-permute-start.10 = (bf16[592,128]{1,0:T(8,128)(2,1)S(1)}, bf16[592,128]{1,0:T(8,128)(2,1)S(1)}, u32[]{:S(2)}, u32[]{:S(2)}) collective-permute-start(bf16[592,128]{1,0:T(8,128)(2,1)S(1)} %get-tuple-element.96), channel_id=1, source_target_pairs={{0,1},{1,0},{2,3},{3,2},{4,5},{5,4},{6,7},{7,6},{8,9},{9,8},{10,11... | collective-permute-start | bytes 454664 | tf_op jit(solution)/shard_map/ppermute | solution.py:706
  35.3 3.4 %collective-permute-start.11 = (bf16[112,128]{1,0:T(8,128)(2,1)S(1)}, bf16[112,128]{1,0:T(8,128)(2,1)S(1)}, u32[]{:S(2)}, u32[]{:S(2)}) collective-permute-start(bf16[112,128]{1,0:T(8,128)(2,1)S(1)} %get-tuple-element.99), channel_id=1, source_target_pairs={{0,24},{2,26},{4,28},{6,30},{8,16},{10,18},{12,20},{14,22},{16,8},... | collective-permute-start | bytes 86024 | tf_op jit(solution)/shard_map/ppermute | solution.py:661
  35.3 3.3 %collective-permute-start.12 = (bf16[112,128]{1,0:T(8,128)(2,1)S(1)}, bf16[112,128]{1,0:T(8,128)(2,1)S(1)}, u32[]{:S(2)}, u32[]{:S(2)}) collective-permute-start(bf16[112,128]{1,0:T(8,128)(2,1)S(1)} %get-tuple-element.100), channel_id=1, source_target_pairs={{0,8},{2,10},{4,12},{6,14},{8,0},{10,2},{12,4},{14,6},{16,24},{18,... | collective-permute-start | bytes 86024 | tf_op jit(solution)/shard_map/ppermute | solution.py:661
  38.6 3.9 %collective-permute-start.13 = (bf16[112,128]{1,0:T(8,128)(2,1)S(1)}, bf16[112,128]{1,0:T(8,128)(2,1)S(1)}, u32[]{:S(2)}, u32[]{:S(2)}) collective-permute-start(bf16[112,128]{1,0:T(8,128)(2,1)S(1)} %get-tuple-element.103), channel_id=1, source_target_pairs={{0,2},{2,0},{4,6},{6,4},{8,10},{10,8},{12,14},{14,12},{16,18},{18,... | collective-permute-start | bytes 86024 | tf_op jit(solution)/shard_map/ppermute | solution.py:661
  40.7 1.9 %collective-permute-start.14 = (bf16[112,128]{1,0:T(8,128)(2,1)S(1)}, bf16[112,128]{1,0:T(8,128)(2,1)S(1)}, u32[]{:S(2)}, u32[]{:S(2)}) collective-permute-start(bf16[112,128]{1,0:T(8,128)(2,1)S(1)} %get-tuple-element.104), channel_id=1, source_target_pairs={{0,8},{2,4},{4,2},{6,14},{8,0},{10,12},{12,10},{14,6},{16,24},{18,... | collective-permute-start | bytes 86024 | tf_op jit(solution)/shard_map/ppermute | solution.py:661
  43.2 5.4 %collective-permute-start.15 = (bf16[592,128]{1,0:T(8,128)(2,1)S(1)}, bf16[592,128]{1,0:T(8,128)(2,1)S(1)}, u32[]{:S(2)}, u32[]{:S(2)}) collective-permute-start(bf16[592,128]{1,0:T(8,128)(2,1)S(1)} %get-tuple-element.108), channel_id=1, source_target_pairs={{0,1},{1,0},{2,3},{3,2},{4,5},{5,4},{6,7},{7,6},{8,9},{9,8},{10,11... | collective-permute-start | bytes 454664 | tf_op jit(solution)/shard_map/ppermute | solution.py:706
  49.7 3.4 %collective-permute-start.16 = (bf16[112,128]{1,0:T(8,128)(2,1)S(1)}, bf16[112,128]{1,0:T(8,128)(2,1)S(1)}, u32[]{:S(2)}, u32[]{:S(2)}) collective-permute-start(bf16[112,128]{1,0:T(8,128)(2,1)S(1)} %get-tuple-element.110), channel_id=1, source_target_pairs={{0,24},{2,26},{4,28},{6,30},{8,16},{10,18},{12,20},{14,22},{16,8},... | collective-permute-start | bytes 86024 | tf_op jit(solution)/shard_map/ppermute | solution.py:661
  49.7 3.3 %collective-permute-start.17 = (bf16[112,128]{1,0:T(8,128)(2,1)S(1)}, bf16[112,128]{1,0:T(8,128)(2,1)S(1)}, u32[]{:S(2)}, u32[]{:S(2)}) collective-permute-start(bf16[112,128]{1,0:T(8,128)(2,1)S(1)} %get-tuple-element.111), channel_id=1, source_target_pairs={{0,8},{2,10},{4,12},{6,14},{8,0},{10,2},{12,4},{14,6},{16,24},{18,... | collective-permute-start | bytes 86024 | tf_op jit(solution)/shard_map/ppermute | solution.py:661
  53.1 3.9 %collective-permute-start.18 = (bf16[112,128]{1,0:T(8,128)(2,1)S(1)}, bf16[112,128]{1,0:T(8,128)(2,1)S(1)}, u32[]{:S(2)}, u32[]{:S(2)}) collective-permute-start(bf16[112,128]{1,0:T(8,128)(2,1)S(1)} %get-tuple-element.114), channel_id=1, source_target_pairs={{0,2},{2,0},{4,6},{6,4},{8,10},{10,8},{12,14},{14,12},{16,18},{18,... | collective-permute-start | bytes 86024 | tf_op jit(solution)/shard_map/ppermute | solution.py:661
  55.1 1.9 %collective-permute-start.19 = (bf16[112,128]{1,0:T(8,128)(2,1)S(1)}, bf16[112,128]{1,0:T(8,128)(2,1)S(1)}, u32[]{:S(2)}, u32[]{:S(2)}) collective-permute-start(bf16[112,128]{1,0:T(8,128)(2,1)S(1)} %get-tuple-element.115), channel_id=1, source_target_pairs={{0,8},{2,4},{4,2},{6,14},{8,0},{10,12},{12,10},{14,6},{16,24},{18,... | collective-permute-start | bytes 86024 | tf_op jit(solution)/shard_map/ppermute | solution.py:661
  57.1 4.2 %collective-permute-start.20 = (bf16[208,128]{1,0:T(8,128)(2,1)S(1)}, bf16[208,128]{1,0:T(8,128)(2,1)S(1)}, u32[]{:S(2)}, u32[]{:S(2)}) collective-permute-start(bf16[208,128]{1,0:T(8,128)(2,1)S(1)} %get-tuple-element.118), channel_id=1, source_target_pairs={{0,1},{1,0},{2,3},{3,2},{4,5},{5,4},{6,7},{7,6},{8,9},{9,8},{10,11... | collective-permute-start | bytes 159752 | tf_op jit(solution)/shard_map/ppermute | solution.py:713

commit v14 on v13

--- a/solution.py
+++ b/solution.py
@@ -401,9 +401,9 @@
     return (value if valid is None else value * valid.astype(F32)).astype(HALO)
 
 
-def add_z(sz, y, j, face):
+def add_z(sz, y, j, face, layers=None):
     c = layer_received(sz, j)
-    for a in range(sz.nx):
+    for a in layers or range(sz.nx):
         for b in range(0, sz.ny, PAD):
             n = min(PAD, sz.ny - b)
             at = pl.ds(a * sz.line_x + b * PAD + c, n, stride=PAD)
@@ -606,14 +606,16 @@
 def finish_body(sz, r, *refs):
     zr = refs[: sz.links]
     out, ra, block, sent = refs[sz.links :]
-    ra[...] = r[...]
-    for j, face in enumerate(zr):
-        add_z(sz, ra, j, face[...].astype(F32))
+    received = [face[...].astype(F32) for face in zr]
     nz = block.shape[2]
     pieces, copies = 3, []
     for k in range(pieces):
         first, last = k * sz.nx // pieces, (k + 1) * sz.nx // pieces
-        value = ra[first * sz.line_x : last * sz.line_x, :]
+        rows = slice(first * sz.line_x, last * sz.line_x)
+        ra[rows, :] = r[rows, :]
+        for j, face in enumerate(received):
+            add_z(sz, ra, j, face, range(first, last))
+        value = ra[rows, :]
         value = value.reshape(last - first, sz.ny, PAD, sz.orb)[:, :, :nz, :]
         block[first:last] = value
         copy = pltpu.make_async_copy(block.at[first:last], out.at[first:last], sent.at[k])

time: 62.4 us -> 62.3 us (level)
  no operation moved by 1% of the time
where the time goes in v14:
time: 62.3 us; the launch traced here: 62.2 us
  waiting for transfers between devices  29.8 us (48%)
  starting transfers between devices  17.3 us (28%)
  Pallas kernels  13.4 us (22%)
  local copies, waits for them, and re-layouts  1.5 us (2%)
    ppermute x16, waiting for transfers between devices, swap_faces(): out.append(lax.ppermute(face, axes, pairs))  13.5 us
    pallas_call x19, Pallas kernels, kernel_call(): pl.pallas_call(with_waits, out_shape=outs, in_specs=[VMEM] * used + [pl.B...  13.4 us
    ppermute x16, starting transfers between devices, swap_faces(): out.append(lax.ppermute(face, axes, pairs))  13.4 us
    ppermute x3, waiting for transfers between devices, local(): lax.ppermute(m, 'gz', ring[s + 1])  12.9 us
    ppermute x1, waiting for transfers between devices, local(): zr = [lax.ppermute(f, 'gz', ring[s]) for f, s in zip(sent, link_shifts(sz))]  3.45 us
    ppermute x3, starting transfers between devices, local(): lax.ppermute(m, 'gz', ring[s + 1])  1.71 us
    ppermute x1, starting transfers between devices, local(): qfaces.append(lax.ppermute(face_rows[j], 'gz', back))  1.58 us
    pad x1, local copies, waits for them, and re-layouts, local(): proj = jnp.pad(proj, ((0, up(nodes, 16) - nodes), (0, 0)))  1.37 us
  transfers between devices with their start and end apart: 21, of which 10 were waited for; matrix products, arithmetic and copies ran while one was open for 0% of the time, Pallas kernels for 13%

profile of v14, /device:TPU:0, one launch (start us, length us, event | category | flops | bytes accessed | tf_op | source)
XLA Modules:
  0.0 62.2 jit_solution(653339659190720473)
XLA Ops:
  0.0 0.0 copy-start
  0.0 1.4 %pad.4.refs_2_.refs_0_ = bf16[352,1536]{1,0:T(8,128)(2,1)S(1)} pad(bf16[343,1536]{1,0:T(8,128)(2,1)} %bitcast.11, bf16[]{:T(256)} %constant.2.clone.1), padding=0_9x0_0 | pad | bytes 2135042 | tf_op jit(solution)/shard_map/jit(_pad)/pad | solution.py:675
  1.4 0.0 copy-done.2
  1.4 0.1 copy-done.1
  1.5 0.1 shard_map.73
  1.6 2.4 %collective-permute-start = (bf16[112,128]{1,0:T(8,128)(2,1)S(1)}, bf16[112,128]{1,0:T(8,128)(2,1)S(1)}, u32[]{:S(2)}, u32[]{:S(2)}) collective-permute-start(bf16[112,128]{1,0:T(8,128)(2,1)S(1)} %get-tuple-element.63), channel_id=1, source_target_pairs={{0,24},{2,26},{4,28},{6,30},{8,16},{10,18},{12,20},{14,22},{16,8},... | collective-permute-start | bytes 86024 | tf_op jit(solution)/shard_map/ppermute | solution.py:663
  4.0 0.7 %collective-permute-start.1 = (bf16[112,128]{1,0:T(8,128)(2,1)S(1)}, bf16[112,128]{1,0:T(8,128)(2,1)S(1)}, u32[]{:S(2)}, u32[]{:S(2)}) collective-permute-start(bf16[112,128]{1,0:T(8,128)(2,1)S(1)} %get-tuple-element.64), channel_id=1, source_target_pairs={{0,8},{2,10},{4,12},{6,14},{8,0},{10,2},{12,4},{14,6},{16,24},{18,... | collective-permute-start | bytes 86024 | tf_op jit(solution)/shard_map/ppermute | solution.py:663
  4.7 2.2 %shard_map.75 = (bf16[1664,384]{1,0:T(8,128)(2,1)S(1)}, bf16[224,384]{1,0:T(8,128)(2,1)S(1)}) custom-call(bf16[352,1536]{1,0:T(8,128)(2,1)S(1)} %pad.4.refs_2_.refs_0_, f32[4,32]{1,0:T(4,128)S(1)} %get-tuple-element.69.refs_1_), custom_call_target="tpu_custom_call" | custom-call | flops 3000000000 | bytes 2531840 | tf_op jit(solution)/shard_map/pallas_call | solution.py:63
  6.9 1.6 %collective-permute-start.4 = (bf16[224,384]{1,0:T(8,128)(2,1)S(1)}, bf16[224,384]{1,0:T(8,128)(2,1)S(1)}, u32[]{:S(2)}, u32[]{:S(2)}) collective-permute-start(bf16[224,384]{1,0:T(8,128)(2,1)S(1)} %get-tuple-element.71.refs_5_), channel_id=1, source_target_pairs={{1,0},{0,1},{3,2},{2,3},{5,4},{4,5},{7,6},{6,7},{9,8},{8,9},{11,10... | collective-permute-start | bytes 516104 | tf_op jit(solution)/shard_map/ppermute | solution.py:690
  8.5 0.0 copy-done
  8.6 0.0 collective-permute-done.refs_0_.refs_1_
  8.6 0.0 collective-permute-done.1.refs_1_.refs_2_
  8.6 1.6 %collective-permute-start.2 = (bf16[112,128]{1,0:T(8,128)(2,1)S(1)}, bf16[112,128]{1,0:T(8,128)(2,1)S(1)}, u32[]{:S(2)}, u32[]{:S(2)}) collective-permute-start(bf16[112,128]{1,0:T(8,128)(2,1)S(1)} %get-tuple-element.67), channel_id=1, source_target_pairs={{0,2},{2,0},{4,6},{6,4},{8,10},{10,8},{12,14},{14,12},{16,18},{18,... | collective-permute-start | bytes 86024 | tf_op jit(solution)/shard_map/ppermute | solution.py:663
  10.3 0.0 collective-permute-start.3
  10.3 0.0 copy-done.3
  10.3 0.0 copy-done.4
  10.3 2.5 %shard_map.76 = (bf16[384,1664]{1,0:T(8,128)(2,1)S(1)}, bf16[400,400]{1,0:T(8,128)(2,1)S(1)}, f32[1600,128]{1,0:T(8,128)S(1)}, bf16[384,384]{1,0:T(8,128)(2,1)S(...) custom-call(bf16[1664,384]{1,0:T(8,128)(2,1)S(1)} %get-tuple-element, ...), custom_call_target="tpu_custom_call" | custom-call | flops 1000000000 | bytes 5791634 | tf_op jit(solution)/shard_map/pallas_call | solution.py:63
  12.8 0.0 collective-permute-done.2.refs_3_
  12.9 0.0 collective-permute-done.3.refs_4_
  12.9 0.6 shard_map.77
  13.4 0.6 collective-permute-start.5
  14.0 0.0 collective-permute-done.4.refs_2_
  14.0 0.8 %shard_map.78.refs_1_ = f32[384,128]{1,0:T(8,128)S(1)} custom-call(f32[384,128]{1,0:T(8,128)S(1)} %get-tuple-element.74.refs_0_, bf16[224,128]{1,0:T(8,128)(2,1)S(1)} %get-tuple-element.75.refs_1_, bf16[224,384]{1,0:T(8,128)(2,1)S(1)} %collective-permute-done.4.refs_2_, bf16[384,384]{1,0:T(8,128)(2,1)S(1)} %get-tuple-element.76.refs_3_, ...), custom_call_target="tpu_custom_call" | custom-call | flops 200000000 | bytes 1507328 | tf_op jit(solution)/shard_map/pallas_call | solution.py:63
  14.8 5.0 %collective-permute-done.5.refs_2_ = bf16[592,128]{1,0:T(8,128)(2,1)S(1)} collective-permute-done((bf16[592,128]{1,0:T(8,128)(2,1)S(1)}, bf16[592,128]{1,0:T(8,128)(2,1)S(1)}, u32[]{:S(2)}, u32[]{:S(2)}) %collective-permute-start.5) | collective-permute-done | bytes 151584 | tf_op jit(solution)/shard_map/ppermute | solution.py:708
  19.8 1.0 %shard_map.79 = (f32[1384,128]{1,0:T(8,128)S(1)}, f32[1384,128]{1,0:T(8,128)S(1)}, bf16[112,128]{1,0:T(8,128)(2,1)S(1)}, bf16[112,128]{1,0:T(8,128)(2,1)S(1)}, f...) custom-call(f32[1384,128]{1,0:T(8,128)S(1)} %get-tuple-element.73.refs_0_, f32[384,128]{1,0:T(8,128)S(1)} %shard_map.78.refs_1_, ...), custom_call_target="tpu_custom_call" | custom-call | flops 600000000 | bytes 5825024 | tf_op jit(solution)/shard_map/pallas_call | solution.py:63
  20.8 0.1 collective-permute-start.6
  20.9 0.6 %collective-permute-start.7 = (bf16[112,128]{1,0:T(8,128)(2,1)S(1)}, bf16[112,128]{1,0:T(8,128)(2,1)S(1)}, u32[]{:S(2)}, u32[]{:S(2)}) collective-permute-start(bf16[112,128]{1,0:T(8,128)(2,1)S(1)} %get-tuple-element.88), channel_id=1, source_target_pairs={{0,8},{2,10},{4,12},{6,14},{8,0},{10,2},{12,4},{14,6},{16,24},{18,... | collective-permute-start | bytes 86024 | tf_op jit(solution)/shard_map/ppermute | solution.py:663
  21.6 2.8 %collective-permute-done.6.refs_0_.refs_2_ = bf16[112,128]{1,0:T(8,128)(2,1)S(1)} collective-permute-done((bf16[112,128]{1,0:T(8,128)(2,1)S(1)}, bf16[112,128]{1,0:T(8,128)(2,1)S(1)}, u32[]{:S(2)}, u32[]{:S(2)}) %collective-permute-start.6) | collective-permute-done | bytes 28704 | tf_op jit(solution)/shard_map/ppermute | solution.py:663
  24.4 0.0 collective-permute-done.7.refs_1_.refs_3_
  24.4 1.9 %collective-permute-start.8 = (bf16[112,128]{1,0:T(8,128)(2,1)S(1)}, bf16[112,128]{1,0:T(8,128)(2,1)S(1)}, u32[]{:S(2)}, u32[]{:S(2)}) collective-permute-start(bf16[112,128]{1,0:T(8,128)(2,1)S(1)} %get-tuple-element.91), channel_id=1, source_target_pairs={{0,2},{2,0},{4,6},{6,4},{8,10},{10,8},{12,14},{14,12},{16,18},{18,... | collective-permute-start | bytes 86024 | tf_op jit(solution)/shard_map/ppermute | solution.py:663
  26.3 0.0 collective-permute-start.9
  26.3 2.1 %collective-permute-done.8.refs_4_ = bf16[112,128]{1,0:T(8,128)(2,1)S(1)} collective-permute-done((bf16[112,128]{1,0:T(8,128)(2,1)S(1)}, bf16[112,128]{1,0:T(8,128)(2,1)S(1)}, u32[]{:S(2)}, u32[]{:S(2)}) %collective-permute-start.8) | collective-permute-done | bytes 28704 | tf_op jit(solution)/shard_map/ppermute | solution.py:663
  28.4 0.0 collective-permute-done.9.refs_5_
  28.4 0.6 shard_map.81
  29.0 0.6 collective-permute-start.10
  29.5 0.8 %shard_map.82.refs_1_ = f32[384,128]{1,0:T(8,128)S(1)} custom-call(f32[384,128]{1,0:T(8,128)S(1)} %get-tuple-element.94.refs_0_, bf16[224,128]{1,0:T(8,128)(2,1)S(1)} %get-tuple-element.95.refs_1_, bf16[224,384]{1,0:T(8,128)(2,1)S(1)} %collective-permute-done.4.refs_2_, bf16[384,384]{1,0:T(8,128)(2,1)S(1)} %get-tuple-element.76.refs_3_, ...), custom_call_target="tpu_custom_call" | custom-call | flops 200000000 | bytes 1507328 | tf_op jit(solution)/shard_map/pallas_call | solution.py:63
  30.4 3.9 %collective-permute-done.10.refs_2_ = bf16[592,128]{1,0:T(8,128)(2,1)S(1)} collective-permute-done((bf16[592,128]{1,0:T(8,128)(2,1)S(1)}, bf16[592,128]{1,0:T(8,128)(2,1)S(1)}, u32[]{:S(2)}, u32[]{:S(2)}) %collective-permute-start.10) | collective-permute-done | bytes 151584 | tf_op jit(solution)/shard_map/ppermute | solution.py:708
  34.2 1.0 %shard_map.83 = (f32[1384,128]{1,0:T(8,128)S(1)}, f32[1384,128]{1,0:T(8,128)S(1)}, bf16[112,128]{1,0:T(8,128)(2,1)S(1)}, bf16[112,128]{1,0:T(8,128)(2,1)S(1)}, f...) custom-call(f32[1384,128]{1,0:T(8,128)S(1)} %get-tuple-element.93.refs_0_, f32[384,128]{1,0:T(8,128)S(1)} %shard_map.82.refs_1_, ...), custom_call_target="tpu_custom_call" | custom-call | flops 600000000 | bytes 5825024 | tf_op jit(solution)/shard_map/pallas_call | solution.py:63
  35.3 0.1 collective-permute-start.11
  35.3 0.8 %collective-permute-start.12 = (bf16[112,128]{1,0:T(8,128)(2,1)S(1)}, bf16[112,128]{1,0:T(8,128)(2,1)S(1)}, u32[]{:S(2)}, u32[]{:S(2)}) collective-permute-start(bf16[112,128]{1,0:T(8,128)(2,1)S(1)} %get-tuple-element.100), channel_id=1, source_target_pairs={{0,8},{2,10},{4,12},{6,14},{8,0},{10,2},{12,4},{14,6},{16,24},{18,... | collective-permute-start | bytes 86024 | tf_op jit(solution)/shard_map/ppermute | solution.py:663
  36.2 2.4 %collective-permute-done.11.refs_0_.refs_3_ = bf16[112,128]{1,0:T(8,128)(2,1)S(1)} collective-permute-done((bf16[112,128]{1,0:T(8,128)(2,1)S(1)}, bf16[112,128]{1,0:T(8,128)(2,1)S(1)}, u32[]{:S(2)}, u32[]{:S(2)}) %collective-permute-start.11) | collective-permute-done | bytes 28704 | tf_op jit(solution)/shard_map/ppermute | solution.py:663
  38.6 0.0 collective-permute-done.12.refs_1_.refs_4_
  38.6 2.1 %collective-permute-start.13 = (bf16[112,128]{1,0:T(8,128)(2,1)S(1)}, bf16[112,128]{1,0:T(8,128)(2,1)S(1)}, u32[]{:S(2)}, u32[]{:S(2)}) collective-permute-start(bf16[112,128]{1,0:T(8,128)(2,1)S(1)} %get-tuple-element.103), channel_id=1, source_target_pairs={{0,2},{2,0},{4,6},{6,4},{8,10},{10,8},{12,14},{14,12},{16,18},{18,... | collective-permute-start | bytes 86024 | tf_op jit(solution)/shard_map/ppermute | solution.py:663
  40.7 0.0 collective-permute-start.14
  40.7 1.8 %collective-permute-done.13.refs_5_ = bf16[112,128]{1,0:T(8,128)(2,1)S(1)} collective-permute-done((bf16[112,128]{1,0:T(8,128)(2,1)S(1)}, bf16[112,128]{1,0:T(8,128)(2,1)S(1)}, u32[]{:S(2)}, u32[]{:S(2)}) %collective-permute-start.13) | collective-permute-done | bytes 28704 | tf_op jit(solution)/shard_map/ppermute | solution.py:663
  42.6 0.0 collective-permute-done.14.refs_6_
  42.6 0.6 %shard_map.85 = (f32[1384,128]{1,0:T(8,128)S(1)}, f32[384,128]{1,0:T(8,128)S(1)}, bf16[224,128]{1,0:T(8,128)(2,1)S(1)}, bf16[592,128]{1,0:T(8,128)(2,1)S(1)}) custom-call(f32[1384,128]{1,0:T(8,128)S(1)} %get-tuple-element.97.refs_0_, f32[1384,128]{1,0:T(8,128)S(1)} %get-tuple-element.98.refs_1_.refs_2_, f32[1384,128]{1,0:T(8,128)S(1)} %get-tuple-element.86.refs_1_.refs_2_, ...), custom_call_target="tpu_custom_call" | custom-call | flops 400000000 | bytes 4632576 | tf_op jit(solution)/shard_map/pallas_call | solution.py:63
  43.2 0.6 collective-permute-start.15
  43.8 0.8 %shard_map.86.refs_1_ = f32[384,128]{1,0:T(8,128)S(1)} custom-call(f32[384,128]{1,0:T(8,128)S(1)} %get-tuple-element.106.refs_0_, bf16[224,128]{1,0:T(8,128)(2,1)S(1)} %get-tuple-element.107.refs_1_, bf16[224,384]{1,0:T(8,128)(2,1)S(1)} %collective-permute-done.4.refs_2_, bf16[384,384]{1,0:T(8,128)(2,1)S(1)} %get-tuple-element.76.refs_3_, ...), custom_call_target="tpu_custom_call" | custom-call | flops 200000000 | bytes 1507328 | tf_op jit(solution)/shard_map/pallas_call | solution.py:63
  44.6 4.0 %collective-permute-done.15.refs_2_ = bf16[592,128]{1,0:T(8,128)(2,1)S(1)} collective-permute-done((bf16[592,128]{1,0:T(8,128)(2,1)S(1)}, bf16[592,128]{1,0:T(8,128)(2,1)S(1)}, u32[]{:S(2)}, u32[]{:S(2)}) %collective-permute-start.15) | collective-permute-done | bytes 151584 | tf_op jit(solution)/shard_map/ppermute | solution.py:708
  48.6 1.0 %shard_map.87 = (f32[1384,128]{1,0:T(8,128)S(1)}, f32[1384,128]{1,0:T(8,128)S(1)}, bf16[112,128]{1,0:T(8,128)(2,1)S(1)}, bf16[112,128]{1,0:T(8,128)(2,1)S(1)}, f...) custom-call(f32[1384,128]{1,0:T(8,128)S(1)} %get-tuple-element.105.refs_0_, f32[384,128]{1,0:T(8,128)S(1)} %shard_map.86.refs_1_, ...), custom_call_target="tpu_custom_call" | custom-call | flops 600000000 | bytes 5825024 | tf_op jit(solution)/shard_map/pallas_call | solution.py:63
  49.7 0.1 collective-permute-start.16
  49.7 1.0 %collective-permute-start.17 = (bf16[112,128]{1,0:T(8,128)(2,1)S(1)}, bf16[112,128]{1,0:T(8,128)(2,1)S(1)}, u32[]{:S(2)}, u32[]{:S(2)}) collective-permute-start(bf16[112,128]{1,0:T(8,128)(2,1)S(1)} %get-tuple-element.111), channel_id=1, source_target_pairs={{0,8},{2,10},{4,12},{6,14},{8,0},{10,2},{12,4},{14,6},{16,24},{18,... | collective-permute-start | bytes 86024 | tf_op jit(solution)/shard_map/ppermute | solution.py:663
  50.7 2.3 %collective-permute-done.16.refs_0_.refs_1_ = bf16[112,128]{1,0:T(8,128)(2,1)S(1)} collective-permute-done((bf16[112,128]{1,0:T(8,128)(2,1)S(1)}, bf16[112,128]{1,0:T(8,128)(2,1)S(1)}, u32[]{:S(2)}, u32[]{:S(2)}) %collective-permute-start.16) | collective-permute-done | bytes 28704 | tf_op jit(solution)/shard_map/ppermute | solution.py:663
  53.0 0.0 collective-permute-done.17.refs_1_.refs_2_
  53.1 2.0 %collective-permute-start.18 = (bf16[112,128]{1,0:T(8,128)(2,1)S(1)}, bf16[112,128]{1,0:T(8,128)(2,1)S(1)}, u32[]{:S(2)}, u32[]{:S(2)}) collective-permute-start(bf16[112,128]{1,0:T(8,128)(2,1)S(1)} %get-tuple-element.114), channel_id=1, source_target_pairs={{0,2},{2,0},{4,6},{6,4},{8,10},{10,8},{12,14},{14,12},{16,18},{18,... | collective-permute-start | bytes 86024 | tf_op jit(solution)/shard_map/ppermute | solution.py:663
  55.1 0.0 collective-permute-start.19
  55.1 1.9 %collective-permute-done.18.refs_3_ = bf16[112,128]{1,0:T(8,128)(2,1)S(1)} collective-permute-done((bf16[112,128]{1,0:T(8,128)(2,1)S(1)}, bf16[112,128]{1,0:T(8,128)(2,1)S(1)}, u32[]{:S(2)}, u32[]{:S(2)}) %collective-permute-start.18) | collective-permute-done | bytes 28704 | tf_op jit(solution)/shard_map/ppermute | solution.py:663
  57.0 0.0 collective-permute-done.19.refs_4_
  57.0 0.1 shard_map.89
  57.1 0.6 collective-permute-start.20
  57.7 0.2 shard_map.90.refs_0_
  57.9 3.4 %collective-permute-done.20.refs_1_ = bf16[208,128]{1,0:T(8,128)(2,1)S(1)} collective-permute-done((bf16[208,128]{1,0:T(8,128)(2,1)S(1)}, bf16[208,128]{1,0:T(8,128)(2,1)S(1)}, u32[]{:S(2)}, u32[]{:S(2)}) %collective-permute-start.20) | collective-permute-done | bytes 53280 | tf_op jit(solution)/shard_map/ppermute | solution.py:715
  61.3 0.9 %shard_map.91 = f32[13,13,7,128]{3,2,1,0:T(8,128)} custom-call(f32[1384,128]{1,0:T(8,128)S(1)} %shard_map.90.refs_0_, bf16[208,128]{1,0:T(8,128)(2,1)S(1)} %collective-permute-done.20.refs_1_), custom_call_target="tpu_custom_call" | custom-call | bytes 1367552 | tf_op jit(solution)/shard_map/pallas_call | solution.py:63
  (12 shorter events, 0.2 us)
Async XLA Ops:
  0.0 8.5 %copy-start = (f32[343,2,2,1]{0,3,2,1:T(1,128)S(1)}, f32[343,2,2,1]{0,3,2,1:T(1,128)}, u32[]{:S(2)}) copy-start(f32[343,2,2,1]{0,3,2,1:T(1,128)} %param.9) | copy-start | bytes 16468
  0.0 1.4 %copy-start.2 = (s32[1,1,1,32,4]{3,4,2,1,0:T(4,128)S(1)}, s32[1,1,1,32,4]{3,4,2,1,0:T(4,128)}, u32[]{:S(2)}) copy-start(s32[1,1,1,32,4]{3,4,2,1,0:T(4,128)} %param.12) | copy-start | bytes 1540
  0.0 1.4 %copy-start.1 = (f32[13,13,7,128]{3,2,1,0:T(8,128)S(1)}, f32[13,13,7,128]{3,2,1,0:T(8,128)}, u32[]{:S(2)}) copy-start(f32[13,13,7,128]{3,2,1,0:T(8,128)} %refs_0_.1) | copy-start | bytes 1817092
  1.6 7.0 %collective-permute-start = (bf16[112,128]{1,0:T(8,128)(2,1)S(1)}, bf16[112,128]{1,0:T(8,128)(2,1)S(1)}, u32[]{:S(2)}, u32[]{:S(2)}) collective-permute-start(bf16[112,128]{1,0:T(8,128)(2,1)S(1)} %get-tuple-element.63), channel_id=1, source_target_pairs={{0,24},{2,26},{4,28},{6,30},{8,16},{10,18},{12,20},{14,22},{16,8},... | collective-permute-start | bytes 86024 | tf_op jit(solution)/shard_map/ppermute | solution.py:663
  4.0 4.6 %collective-permute-start.1 = (bf16[112,128]{1,0:T(8,128)(2,1)S(1)}, bf16[112,128]{1,0:T(8,128)(2,1)S(1)}, u32[]{:S(2)}, u32[]{:S(2)}) collective-permute-start(bf16[112,128]{1,0:T(8,128)(2,1)S(1)} %get-tuple-element.64), channel_id=1, source_target_pairs={{0,8},{2,10},{4,12},{6,14},{8,0},{10,2},{12,4},{14,6},{16,24},{18,... | collective-permute-start | bytes 86024 | tf_op jit(solution)/shard_map/ppermute | solution.py:663
  4.7 5.6 %copy-start.3 = (bf16[343,343]{1,0:T(8,128)(2,1)S(1)}, bf16[343,343]{1,0:T(8,128)(2,1)}, u32[]{:S(2)}) copy-start(bf16[343,343]{1,0:T(8,128)(2,1)} %refs_1_.1) | copy-start | bytes 705898
  4.7 5.6 %copy-start.4 = (f32[64,12,12]{0,2,1:T(8,128)S(1)}, f32[64,12,12]{0,2,1:T(8,128)}, u32[]{:S(2)}) copy-start(f32[64,12,12]{0,2,1:T(8,128)} %param.13) | copy-start | bytes 110596
  4.7 5.6 %copy-start.5 = (s32[1,1,2,32]{3,2,1,0:T(2,128)S(1)}, s32[1,1,2,32]{3,2,1,0:T(2,128)}, u32[]{:S(2)}) copy-start(s32[1,1,2,32]{3,2,1,0:T(2,128)} %param.11) | copy-start | bytes 772
  6.9 7.1 %collective-permute-start.4 = (bf16[224,384]{1,0:T(8,128)(2,1)S(1)}, bf16[224,384]{1,0:T(8,128)(2,1)S(1)}, u32[]{:S(2)}, u32[]{:S(2)}) collective-permute-start(bf16[224,384]{1,0:T(8,128)(2,1)S(1)} %get-tuple-element.71.refs_5_), channel_id=1, source_target_pairs={{1,0},{0,1},{3,2},{2,3},{5,4},{4,5},{7,6},{6,7},{9,8},{8,9},{11,10... | collective-permute-start | bytes 516104 | tf_op jit(solution)/shard_map/ppermute | solution.py:690
  8.6 4.2 %collective-permute-start.2 = (bf16[112,128]{1,0:T(8,128)(2,1)S(1)}, bf16[112,128]{1,0:T(8,128)(2,1)S(1)}, u32[]{:S(2)}, u32[]{:S(2)}) collective-permute-start(bf16[112,128]{1,0:T(8,128)(2,1)S(1)} %get-tuple-element.67), channel_id=1, source_target_pairs={{0,2},{2,0},{4,6},{6,4},{8,10},{10,8},{12,14},{14,12},{16,18},{18,... | collective-permute-start | bytes 86024 | tf_op jit(solution)/shard_map/ppermute | solution.py:663
  10.3 2.6 %collective-permute-start.3 = (bf16[112,128]{1,0:T(8,128)(2,1)S(1)}, bf16[112,128]{1,0:T(8,128)(2,1)S(1)}, u32[]{:S(2)}, u32[]{:S(2)}) collective-permute-start(bf16[112,128]{1,0:T(8,128)(2,1)S(1)} %get-tuple-element.68), channel_id=1, source_target_pairs={{0,8},{2,4},{4,2},{6,14},{8,0},{10,12},{12,10},{14,6},{16,24},{18,... | collective-permute-start | bytes 86024 | tf_op jit(solution)/shard_map/ppermute | solution.py:663
  13.4 6.4 %collective-permute-start.5 = (bf16[592,128]{1,0:T(8,128)(2,1)S(1)}, bf16[592,128]{1,0:T(8,128)(2,1)S(1)}, u32[]{:S(2)}, u32[]{:S(2)}) collective-permute-start(bf16[592,128]{1,0:T(8,128)(2,1)S(1)} %get-tuple-element.79), channel_id=1, source_target_pairs={{0,1},{1,0},{2,3},{3,2},{4,5},{5,4},{6,7},{7,6},{8,9},{9,8},{10,11... | collective-permute-start | bytes 454664 | tf_op jit(solution)/shard_map/ppermute | solution.py:708
  20.8 3.6 %collective-permute-start.6 = (bf16[112,128]{1,0:T(8,128)(2,1)S(1)}, bf16[112,128]{1,0:T(8,128)(2,1)S(1)}, u32[]{:S(2)}, u32[]{:S(2)}) collective-permute-start(bf16[112,128]{1,0:T(8,128)(2,1)S(1)} %get-tuple-element.87), channel_id=1, source_target_pairs={{0,24},{2,26},{4,28},{6,30},{8,16},{10,18},{12,20},{14,22},{16,8},... | collective-permute-start | bytes 86024 | tf_op jit(solution)/shard_map/ppermute | solution.py:663
  20.9 3.5 %collective-permute-start.7 = (bf16[112,128]{1,0:T(8,128)(2,1)S(1)}, bf16[112,128]{1,0:T(8,128)(2,1)S(1)}, u32[]{:S(2)}, u32[]{:S(2)}) collective-permute-start(bf16[112,128]{1,0:T(8,128)(2,1)S(1)} %get-tuple-element.88), channel_id=1, source_target_pairs={{0,8},{2,10},{4,12},{6,14},{8,0},{10,2},{12,4},{14,6},{16,24},{18,... | collective-permute-start | bytes 86024 | tf_op jit(solution)/shard_map/ppermute | solution.py:663
  24.4 3.9 %collective-permute-start.8 = (bf16[112,128]{1,0:T(8,128)(2,1)S(1)}, bf16[112,128]{1,0:T(8,128)(2,1)S(1)}, u32[]{:S(2)}, u32[]{:S(2)}) collective-permute-start(bf16[112,128]{1,0:T(8,128)(2,1)S(1)} %get-tuple-element.91), channel_id=1, source_target_pairs={{0,2},{2,0},{4,6},{6,4},{8,10},{10,8},{12,14},{14,12},{16,18},{18,... | collective-permute-start | bytes 86024 | tf_op jit(solution)/shard_map/ppermute | solution.py:663
  26.3 2.1 %collective-permute-start.9 = (bf16[112,128]{1,0:T(8,128)(2,1)S(1)}, bf16[112,128]{1,0:T(8,128)(2,1)S(1)}, u32[]{:S(2)}, u32[]{:S(2)}) collective-permute-start(bf16[112,128]{1,0:T(8,128)(2,1)S(1)} %get-tuple-element.92), channel_id=1, source_target_pairs={{0,8},{2,4},{4,2},{6,14},{8,0},{10,12},{12,10},{14,6},{16,24},{18,... | collective-permute-start | bytes 86024 | tf_op jit(solution)/shard_map/ppermute | solution.py:663
  29.0 5.3 %collective-permute-start.10 = (bf16[592,128]{1,0:T(8,128)(2,1)S(1)}, bf16[592,128]{1,0:T(8,128)(2,1)S(1)}, u32[]{:S(2)}, u32[]{:S(2)}) collective-permute-start(bf16[592,128]{1,0:T(8,128)(2,1)S(1)} %get-tuple-element.96), channel_id=1, source_target_pairs={{0,1},{1,0},{2,3},{3,2},{4,5},{5,4},{6,7},{7,6},{8,9},{9,8},{10,11... | collective-permute-start | bytes 454664 | tf_op jit(solution)/shard_map/ppermute | solution.py:708
  35.3 3.4 %collective-permute-start.11 = (bf16[112,128]{1,0:T(8,128)(2,1)S(1)}, bf16[112,128]{1,0:T(8,128)(2,1)S(1)}, u32[]{:S(2)}, u32[]{:S(2)}) collective-permute-start(bf16[112,128]{1,0:T(8,128)(2,1)S(1)} %get-tuple-element.99), channel_id=1, source_target_pairs={{0,24},{2,26},{4,28},{6,30},{8,16},{10,18},{12,20},{14,22},{16,8},... | collective-permute-start | bytes 86024 | tf_op jit(solution)/shard_map/ppermute | solution.py:663
  35.3 3.3 %collective-permute-start.12 = (bf16[112,128]{1,0:T(8,128)(2,1)S(1)}, bf16[112,128]{1,0:T(8,128)(2,1)S(1)}, u32[]{:S(2)}, u32[]{:S(2)}) collective-permute-start(bf16[112,128]{1,0:T(8,128)(2,1)S(1)} %get-tuple-element.100), channel_id=1, source_target_pairs={{0,8},{2,10},{4,12},{6,14},{8,0},{10,2},{12,4},{14,6},{16,24},{18,... | collective-permute-start | bytes 86024 | tf_op jit(solution)/shard_map/ppermute | solution.py:663
  38.6 3.9 %collective-permute-start.13 = (bf16[112,128]{1,0:T(8,128)(2,1)S(1)}, bf16[112,128]{1,0:T(8,128)(2,1)S(1)}, u32[]{:S(2)}, u32[]{:S(2)}) collective-permute-start(bf16[112,128]{1,0:T(8,128)(2,1)S(1)} %get-tuple-element.103), channel_id=1, source_target_pairs={{0,2},{2,0},{4,6},{6,4},{8,10},{10,8},{12,14},{14,12},{16,18},{18,... | collective-permute-start | bytes 86024 | tf_op jit(solution)/shard_map/ppermute | solution.py:663
  40.7 1.9 %collective-permute-start.14 = (bf16[112,128]{1,0:T(8,128)(2,1)S(1)}, bf16[112,128]{1,0:T(8,128)(2,1)S(1)}, u32[]{:S(2)}, u32[]{:S(2)}) collective-permute-start(bf16[112,128]{1,0:T(8,128)(2,1)S(1)} %get-tuple-element.104), channel_id=1, source_target_pairs={{0,8},{2,4},{4,2},{6,14},{8,0},{10,12},{12,10},{14,6},{16,24},{18,... | collective-permute-start | bytes 86024 | tf_op jit(solution)/shard_map/ppermute | solution.py:663
  43.2 5.4 %collective-permute-start.15 = (bf16[592,128]{1,0:T(8,128)(2,1)S(1)}, bf16[592,128]{1,0:T(8,128)(2,1)S(1)}, u32[]{:S(2)}, u32[]{:S(2)}) collective-permute-start(bf16[592,128]{1,0:T(8,128)(2,1)S(1)} %get-tuple-element.108), channel_id=1, source_target_pairs={{0,1},{1,0},{2,3},{3,2},{4,5},{5,4},{6,7},{7,6},{8,9},{9,8},{10,11... | collective-permute-start | bytes 454664 | tf_op jit(solution)/shard_map/ppermute | solution.py:708
  49.7 3.4 %collective-permute-start.16 = (bf16[112,128]{1,0:T(8,128)(2,1)S(1)}, bf16[112,128]{1,0:T(8,128)(2,1)S(1)}, u32[]{:S(2)}, u32[]{:S(2)}) collective-permute-start(bf16[112,128]{1,0:T(8,128)(2,1)S(1)} %get-tuple-element.110), channel_id=1, source_target_pairs={{0,24},{2,26},{4,28},{6,30},{8,16},{10,18},{12,20},{14,22},{16,8},... | collective-permute-start | bytes 86024 | tf_op jit(solution)/shard_map/ppermute | solution.py:663
  49.7 3.3 %collective-permute-start.17 = (bf16[112,128]{1,0:T(8,128)(2,1)S(1)}, bf16[112,128]{1,0:T(8,128)(2,1)S(1)}, u32[]{:S(2)}, u32[]{:S(2)}) collective-permute-start(bf16[112,128]{1,0:T(8,128)(2,1)S(1)} %get-tuple-element.111), channel_id=1, source_target_pairs={{0,8},{2,10},{4,12},{6,14},{8,0},{10,2},{12,4},{14,6},{16,24},{18,... | collective-permute-start | bytes 86024 | tf_op jit(solution)/shard_map/ppermute | solution.py:663
  53.1 3.9 %collective-permute-start.18 = (bf16[112,128]{1,0:T(8,128)(2,1)S(1)}, bf16[112,128]{1,0:T(8,128)(2,1)S(1)}, u32[]{:S(2)}, u32[]{:S(2)}) collective-permute-start(bf16[112,128]{1,0:T(8,128)(2,1)S(1)} %get-tuple-element.114), channel_id=1, source_target_pairs={{0,2},{2,0},{4,6},{6,4},{8,10},{10,8},{12,14},{14,12},{16,18},{18,... | collective-permute-start | bytes 86024 | tf_op jit(solution)/shard_map/ppermute | solution.py:663
  55.1 1.9 %collective-permute-start.19 = (bf16[112,128]{1,0:T(8,128)(2,1)S(1)}, bf16[112,128]{1,0:T(8,128)(2,1)S(1)}, u32[]{:S(2)}, u32[]{:S(2)}) collective-permute-start(bf16[112,128]{1,0:T(8,128)(2,1)S(1)} %get-tuple-element.115), channel_id=1, source_target_pairs={{0,8},{2,4},{4,2},{6,14},{8,0},{10,12},{12,10},{14,6},{16,24},{18,... | collective-permute-start | bytes 86024 | tf_op jit(solution)/shard_map/ppermute | solution.py:663
  57.1 4.2 %collective-permute-start.20 = (bf16[208,128]{1,0:T(8,128)(2,1)S(1)}, bf16[208,128]{1,0:T(8,128)(2,1)S(1)}, u32[]{:S(2)}, u32[]{:S(2)}) collective-permute-start(bf16[208,128]{1,0:T(8,128)(2,1)S(1)} %get-tuple-element.118), channel_id=1, source_target_pairs={{0,1},{1,0},{2,3},{3,2},{4,5},{5,4},{6,7},{7,6},{8,9},{9,8},{10,11... | collective-permute-start | bytes 159752 | tf_op jit(solution)/shard_map/ppermute | solution.py:715
